TPU v7x, 256 devices: a whole 4x4x8 slice. The times are simulated.
256 devices in a mesh: seq: 128 (over z, x_lo, y, core), head: 2 (over x_hi).
Axes of the slice: x: 4 (x_hi: 2, x_lo: 2; x = x_hi * 2 + x_lo), y: 4, z: 8, core: 2. Of those that a mesh axis runs over, the one named last changes fastest.
Arguments:
- queries: bfloat16 [65536, 2, 1024], P('seq', None, 'head'), may hold values from -6 to 6
- key_rows: bfloat16 [65536, 2, 1024], P('seq', None, 'head'), may hold values from -6 to 6
- value_rows: bfloat16 [65536, 2, 1024], P('seq', None, 'head'), may hold values from -32 to 32
- cotangent: bfloat16 [65536, 2, 1024], P('seq', None, 'head'), may hold values from -6 to 6
Outputs:
- normed: bfloat16 [65536, 2, 1024], P('seq', None, 'head')
- grad_queries: bfloat16 [65536, 2, 1024], P('seq', None, 'head')
- grad_keys: bfloat16 [65536, 2, 1024], P('seq', None, 'head')
- grad_values: bfloat16 [65536, 2, 1024], P('seq', None, 'head')
All inputs are finite; a program needn't handle non-finite values.
Results may differ from a plain program's by a relative error of at most 0.018.
Values may be sent and summed in bfloat16 or wider, within the bound.
No kernel may reach another device: no remote copies, remote signals or barrier semaphores. Data moves between devices by JAX's collectives and lax.ppermute only.
A program may use at most 128 MiB of HBM per device.

v0:
```python
import jax
import jax.numpy as jnp
from jax import lax
from jax.sharding import PartitionSpec as P

BLOCK = 512
SUMM = 4
HD = 128
COLS = 1024


epsilon = 1e-06


def softmax_rows(query_grp, key_grp, value_grp, visible):
    scores = jnp.einsum(
        "gqd,gkd->gqk", query_grp, key_grp, preferred_element_type=jnp.float32
    ) * HD ** (-0.5)
    scores = jnp.where(visible, scores, -jnp.inf)
    row_max = jnp.max(scores, axis=-1, keepdims=True)
    expo_rows = jnp.exp(scores - row_max)
    probability = expo_rows / jnp.sum(expo_rows, axis=-1, keepdims=True)
    weights = probability.astype(jnp.bfloat16)
    attended = jnp.einsum(
        "gqk,gkd->gqd", weights, value_grp, preferred_element_type=jnp.float32
    ).astype(jnp.bfloat16)
    return (probability, weights, attended)


def back_scores(key_grp, value_grp, probability, attended, grad_attn):
    grad_prob = jnp.einsum("gqd,gkd->gqk", grad_attn, value_grp, preferred_element_type=jnp.float32)
    row_dot = jnp.sum(
        grad_attn.astype(jnp.float32) * attended.astype(jnp.float32), axis=-1, keepdims=True
    )
    grad_score = (probability * (grad_prob - row_dot) * HD ** (-0.5)).astype(jnp.bfloat16)
    grad_query = jnp.einsum("gqk,gkd->gqd", grad_score, key_grp, preferred_element_type=jnp.float32)
    return (grad_score, grad_query)


def normalize(attn_part, cot_part, square_sum, cross_sum):
    scaling = lax.rsqrt(square_sum / (2 * COLS) + epsilon)[..., None]
    attn_wide = attn_part.astype(jnp.float32)
    normed_part = (attn_wide * scaling).astype(jnp.bfloat16)
    grad_part = (
        scaling * cot_part.astype(jnp.float32)
        - attn_wide * scaling**3 * cross_sum[..., None] / (2 * COLS)
    ).astype(jnp.bfloat16)
    return (normed_part, grad_part)


def head_totals(square_part, cross_part):
    return lax.psum((square_part, cross_part), "head")


def shards(queries, key_rows, value_rows, cotangent):
    tok_rows, kind_count, width = queries.shape
    seq_count = lax.axis_size("seq")
    local_blocks = tok_rows // BLOCK
    all_blocks = local_blocks * seq_count
    offsets = BLOCK // seq_count
    heads_dev = width // HD
    groups = offsets * heads_dev
    fixed_groups = local_blocks * heads_dev
    first_block = lax.axis_index("seq") * local_blocks

    def blocked(array):
        return array.reshape(local_blocks, BLOCK, width)

    def grouped(array):
        return (
            array.reshape(all_blocks, offsets, heads_dev, HD)
            .transpose(1, 2, 0, 3)
            .reshape(groups, all_blocks, HD)
        )

    def ungrouped(array):
        return (
            array.reshape(offsets, heads_dev, all_blocks, HD)
            .transpose(2, 0, 1, 3)
            .reshape(all_blocks, offsets, width)
        )

    def head_major(array):
        return (
            array.reshape(local_blocks, BLOCK, heads_dev, HD)
            .transpose(0, 2, 1, 3)
            .reshape(fixed_groups, BLOCK, HD)
        )

    def token_major(array):
        return (
            array.reshape(local_blocks, heads_dev, BLOCK, HD)
            .transpose(0, 2, 1, 3)
            .reshape(local_blocks, BLOCK, width)
        )

    causal = jnp.tril(jnp.ones((all_blocks, all_blocks), jnp.bool_))[None]
    fixed_query = head_major(queries[:, 1])
    fixed_key = head_major(key_rows[:, 1])
    fixed_value = head_major(value_rows[:, 1])
    summary_keys = blocked(key_rows[:, 1])[:, BLOCK - SUMM :].reshape(local_blocks * SUMM, width)
    summary_values = blocked(value_rows[:, 1])[:, BLOCK - SUMM :].reshape(
        local_blocks * SUMM, width
    )
    all_keys, all_values = (
        lax.all_gather(summary_keys, "seq", axis=0, tiled=True),
        lax.all_gather(summary_values, "seq", axis=0, tiled=True),
    )
    total_summ = all_keys.shape[0]

    def spread(array):
        heads_first = array.reshape(total_summ, heads_dev, HD).transpose(1, 0, 2)
        return heads_first[None].reshape(fixed_groups, total_summ, HD)

    key_cat = jnp.concatenate([fixed_key, spread(all_keys)], 1)
    value_cat = jnp.concatenate([fixed_value, spread(all_values)], 1)
    own_mask = jnp.tril(jnp.ones((BLOCK, BLOCK), jnp.bool_))
    summ_block = jnp.arange(total_summ, dtype=jnp.int32) // SUMM
    earlier = (
        summ_block[None, :] < (first_block + jnp.arange(local_blocks, dtype=jnp.int32))[:, None]
    )
    visible = jnp.concatenate(
        [own_mask[None], jnp.broadcast_to(earlier[:, None, :], (local_blocks, BLOCK, total_summ))],
        2,
    )
    visible = jnp.broadcast_to(
        visible[:, None], (local_blocks, heads_dev, BLOCK, BLOCK + total_summ)
    ).reshape(fixed_groups, BLOCK, BLOCK + total_summ)
    fixed_prob, fixed_weights, fixed_attended = softmax_rows(
        fixed_query, key_cat, value_cat, visible
    )
    fixed_attn = token_major(fixed_attended)
    fixed_cot = blocked(cotangent[:, 1])
    fixed_wide = fixed_attn.astype(jnp.float32)
    fixed_square = jnp.sum(fixed_wide * fixed_wide, axis=-1)
    fixed_cross = jnp.sum(fixed_cot.astype(jnp.float32) * fixed_wide, axis=-1)
    strided_cot = blocked(cotangent[:, 0])
    query_off, key_off, value_off = (
        lax.all_to_all(blocked(queries[:, 0]), "seq", split_axis=1, concat_axis=0, tiled=True),
        lax.all_to_all(blocked(key_rows[:, 0]), "seq", split_axis=1, concat_axis=0, tiled=True),
        lax.all_to_all(blocked(value_rows[:, 0]), "seq", split_axis=1, concat_axis=0, tiled=True),
    )
    query_grp, key_grp, value_grp = (grouped(query_off), grouped(key_off), grouped(value_off))
    strided_prob, strided_weights, strided_attended = softmax_rows(
        query_grp, key_grp, value_grp, causal
    )
    strided_attn = lax.all_to_all(
        ungrouped(strided_attended), "seq", split_axis=0, concat_axis=1, tiled=True
    )
    strided_wide = strided_attn.astype(jnp.float32)
    square_sum, cross_sum = head_totals(
        fixed_square + jnp.sum(strided_wide * strided_wide, axis=-1),
        fixed_cross + jnp.sum(strided_cot.astype(jnp.float32) * strided_wide, axis=-1),
    )
    strided_normed, strided_grad = normalize(strided_attn, strided_cot, square_sum, cross_sum)
    grad_grp = grouped(lax.all_to_all(strided_grad, "seq", split_axis=1, concat_axis=0, tiled=True))
    grad_score, grad_query = back_scores(
        key_grp, value_grp, strided_prob, strided_attended, grad_grp
    )
    grad_key = jnp.einsum("gqk,gqd->gkd", grad_score, query_grp, preferred_element_type=jnp.float32)
    grad_value = jnp.einsum(
        "gqk,gqd->gkd", strided_weights, grad_grp, preferred_element_type=jnp.float32
    )
    grad_query_off = ungrouped(grad_query.astype(jnp.bfloat16))
    grad_key_off = ungrouped(grad_key.astype(jnp.bfloat16))
    grad_value_off = ungrouped(grad_value.astype(jnp.bfloat16))
    strided_gq, strided_gk, strided_gv = (
        lax.all_to_all(grad_query_off, "seq", split_axis=0, concat_axis=1, tiled=True),
        lax.all_to_all(grad_key_off, "seq", split_axis=0, concat_axis=1, tiled=True),
        lax.all_to_all(grad_value_off, "seq", split_axis=0, concat_axis=1, tiled=True),
    )
    fixed_normed, fixed_grad = normalize(fixed_attn, fixed_cot, square_sum, cross_sum)
    fixed_grad_grp = head_major(fixed_grad)
    grad_score, fixed_gq = back_scores(
        key_cat, value_cat, fixed_prob, fixed_attended, fixed_grad_grp
    )
    fixed_gk = jnp.einsum(
        "gqk,gqd->gkd", grad_score[:, :, :BLOCK], fixed_query, preferred_element_type=jnp.float32
    )
    fixed_gv = jnp.einsum(
        "gqk,gqd->gkd",
        fixed_weights[:, :, :BLOCK],
        fixed_grad_grp,
        preferred_element_type=jnp.float32,
    )
    summ_score = grad_score[:, :, BLOCK:].reshape(local_blocks, heads_dev, BLOCK, total_summ)
    summ_weights = fixed_weights[:, :, BLOCK:].reshape(local_blocks, heads_dev, BLOCK, total_summ)
    query_four = fixed_query.reshape(local_blocks, heads_dev, BLOCK, HD)
    grad_four = fixed_grad_grp.reshape(local_blocks, heads_dev, BLOCK, HD)
    key_term = jnp.einsum(
        "bhqs,bhqd->shd", summ_score, query_four, preferred_element_type=jnp.float32
    ).reshape(local_blocks * SUMM * lax.axis_size("seq"), width)
    value_term = jnp.einsum(
        "bhqs,bhqd->shd", summ_weights, grad_four, preferred_element_type=jnp.float32
    ).reshape(local_blocks * SUMM * lax.axis_size("seq"), width)
    summ_grads = lax.psum_scatter(
        jnp.stack([key_term, value_term], 1), "seq", scatter_dimension=0, tiled=True
    )
    summ_grads = summ_grads.reshape(local_blocks, SUMM, 2, width)
    key_total = token_major(fixed_gk).at[:, BLOCK - SUMM :].add(summ_grads[:, :, 0])
    value_total = token_major(fixed_gv).at[:, BLOCK - SUMM :].add(summ_grads[:, :, 1])

    def kinds_stacked(strided_part, fixed_part):
        return jnp.stack(
            [
                strided_part.reshape(tok_rows, width),
                fixed_part.reshape(tok_rows, width).astype(jnp.bfloat16),
            ],
            1,
        )

    return (
        kinds_stacked(strided_normed, fixed_normed),
        kinds_stacked(strided_gq, token_major(fixed_gq)),
        kinds_stacked(strided_gk, key_total),
        kinds_stacked(strided_gv, value_total),
    )


def solution(mesh):
    in_specs = (
        P("seq", None, "head"),
        P("seq", None, "head"),
        P("seq", None, "head"),
        P("seq", None, "head"),
    )
    out_specs = (
        P("seq", None, "head"),
        P("seq", None, "head"),
        P("seq", None, "head"),
        P("seq", None, "head"),
    )
    return jax.shard_map(shards, mesh=mesh, in_specs=in_specs, out_specs=out_specs, check_vma=False)
```

profile of v0, /device:TPU:1, one launch (start us, length us, event | category | flops | bytes accessed | tf_op | source)
XLA Modules:
  0.0 1676.7 jit_solution(17033425150112396349)
XLA Ops:
  7.2 3.3 fusion.72
  12.0 4.6 reduce.22
  16.6 2.2 reshape.725
  18.7 15.3 all-to-all-start
  37.2 1.5 fusion.71
  42.2 160.5 %all-gather = bf16[1,512,512]{2,0,1:T(2,128)(2,1)S(1)} all-gather(bf16[1,4,512]{2,0,1:T(2,128)(2,1)S(1)} %copy.180), channel_id=2, replica_groups=mesh['seq'=128,'head'=2] {'seq'}, dimensions={1}, use_global_device_ids=true | all-gather | bytes 528384 | tf_op jit(solution)/shard_map/all_gather | solution.py:106
  202.7 1.5 copy.181
  206.0 3.8 reduce.23
  210.9 1.5 fusion.73
  213.6 4.6 reduce.21
  218.1 2.2 reshape.723
  220.4 154.1 %all-gather.1 = bf16[1,512,512]{2,0,1:T(2,128)(2,1)S(1)} all-gather(bf16[1,4,512]{2,0,1:T(2,128)(2,1)S(1)} %copy.187), channel_id=3, replica_groups=mesh['seq'=128,'head'=2] {'seq'}, dimensions={1}, use_global_device_ids=true | all-gather | bytes 528384 | tf_op jit(solution)/shard_map/all_gather | solution.py:107
  374.5 7.2 all-to-all-start.1
  382.8 2.0 slice_convert_fusion
  384.8 7.8 fusion.75
  392.6 7.9 all-to-all-done.1
  400.5 7.1 all-to-all-start.2
  407.6 2.3 copy.186
  409.9 3.6 copy.199
  413.5 2.3 copy.188
  415.8 3.6 reshape.726
  419.3 3.1 bitcast_reduce_fusion.2
  423.5 3.6 reshape.728
  427.1 3.1 bitcast_reduce_fusion.1
  430.4 1.7 fusion.21
  433.5 3.7 reshape.724
  437.2 3.9 bitcast_reduce_fusion.3
  444.4 12.7 all-to-all-start.3
  457.1 4.7 fusion.7
  463.8 1.9 copy.191
  465.7 10.5 all-to-all-done.3
  477.0 2.4 reshape.699
  479.4 5.7 fusion.27
  485.1 5.3 all-reduce.1
  490.4 4.4 fusion.80
  494.8 1.6 multiply_reduce_fusion
  496.4 4.7 reduce.24
  502.3 7.0 all-to-all-start.4
  509.3 6.0 multiply_convert_fusion
  515.2 13.2 all-to-all-done.4
  528.9 3.1 bitcast_reduce_fusion
  532.6 2.2 convolution_convert_fusion.2
  536.0 6.5 all-to-all-start.7
  542.5 3.4 fusion.12
  545.9 1.6 copy.215
  547.5 2.6 fusion.10
  551.3 1.5 fusion.81
  552.9 3.4 convolution_convert_fusion.5
  556.3 2.3 copy.255
  558.6 2.9 all-to-all-done.7
  561.4 10.0 all-to-all-start.5
  571.5 2.7 pad_maximum_fusion
  576.2 2.0 copy.223
  578.3 1.8 convolution_convert_fusion.3
  581.3 8.9 all-to-all-done.5
  590.2 5.8 all-to-all-start.6
  596.1 3.3 convolution_convert_fusion.4
  599.7 2.4 fusion.14
  602.5 2.4 fusion.8
  606.7 2.0 copy.224
  609.9 5.3 all-to-all-done.6
  615.4 1049.2 %all-reduce.4.cloned.1.call-done = f32[512,2,512]{2,0,1:T(8,128)} async-done(((f32[512,2,512]{2,0,1:T(8,128)}), f32[512,2,512]{2,0,1:T(8,128)}) %all-reduce.4.cloned.1.call-update) | async-done | bytes 2097168
  1665.5 2.0 copy.226
  1667.6 2.0 copy.225
  (119 shorter events, 34.0 us)
Async XLA Ops:
  10.6 26.6 %copy-start.4 = (bf16[512,2,512]{2,1,0:T(2,128)(2,1)S(1)}, bf16[512,2,512]{2,1,0:T(2,128)(2,1)}, u32[]{:S(2)}) copy-start(bf16[512,2,512]{2,1,0:T(2,128)(2,1)} %param.9) | copy-start | bytes 3145732
  18.7 355.8 %all-to-all-start = ((bf16[128,2,1024]{2,1,0:T(2,128)(2,1)}), bf16[128,2,1024]{2,1,0:T(2,128)(2,1)}, u32[]{:S(2)}, u32[]{:S(2)}) async-start(bf16[128,2,1024]{2,1,0:T(2,128)(2,1)} %reshape.725), calls=%async_computation | async-start | bytes 1048576 | tf_op jit(solution)/shard_map/all_to_all | solution.py:139
  35.4 0.8 copy-start.7
  41.1 164.1 %copy-start.12 = (bf16[1,512,512]{2,1,0:T(8,128)(2,1)S(1)}, bf16[1,512,512]{2,1,0:T(8,128)(2,1)}, u32[]{:S(2)}) copy-start(bf16[1,512,512]{2,1,0:T(8,128)(2,1)} %get-tuple-element.65) | copy-start | bytes 1572868
  42.1 168.8 %copy-start.5 = (bf16[512,2,512]{2,1,0:T(2,128)(2,1)S(1)}, bf16[512,2,512]{2,1,0:T(2,128)(2,1)}, u32[]{:S(2)}) copy-start(bf16[512,2,512]{2,1,0:T(2,128)(2,1)} %param.10) | copy-start | bytes 3145732
  212.7 170.1 %copy-start = (bf16[512,2,512]{2,1,0:T(2,128)(2,1)S(1)}, bf16[512,2,512]{2,1,0:T(2,128)(2,1)}, u32[]{:S(2)}) copy-start(bf16[512,2,512]{2,1,0:T(2,128)(2,1)} %param.11) | copy-start | bytes 3145732
  374.5 26.0 %all-to-all-start.1 = ((bf16[128,2,1024]{2,1,0:T(2,128)(2,1)}), bf16[128,2,1024]{2,1,0:T(2,128)(2,1)}, u32[]{:S(2)}, u32[]{:S(2)}) async-start(bf16[128,2,1024]{2,1,0:T(2,128)(2,1)} %reshape.727), calls=%async_computation.1 | async-start | bytes 1048576 | tf_op jit(solution)/shard_map/all_to_all | solution.py:140
  400.5 32.9 %all-to-all-start.2 = ((bf16[128,2,1024]{2,1,0:T(2,128)(2,1)}), bf16[128,2,1024]{2,1,0:T(2,128)(2,1)}, u32[]{:S(2)}, u32[]{:S(2)}) async-start(bf16[128,2,1024]{2,1,0:T(2,128)(2,1)} %reshape.723), calls=%async_computation.2 | async-start | bytes 1048576 | tf_op jit(solution)/shard_map/all_to_all | solution.py:141
  430.4 3.0 copy-start.14
  432.2 11.0 copy-start.6
  442.7 19.0 %copy-start.15 = (bf16[4,4,128,128]{2,3,1,0:T(8,128)(2,1)}, bf16[4,4,128,128]{2,3,1,0:T(8,128)(2,1)S(1)}, u32[]{:S(2)}) copy-start(bf16[4,4,128,128]{2,3,1,0:T(8,128)(2,1)S(1)} %copy.174) | copy-start | bytes 1572868
  443.2 18.6 %copy-start.23 = (bf16[16,128,128]{1,2,0:T(8,128)(2,1)}, bf16[16,128,128]{1,2,0:T(8,128)(2,1)S(1)}, u32[]{:S(2)}) copy-start(bf16[16,128,128]{1,2,0:T(8,128)(2,1)S(1)} %convolution_convert_fusion.1) | copy-start | bytes 1572868
  444.4 31.8 %all-to-all-start.3 = ((bf16[128,4,512]{2,1,0:T(4,128)(2,1)}), bf16[128,4,512]{2,1,0:T(4,128)(2,1)S(1)}, u32[]{:S(2)}, u32[]{:S(2)}) async-start(bf16[128,4,512]{2,1,0:T(4,128)(2,1)} %copy.248), calls=%async_computation.3 | async-start | bytes 1048576 | tf_op jit(solution)/shard_map/all_to_all | solution.py:147
  457.1 4.7 copy-start.20
  457.1 4.7 copy-start.22
  461.8 2.0 copy-start.1
  476.1 0.8 copy-start.2
  494.8 14.4 copy-start.21
  496.4 18.8 %copy-start.10 = (bf16[4,512,128]{1,2,0:T(8,128)(2,1)}, bf16[4,512,128]{1,2,0:T(8,128)(2,1)S(1)}, u32[]{:S(2)}) copy-start(bf16[4,512,128]{1,2,0:T(8,128)(2,1)S(1)} %get-tuple-element.45) | copy-start | bytes 1572868
  502.3 26.2 %all-to-all-start.4 = ((bf16[128,2,1024]{2,1,0:T(2,128)(2,1)}), bf16[128,2,1024]{2,1,0:T(2,128)(2,1)S(1)}, u32[]{:S(2)}, u32[]{:S(2)}) async-start(bf16[128,2,1024]{2,1,0:T(2,128)(2,1)} %reshape.729), calls=%async_computation.4 | async-start | bytes 1048576 | tf_op jit(solution)/shard_map/all_to_all | solution.py:156
  532.1 10.4 copy-start.8
  532.6 13.3 copy-start.16
  536.0 25.4 %all-to-all-start.7 = ((bf16[128,4,512]{2,1,0:T(4,128)(2,1)}), bf16[128,4,512]{2,1,0:T(4,128)(2,1)}, u32[]{:S(2)}, u32[]{:S(2)}) async-start(bf16[128,4,512]{2,1,0:T(4,128)(2,1)} %copy.263), calls=%async_computation.7 | async-start | bytes 1048576 | tf_op jit(solution)/shard_map/all_to_all | solution.py:170
  552.9 8.5 copy-start.18
  561.4 28.8 %all-to-all-start.5 = ((bf16[128,4,512]{2,1,0:T(4,128)(2,1)}), bf16[128,4,512]{2,1,0:T(4,128)(2,1)}, u32[]{:S(2)}, u32[]{:S(2)}) async-start(bf16[128,4,512]{2,1,0:T(4,128)(2,1)} %copy.255), calls=%async_computation.5 | async-start | bytes 1048576 | tf_op jit(solution)/shard_map/all_to_all | solution.py:168
  571.4 3.2 copy-start.24
  571.4 4.4 copy-start.3
  571.4 1093.2 %all-reduce.4.cloned.1.call-start = ((), (), s32[]{:S(2)}) async-start(), calls=%async_computation.8 | async-start | bytes 4194304
  575.8 2.5 copy-start.13
  576.1 2.2 copy-start.17
  576.1 2.2 copy-start.19
  590.2 25.0 %all-to-all-start.6 = ((bf16[128,4,512]{2,1,0:T(4,128)(2,1)}), bf16[128,4,512]{2,1,0:T(4,128)(2,1)S(1)}, u32[]{:S(2)}, u32[]{:S(2)}) async-start(bf16[128,4,512]{2,1,0:T(4,128)(2,1)} %copy.258), calls=%async_computation.6 | async-start | bytes 1048576 | tf_op jit(solution)/shard_map/all_to_all | solution.py:169
  596.1 3.6 copy-start.9
  599.4 3.1 copy-start.11
Sparse Core Ops, SparseCore 0:
  574.9 1089.6 all-reduce.3
where the time goes:
time: 1690 us; the launch traced here: 1680 us
  waiting for transfers between devices  1100 us (65%)
  blocking collectives  320 us (19%)
  local copies, waits for them, and re-layouts  89.8 us (5%)
  starting transfers between devices  71.5 us (4%)
  other arithmetic  42.2 us (2%)
  matrix products  39.7 us (2%)
    unnamed x2, waiting for transfers between devices  1050 us
    all_gather x1, blocking collectives, shards(): lax.all_gather(summary_keys, 'seq', axis=0, tiled=True)  161 us
    all_gather x1, blocking collectives, shards(): lax.all_gather(summary_values, 'seq', axis=0, tiled=True)  154 us
  transfers between devices with their start and end apart: 9, of which 7 were waited for; matrix products, arithmetic and copies ran while one was open for 7% of the time, Pallas kernels for 0%

commit v1 on v0

v1 whole, which is shorter than its diff:
```python
import jax
import jax.numpy as jnp
from jax import lax
from jax.experimental import pallas as pl
from jax.experimental.pallas import tpu as pltpu
from jax.sharding import PartitionSpec as P

BLOCK = 512
SUMM = 4
HD = 128
COLS = 1024
NB = 128
HEADS = 4
OFFS = 4
WIDTH = HEADS * HD
PARTS = (8, 2, 4, 2)

epsilon = 1e-06
scale = HD ** (-0.5)
F32 = jnp.float32
BF16 = jnp.bfloat16


def iotas(shape):
    return (
        lax.broadcasted_iota(jnp.int32, shape, 0),
        lax.broadcasted_iota(jnp.int32, shape, 1),
    )


def one_hot(hit):
    return jnp.where(hit, 1.0, 0.0).astype(BF16)


def dot(a, b):
    return jnp.dot(a, b, preferred_element_type=F32)


def dot_nt(a, b):
    return lax.dot_general(a, b, (((1,), (1,)), ((), ())), preferred_element_type=F32)


def dot_tn(a, b):
    return lax.dot_general(a, b, (((0,), (0,)), ((), ())), preferred_element_type=F32)


def call(kernel, grid, in_specs, out_specs, out_shape, flops, nbytes, scratch=(), vmem=60):
    return pl.pallas_call(
        kernel,
        grid=(grid,),
        in_specs=in_specs,
        out_specs=out_specs,
        out_shape=out_shape,
        scratch_shapes=list(scratch),
        compiler_params=pltpu.CompilerParams(vmem_limit_bytes=vmem * 2**20),
        cost_estimate=pl.CostEstimate(flops=flops, bytes_accessed=nbytes, transcendentals=0),
    )


def spec(block, *index):
    return pl.BlockSpec(block, lambda i: tuple(i if at == "i" else at for at in index))


def pack_strided_kernel(q_ref, k_ref, v_ref, c_ref, send_ref, pick_ref):
    @pl.when(pl.program_id(0) == 0)
    def _():
        row, col = iotas((256, 512))
        home, array, offset = row >> 4, (row >> 2) & 3, row & 3
        pick_ref[...] = one_hot(col == array * 128 + (home * OFFS + offset) * 2)

    rows = jnp.concatenate(
        [ref[...].reshape(128, WIDTH) for ref in (q_ref, k_ref, v_ref, c_ref)], 0
    )
    send_ref[...] = dot(pick_ref[...], rows).astype(BF16).reshape(16, 16, WIDTH)


def pack_strided(arrays):
    return call(
        pack_strided_kernel,
        8,
        [spec((64, 2, WIDTH), "i", 0, 0)] * 4,
        spec((16, 16, WIDTH), "i", 0, 0),
        jax.ShapeDtypeStruct((NB, 16, WIDTH), BF16),
        10**9,
        6 * 2**20,
        [pltpu.VMEM((256, 512), BF16)],
    )(*arrays)


def pack_fixed_kernel(q_ref, k_ref, v_ref, c_ref, out_ref):
    row, col = iotas((64, 128))
    pick = one_hot(col == 2 * row + 1)
    for at, ref in enumerate((q_ref, k_ref, v_ref, c_ref)):
        out_ref[at] = dot(pick, ref[...].reshape(128, WIDTH)).astype(BF16)


def pack_fixed(arrays):
    return call(
        pack_fixed_kernel,
        8,
        [spec((64, 2, WIDTH), "i", 0, 0)] * 4,
        spec((4, 64, WIDTH), 0, "i", 0),
        jax.ShapeDtypeStruct((4, BLOCK, WIDTH), BF16),
        10**9,
        6 * 2**20,
    )(*arrays)


def fixed_probabilities(query, key, summ_key, seen):
    row, col = iotas((BLOCK, BLOCK))
    own = jnp.where(col <= row, dot_nt(query, key) * scale, -jnp.inf)
    far = jnp.where(seen > 0, dot_nt(query, summ_key) * scale, -jnp.inf)
    top = jnp.maximum(
        jnp.max(own, axis=-1, keepdims=True), jnp.max(far, axis=-1, keepdims=True)
    )
    own = jnp.exp(own - top)
    far = jnp.exp(far - top)
    total = jnp.sum(own, axis=-1, keepdims=True) + jnp.sum(far, axis=-1, keepdims=True)
    inverse = 1.0 / total
    return own * inverse, far * inverse


def fixed_forward_kernel(rows_ref, summ_ref, seen_ref, attn_ref, sums_ref):
    own, far = fixed_probabilities(rows_ref[0], rows_ref[1], summ_ref[:, :HD], seen_ref[...])
    attn = (
        dot(own.astype(BF16), rows_ref[2]) + dot(far.astype(BF16), summ_ref[:, HD:])
    ).astype(BF16)
    attn_ref[...] = attn
    wide = attn.astype(F32)
    square = jnp.sum(wide * wide, axis=-1, keepdims=True)
    cross = jnp.sum(wide * rows_ref[3].astype(F32), axis=-1, keepdims=True)
    lane = lax.broadcasted_iota(jnp.int32, (BLOCK, 8), 1)
    part = jnp.where(lane == 0, square, jnp.where(lane == 1, cross, 0.0))

    @pl.when(pl.program_id(0) == 0)
    def _():
        sums_ref[...] = part

    @pl.when(pl.program_id(0) > 0)
    def _():
        sums_ref[...] += part


def fixed_forward(rows, summ, seen):
    return call(
        fixed_forward_kernel,
        HEADS,
        [
            spec((4, BLOCK, HD), 0, 0, "i"),
            spec((BLOCK, 2 * HD), 0, "i"),
            spec((1, BLOCK), 0, 0),
        ],
        [spec((BLOCK, HD), 0, "i"), spec((BLOCK, 8), 0, 0)],
        [
            jax.ShapeDtypeStruct((BLOCK, WIDTH), BF16),
            jax.ShapeDtypeStruct((BLOCK, 8), F32),
        ],
        4 * 10**9,
        4 * 2**20,
    )(rows, summ, seen)


def swap_matrix():
    row, col = iotas((256, 256))
    return one_hot(col == ((row & 15) << 4) + (row >> 4))


def strided_forward_kernel(recv_ref, fixed_ref, grp_ref, attn_ref, prob_ref, sums_ref):
    swap = swap_matrix()
    for at in range(0, NB, 16):
        rows = recv_ref[at : at + 16].reshape(256, HD)
        grp_ref[0, :, :, at : at + 16, :] = (
            dot(swap, rows).astype(BF16).reshape(4, OFFS, 16, HD)
        )
    row, col = iotas((NB, NB))
    lane = lax.broadcasted_iota(jnp.int32, (NB, 16), 1)
    part = jnp.zeros((NB, 16), F32)
    for at in range(OFFS):
        scores = jnp.where(col <= row, dot_nt(grp_ref[0, 0, at], grp_ref[0, 1, at]) * scale, -jnp.inf)
        expo = jnp.exp(scores - jnp.max(scores, axis=-1, keepdims=True))
        prob = expo * (1.0 / jnp.sum(expo, axis=-1, keepdims=True))
        attn = dot(prob.astype(BF16), grp_ref[0, 2, at]).astype(BF16)
        prob_ref[0, at] = prob
        attn_ref[0, at] = attn
        wide = attn.astype(F32)
        square = jnp.sum(wide * wide, axis=-1, keepdims=True)
        cross = jnp.sum(wide * grp_ref[0, 3, at].astype(F32), axis=-1, keepdims=True)
        part += jnp.where(lane == 8 + at, square, jnp.where(lane == 12 + at, cross, 0.0))

    @pl.when(pl.program_id(0) == 0)
    def _():
        sums_ref[...] = fixed_ref[...] + part

    @pl.when(pl.program_id(0) > 0)
    def _():
        sums_ref[...] += part


def strided_forward(recv, fixed_sums):
    return call(
        strided_forward_kernel,
        HEADS,
        [spec((NB, 16, HD), 0, 0, "i"), spec((NB, 16), 0, 0)],
        [
            spec((1, 4, OFFS, NB, HD), "i", 0, 0, 0, 0),
            spec((1, OFFS, NB, HD), "i", 0, 0, 0),
            spec((1, OFFS, NB, NB), "i", 0, 0, 0),
            spec((NB, 16), 0, 0),
        ],
        [
            jax.ShapeDtypeStruct((HEADS, 4, OFFS, NB, HD), BF16),
            jax.ShapeDtypeStruct((HEADS, OFFS, NB, HD), BF16),
            jax.ShapeDtypeStruct((HEADS, OFFS, NB, NB), F32),
            jax.ShapeDtypeStruct((NB, 16), F32),
        ],
        10**9,
        6 * 2**20,
    )(recv, fixed_sums)


def normalize(wide, cotangent, square, cross):
    scaling = lax.rsqrt(square / (2 * COLS) + epsilon)
    normed = (wide * scaling).astype(BF16)
    grad = (
        scaling * cotangent.astype(F32) - wide * (scaling * scaling * scaling * cross / (2 * COLS))
    ).astype(BF16)
    return normed, grad, jnp.sum(grad.astype(F32) * wide, axis=-1, keepdims=True)


def strided_backward_kernel(grp_ref, attn_ref, prob_ref, mine_ref, other_ref, send_ref, out_ref):
    total = mine_ref[...] + other_ref[...]
    for at in range(OFFS):
        wide = attn_ref[0, at].astype(F32)
        normed, grad, row_dot = normalize(
            wide, grp_ref[0, 3, at], total[:, at : at + 1], total[:, 4 + at : 5 + at]
        )
        prob = prob_ref[0, at]
        grad_prob = dot_nt(grad, grp_ref[0, 2, at])
        grad_score = (prob * (grad_prob - row_dot) * scale).astype(BF16)
        out_ref[0, at] = normed
        out_ref[1, at] = dot(grad_score, grp_ref[0, 1, at]).astype(BF16)
        out_ref[2, at] = dot_tn(grad_score, grp_ref[0, 0, at]).astype(BF16)
        out_ref[3, at] = dot_tn(prob.astype(BF16), grad).astype(BF16)
    swap = swap_matrix()
    for at in range(0, NB, 16):
        rows = out_ref[:, :, at : at + 16, :].reshape(256, HD)
        send_ref[at : at + 16] = dot(swap, rows).astype(BF16).reshape(16, 16, HD)


def strided_backward(grp, attn, prob, mine, other):
    return call(
        strided_backward_kernel,
        HEADS,
        [
            spec((1, 4, OFFS, NB, HD), "i", 0, 0, 0, 0),
            spec((1, OFFS, NB, HD), "i", 0, 0, 0),
            spec((1, OFFS, NB, NB), "i", 0, 0, 0),
            spec((NB, 16), 0, 0),
            spec((NB, 16), 0, 0),
        ],
        spec((NB, 16, HD), 0, 0, "i"),
        jax.ShapeDtypeStruct((NB, 16, WIDTH), BF16),
        10**9,
        6 * 2**20,
        [pltpu.VMEM((4, OFFS, NB, HD), BF16)],
    )(grp, attn, prob, mine, other)


def fixed_backward_kernel(rows_ref, summ_ref, seen_ref, attn_ref, sums_ref, out_ref, part_ref):
    query, key, value = rows_ref[0], rows_ref[1], rows_ref[2]
    summ_key, summ_value = summ_ref[:, :HD], summ_ref[:, HD:]
    own, far = fixed_probabilities(query, key, summ_key, seen_ref[...])
    wide = attn_ref[...].astype(F32)
    normed, grad, row_dot = normalize(wide, rows_ref[3], sums_ref[:, 0:1], sums_ref[:, 1:2])
    out_ref[0] = normed
    own_score = (own * (dot_nt(grad, value) - row_dot) * scale).astype(BF16)
    far_score = (far * (dot_nt(grad, summ_value) - row_dot) * scale).astype(BF16)
    out_ref[1] = (dot(own_score, key) + dot(far_score, summ_key)).astype(BF16)
    grad_key = dot_tn(own_score, query)
    grad_value = dot_tn(own.astype(BF16), grad)
    out_ref[2] = grad_key.astype(BF16)
    out_ref[3] = grad_value.astype(BF16)
    part_ref[:, :HD] = dot_tn(far_score, query)
    part_ref[:, HD:] = dot_tn(far.astype(BF16), grad)
    row = lax.broadcasted_iota(jnp.int32, (8, HD), 0)
    for at, grads in ((0, grad_key), (HD, grad_value)):
        tail = pltpu.roll(grads[BLOCK - 8 :], SUMM, 0)
        part_ref[0:8, at : at + HD] += jnp.where(row < SUMM, tail, 0.0)


def fixed_backward(rows, summ, seen, attn, sums):
    return call(
        fixed_backward_kernel,
        HEADS,
        [
            spec((4, BLOCK, HD), 0, 0, "i"),
            spec((BLOCK, 2 * HD), 0, "i"),
            spec((1, BLOCK), 0, 0),
            spec((BLOCK, HD), 0, "i"),
            spec((BLOCK, 2), 0, 0),
        ],
        [spec((4, BLOCK, HD), 0, 0, "i"), spec((BLOCK, 2 * HD), 0, "i")],
        [
            jax.ShapeDtypeStruct((4, BLOCK, WIDTH), BF16),
            jax.ShapeDtypeStruct((BLOCK, 2 * WIDTH), F32),
        ],
        8 * 10**9,
        8 * 2**20,
    )(rows, summ, seen, attn, sums)


def unpack_kernel(recv_ref, fixed_ref, *refs):
    out_refs, pick_ref = refs[:4], refs[4]

    @pl.when(pl.program_id(0) == 0)
    def _():
        row, col = iotas((512, 512))
        array, token, kind = row >> 7, (row & 127) >> 1, row & 1
        strided = ((token >> 2) << 4) + array * OFFS + (token & 3)
        fixed = 256 + array * 64 + token
        pick_ref[...] = one_hot(col == jnp.where(kind == 0, strided, fixed))

    rows = jnp.concatenate(
        [recv_ref[...].reshape(256, WIDTH), fixed_ref[...].reshape(256, WIDTH)], 0
    )
    for at, ref in enumerate(out_refs):
        picked = dot(pick_ref[at * 128 : (at + 1) * 128], rows).astype(BF16)
        ref[...] = picked.reshape(64, 2, WIDTH)


def unpack(recv, fixed):
    return call(
        unpack_kernel,
        8,
        [spec((16, 16, WIDTH), "i", 0, 0), spec((4, 64, WIDTH), 0, "i", 0)],
        [spec((64, 2, WIDTH), "i", 0, 0)] * 4,
        [jax.ShapeDtypeStruct((BLOCK, 2, WIDTH), BF16)] * 4,
        2 * 10**9,
        8 * 2**20,
        [pltpu.VMEM((512, 512), BF16)],
    )(recv, fixed)


def place(index):
    coords = []
    for size in PARTS[::-1]:
        coords.append(index % size)
        index = index // size
    return coords[::-1]


def joined(coords):
    index = 0
    for size, at in zip(PARTS, coords):
        index = index * size + at
    return index


def shift(array, part, step):
    perm = []
    for source in range(NB):
        coords = place(source)
        coords[part] = (coords[part] + step) % PARTS[part]
        perm.append((source, joined(coords)))
    return lax.ppermute(array, "seq", perm)


ROUNDS = (
    ((0, 1, 1), (0, -1, 1)),
    ((0, 3, 3), (0, -3, 2)),
    ((2, 1, 8), (2, -1, 8), (2, 2, 8)),
    ((1, 1, 32),),
    ((3, 1, 64),),
)


def gather_summaries(held, rounds):
    for steps in rounds:
        moved = [shift(held[: slots * SUMM], part, step) for part, step, slots in steps]
        held = jnp.concatenate([held] + moved, 0)
    return held


def scatter_summaries(parts):
    for steps in ROUNDS[::-1]:
        kept = parts.shape[0] - SUMM * sum(slots for _, _, slots in steps)
        total, at = parts[:kept], kept
        for part, step, slots in steps:
            rows = slots * SUMM
            moved = shift(parts[at : at + rows].astype(BF16), part, -step).astype(F32)
            total = total + jnp.pad(moved, ((0, kept - rows), (0, 0)))
            at += rows
        parts = total
    return parts


def slot_blocks(me):
    back = [(0,) * len(PARTS)]
    for steps in ROUNDS:
        back = back + [
            tuple(by + step * (at == part) for at, by in enumerate(slot))
            for part, step, slots in steps
            for slot in back[:slots]
        ]
    back = jnp.array(back, jnp.int32)
    coords = [(at - back[:, n]) % size for n, (at, size) in enumerate(zip(place(me), PARTS))]
    return joined(coords)


def shards(queries, key_rows, value_rows, cotangent):
    me = lax.axis_index("seq")
    arrays = (queries, key_rows, value_rows, cotangent)
    send = pack_strided(arrays)
    tails = [a[BLOCK - SUMM :, 1].reshape(SUMM, HEADS, 1, HD) for a in (key_rows, value_rows)]
    own_summ = jnp.concatenate(tails, 2).reshape(SUMM, 2 * WIDTH)
    summ = gather_summaries(own_summ, ROUNDS[:2])
    send, summ = lax.optimization_barrier((send, summ))
    recv = lax.all_to_all(send, "seq", 0, 0, tiled=True)
    summ = gather_summaries(summ, ROUNDS[2:])
    seen = jnp.repeat((slot_blocks(me) < me).astype(jnp.int32), SUMM)[None]
    rows = pack_fixed(arrays)
    fixed_attn, fixed_sums = fixed_forward(rows, summ, seen)
    fixed_send = fixed_sums[:, :2].reshape(NB, OFFS, 2).transpose(0, 2, 1).reshape(NB, 8)
    fixed_send = jnp.pad(fixed_send, ((0, 0), (0, 8)))
    grp, attn, prob, sums = strided_forward(recv, fixed_send)
    sums_other = lax.ppermute(sums, "head", [(0, 1), (1, 0)])
    sums_both = jnp.broadcast_to(sums[:, None], (NB, 2, 16)).reshape(2 * NB, 16)
    sums_in = lax.all_to_all(sums_both, ("seq", "head"), 0, 0, tiled=True).reshape(NB, 2, 16)
    mine = jnp.sum(sums_in, 1)
    other = sums + sums_other
    other = jnp.concatenate([other[:, 8:], other[:, :8]], 1)
    send_back = strided_backward(grp, attn, prob, mine, other)
    recv_back = lax.all_to_all(send_back, "seq", 0, 0, tiled=True)
    block_sums = (mine + other)[:, 8:].reshape(NB, 2, OFFS).transpose(0, 2, 1).reshape(BLOCK, 2)
    fixed_out, parts = fixed_backward(rows, summ, seen, fixed_attn, block_sums)
    totals = scatter_summaries(parts).astype(BF16).reshape(SUMM, HEADS, 2, HD)
    totals = totals.transpose(2, 0, 1, 3).reshape(2, SUMM, WIDTH)
    fixed_out = lax.dynamic_update_slice(fixed_out, totals, (2, BLOCK - SUMM, 0))
    return tuple(unpack(recv_back, fixed_out))


def solution(mesh):
    specs = (P("seq", None, "head"),) * 4
    return jax.shard_map(shards, mesh=mesh, in_specs=specs, out_specs=specs, check_vma=False)
```

time: 1690 us -> 201 us (0.12)
  waiting for transfers between devices: 1100 us -> 63.5 us
  blocking collectives: 320 us -> 0 us
  local copies, waits for them, and re-layouts: 89.8 us -> 13.4 us
  Pallas kernels: 0 us -> 57.9 us
  matrix products: 39.7 us -> 0 us
  other arithmetic: 42.2 us -> 3.31 us
    unnamed x2 -> x0, waiting for transfers between devices: 1050 us -> none
    all_gather x2 -> x0, blocking collectives: 315 us -> none  [the longest x1 161 us: shards(): lax.all_gather(summary_keys, 'seq', axis=0, tiled=True)]
    pallas_call x0 -> x7, Pallas kernels: none -> 57.9 us  [the longest x1 10.5 us: fixed_backward(): call(fixed_backward_kernel, HEADS, [spec((4, BLOCK, HD), 0, 0, 'i'), spec...]
    all_to_all x8 -> x3, starting transfers between devices: 71.5 us -> 24.8 us  [the longest x1 11.9 us: shards(): recv = lax.all_to_all(send, 'seq', 0, 0, tiled=True)]
    ppermute x0 -> x19, waiting for transfers between devices: none -> 45 us  [the longest x18 45 us: shift(): return lax.ppermute(array, 'seq', perm)]
    ppermute x0 -> x19, starting transfers between devices: none -> 35.4 us  [the longest x18 32.7 us: shift(): return lax.ppermute(array, 'seq', perm)]
    dot_general x13 -> x0, matrix products: 31.9 us -> none  [the longest x2 7.52 us: back_scores(): jnp.einsum('gqd,gkd->gqk', grad_attn, value_grp, preferred_element_type=j...]
    all_to_all x8 -> x3, waiting for transfers between devices: 48.7 us -> 18.5 us  [the longest x1 11.1 us: shards(): lax.all_to_all(sums_both, ('seq', 'head'), 0, 0, tiled=True)]
  transfers between devices with their start and end apart: 9 -> 22, of which waited for: 7 -> 15; matrix products, arithmetic and copies ran while one was open for 7% -> 6% of each run, Pallas kernels for 0% -> 17%
where the time goes in v1:
time: 201 us; the launch traced here: 199 us
  waiting for transfers between devices  63.5 us (32%)
  starting transfers between devices  60.2 us (30%)
  Pallas kernels  57.9 us (29%)
  local copies, waits for them, and re-layouts  13.4 us (7%)
  other arithmetic  3.31 us (2%)
    ppermute x18, waiting for transfers between devices, shift(): return lax.ppermute(array, 'seq', perm)  45 us
    ppermute x18, starting transfers between devices, shift(): return lax.ppermute(array, 'seq', perm)  32.7 us
    all_to_all x1, starting transfers between devices, shards(): recv = lax.all_to_all(send, 'seq', 0, 0, tiled=True)  11.9 us
    all_to_all x1, waiting for transfers between devices, shards(): lax.all_to_all(sums_both, ('seq', 'head'), 0, 0, tiled=True)  11.1 us
    pallas_call x1, Pallas kernels, fixed_backward(): call(fixed_backward_kernel, HEADS, [spec((4, BLOCK, HD), 0, 0, 'i'), spec...  10.5 us
    pallas_call x1, Pallas kernels, fixed_forward(): call(fixed_forward_kernel, HEADS, [spec((4, BLOCK, HD), 0, 0, 'i'), spec(...  8.64 us
    pallas_call x1, Pallas kernels, strided_forward(): call(strided_forward_kernel, HEADS, [spec((NB, 16, HD), 0, 0, 'i'), spec(...  8.5 us
    pallas_call x1, Pallas kernels, strided_backward(): call(strided_backward_kernel, HEADS, [spec((1, 4, OFFS, NB, HD), 'i', 0,...  8.34 us
  transfers between devices with their start and end apart: 22, of which 15 were waited for; matrix products, arithmetic and copies ran while one was open for 6% of the time, Pallas kernels for 17%

profile of v1, /device:TPU:1, one launch (start us, length us, event | category | flops | bytes accessed | tf_op | source)
XLA Modules:
  0.0 199.2 jit_solution(8098198812470415688)
XLA Ops:
  0.6 0.7 slice_reduce_fusion.1
  1.4 0.7 slice_reduce_fusion
  2.2 2.5 %collective-permute-start = (bf16[4,1024]{1,0:T(4,128)(2,1)S(1)}, bf16[4,1024]{1,0:T(4,128)(2,1)S(1)}, u32[]{:S(2)}, u32[]{:S(2)}) collective-permute-start(bf16[4,1024]{1,0:T(4,128)(2,1)S(1)} %reshape.46), channel_id=1, source_target_pairs={{0,32},{2,34},{4,36},{6,38},{8,40},{10,42},{12,44},{14,46},{16,48}... | collective-permute-start | bytes 24584 | tf_op jit(solution)/shard_map/ppermute | solution.py:365
  4.7 4.0 %collective-permute-start.1 = (bf16[4,1024]{1,0:T(4,128)(2,1)S(1)}, bf16[4,1024]{1,0:T(4,128)(2,1)S(1)}, u32[]{:S(2)}, u32[]{:S(2)}) collective-permute-start(bf16[4,1024]{1,0:T(4,128)(2,1)S(1)} %reshape.46), channel_id=1, source_target_pairs={{0,224},{2,226},{4,228},{6,230},{8,232},{10,234},{12,236},{14,238}... | collective-permute-start | bytes 24584 | tf_op jit(solution)/shard_map/ppermute | solution.py:365
  8.7 1.0 collective-permute-done
  9.7 2.4 %collective-permute-start.3 = (bf16[8,1024]{1,0:T(8,128)(2,1)S(1)}, bf16[8,1024]{1,0:T(8,128)(2,1)S(1)}, u32[]{:S(2)}, u32[]{:S(2)}) collective-permute-start(bf16[8,1024]{1,0:T(8,128)(2,1)S(1)} %pad_maximum_fusion.2), channel_id=1, source_target_pairs={{0,160},{2,162},{4,164},{6,166},{8,168},{10,170},{12,172},{14,174}... | collective-permute-start | bytes 49160 | tf_op jit(solution)/shard_map/ppermute | solution.py:365
  12.2 1.9 collective-permute-start.2
  14.1 7.3 %shard_map.84 = bf16[128,16,512]{2,1,0:T(8,128)(2,1)} custom-call(bf16[512,2,512]{2,1,0:T(2,128)(2,1)} %q_ref.3, bf16[512,2,512]{2,1,0:T(2,128)(2,1)} %k_ref.3, bf16[512,2,512]{2,1,0:T(2,128)(2,1)} %v_ref.3, bf16[512,2,512]{2,1,0:T(2,128)(2,1)} %c_ref.3), custom_call_target="tpu_custom_call" | custom-call | flops 1000000000 | bytes 6291456 | tf_op jit(solution)/shard_map/pallas_call | solution.py:78
  21.4 0.2 concatenate.30
  21.6 11.9 %all-to-all-start = ((bf16[128,16,512]{2,1,0:T(8,128)(2,1)}), bf16[128,16,512]{2,1,0:T(8,128)(2,1)S(1)}, u32[]{:S(2)}, u32[]{:S(2)}) async-start(bf16[128,16,512]{2,1,0:T(8,128)(2,1)} %shard_map.84), calls=%async_computation | async-start | bytes 4194304 | tf_op jit(solution)/shard_map/all_to_all | solution.py:418
  33.6 3.0 %collective-permute-start.6 = (bf16[32,1024]{1,0:T(8,128)(2,1)S(1)}, bf16[32,1024]{1,0:T(8,128)(2,1)S(1)}, u32[]{:S(2)}, u32[]{:S(2)}) collective-permute-start(bf16[32,1024]{1,0:T(8,128)(2,1)S(1)} %concatenate.30), channel_id=1, source_target_pairs={{0,8},{2,10},{4,12},{6,14},{8,0},{10,2},{12,4},{14,6},{16,24},{18,... | collective-permute-start | bytes 196616 | tf_op jit(solution)/shard_map/ppermute | solution.py:365
  36.5 0.9 collective-permute-start.5
  37.4 0.6 collective-permute-start.4
  38.0 4.3 %collective-permute-done.6 = bf16[32,1024]{1,0:T(8,128)(2,1)S(1)} collective-permute-done((bf16[32,1024]{1,0:T(8,128)(2,1)S(1)}, bf16[32,1024]{1,0:T(8,128)(2,1)S(1)}, u32[]{:S(2)}, u32[]{:S(2)}) %collective-permute-start.6) | collective-permute-done | bytes 65568 | tf_op jit(solution)/shard_map/ppermute | solution.py:365
  42.3 1.4 collective-permute-done.5
  43.7 1.7 collective-permute-done.4
  45.5 1.1 collective-permute-start.7
  46.6 9.3 %collective-permute-done.7 = bf16[128,1024]{1,0:T(8,128)(2,1)S(1)} collective-permute-done((bf16[128,1024]{1,0:T(8,128)(2,1)S(1)}, bf16[128,1024]{1,0:T(8,128)(2,1)S(1)}, u32[]{:S(2)}, u32[]{:S(2)}) %collective-permute-start.7) | collective-permute-done | bytes 262176 | tf_op jit(solution)/shard_map/ppermute | solution.py:365
  55.9 2.4 %collective-permute-start.8 = (bf16[256,1024]{1,0:T(8,128)(2,1)S(1)}, bf16[256,1024]{1,0:T(8,128)(2,1)S(1)}, u32[]{:S(2)}, u32[]{:S(2)}) collective-permute-start(bf16[256,1024]{1,0:T(8,128)(2,1)S(1)} %get-tuple-element.33), channel_id=1, source_target_pairs={{0,2},{2,0},{4,6},{6,4},{8,10},{10,8},{12,14},{14,12},{16,18},{18,... | collective-permute-start | bytes 1572872 | tf_op jit(solution)/shard_map/ppermute | solution.py:365
  58.4 0.1 broadcast_in_dim.4
  58.5 0.7 broadcast_in_dim_reshape.3.seen_ref
  59.2 6.9 %shard_map.85.rows_ref = bf16[4,512,512]{2,1,0:T(8,128)(2,1)} custom-call(bf16[512,2,512]{2,1,0:T(2,128)(2,1)} %q_ref.3, bf16[512,2,512]{2,1,0:T(2,128)(2,1)} %k_ref.3, bf16[512,2,512]{2,1,0:T(2,128)(2,1)} %v_ref.3, bf16[512,2,512]{2,1,0:T(2,128)(2,1)} %c_ref.3), custom_call_target="tpu_custom_call" | custom-call | flops 1000000000 | bytes 6291456 | tf_op jit(solution)/shard_map/pallas_call | solution.py:98
  66.2 0.8 constant_dynamic-update-slice_fusion.5.summ_ref
  67.0 8.6 %shard_map.86 = (bf16[512,512]{1,0:T(8,128)(2,1)}, f32[512,8]{1,0:T(8,128)}) custom-call(bf16[4,512,512]{2,1,0:T(8,128)(2,1)} %shard_map.85.rows_ref, bf16[512,1024]{1,0:T(8,128)(2,1)} %constant_dynamic-update-slice_fusion.5.summ_ref, s32[1,512]{1,0:T(1,128)} %broadcast_in_dim_reshape.3.seen_ref), custom_call_target="tpu_custom_call" | custom-call | flops 4000000000 | bytes 4194304 | tf_op jit(solution)/shard_map/pallas_call | solution.py:145
  75.6 1.0 copy.21
  76.7 0.1 copy.22
  76.8 0.6 pad.11.fixed_ref
  77.4 7.4 %all-to-all-done.recv_ref = bf16[128,16,512]{2,1,0:T(8,128)(2,1)S(1)} async-done(((bf16[128,16,512]{2,1,0:T(8,128)(2,1)}), bf16[128,16,512]{2,1,0:T(8,128)(2,1)S(1)}, u32[]{:S(2)}, u32[]{:S(2)}) %all-to-all-start) | async-done | bytes 2097184 | tf_op jit(solution)/shard_map/all_to_all | solution.py:418
  84.9 1.3 copy-done
  86.2 8.5 %shard_map.87 = (bf16[4,4,4,128,128]{4,3,2,1,0:T(8,128)(2,1)}, bf16[4,4,128,128]{3,2,1,0:T(8,128)(2,1)}, f32[4,4,128,128]{3,2,1,0:T(8,128)}, f32[128,16]{1,0:T(8,128)}) custom-call(bf16[128,16,512]{2,1,0:T(8,128)(2,1)} %copy-done, f32[128,16]{1,0:T(8,128)} %pad.11.fixed_ref), custom_call_target="tpu_custom_call" | custom-call | flops 1000000000 | bytes 6291456 | tf_op jit(solution)/shard_map/pallas_call | solution.py:200
  94.7 2.7 %collective-permute-start.9 = (f32[128,16]{1,0:T(8,128)}, f32[128,16]{1,0:T(8,128)S(1)}, u32[]{:S(2)}, u32[]{:S(2)}) collective-permute-start(f32[128,16]{1,0:T(8,128)} %get-tuple-element.20), channel_id=1, source_target_pairs={{0,1},{1,0},{2,3},{3,2},{4,5},{5,4},{6,7},{7,6},{8,9},{9,8},{10,11... | collective-permute-start | bytes 24584 | tf_op jit(solution)/shard_map/ppermute | solution.py:426
  97.4 1.6 broadcast_in_dim.10
  99.0 6.6 %all-to-all-start.1 = ((f32[256,1,16]{2,1,0:T(1,128)}), f32[256,1,16]{2,1,0:T(1,128)S(1)}, u32[]{:S(2)}, u32[]{:S(2)}) async-start(f32[256,1,16]{2,1,0:T(1,128)} %bitcast.7), calls=%async_computation.1 | async-start | bytes 262144 | tf_op jit(solution)/shard_map/all_to_all | solution.py:428
  105.6 0.8 add.91
  106.4 0.1 fusion.21
  106.6 0.7 copy.25.other_ref
  107.4 11.1 %all-to-all-done.1 = f32[256,1,16]{2,1,0:T(1,128)S(1)} async-done(((f32[256,1,16]{2,1,0:T(1,128)}), f32[256,1,16]{2,1,0:T(1,128)S(1)}, u32[]{:S(2)}, u32[]{:S(2)}) %all-to-all-start.1) | async-done | bytes 16416 | tf_op jit(solution)/shard_map/all_to_all | solution.py:428
  118.5 0.8 reduce_sum.9.mine_ref
  119.2 8.3 %shard_map.88 = bf16[128,16,512]{2,1,0:T(8,128)(2,1)} custom-call(bf16[4,4,4,128,128]{4,3,2,1,0:T(8,128)(2,1)} %get-tuple-element.17.grp_ref, bf16[4,4,128,128]{3,2,1,0:T(8,128)(2,1)} %get-tuple-element.18.attn_ref, f32[4,4,128,128]{3,2,1,0:T(8,128)} %get-tuple-element.19.prob_ref, f32[128,16]{1,0:T(8,128)} %reduce_sum.9.mine_ref, f32[128,16]{1,0:T(8,128)} %copy.25.other_ref), custom_call_target="tpu_custom_call" | custom-call | flops 1000000000 | bytes 6291456 | tf_op jit(solution)/shard_map/pallas_call | solution.py:251
  127.6 6.3 %all-to-all-start.2 = ((bf16[128,16,512]{2,1,0:T(8,128)(2,1)}), bf16[128,16,512]{2,1,0:T(8,128)(2,1)S(1)}, u32[]{:S(2)}, u32[]{:S(2)}) async-start(bf16[128,16,512]{2,1,0:T(8,128)(2,1)} %shard_map.88), calls=%async_computation.2 | async-start | bytes 4194304 | tf_op jit(solution)/shard_map/all_to_all | solution.py:433
  133.9 0.1 slice_add_fusion.3
  134.0 0.9 copy.28
  134.9 10.5 %shard_map.89 = (bf16[4,512,512]{2,1,0:T(8,128)(2,1)}, f32[512,1024]{1,0:T(8,128)}) custom-call(bf16[4,512,512]{2,1,0:T(8,128)(2,1)} %shard_map.85.rows_ref, bf16[512,1024]{1,0:T(8,128)(2,1)} %constant_dynamic-update-slice_fusion.5.summ_ref, s32[1,512]{1,0:T(1,128)} %broadcast_in_dim_reshape.3.seen_ref, bf16[512,512]{1,0:T(8,128)(2,1)} %get-tuple-element.21.attn_ref, ...), custom_call_target="tpu_custom_call" | custom-call | flops 8000000000 | bytes 8388608 | tf_op jit(solution)/shard_map/pallas_call | solution.py:292
  145.4 1.3 slice.145
  146.7 1.1 collective-permute-start.10
  147.8 1.5 collective-permute-done.10
  149.3 1.4 convert_add_fusion
  150.7 0.9 collective-permute-start.11
  151.6 10.9 %collective-permute-done.11 = bf16[128,1024]{1,0:T(8,128)(2,1)S(1)} collective-permute-done((bf16[128,1024]{1,0:T(8,128)(2,1)S(1)}, bf16[128,1024]{1,0:T(8,128)(2,1)S(1)}, u32[]{:S(2)}, u32[]{:S(2)}) %collective-permute-start.11) | collective-permute-done | bytes 262176 | tf_op jit(solution)/shard_map/ppermute | solution.py:365
  162.5 0.1 fusion.19
  162.7 3.1 %collective-permute-start.12 = (bf16[32,1024]{1,0:T(8,128)(2,1)S(1)}, bf16[32,1024]{1,0:T(8,128)(2,1)S(1)}, u32[]{:S(2)}, u32[]{:S(2)}) collective-permute-start(bf16[32,1024]{1,0:T(8,128)(2,1)S(1)} %get-tuple-element.30), channel_id=1, source_target_pairs={{0,12},{2,14},{4,0},{6,2},{8,4},{10,6},{12,8},{14,10},{16,28},{18,... | collective-permute-start | bytes 196616 | tf_op jit(solution)/shard_map/ppermute | solution.py:365
  165.8 0.7 collective-permute-start.13
  166.5 1.8 collective-permute-done.12
  168.2 2.7 %collective-permute-done.14 = bf16[32,1024]{1,0:T(8,128)(2,1)S(1)} collective-permute-done((bf16[32,1024]{1,0:T(8,128)(2,1)S(1)}, bf16[32,1024]{1,0:T(8,128)(2,1)S(1)}, u32[]{:S(2)}, u32[]{:S(2)}) %collective-permute-start.14) | collective-permute-done | bytes 65568 | tf_op jit(solution)/shard_map/ppermute | solution.py:365
  170.9 0.8 collective-permute-done.13
  171.8 6.0 %collective-permute-start.15 = (bf16[12,1024]{1,0:T(8,128)(2,1)S(1)}, bf16[12,1024]{1,0:T(8,128)(2,1)S(1)}, u32[]{:S(2)}, u32[]{:S(2)}) collective-permute-start(bf16[12,1024]{1,0:T(8,128)(2,1)S(1)} %slice.119), channel_id=1, source_target_pairs={{0,160},{2,162},{4,164},{6,166},{8,168},{10,170},{12,172},{14,174}... | collective-permute-start | bytes 73736 | tf_op jit(solution)/shard_map/ppermute | solution.py:365
  177.8 6.1 %collective-permute-done.16 = bf16[8,1024]{1,0:T(8,128)(2,1)S(1)} collective-permute-done((bf16[8,1024]{1,0:T(8,128)(2,1)S(1)}, bf16[8,1024]{1,0:T(8,128)(2,1)S(1)}, u32[]{:S(2)}, u32[]{:S(2)}) %collective-permute-start.16) | collective-permute-done | bytes 16416 | tf_op jit(solution)/shard_map/ppermute | solution.py:365
  183.9 1.8 collective-permute-start.17
  185.7 0.2 collective-permute-start.18
  185.9 1.0 collective-permute-done.17
  186.9 2.5 %collective-permute-done.18 = bf16[4,1024]{1,0:T(4,128)(2,1)S(1)} collective-permute-done((bf16[4,1024]{1,0:T(4,128)(2,1)S(1)}, bf16[4,1024]{1,0:T(4,128)(2,1)S(1)}, u32[]{:S(2)}, u32[]{:S(2)}) %collective-permute-start.18) | collective-permute-done | bytes 8224 | tf_op jit(solution)/shard_map/ppermute | solution.py:365
  189.5 0.6 constant_dynamic-update-slice_fusion.11.fixed_ref
  190.1 1.4 copy-done.1
  191.5 7.7 %shard_map.90 = (bf16[512,2,512]{2,1,0:T(2,128)(2,1)}, bf16[512,2,512]{2,1,0:T(2,128)(2,1)}, bf16[512,2,512]{2,1,0:T(2,128)(2,1)}, bf16[512,2,512]{2,1,0:T(2,128)(2,1)}) custom-call(bf16[128,16,512]{2,1,0:T(8,128)(2,1)} %copy-done.1, bf16[4,512,512]{2,1,0:T(8,128)(2,1)} %constant_dynamic-update-slice_fusion.11.fixed_ref), custom_call_target="tpu_custom_call" | custom-call | flops 2000000000 | bytes 8388608 | tf_op jit(solution)/shard_map/pallas_call | solution.py:332
  (54 shorter events, 0.6 us)
Async XLA Ops:
  2.2 7.5 %collective-permute-start = (bf16[4,1024]{1,0:T(4,128)(2,1)S(1)}, bf16[4,1024]{1,0:T(4,128)(2,1)S(1)}, u32[]{:S(2)}, u32[]{:S(2)}) collective-permute-start(bf16[4,1024]{1,0:T(4,128)(2,1)S(1)} %reshape.46), channel_id=1, source_target_pairs={{0,32},{2,34},{4,36},{6,38},{8,40},{10,42},{12,44},{14,46},{16,48}... | collective-permute-start | bytes 24584 | tf_op jit(solution)/shard_map/ppermute | solution.py:365
  4.7 7.4 %collective-permute-start.1 = (bf16[4,1024]{1,0:T(4,128)(2,1)S(1)}, bf16[4,1024]{1,0:T(4,128)(2,1)S(1)}, u32[]{:S(2)}, u32[]{:S(2)}) collective-permute-start(bf16[4,1024]{1,0:T(4,128)(2,1)S(1)} %reshape.46), channel_id=1, source_target_pairs={{0,224},{2,226},{4,228},{6,230},{8,232},{10,234},{12,236},{14,238}... | collective-permute-start | bytes 24584 | tf_op jit(solution)/shard_map/ppermute | solution.py:365
  9.7 11.6 %collective-permute-start.3 = (bf16[8,1024]{1,0:T(8,128)(2,1)S(1)}, bf16[8,1024]{1,0:T(8,128)(2,1)S(1)}, u32[]{:S(2)}, u32[]{:S(2)}) collective-permute-start(bf16[8,1024]{1,0:T(8,128)(2,1)S(1)} %pad_maximum_fusion.2), channel_id=1, source_target_pairs={{0,160},{2,162},{4,164},{6,166},{8,168},{10,170},{12,172},{14,174}... | collective-permute-start | bytes 49160 | tf_op jit(solution)/shard_map/ppermute | solution.py:365
  12.2 9.2 %collective-permute-start.2 = (bf16[12,1024]{1,0:T(8,128)(2,1)S(1)}, bf16[12,1024]{1,0:T(8,128)(2,1)S(1)}, u32[]{:S(2)}, u32[]{:S(2)}) collective-permute-start(bf16[12,1024]{1,0:T(8,128)(2,1)S(1)} %pad_maximum_fusion.1), channel_id=1, source_target_pairs={{0,96},{2,98},{4,100},{6,102},{8,104},{10,106},{12,108},{14,110},{... | collective-permute-start | bytes 73736 | tf_op jit(solution)/shard_map/ppermute | solution.py:365
  21.6 63.3 %all-to-all-start = ((bf16[128,16,512]{2,1,0:T(8,128)(2,1)}), bf16[128,16,512]{2,1,0:T(8,128)(2,1)S(1)}, u32[]{:S(2)}, u32[]{:S(2)}) async-start(bf16[128,16,512]{2,1,0:T(8,128)(2,1)} %shard_map.84), calls=%async_computation | async-start | bytes 4194304 | tf_op jit(solution)/shard_map/all_to_all | solution.py:418
  33.5 24.9 %copy-start.5 = (s32[128,1]{0,1:T(1,128)S(1)}, s32[128,1]{0,1:T(1,128)}, u32[]{:S(2)}) copy-start(s32[128,1]{0,1:T(1,128)} %constant.116) | copy-start | bytes 1540
  33.5 24.9 %copy-start.6 = (s32[128,1]{0,1:T(1,128)S(1)}, s32[128,1]{0,1:T(1,128)}, u32[]{:S(2)}) copy-start(s32[128,1]{0,1:T(1,128)} %constant.115) | copy-start | bytes 1540
  33.5 24.8 %copy-start.7 = (s32[128,1]{0,1:T(1,128)S(1)}, s32[128,1]{0,1:T(1,128)}, u32[]{:S(2)}) copy-start(s32[128,1]{0,1:T(1,128)} %constant.114) | copy-start | bytes 1540
  33.5 24.8 %copy-start.8 = (s32[128,1]{0,1:T(1,128)S(1)}, s32[128,1]{0,1:T(1,128)}, u32[]{:S(2)}) copy-start(s32[128,1]{0,1:T(1,128)} %constant.113) | copy-start | bytes 1540
  33.6 8.7 %collective-permute-start.6 = (bf16[32,1024]{1,0:T(8,128)(2,1)S(1)}, bf16[32,1024]{1,0:T(8,128)(2,1)S(1)}, u32[]{:S(2)}, u32[]{:S(2)}) collective-permute-start(bf16[32,1024]{1,0:T(8,128)(2,1)S(1)} %concatenate.30), channel_id=1, source_target_pairs={{0,8},{2,10},{4,12},{6,14},{8,0},{10,2},{12,4},{14,6},{16,24},{18,... | collective-permute-start | bytes 196616 | tf_op jit(solution)/shard_map/ppermute | solution.py:365
  36.5 7.2 %collective-permute-start.5 = (bf16[32,1024]{1,0:T(8,128)(2,1)S(1)}, bf16[32,1024]{1,0:T(8,128)(2,1)S(1)}, u32[]{:S(2)}, u32[]{:S(2)}) collective-permute-start(bf16[32,1024]{1,0:T(8,128)(2,1)S(1)} %concatenate.30), channel_id=1, source_target_pairs={{0,12},{2,14},{4,0},{6,2},{8,4},{10,6},{12,8},{14,10},{16,28},{18,... | collective-permute-start | bytes 196616 | tf_op jit(solution)/shard_map/ppermute | solution.py:365
  37.4 8.0 %collective-permute-start.4 = (bf16[32,1024]{1,0:T(8,128)(2,1)S(1)}, bf16[32,1024]{1,0:T(8,128)(2,1)S(1)}, u32[]{:S(2)}, u32[]{:S(2)}) collective-permute-start(bf16[32,1024]{1,0:T(8,128)(2,1)S(1)} %concatenate.30), channel_id=1, source_target_pairs={{0,4},{2,6},{4,8},{6,10},{8,12},{10,14},{12,0},{14,2},{16,20},{18,... | collective-permute-start | bytes 196616 | tf_op jit(solution)/shard_map/ppermute | solution.py:365
  45.5 10.4 %collective-permute-start.7 = (bf16[128,1024]{1,0:T(8,128)(2,1)S(1)}, bf16[128,1024]{1,0:T(8,128)(2,1)S(1)}, u32[]{:S(2)}, u32[]{:S(2)}) collective-permute-start(bf16[128,1024]{1,0:T(8,128)(2,1)S(1)} %pad_maximum_fusion), channel_id=1, source_target_pairs={{0,16},{2,18},{4,20},{6,22},{8,24},{10,26},{12,28},{14,30},{16,0},... | collective-permute-start | bytes 786440 | tf_op jit(solution)/shard_map/ppermute | solution.py:365
  55.9 2.4 %copy-start.4 = (bf16[512,1024]{1,0:T(8,128)(2,1)}, bf16[512,1024]{1,0:T(8,128)(2,1)S(1)}, u32[]{:S(2)}) copy-start(bf16[512,1024]{1,0:T(8,128)(2,1)S(1)} %get-tuple-element.34) | copy-start | bytes 3145732
  55.9 10.2 %collective-permute-start.8 = (bf16[256,1024]{1,0:T(8,128)(2,1)S(1)}, bf16[256,1024]{1,0:T(8,128)(2,1)S(1)}, u32[]{:S(2)}, u32[]{:S(2)}) collective-permute-start(bf16[256,1024]{1,0:T(8,128)(2,1)S(1)} %get-tuple-element.33), channel_id=1, source_target_pairs={{0,2},{2,0},{4,6},{6,4},{8,10},{10,8},{12,14},{14,12},{16,18},{18,... | collective-permute-start | bytes 1572872 | tf_op jit(solution)/shard_map/ppermute | solution.py:365
  84.9 1.3 copy-start
  94.7 10.9 %collective-permute-start.9 = (f32[128,16]{1,0:T(8,128)}, f32[128,16]{1,0:T(8,128)S(1)}, u32[]{:S(2)}, u32[]{:S(2)}) collective-permute-start(f32[128,16]{1,0:T(8,128)} %get-tuple-element.20), channel_id=1, source_target_pairs={{0,1},{1,0},{2,3},{3,2},{4,5},{5,4},{6,7},{7,6},{8,9},{9,8},{10,11... | collective-permute-start | bytes 24584 | tf_op jit(solution)/shard_map/ppermute | solution.py:426
  99.0 19.5 %all-to-all-start.1 = ((f32[256,1,16]{2,1,0:T(1,128)}), f32[256,1,16]{2,1,0:T(1,128)S(1)}, u32[]{:S(2)}, u32[]{:S(2)}) async-start(f32[256,1,16]{2,1,0:T(1,128)} %bitcast.7), calls=%async_computation.1 | async-start | bytes 262144 | tf_op jit(solution)/shard_map/all_to_all | solution.py:428
  127.6 6.3 %copy-start.2 = (f32[128,16]{1,0:T(8,128)S(1)}, f32[128,16]{1,0:T(8,128)}, u32[]{:S(2)}) copy-start(f32[128,16]{1,0:T(8,128)} %reduce_sum.9.mine_ref) | copy-start | bytes 24580
  127.6 6.3 %copy-start.3 = (f32[128,16]{1,0:T(8,128)S(1)}, f32[128,16]{1,0:T(8,128)}, u32[]{:S(2)}) copy-start(f32[128,16]{1,0:T(8,128)} %copy.25.other_ref) | copy-start | bytes 24580
  127.6 62.5 %all-to-all-start.2 = ((bf16[128,16,512]{2,1,0:T(8,128)(2,1)}), bf16[128,16,512]{2,1,0:T(8,128)(2,1)S(1)}, u32[]{:S(2)}, u32[]{:S(2)}) async-start(bf16[128,16,512]{2,1,0:T(8,128)(2,1)} %shard_map.88), calls=%async_computation.2 | async-start | bytes 4194304 | tf_op jit(solution)/shard_map/all_to_all | solution.py:433
  146.7 2.6 %collective-permute-start.10 = (bf16[256,1024]{1,0:T(8,128)(2,1)S(1)}, bf16[256,1024]{1,0:T(8,128)(2,1)S(1)}, u32[]{:S(2)}, u32[]{:S(2)}) collective-permute-start(bf16[256,1024]{1,0:T(8,128)(2,1)S(1)} %slice.145), channel_id=1, source_target_pairs={{0,2},{2,0},{4,6},{6,4},{8,10},{10,8},{12,14},{14,12},{16,18},{18,... | collective-permute-start | bytes 1572872 | tf_op jit(solution)/shard_map/ppermute | solution.py:365
  150.7 11.8 %collective-permute-start.11 = (bf16[128,1024]{1,0:T(8,128)(2,1)S(1)}, bf16[128,1024]{1,0:T(8,128)(2,1)S(1)}, u32[]{:S(2)}, u32[]{:S(2)}) collective-permute-start(bf16[128,1024]{1,0:T(8,128)(2,1)S(1)} %slice.146), channel_id=1, source_target_pairs={{0,16},{2,18},{4,20},{6,22},{8,24},{10,26},{12,28},{14,30},{16,0},... | collective-permute-start | bytes 786440 | tf_op jit(solution)/shard_map/ppermute | solution.py:365
  162.7 5.6 %collective-permute-start.12 = (bf16[32,1024]{1,0:T(8,128)(2,1)S(1)}, bf16[32,1024]{1,0:T(8,128)(2,1)S(1)}, u32[]{:S(2)}, u32[]{:S(2)}) collective-permute-start(bf16[32,1024]{1,0:T(8,128)(2,1)S(1)} %get-tuple-element.30), channel_id=1, source_target_pairs={{0,12},{2,14},{4,0},{6,2},{8,4},{10,6},{12,8},{14,10},{16,28},{18,... | collective-permute-start | bytes 196616 | tf_op jit(solution)/shard_map/ppermute | solution.py:365
  165.8 5.1 %collective-permute-start.14 = (bf16[32,1024]{1,0:T(8,128)(2,1)S(1)}, bf16[32,1024]{1,0:T(8,128)(2,1)S(1)}, u32[]{:S(2)}, u32[]{:S(2)}) collective-permute-start(bf16[32,1024]{1,0:T(8,128)(2,1)S(1)} %get-tuple-element.31), channel_id=1, source_target_pairs={{0,8},{2,10},{4,12},{6,14},{8,0},{10,2},{12,4},{14,6},{16,24},{18,... | collective-permute-start | bytes 196616 | tf_op jit(solution)/shard_map/ppermute | solution.py:365
  165.8 5.9 %collective-permute-start.13 = (bf16[32,1024]{1,0:T(8,128)(2,1)S(1)}, bf16[32,1024]{1,0:T(8,128)(2,1)S(1)}, u32[]{:S(2)}, u32[]{:S(2)}) collective-permute-start(bf16[32,1024]{1,0:T(8,128)(2,1)S(1)} %get-tuple-element.32), channel_id=1, source_target_pairs={{0,4},{2,6},{4,8},{6,10},{8,12},{10,14},{12,0},{14,2},{16,20},{18,... | collective-permute-start | bytes 196616 | tf_op jit(solution)/shard_map/ppermute | solution.py:365
  171.8 12.1 %collective-permute-start.15 = (bf16[12,1024]{1,0:T(8,128)(2,1)S(1)}, bf16[12,1024]{1,0:T(8,128)(2,1)S(1)}, u32[]{:S(2)}, u32[]{:S(2)}) collective-permute-start(bf16[12,1024]{1,0:T(8,128)(2,1)S(1)} %slice.119), channel_id=1, source_target_pairs={{0,160},{2,162},{4,164},{6,166},{8,168},{10,170},{12,172},{14,174}... | collective-permute-start | bytes 73736 | tf_op jit(solution)/shard_map/ppermute | solution.py:365
  177.8 6.1 %collective-permute-start.16 = (bf16[8,1024]{1,0:T(8,128)(2,1)S(1)}, bf16[8,1024]{1,0:T(8,128)(2,1)S(1)}, u32[]{:S(2)}, u32[]{:S(2)}) collective-permute-start(bf16[8,1024]{1,0:T(8,128)(2,1)S(1)} %slice.120), channel_id=1, source_target_pairs={{0,96},{2,98},{4,100},{6,102},{8,104},{10,106},{12,108},{14,110},{... | collective-permute-start | bytes 49160 | tf_op jit(solution)/shard_map/ppermute | solution.py:365
  183.9 2.9 %collective-permute-start.17 = (bf16[4,1024]{1,0:T(4,128)(2,1)S(1)}, bf16[4,1024]{1,0:T(4,128)(2,1)S(1)}, u32[]{:S(2)}, u32[]{:S(2)}) collective-permute-start(bf16[4,1024]{1,0:T(4,128)(2,1)S(1)} %get-tuple-element.45), channel_id=1, source_target_pairs={{0,224},{2,226},{4,228},{6,230},{8,232},{10,234},{12,236},{14,238}... | collective-permute-start | bytes 24584 | tf_op jit(solution)/shard_map/ppermute | solution.py:365
  185.7 3.7 %collective-permute-start.18 = (bf16[4,1024]{1,0:T(4,128)(2,1)S(1)}, bf16[4,1024]{1,0:T(4,128)(2,1)S(1)}, u32[]{:S(2)}, u32[]{:S(2)}) collective-permute-start(bf16[4,1024]{1,0:T(4,128)(2,1)S(1)} %get-tuple-element.46), channel_id=1, source_target_pairs={{0,32},{2,34},{4,36},{6,38},{8,40},{10,42},{12,44},{14,46},{16,48}... | collective-permute-start | bytes 24584 | tf_op jit(solution)/shard_map/ppermute | solution.py:365
  190.1 1.4 copy-start.1

commit v2 on v1

--- a/solution.py
+++ b/solution.py
@@ -14,6 +14,7 @@
 OFFS = 4
 WIDTH = HEADS * HD
 PARTS = (8, 2, 4, 2)
+VMEM3, VMEM4, VMEM6 = 32, 32, 32
 
 epsilon = 1e-06
 scale = HD ** (-0.5)
@@ -42,6 +43,21 @@
 
 def dot_tn(a, b):
     return lax.dot_general(a, b, (((0,), (0,)), ((), ())), preferred_element_type=F32)
+
+
+def batch_dot(a, b, left, right):
+    return lax.dot_general(
+        a, b, (((left,), (right,)), ((0,), (0,))), preferred_element_type=F32
+    )
+
+
+def flat(array):
+    split = array.reshape(BLOCK, 2, HEADS, HD).transpose(0, 2, 1, 3)
+    return split.reshape(BLOCK * HEADS * 2, HD)
+
+
+def unflat(rows):
+    return rows.reshape(BLOCK, HEADS, 2, HD).transpose(0, 2, 1, 3).reshape(BLOCK, 2, WIDTH)
 
 
 def call(kernel, grid, in_specs, out_specs, out_shape, flops, nbytes, scratch=(), vmem=60):
@@ -64,42 +80,58 @@
 def pack_strided_kernel(q_ref, k_ref, v_ref, c_ref, send_ref, pick_ref):
     @pl.when(pl.program_id(0) == 0)
     def _():
-        row, col = iotas((256, 512))
-        home, array, offset = row >> 4, (row >> 2) & 3, row & 3
-        pick_ref[...] = one_hot(col == array * 128 + (home * OFFS + offset) * 2)
-
-    rows = jnp.concatenate(
-        [ref[...].reshape(128, WIDTH) for ref in (q_ref, k_ref, v_ref, c_ref)], 0
-    )
-    send_ref[...] = dot(pick_ref[...], rows).astype(BF16).reshape(16, 16, WIDTH)
+        row, col = iotas((128, 256))
+        home, head, array, offset = row >> 6, (row >> 4) & 3, (row >> 2) & 3, row & 3
+        pick_ref[...] = one_hot(col == array * 64 + ((home * OFFS + offset) * HEADS + head) * 2)
+
+    pick = pick_ref[...]
+    for at in range(0, 32, 2):
+        pair = [
+            jnp.concatenate([ref[64 * n : 64 * (n + 1)] for n in (at, at + 1)], 1)
+            for ref in (q_ref, k_ref, v_ref, c_ref)
+        ]
+        picked = dot(pick, jnp.concatenate(pair, 0)).astype(BF16)
+        for n in range(2):
+            for home in range(2):
+                for head in range(HEADS):
+                    row = home * 64 + head * 16
+                    send_ref[2 * (at + n) + home, :, head * HD : (head + 1) * HD] = picked[
+                        row : row + 16, n * HD : (n + 1) * HD
+                    ]
 
 
 def pack_strided(arrays):
     return call(
         pack_strided_kernel,
-        8,
-        [spec((64, 2, WIDTH), "i", 0, 0)] * 4,
-        spec((16, 16, WIDTH), "i", 0, 0),
+        2,
+        [spec((2048, HD), "i", 0)] * 4,
+        spec((64, 16, WIDTH), "i", 0, 0),
         jax.ShapeDtypeStruct((NB, 16, WIDTH), BF16),
         10**9,
         6 * 2**20,
-        [pltpu.VMEM((256, 512), BF16)],
+        [pltpu.VMEM((128, 256), BF16)],
     )(*arrays)
 
 
 def pack_fixed_kernel(q_ref, k_ref, v_ref, c_ref, out_ref):
     row, col = iotas((64, 128))
-    pick = one_hot(col == 2 * row + 1)
-    for at, ref in enumerate((q_ref, k_ref, v_ref, c_ref)):
-        out_ref[at] = dot(pick, ref[...].reshape(128, WIDTH)).astype(BF16)
+    pick = one_hot(col == ((row & 15) * HEADS + (row >> 4)) * 2 + 1)
+    for at in range(16):
+        rows = [ref[128 * at : 128 * (at + 1)] for ref in (q_ref, k_ref, v_ref, c_ref)]
+        picked = dot(pick, jnp.concatenate(rows, 1)).astype(BF16)
+        for array in range(4):
+            for head in range(HEADS):
+                out_ref[array, 16 * at : 16 * (at + 1), head * HD : (head + 1) * HD] = picked[
+                    16 * head : 16 * (head + 1), array * HD : (array + 1) * HD
+                ]
 
 
 def pack_fixed(arrays):
     return call(
         pack_fixed_kernel,
-        8,
-        [spec((64, 2, WIDTH), "i", 0, 0)] * 4,
-        spec((4, 64, WIDTH), 0, "i", 0),
+        2,
+        [spec((2048, HD), "i", 0)] * 4,
+        spec((4, BLOCK // 2, WIDTH), 0, "i", 0),
         jax.ShapeDtypeStruct((4, BLOCK, WIDTH), BF16),
         10**9,
         6 * 2**20,
@@ -165,56 +197,60 @@
     return one_hot(col == ((row & 15) << 4) + (row >> 4))
 
 
-def strided_forward_kernel(recv_ref, fixed_ref, grp_ref, attn_ref, prob_ref, sums_ref):
+def strided_forward_kernel(recv_ref, fixed_ref, grp_ref, attn_ref, prob_ref, sums_ref, send_ref):
     swap = swap_matrix()
     for at in range(0, NB, 16):
-        rows = recv_ref[at : at + 16].reshape(256, HD)
-        grp_ref[0, :, :, at : at + 16, :] = (
-            dot(swap, rows).astype(BF16).reshape(4, OFFS, 16, HD)
-        )
+        rows = dot(swap, recv_ref[at : at + 16].reshape(256, WIDTH)).astype(BF16)
+        for head in range(HEADS):
+            grp_ref[head, :, :, at : at + 16, :] = rows[:, head * HD : (head + 1) * HD].reshape(
+                4, OFFS, 16, HD
+            )
     row, col = iotas((NB, NB))
-    lane = lax.broadcasted_iota(jnp.int32, (NB, 16), 1)
-    part = jnp.zeros((NB, 16), F32)
-    for at in range(OFFS):
-        scores = jnp.where(col <= row, dot_nt(grp_ref[0, 0, at], grp_ref[0, 1, at]) * scale, -jnp.inf)
+    square, cross = 0.0, 0.0
+    for head in range(HEADS):
+        scores = batch_dot(grp_ref[head, 0], grp_ref[head, 1], 2, 2) * scale
+        scores = jnp.where((col <= row)[None], scores, -jnp.inf)
         expo = jnp.exp(scores - jnp.max(scores, axis=-1, keepdims=True))
         prob = expo * (1.0 / jnp.sum(expo, axis=-1, keepdims=True))
-        attn = dot(prob.astype(BF16), grp_ref[0, 2, at]).astype(BF16)
-        prob_ref[0, at] = prob
-        attn_ref[0, at] = attn
+        attn = batch_dot(prob.astype(BF16), grp_ref[head, 2], 2, 1).astype(BF16)
+        prob_ref[head] = prob
+        attn_ref[head] = attn
         wide = attn.astype(F32)
-        square = jnp.sum(wide * wide, axis=-1, keepdims=True)
-        cross = jnp.sum(wide * grp_ref[0, 3, at].astype(F32), axis=-1, keepdims=True)
-        part += jnp.where(lane == 8 + at, square, jnp.where(lane == 12 + at, cross, 0.0))
-
-    @pl.when(pl.program_id(0) == 0)
-    def _():
-        sums_ref[...] = fixed_ref[...] + part
-
-    @pl.when(pl.program_id(0) > 0)
-    def _():
-        sums_ref[...] += part
+        square += wide * wide
+        cross += wide * grp_ref[head, 3].astype(F32)
+    square = jnp.sum(square, axis=-1, keepdims=True)
+    cross = jnp.sum(cross, axis=-1, keepdims=True)
+    lane = lax.broadcasted_iota(jnp.int32, (NB, HD), 1)
+    part = fixed_ref[...]
+    for at in range(OFFS):
+        part += jnp.where(lane == 8 + at, square[at], jnp.where(lane == 12 + at, cross[at], 0.0))
+    sums_ref[...] = part
+    for head in range(2):
+        send_ref[head * NB : (head + 1) * NB] = part.reshape(NB, 1, HD)
 
 
 def strided_forward(recv, fixed_sums):
     return call(
         strided_forward_kernel,
-        HEADS,
-        [spec((NB, 16, HD), 0, 0, "i"), spec((NB, 16), 0, 0)],
-        [
-            spec((1, 4, OFFS, NB, HD), "i", 0, 0, 0, 0),
-            spec((1, OFFS, NB, HD), "i", 0, 0, 0),
-            spec((1, OFFS, NB, NB), "i", 0, 0, 0),
-            spec((NB, 16), 0, 0),
+        1,
+        [spec((NB, 16, WIDTH), 0, 0, 0), spec((NB, HD), 0, 0)],
+        [
+            spec((HEADS, 4, OFFS, NB, HD), 0, 0, 0, 0, 0),
+            spec((HEADS, OFFS, NB, HD), 0, 0, 0, 0),
+            spec((HEADS, OFFS, NB, NB), 0, 0, 0, 0),
+            spec((NB, HD), 0, 0),
+            spec((2 * NB, 1, HD), 0, 0, 0),
         ],
         [
             jax.ShapeDtypeStruct((HEADS, 4, OFFS, NB, HD), BF16),
             jax.ShapeDtypeStruct((HEADS, OFFS, NB, HD), BF16),
             jax.ShapeDtypeStruct((HEADS, OFFS, NB, NB), F32),
-            jax.ShapeDtypeStruct((NB, 16), F32),
+            jax.ShapeDtypeStruct((NB, HD), F32),
+            jax.ShapeDtypeStruct((2 * NB, 1, HD), F32),
         ],
         10**9,
         6 * 2**20,
+        vmem=VMEM3,
     )(recv, fixed_sums)
 
 
@@ -227,43 +263,54 @@
     return normed, grad, jnp.sum(grad.astype(F32) * wide, axis=-1, keepdims=True)
 
 
-def strided_backward_kernel(grp_ref, attn_ref, prob_ref, mine_ref, other_ref, send_ref, out_ref):
-    total = mine_ref[...] + other_ref[...]
-    for at in range(OFFS):
-        wide = attn_ref[0, at].astype(F32)
-        normed, grad, row_dot = normalize(
-            wide, grp_ref[0, 3, at], total[:, at : at + 1], total[:, 4 + at : 5 + at]
-        )
-        prob = prob_ref[0, at]
-        grad_prob = dot_nt(grad, grp_ref[0, 2, at])
+def strided_backward_kernel(
+    grp_ref, attn_ref, prob_ref, sums_ref, other_ref, recv_ref, send_ref, block_ref, out_ref
+):
+    both = sums_ref[:, :16] + other_ref[...]
+    moved = (recv_ref[:NB] + recv_ref[NB:]).reshape(NB, HD)
+    block_ref[...] = both[:, :8] + moved[:, 8:16]
+    total = both[:, 8:] + moved[:, :8]
+    square = jnp.stack([total[:, at : at + 1] for at in range(OFFS)])
+    cross = jnp.stack([total[:, OFFS + at : OFFS + at + 1] for at in range(OFFS)])
+    for head in range(HEADS):
+        wide = attn_ref[head].astype(F32)
+        normed, grad, row_dot = normalize(wide, grp_ref[head, 3], square, cross)
+        prob = prob_ref[head]
+        grad_prob = batch_dot(grad, grp_ref[head, 2], 2, 2)
         grad_score = (prob * (grad_prob - row_dot) * scale).astype(BF16)
-        out_ref[0, at] = normed
-        out_ref[1, at] = dot(grad_score, grp_ref[0, 1, at]).astype(BF16)
-        out_ref[2, at] = dot_tn(grad_score, grp_ref[0, 0, at]).astype(BF16)
-        out_ref[3, at] = dot_tn(prob.astype(BF16), grad).astype(BF16)
+        out_ref[head, 0] = normed
+        out_ref[head, 1] = batch_dot(grad_score, grp_ref[head, 1], 2, 1).astype(BF16)
+        out_ref[head, 2] = batch_dot(grad_score, grp_ref[head, 0], 1, 1).astype(BF16)
+        out_ref[head, 3] = batch_dot(prob.astype(BF16), grad, 1, 1).astype(BF16)
     swap = swap_matrix()
     for at in range(0, NB, 16):
-        rows = out_ref[:, :, at : at + 16, :].reshape(256, HD)
-        send_ref[at : at + 16] = dot(swap, rows).astype(BF16).reshape(16, 16, HD)
-
-
-def strided_backward(grp, attn, prob, mine, other):
+        rows = [out_ref[head, :, :, at : at + 16, :].reshape(256, HD) for head in range(HEADS)]
+        moved = dot(swap, jnp.concatenate(rows, 1)).astype(BF16)
+        send_ref[at : at + 16] = moved.reshape(16, 16, WIDTH)
+
+
+def strided_backward(grp, attn, prob, sums, other, recv):
     return call(
         strided_backward_kernel,
-        HEADS,
-        [
-            spec((1, 4, OFFS, NB, HD), "i", 0, 0, 0, 0),
-            spec((1, OFFS, NB, HD), "i", 0, 0, 0),
-            spec((1, OFFS, NB, NB), "i", 0, 0, 0),
+        1,
+        [
+            spec((HEADS, 4, OFFS, NB, HD), 0, 0, 0, 0, 0),
+            spec((HEADS, OFFS, NB, HD), 0, 0, 0, 0),
+            spec((HEADS, OFFS, NB, NB), 0, 0, 0, 0),
+            spec((NB, HD), 0, 0),
             spec((NB, 16), 0, 0),
-            spec((NB, 16), 0, 0),
-        ],
-        spec((NB, 16, HD), 0, 0, "i"),
-        jax.ShapeDtypeStruct((NB, 16, WIDTH), BF16),
+            spec((2 * NB, 1, HD), 0, 0, 0),
+        ],
+        [spec((NB, 16, WIDTH), 0, 0, 0), spec((NB, 8), 0, 0)],
+        [
+            jax.ShapeDtypeStruct((NB, 16, WIDTH), BF16),
+            jax.ShapeDtypeStruct((NB, 8), F32),
+        ],
         10**9,
         6 * 2**20,
-        [pltpu.VMEM((4, OFFS, NB, HD), BF16)],
-    )(grp, attn, prob, mine, other)
+        [pltpu.VMEM((HEADS, 4, OFFS, NB, HD), BF16)],
+        vmem=VMEM4,
+    )(grp, attn, prob, sums, other, recv)
 
 
 def fixed_backward_kernel(rows_ref, summ_ref, seen_ref, attn_ref, sums_ref, out_ref, part_ref):
@@ -309,36 +356,69 @@
     )(rows, summ, seen, attn, sums)
 
 
-def unpack_kernel(recv_ref, fixed_ref, *refs):
-    out_refs, pick_ref = refs[:4], refs[4]
+def unpack_kernel(recv_ref, fixed_ref, tail_ref, *refs):
+    out_refs, strided_ref, own_ref = refs[:4], refs[4], refs[5]
 
     @pl.when(pl.program_id(0) == 0)
     def _():
-        row, col = iotas((512, 512))
-        array, token, kind = row >> 7, (row & 127) >> 1, row & 1
-        strided = ((token >> 2) << 4) + array * OFFS + (token & 3)
-        fixed = 256 + array * 64 + token
-        pick_ref[...] = one_hot(col == jnp.where(kind == 0, strided, fixed))
-
-    rows = jnp.concatenate(
-        [recv_ref[...].reshape(256, WIDTH), fixed_ref[...].reshape(256, WIDTH)], 0
-    )
-    for at, ref in enumerate(out_refs):
-        picked = dot(pick_ref[at * 128 : (at + 1) * 128], rows).astype(BF16)
-        ref[...] = picked.reshape(64, 2, WIDTH)
-
-
-def unpack(recv, fixed):
-    return call(
+        row, col = iotas((512, 256))
+        array, token, head, kind = row >> 7, (row >> 3) & 15, (row >> 1) & 3, row & 1
+        source = (token >> 2) * 64 + head * 16 + array * OFFS + (token & 3)
+        strided_ref[...] = one_hot((kind == 0) & (col == source))
+        row, col = iotas((128, 64))
+        token, head, kind = row >> 3, (row >> 1) & 3, row & 1
+        own_ref[...] = one_hot((kind == 1) & (col == head * 16 + token))
+
+    last = pl.program_id(0) == 1
+    end = lax.broadcasted_iota(jnp.int32, (16, WIDTH), 0) >= 16 - SUMM
+    for at in range(0, 16, 2):
+        rows = [
+            jnp.concatenate(
+                [
+                    recv_ref[4 * n + home, :, head * HD : (head + 1) * HD]
+                    for home in range(4)
+                    for head in range(HEADS)
+                ],
+                0,
+            )
+            for n in (at, at + 1)
+        ]
+        strided = dot(strided_ref[...], jnp.concatenate(rows, 1))
+        for n in range(2):
+            tile = 16 * (at + n)
+            fixed = [fixed_ref[array, tile : tile + 16] for array in range(4)]
+            if tile == BLOCK // 2 - 16:
+                for array in (2, 3):
+                    fixed[array] = jnp.where(end & last, tail_ref[array - 2], fixed[array])
+            rows = [
+                jnp.concatenate([part[:, head * HD : (head + 1) * HD] for part in fixed], 1)
+                for head in range(HEADS)
+            ]
+            own = dot(own_ref[...], jnp.concatenate(rows, 0))
+            for array in range(4):
+                out_refs[array][8 * tile : 8 * tile + 128] = (
+                    strided[array * 128 : (array + 1) * 128, n * HD : (n + 1) * HD]
+                    + own[:, array * HD : (array + 1) * HD]
+                ).astype(BF16)
+
+
+def unpack(recv, fixed, tail):
+    rows = call(
         unpack_kernel,
-        8,
-        [spec((16, 16, WIDTH), "i", 0, 0), spec((4, 64, WIDTH), 0, "i", 0)],
-        [spec((64, 2, WIDTH), "i", 0, 0)] * 4,
-        [jax.ShapeDtypeStruct((BLOCK, 2, WIDTH), BF16)] * 4,
+        2,
+        [
+            spec((NB // 2, 16, WIDTH), "i", 0, 0),
+            spec((4, BLOCK // 2, WIDTH), 0, "i", 0),
+            spec((2, 16, WIDTH), 0, 0, 0),
+        ],
+        [spec((BLOCK * 4, HD), "i", 0)] * 4,
+        [jax.ShapeDtypeStruct((BLOCK * 8, HD), BF16)] * 4,
         2 * 10**9,
         8 * 2**20,
-        [pltpu.VMEM((512, 512), BF16)],
-    )(recv, fixed)
+        [pltpu.VMEM((512, 256), BF16), pltpu.VMEM((128, 64), BF16)],
+        vmem=VMEM6,
+    )(recv, fixed, tail)
+    return tuple(unflat(array) for array in rows)
 
 
 def place(index):
@@ -409,7 +489,7 @@
 
 def shards(queries, key_rows, value_rows, cotangent):
     me = lax.axis_index("seq")
-    arrays = (queries, key_rows, value_rows, cotangent)
+    arrays = tuple(flat(array) for array in (queries, key_rows, value_rows, cotangent))
     send = pack_strided(arrays)
     tails = [a[BLOCK - SUMM :, 1].reshape(SUMM, HEADS, 1, HD) for a in (key_rows, value_rows)]
     own_summ = jnp.concatenate(tails, 2).reshape(SUMM, 2 * WIDTH)
@@ -421,22 +501,18 @@
     rows = pack_fixed(arrays)
     fixed_attn, fixed_sums = fixed_forward(rows, summ, seen)
     fixed_send = fixed_sums[:, :2].reshape(NB, OFFS, 2).transpose(0, 2, 1).reshape(NB, 8)
-    fixed_send = jnp.pad(fixed_send, ((0, 0), (0, 8)))
-    grp, attn, prob, sums = strided_forward(recv, fixed_send)
-    sums_other = lax.ppermute(sums, "head", [(0, 1), (1, 0)])
-    sums_both = jnp.broadcast_to(sums[:, None], (NB, 2, 16)).reshape(2 * NB, 16)
-    sums_in = lax.all_to_all(sums_both, ("seq", "head"), 0, 0, tiled=True).reshape(NB, 2, 16)
-    mine = jnp.sum(sums_in, 1)
-    other = sums + sums_other
-    other = jnp.concatenate([other[:, 8:], other[:, :8]], 1)
-    send_back = strided_backward(grp, attn, prob, mine, other)
+    fixed_send = jnp.pad(fixed_send, ((0, 0), (0, HD - 8)))
+    grp, attn, prob, sums, sums_both = strided_forward(recv, fixed_send)
+    sums_in = lax.all_to_all(sums_both, ("head", "seq"), 0, 0, tiled=True)
+    sums_other = lax.ppermute(sums[:, :16], "head", [(0, 1), (1, 0)])
+    send_back, block_sums = strided_backward(grp, attn, prob, sums, sums_other, sums_in)
     recv_back = lax.all_to_all(send_back, "seq", 0, 0, tiled=True)
-    block_sums = (mine + other)[:, 8:].reshape(NB, 2, OFFS).transpose(0, 2, 1).reshape(BLOCK, 2)
+    block_sums = block_sums.reshape(NB, 2, OFFS).transpose(0, 2, 1).reshape(BLOCK, 2)
     fixed_out, parts = fixed_backward(rows, summ, seen, fixed_attn, block_sums)
     totals = scatter_summaries(parts).astype(BF16).reshape(SUMM, HEADS, 2, HD)
     totals = totals.transpose(2, 0, 1, 3).reshape(2, SUMM, WIDTH)
-    fixed_out = lax.dynamic_update_slice(fixed_out, totals, (2, BLOCK - SUMM, 0))
-    return tuple(unpack(recv_back, fixed_out))
+    tail = jnp.pad(totals, ((0, 0), (16 - SUMM, 0), (0, 0)))
+    return unpack(recv_back, fixed_out, tail)
 
 
 def solution(mesh):

time: 201 us -> 183 us (0.910)
  Pallas kernels: 57.9 us -> 36 us
  waiting for transfers between devices: 63.5 us -> 66.3 us
    pallas_call x5, Pallas kernels: 38.8 us -> 16.8 us  [the longest x1 4.2 us: unpack(): call(unpack_kernel, 2, [spec((NB // 2, 16, WIDTH), 'i', 0, 0), spec((4, B...]
    unnamed x24 -> x26, local copies, waits for them, and re-layouts: 2.89 us -> 7.74 us
    all_to_all x1, waiting for transfers between devices: 7.42 us -> 11.3 us  [shards(): recv = lax.all_to_all(send, 'seq', 0, 0, tiled=True)]
    all_to_all x1, waiting for transfers between devices: 11.1 us -> 7.41 us  [shards(): sums_in = lax.all_to_all(sums_both, ('head', 'seq'), 0, 0, tiled=True)]
    ppermute x1, waiting for transfers between devices: 0.01 us -> 2.17 us  [shards(): sums_other = lax.ppermute(sums[:, :16], 'head', [(0, 1), (1, 0)])]
  transfers between devices with their start and end apart: 22 -> 22, of which waited for: 15 -> 17; matrix products, arithmetic and copies ran while one was open for 6% -> 4% of each run, Pallas kernels for 17% -> 14%
where the time goes in v2:
time: 183 us; the launch traced here: 181 us
  waiting for transfers between devices  66.3 us (36%)
  starting transfers between devices  62 us (34%)
  Pallas kernels  36 us (20%)
  local copies, waits for them, and re-layouts  14.6 us (8%)
    ppermute x18, waiting for transfers between devices, shift(): return lax.ppermute(array, 'seq', perm)  45.5 us
    ppermute x18, starting transfers between devices, shift(): return lax.ppermute(array, 'seq', perm)  32.8 us
    all_to_all x1, starting transfers between devices, shards(): recv = lax.all_to_all(send, 'seq', 0, 0, tiled=True)  11.6 us
    all_to_all x1, waiting for transfers between devices, shards(): recv = lax.all_to_all(send, 'seq', 0, 0, tiled=True)  11.3 us
    pallas_call x1, Pallas kernels, fixed_backward(): call(fixed_backward_kernel, HEADS, [spec((4, BLOCK, HD), 0, 0, 'i'), spec...  10.5 us
    pallas_call x1, Pallas kernels, fixed_forward(): call(fixed_forward_kernel, HEADS, [spec((4, BLOCK, HD), 0, 0, 'i'), spec(...  8.64 us
    all_to_all x1, starting transfers between devices, shards(): sums_in = lax.all_to_all(sums_both, ('head', 'seq'), 0, 0, tiled=True)  8.24 us
    unnamed x26, local copies, waits for them, and re-layouts  7.74 us
  transfers between devices with their start and end apart: 22, of which 17 were waited for; matrix products, arithmetic and copies ran while one was open for 4% of the time, Pallas kernels for 14%

profile of v2, /device:TPU:1, one launch (start us, length us, event | category | flops | bytes accessed | tf_op | source)
XLA Modules:
  0.0 181.4 jit_solution(4817556428027024814)
XLA Ops:
  0.6 0.7 slice_reduce_fusion.1
  1.4 0.7 slice_reduce_fusion
  2.2 2.5 %collective-permute-start = (bf16[4,1024]{1,0:T(4,128)(2,1)S(1)}, bf16[4,1024]{1,0:T(4,128)(2,1)S(1)}, u32[]{:S(2)}, u32[]{:S(2)}) collective-permute-start(bf16[4,1024]{1,0:T(4,128)(2,1)S(1)} %reshape.93), channel_id=1, source_target_pairs={{0,32},{2,34},{4,36},{6,38},{8,40},{10,42},{12,44},{14,46},{16,48}... | collective-permute-start | bytes 24584 | tf_op jit(solution)/shard_map/ppermute | solution.py:445
  4.7 4.0 %collective-permute-start.1 = (bf16[4,1024]{1,0:T(4,128)(2,1)S(1)}, bf16[4,1024]{1,0:T(4,128)(2,1)S(1)}, u32[]{:S(2)}, u32[]{:S(2)}) collective-permute-start(bf16[4,1024]{1,0:T(4,128)(2,1)S(1)} %reshape.93), channel_id=1, source_target_pairs={{0,224},{2,226},{4,228},{6,230},{8,232},{10,234},{12,236},{14,238}... | collective-permute-start | bytes 24584 | tf_op jit(solution)/shard_map/ppermute | solution.py:445
  8.7 1.0 collective-permute-done
  9.7 2.4 %collective-permute-start.3 = (bf16[8,1024]{1,0:T(8,128)(2,1)S(1)}, bf16[8,1024]{1,0:T(8,128)(2,1)S(1)}, u32[]{:S(2)}, u32[]{:S(2)}) collective-permute-start(bf16[8,1024]{1,0:T(8,128)(2,1)S(1)} %pad_maximum_fusion.2), channel_id=1, source_target_pairs={{0,160},{2,162},{4,164},{6,166},{8,168},{10,170},{12,172},{14,174}... | collective-permute-start | bytes 49160 | tf_op jit(solution)/shard_map/ppermute | solution.py:445
  12.2 1.9 %collective-permute-start.2 = (bf16[12,1024]{1,0:T(8,128)(2,1)S(1)}, bf16[12,1024]{1,0:T(8,128)(2,1)S(1)}, u32[]{:S(2)}, u32[]{:S(2)}) collective-permute-start(bf16[12,1024]{1,0:T(8,128)(2,1)S(1)} %pad_maximum_fusion.1), channel_id=1, source_target_pairs={{0,96},{2,98},{4,100},{6,102},{8,104},{10,106},{12,108},{14,110},{... | collective-permute-start | bytes 73736 | tf_op jit(solution)/shard_map/ppermute | solution.py:445
  14.1 3.6 %shard_map.84 = bf16[128,16,512]{2,1,0:T(8,128)(2,1)} custom-call(bf16[4096,128]{1,0:T(8,128)(2,1)} %bitcast.80, bf16[4096,128]{1,0:T(8,128)(2,1)} %bitcast.76, bf16[4096,128]{1,0:T(8,128)(2,1)} %bitcast.78, bf16[4096,128]{1,0:T(8,128)(2,1)} %bitcast.82), custom_call_target="tpu_custom_call" | custom-call | flops 1000000000 | bytes 6291456 | tf_op jit(solution)/shard_map/pallas_call | solution.py:104
  17.7 0.4 collective-permute-done.2
  18.0 0.2 concatenate.27
  18.2 11.6 %all-to-all-start = ((bf16[128,16,512]{2,1,0:T(8,128)(2,1)}), bf16[128,16,512]{2,1,0:T(8,128)(2,1)S(1)}, u32[]{:S(2)}, u32[]{:S(2)}) async-start(bf16[128,16,512]{2,1,0:T(8,128)(2,1)} %shard_map.84), calls=%async_computation | async-start | bytes 4194304 | tf_op jit(solution)/shard_map/all_to_all | solution.py:498
  29.8 0.0 copy-start.7
  29.8 0.0 copy-start.8
  29.9 3.0 %collective-permute-start.6 = (bf16[32,1024]{1,0:T(8,128)(2,1)S(1)}, bf16[32,1024]{1,0:T(8,128)(2,1)S(1)}, u32[]{:S(2)}, u32[]{:S(2)}) collective-permute-start(bf16[32,1024]{1,0:T(8,128)(2,1)S(1)} %concatenate.27), channel_id=1, source_target_pairs={{0,8},{2,10},{4,12},{6,14},{8,0},{10,2},{12,4},{14,6},{16,24},{18,... | collective-permute-start | bytes 196616 | tf_op jit(solution)/shard_map/ppermute | solution.py:445
  32.8 0.9 collective-permute-start.5
  33.7 0.6 collective-permute-start.4
  34.3 4.3 %collective-permute-done.6 = bf16[32,1024]{1,0:T(8,128)(2,1)S(1)} collective-permute-done((bf16[32,1024]{1,0:T(8,128)(2,1)S(1)}, bf16[32,1024]{1,0:T(8,128)(2,1)S(1)}, u32[]{:S(2)}, u32[]{:S(2)}) %collective-permute-start.6) | collective-permute-done | bytes 65568 | tf_op jit(solution)/shard_map/ppermute | solution.py:445
  38.6 1.4 collective-permute-done.5
  40.0 1.7 collective-permute-done.4
  41.8 1.1 collective-permute-start.7
  42.9 9.3 %collective-permute-done.7 = bf16[128,1024]{1,0:T(8,128)(2,1)S(1)} collective-permute-done((bf16[128,1024]{1,0:T(8,128)(2,1)S(1)}, bf16[128,1024]{1,0:T(8,128)(2,1)S(1)}, u32[]{:S(2)}, u32[]{:S(2)}) %collective-permute-start.7) | collective-permute-done | bytes 262176 | tf_op jit(solution)/shard_map/ppermute | solution.py:445
  52.2 2.6 %collective-permute-start.8 = (bf16[256,1024]{1,0:T(8,128)(2,1)S(1)}, bf16[256,1024]{1,0:T(8,128)(2,1)S(1)}, u32[]{:S(2)}, u32[]{:S(2)}) collective-permute-start(bf16[256,1024]{1,0:T(8,128)(2,1)S(1)} %get-tuple-element.47), channel_id=1, source_target_pairs={{0,2},{2,0},{4,6},{6,4},{8,10},{10,8},{12,14},{14,12},{16,18},{18,... | collective-permute-start | bytes 1572872 | tf_op jit(solution)/shard_map/ppermute | solution.py:445
  54.9 0.1 broadcast_in_dim.3
  55.0 0.7 broadcast_in_dim_reshape.3.seen_ref
  55.7 3.5 %shard_map.85.rows_ref = bf16[4,512,512]{2,1,0:T(8,128)(2,1)} custom-call(bf16[4096,128]{1,0:T(8,128)(2,1)} %bitcast.81, bf16[4096,128]{1,0:T(8,128)(2,1)} %bitcast.77, bf16[4096,128]{1,0:T(8,128)(2,1)} %bitcast.79, bf16[4096,128]{1,0:T(8,128)(2,1)} %bitcast.83), custom_call_target="tpu_custom_call" | custom-call | flops 1000000000 | bytes 6291456 | tf_op jit(solution)/shard_map/pallas_call | solution.py:130
  59.2 0.8 constant_dynamic-update-slice_fusion.5.summ_ref
  60.0 8.6 %shard_map.86 = (bf16[512,512]{1,0:T(8,128)(2,1)}, f32[512,8]{1,0:T(8,128)}) custom-call(bf16[4,512,512]{2,1,0:T(8,128)(2,1)} %shard_map.85.rows_ref, bf16[512,1024]{1,0:T(8,128)(2,1)} %constant_dynamic-update-slice_fusion.5.summ_ref, s32[1,512]{1,0:T(1,128)} %broadcast_in_dim_reshape.3.seen_ref), custom_call_target="tpu_custom_call" | custom-call | flops 4000000000 | bytes 4194304 | tf_op jit(solution)/shard_map/pallas_call | solution.py:177
  68.7 1.0 copy.27
  69.7 0.1 copy.28
  69.9 11.3 %all-to-all-done.recv_ref = bf16[128,16,512]{2,1,0:T(8,128)(2,1)S(1)} async-done(((bf16[128,16,512]{2,1,0:T(8,128)(2,1)}), bf16[128,16,512]{2,1,0:T(8,128)(2,1)S(1)}, u32[]{:S(2)}, u32[]{:S(2)}) %all-to-all-start) | async-done | bytes 2097184 | tf_op jit(solution)/shard_map/all_to_all | solution.py:498
  81.2 3.1 %shard_map.87 = (bf16[4,4,4,128,128]{4,3,2,1,0:T(8,128)(2,1)S(1)}, bf16[4,4,128,128]{3,2,1,0:T(8,128)(2,1)S(1)}, f32[4,4,128,128]{3,2,1,0:T(8,128)S(1)}, f32[128,128]{1,0:T(8,128)S(1)}, f32[256,1,128]{2,1,0:T(1,128)}) custom-call(bf16[128,16,512]{2,1,0:T(8,128)(2,1)S(1)} %all-to-all-done.recv_ref, f32[128,128]{1,0:T(8,128)S(1)} %pad.15.fixed_ref), custom_call_target="tpu_custom_call" | custom-call | flops 1000000000 | bytes 6291456 | tf_op jit(solution)/shard_map/pallas_call | solution.py:233
  84.3 1.3 copy-done.1
  85.6 0.8 copy-done.3
  86.4 8.2 %all-to-all-start.1 = ((f32[256,1,128]{2,1,0:T(1,128)}), f32[256,1,128]{2,1,0:T(1,128)S(1)}, u32[]{:S(2)}, u32[]{:S(2)}) async-start(f32[256,1,128]{2,1,0:T(1,128)} %get-tuple-element.28), calls=%async_computation.1 | async-start | bytes 262144 | tf_op jit(solution)/shard_map/all_to_all | solution.py:506
  94.6 3.0 %collective-permute-start.9 = (f32[128,16]{1,0:T(8,128)S(1)}, f32[128,16]{1,0:T(8,128)S(1)}, u32[]{:S(2)}, u32[]{:S(2)}) collective-permute-start(f32[128,16]{1,0:T(8,128)S(1)} %bitcast.75), channel_id=1, source_target_pairs={{0,1},{1,0},{2,3},{3,2},{4,5},{5,4},{6,7},{7,6},{8,9},{9,8},{10,11... | collective-permute-start | bytes 24584 | tf_op jit(solution)/shard_map/ppermute | solution.py:507
  97.6 2.2 %collective-permute-done.9.other_ref = f32[128,16]{1,0:T(8,128)S(1)} collective-permute-done((f32[128,16]{1,0:T(8,128)S(1)}, f32[128,16]{1,0:T(8,128)S(1)}, u32[]{:S(2)}, u32[]{:S(2)}) %collective-permute-start.9) | collective-permute-done | bytes 8224 | tf_op jit(solution)/shard_map/ppermute | solution.py:507
  99.8 7.4 %all-to-all-done.1.recv_ref = f32[256,1,128]{2,1,0:T(1,128)S(1)} async-done(((f32[256,1,128]{2,1,0:T(1,128)}), f32[256,1,128]{2,1,0:T(1,128)S(1)}, u32[]{:S(2)}, u32[]{:S(2)}) %all-to-all-start.1) | async-done | bytes 131104 | tf_op jit(solution)/shard_map/all_to_all | solution.py:506
  107.2 1.6 copy-done.2
  108.8 1.0 copy-done.4
  109.8 2.4 %shard_map.88 = (bf16[128,16,512]{2,1,0:T(8,128)(2,1)S(1)}, f32[128,8]{1,0:T(8,128)S(1)}) custom-call(bf16[4,4,4,128,128]{4,3,2,1,0:T(8,128)(2,1)S(1)} %copy-done.2, bf16[4,4,128,128]{3,2,1,0:T(8,128)(2,1)S(1)} %copy-done.4, f32[4,4,128,128]{3,2,1,0:T(8,128)S(1)} %get-tuple-element.26.prob_ref, f32[128,128]{1,0:T(8,128)S(1)} %get-tuple-element.27.sums_ref, ...), custom_call_target="tpu_custom_call" | custom-call | flops 1000000000 | bytes 6291456 | tf_op jit(solution)/shard_map/pallas_call | solution.py:293
  112.2 1.3 copy-done
  113.6 6.3 %all-to-all-start.2 = ((bf16[128,16,512]{2,1,0:T(8,128)(2,1)}), bf16[128,16,512]{2,1,0:T(8,128)(2,1)S(1)}, u32[]{:S(2)}, u32[]{:S(2)}) async-start(bf16[128,16,512]{2,1,0:T(8,128)(2,1)} %copy-done), calls=%async_computation.2 | async-start | bytes 4194304 | tf_op jit(solution)/shard_map/all_to_all | solution.py:509
  120.0 0.9 copy.30
  120.8 10.5 %shard_map.89 = (bf16[4,512,512]{2,1,0:T(8,128)(2,1)}, f32[512,1024]{1,0:T(8,128)}) custom-call(bf16[4,512,512]{2,1,0:T(8,128)(2,1)} %shard_map.85.rows_ref, bf16[512,1024]{1,0:T(8,128)(2,1)} %constant_dynamic-update-slice_fusion.5.summ_ref, s32[1,512]{1,0:T(1,128)} %broadcast_in_dim_reshape.3.seen_ref, bf16[512,512]{1,0:T(8,128)(2,1)} %get-tuple-element.30.attn_ref, ...), custom_call_target="tpu_custom_call" | custom-call | flops 8000000000 | bytes 8388608 | tf_op jit(solution)/shard_map/pallas_call | solution.py:339
  131.3 1.3 slice.131
  132.6 1.3 collective-permute-start.10
  133.9 1.5 collective-permute-done.10
  135.5 1.4 convert_add_fusion
  136.9 0.7 collective-permute-start.11
  137.5 11.1 %collective-permute-done.11 = bf16[128,1024]{1,0:T(8,128)(2,1)S(1)} collective-permute-done((bf16[128,1024]{1,0:T(8,128)(2,1)S(1)}, bf16[128,1024]{1,0:T(8,128)(2,1)S(1)}, u32[]{:S(2)}, u32[]{:S(2)}) %collective-permute-start.11) | collective-permute-done | bytes 262176 | tf_op jit(solution)/shard_map/ppermute | solution.py:445
  148.7 0.1 fusion.19
  148.8 3.0 %collective-permute-start.12 = (bf16[32,1024]{1,0:T(8,128)(2,1)S(1)}, bf16[32,1024]{1,0:T(8,128)(2,1)S(1)}, u32[]{:S(2)}, u32[]{:S(2)}) collective-permute-start(bf16[32,1024]{1,0:T(8,128)(2,1)S(1)} %get-tuple-element.44), channel_id=1, source_target_pairs={{0,12},{2,14},{4,0},{6,2},{8,4},{10,6},{12,8},{14,10},{16,28},{18,... | collective-permute-start | bytes 196616 | tf_op jit(solution)/shard_map/ppermute | solution.py:445
  151.8 0.7 collective-permute-start.13
  152.5 1.8 %collective-permute-done.12 = bf16[32,1024]{1,0:T(8,128)(2,1)S(1)} collective-permute-done((bf16[32,1024]{1,0:T(8,128)(2,1)S(1)}, bf16[32,1024]{1,0:T(8,128)(2,1)S(1)}, u32[]{:S(2)}, u32[]{:S(2)}) %collective-permute-start.12) | collective-permute-done | bytes 65568 | tf_op jit(solution)/shard_map/ppermute | solution.py:445
  154.3 2.6 %collective-permute-done.14 = bf16[32,1024]{1,0:T(8,128)(2,1)S(1)} collective-permute-done((bf16[32,1024]{1,0:T(8,128)(2,1)S(1)}, bf16[32,1024]{1,0:T(8,128)(2,1)S(1)}, u32[]{:S(2)}, u32[]{:S(2)}) %collective-permute-start.14) | collective-permute-done | bytes 65568 | tf_op jit(solution)/shard_map/ppermute | solution.py:445
  157.0 0.8 collective-permute-done.13
  157.9 6.5 %collective-permute-start.15 = (bf16[12,1024]{1,0:T(8,128)(2,1)S(1)}, bf16[12,1024]{1,0:T(8,128)(2,1)S(1)}, u32[]{:S(2)}, u32[]{:S(2)}) collective-permute-start(bf16[12,1024]{1,0:T(8,128)(2,1)S(1)} %slice.107), channel_id=1, source_target_pairs={{0,160},{2,162},{4,164},{6,166},{8,168},{10,170},{12,172},{14,174}... | collective-permute-start | bytes 73736 | tf_op jit(solution)/shard_map/ppermute | solution.py:445
  164.4 6.0 %collective-permute-done.16 = bf16[8,1024]{1,0:T(8,128)(2,1)S(1)} collective-permute-done((bf16[8,1024]{1,0:T(8,128)(2,1)S(1)}, bf16[8,1024]{1,0:T(8,128)(2,1)S(1)}, u32[]{:S(2)}, u32[]{:S(2)}) %collective-permute-start.16) | collective-permute-done | bytes 16416 | tf_op jit(solution)/shard_map/ppermute | solution.py:445
  170.5 1.3 collective-permute-start.17
  171.8 0.2 collective-permute-start.18
  172.0 1.0 collective-permute-done.17
  173.0 2.4 %collective-permute-done.18 = bf16[4,1024]{1,0:T(4,128)(2,1)S(1)} collective-permute-done((bf16[4,1024]{1,0:T(4,128)(2,1)S(1)}, bf16[4,1024]{1,0:T(4,128)(2,1)S(1)}, u32[]{:S(2)}, u32[]{:S(2)}) %collective-permute-start.18) | collective-permute-done | bytes 8224 | tf_op jit(solution)/shard_map/ppermute | solution.py:445
  175.6 1.6 copy-done.5
  177.2 4.2 %shard_map.90 = (bf16[4096,128]{1,0:T(8,128)(2,1)}, bf16[4096,128]{1,0:T(8,128)(2,1)}, bf16[4096,128]{1,0:T(8,128)(2,1)}, bf16[4096,128]{1,0:T(8,128)(2,1)}) custom-call(bf16[128,16,512]{2,1,0:T(8,128)(2,1)S(1)} %all-to-all-done.2.recv_ref, bf16[4,512,512]{2,1,0:T(8,128)(2,1)S(1)} %copy-done.5, bf16[2,16,512]{2,1,0:T(8,128)(2,1)S(1)} %pad.18.tail_ref), custom_call_target="tpu_custom_call" | custom-call | flops 2000000000 | bytes 8388608 | tf_op jit(solution)/shard_map/pallas_call | solution.py:406
  (49 shorter events, 0.5 us)
Async XLA Ops:
  2.2 7.5 %collective-permute-start = (bf16[4,1024]{1,0:T(4,128)(2,1)S(1)}, bf16[4,1024]{1,0:T(4,128)(2,1)S(1)}, u32[]{:S(2)}, u32[]{:S(2)}) collective-permute-start(bf16[4,1024]{1,0:T(4,128)(2,1)S(1)} %reshape.93), channel_id=1, source_target_pairs={{0,32},{2,34},{4,36},{6,38},{8,40},{10,42},{12,44},{14,46},{16,48}... | collective-permute-start | bytes 24584 | tf_op jit(solution)/shard_map/ppermute | solution.py:445
  4.7 7.4 %collective-permute-start.1 = (bf16[4,1024]{1,0:T(4,128)(2,1)S(1)}, bf16[4,1024]{1,0:T(4,128)(2,1)S(1)}, u32[]{:S(2)}, u32[]{:S(2)}) collective-permute-start(bf16[4,1024]{1,0:T(4,128)(2,1)S(1)} %reshape.93), channel_id=1, source_target_pairs={{0,224},{2,226},{4,228},{6,230},{8,232},{10,234},{12,236},{14,238}... | collective-permute-start | bytes 24584 | tf_op jit(solution)/shard_map/ppermute | solution.py:445
  9.7 8.0 %collective-permute-start.3 = (bf16[8,1024]{1,0:T(8,128)(2,1)S(1)}, bf16[8,1024]{1,0:T(8,128)(2,1)S(1)}, u32[]{:S(2)}, u32[]{:S(2)}) collective-permute-start(bf16[8,1024]{1,0:T(8,128)(2,1)S(1)} %pad_maximum_fusion.2), channel_id=1, source_target_pairs={{0,160},{2,162},{4,164},{6,166},{8,168},{10,170},{12,172},{14,174}... | collective-permute-start | bytes 49160 | tf_op jit(solution)/shard_map/ppermute | solution.py:445
  12.2 5.9 %collective-permute-start.2 = (bf16[12,1024]{1,0:T(8,128)(2,1)S(1)}, bf16[12,1024]{1,0:T(8,128)(2,1)S(1)}, u32[]{:S(2)}, u32[]{:S(2)}) collective-permute-start(bf16[12,1024]{1,0:T(8,128)(2,1)S(1)} %pad_maximum_fusion.1), channel_id=1, source_target_pairs={{0,96},{2,98},{4,100},{6,102},{8,104},{10,106},{12,108},{14,110},{... | collective-permute-start | bytes 73736 | tf_op jit(solution)/shard_map/ppermute | solution.py:445
  18.2 62.9 %all-to-all-start = ((bf16[128,16,512]{2,1,0:T(8,128)(2,1)}), bf16[128,16,512]{2,1,0:T(8,128)(2,1)S(1)}, u32[]{:S(2)}, u32[]{:S(2)}) async-start(bf16[128,16,512]{2,1,0:T(8,128)(2,1)} %shard_map.84), calls=%async_computation | async-start | bytes 4194304 | tf_op jit(solution)/shard_map/all_to_all | solution.py:498
  29.8 25.0 %copy-start.7 = (s32[128,1]{0,1:T(1,128)S(1)}, s32[128,1]{0,1:T(1,128)}, u32[]{:S(2)}) copy-start(s32[128,1]{0,1:T(1,128)} %constant.116) | copy-start | bytes 1540
  29.8 25.0 %copy-start.8 = (s32[128,1]{0,1:T(1,128)S(1)}, s32[128,1]{0,1:T(1,128)}, u32[]{:S(2)}) copy-start(s32[128,1]{0,1:T(1,128)} %constant.115) | copy-start | bytes 1540
  29.8 25.0 %copy-start.9 = (s32[128,1]{0,1:T(1,128)S(1)}, s32[128,1]{0,1:T(1,128)}, u32[]{:S(2)}) copy-start(s32[128,1]{0,1:T(1,128)} %constant.114) | copy-start | bytes 1540
  29.8 25.0 %copy-start.10 = (s32[128,1]{0,1:T(1,128)S(1)}, s32[128,1]{0,1:T(1,128)}, u32[]{:S(2)}) copy-start(s32[128,1]{0,1:T(1,128)} %constant.113) | copy-start | bytes 1540
  29.9 8.7 %collective-permute-start.6 = (bf16[32,1024]{1,0:T(8,128)(2,1)S(1)}, bf16[32,1024]{1,0:T(8,128)(2,1)S(1)}, u32[]{:S(2)}, u32[]{:S(2)}) collective-permute-start(bf16[32,1024]{1,0:T(8,128)(2,1)S(1)} %concatenate.27), channel_id=1, source_target_pairs={{0,8},{2,10},{4,12},{6,14},{8,0},{10,2},{12,4},{14,6},{16,24},{18,... | collective-permute-start | bytes 196616 | tf_op jit(solution)/shard_map/ppermute | solution.py:445
  32.8 7.2 %collective-permute-start.5 = (bf16[32,1024]{1,0:T(8,128)(2,1)S(1)}, bf16[32,1024]{1,0:T(8,128)(2,1)S(1)}, u32[]{:S(2)}, u32[]{:S(2)}) collective-permute-start(bf16[32,1024]{1,0:T(8,128)(2,1)S(1)} %concatenate.27), channel_id=1, source_target_pairs={{0,12},{2,14},{4,0},{6,2},{8,4},{10,6},{12,8},{14,10},{16,28},{18,... | collective-permute-start | bytes 196616 | tf_op jit(solution)/shard_map/ppermute | solution.py:445
  33.7 8.0 %collective-permute-start.4 = (bf16[32,1024]{1,0:T(8,128)(2,1)S(1)}, bf16[32,1024]{1,0:T(8,128)(2,1)S(1)}, u32[]{:S(2)}, u32[]{:S(2)}) collective-permute-start(bf16[32,1024]{1,0:T(8,128)(2,1)S(1)} %concatenate.27), channel_id=1, source_target_pairs={{0,4},{2,6},{4,8},{6,10},{8,12},{10,14},{12,0},{14,2},{16,20},{18,... | collective-permute-start | bytes 196616 | tf_op jit(solution)/shard_map/ppermute | solution.py:445
  41.8 10.4 %collective-permute-start.7 = (bf16[128,1024]{1,0:T(8,128)(2,1)S(1)}, bf16[128,1024]{1,0:T(8,128)(2,1)S(1)}, u32[]{:S(2)}, u32[]{:S(2)}) collective-permute-start(bf16[128,1024]{1,0:T(8,128)(2,1)S(1)} %pad_maximum_fusion), channel_id=1, source_target_pairs={{0,16},{2,18},{4,20},{6,22},{8,24},{10,26},{12,28},{14,30},{16,0},... | collective-permute-start | bytes 786440 | tf_op jit(solution)/shard_map/ppermute | solution.py:445
  52.2 2.6 %copy-start.6 = (bf16[512,1024]{1,0:T(8,128)(2,1)}, bf16[512,1024]{1,0:T(8,128)(2,1)S(1)}, u32[]{:S(2)}) copy-start(bf16[512,1024]{1,0:T(8,128)(2,1)S(1)} %get-tuple-element.48) | copy-start | bytes 3145732
  52.2 7.0 %collective-permute-start.8 = (bf16[256,1024]{1,0:T(8,128)(2,1)S(1)}, bf16[256,1024]{1,0:T(8,128)(2,1)S(1)}, u32[]{:S(2)}, u32[]{:S(2)}) collective-permute-start(bf16[256,1024]{1,0:T(8,128)(2,1)S(1)} %get-tuple-element.47), channel_id=1, source_target_pairs={{0,2},{2,0},{4,6},{6,4},{8,10},{10,8},{12,14},{14,12},{16,18},{18,... | collective-permute-start | bytes 1572872 | tf_op jit(solution)/shard_map/ppermute | solution.py:445
  84.3 1.3 copy-start.1
  85.6 0.8 copy-start.3
  86.4 20.8 %all-to-all-start.1 = ((f32[256,1,128]{2,1,0:T(1,128)}), f32[256,1,128]{2,1,0:T(1,128)S(1)}, u32[]{:S(2)}, u32[]{:S(2)}) async-start(f32[256,1,128]{2,1,0:T(1,128)} %get-tuple-element.28), calls=%async_computation.1 | async-start | bytes 262144 | tf_op jit(solution)/shard_map/all_to_all | solution.py:506
  94.6 5.1 %collective-permute-start.9 = (f32[128,16]{1,0:T(8,128)S(1)}, f32[128,16]{1,0:T(8,128)S(1)}, u32[]{:S(2)}, u32[]{:S(2)}) collective-permute-start(f32[128,16]{1,0:T(8,128)S(1)} %bitcast.75), channel_id=1, source_target_pairs={{0,1},{1,0},{2,3},{3,2},{4,5},{5,4},{6,7},{7,6},{8,9},{9,8},{10,11... | collective-permute-start | bytes 24584 | tf_op jit(solution)/shard_map/ppermute | solution.py:507
  107.2 1.6 copy-start.2
  108.8 1.0 copy-start.4
  112.2 1.3 copy-start
  113.6 62.0 %all-to-all-start.2 = ((bf16[128,16,512]{2,1,0:T(8,128)(2,1)}), bf16[128,16,512]{2,1,0:T(8,128)(2,1)S(1)}, u32[]{:S(2)}, u32[]{:S(2)}) async-start(bf16[128,16,512]{2,1,0:T(8,128)(2,1)} %copy-done), calls=%async_computation.2 | async-start | bytes 4194304 | tf_op jit(solution)/shard_map/all_to_all | solution.py:509
  132.6 2.8 %collective-permute-start.10 = (bf16[256,1024]{1,0:T(8,128)(2,1)S(1)}, bf16[256,1024]{1,0:T(8,128)(2,1)S(1)}, u32[]{:S(2)}, u32[]{:S(2)}) collective-permute-start(bf16[256,1024]{1,0:T(8,128)(2,1)S(1)} %slice.131), channel_id=1, source_target_pairs={{0,2},{2,0},{4,6},{6,4},{8,10},{10,8},{12,14},{14,12},{16,18},{18,... | collective-permute-start | bytes 1572872 | tf_op jit(solution)/shard_map/ppermute | solution.py:445
  136.9 11.8 %collective-permute-start.11 = (bf16[128,1024]{1,0:T(8,128)(2,1)S(1)}, bf16[128,1024]{1,0:T(8,128)(2,1)S(1)}, u32[]{:S(2)}, u32[]{:S(2)}) collective-permute-start(bf16[128,1024]{1,0:T(8,128)(2,1)S(1)} %slice.132), channel_id=1, source_target_pairs={{0,16},{2,18},{4,20},{6,22},{8,24},{10,26},{12,28},{14,30},{16,0},... | collective-permute-start | bytes 786440 | tf_op jit(solution)/shard_map/ppermute | solution.py:445
  148.8 5.5 %collective-permute-start.12 = (bf16[32,1024]{1,0:T(8,128)(2,1)S(1)}, bf16[32,1024]{1,0:T(8,128)(2,1)S(1)}, u32[]{:S(2)}, u32[]{:S(2)}) collective-permute-start(bf16[32,1024]{1,0:T(8,128)(2,1)S(1)} %get-tuple-element.44), channel_id=1, source_target_pairs={{0,12},{2,14},{4,0},{6,2},{8,4},{10,6},{12,8},{14,10},{16,28},{18,... | collective-permute-start | bytes 196616 | tf_op jit(solution)/shard_map/ppermute | solution.py:445
  151.8 5.2 %collective-permute-start.14 = (bf16[32,1024]{1,0:T(8,128)(2,1)S(1)}, bf16[32,1024]{1,0:T(8,128)(2,1)S(1)}, u32[]{:S(2)}, u32[]{:S(2)}) collective-permute-start(bf16[32,1024]{1,0:T(8,128)(2,1)S(1)} %get-tuple-element.45), channel_id=1, source_target_pairs={{0,8},{2,10},{4,12},{6,14},{8,0},{10,2},{12,4},{14,6},{16,24},{18,... | collective-permute-start | bytes 196616 | tf_op jit(solution)/shard_map/ppermute | solution.py:445
  151.8 6.0 %collective-permute-start.13 = (bf16[32,1024]{1,0:T(8,128)(2,1)S(1)}, bf16[32,1024]{1,0:T(8,128)(2,1)S(1)}, u32[]{:S(2)}, u32[]{:S(2)}) collective-permute-start(bf16[32,1024]{1,0:T(8,128)(2,1)S(1)} %get-tuple-element.46), channel_id=1, source_target_pairs={{0,4},{2,6},{4,8},{6,10},{8,12},{10,14},{12,0},{14,2},{16,20},{18,... | collective-permute-start | bytes 196616 | tf_op jit(solution)/shard_map/ppermute | solution.py:445
  157.9 12.6 %collective-permute-start.15 = (bf16[12,1024]{1,0:T(8,128)(2,1)S(1)}, bf16[12,1024]{1,0:T(8,128)(2,1)S(1)}, u32[]{:S(2)}, u32[]{:S(2)}) collective-permute-start(bf16[12,1024]{1,0:T(8,128)(2,1)S(1)} %slice.107), channel_id=1, source_target_pairs={{0,160},{2,162},{4,164},{6,166},{8,168},{10,170},{12,172},{14,174}... | collective-permute-start | bytes 73736 | tf_op jit(solution)/shard_map/ppermute | solution.py:445
  164.4 6.0 %collective-permute-start.16 = (bf16[8,1024]{1,0:T(8,128)(2,1)S(1)}, bf16[8,1024]{1,0:T(8,128)(2,1)S(1)}, u32[]{:S(2)}, u32[]{:S(2)}) collective-permute-start(bf16[8,1024]{1,0:T(8,128)(2,1)S(1)} %slice.108), channel_id=1, source_target_pairs={{0,96},{2,98},{4,100},{6,102},{8,104},{10,106},{12,108},{14,110},{... | collective-permute-start | bytes 49160 | tf_op jit(solution)/shard_map/ppermute | solution.py:445
  170.5 2.6 %collective-permute-start.17 = (bf16[4,1024]{1,0:T(4,128)(2,1)S(1)}, bf16[4,1024]{1,0:T(4,128)(2,1)S(1)}, u32[]{:S(2)}, u32[]{:S(2)}) collective-permute-start(bf16[4,1024]{1,0:T(4,128)(2,1)S(1)} %get-tuple-element.57), channel_id=1, source_target_pairs={{0,224},{2,226},{4,228},{6,230},{8,232},{10,234},{12,236},{14,238}... | collective-permute-start | bytes 24584 | tf_op jit(solution)/shard_map/ppermute | solution.py:445
  171.8 3.7 %collective-permute-start.18 = (bf16[4,1024]{1,0:T(4,128)(2,1)S(1)}, bf16[4,1024]{1,0:T(4,128)(2,1)S(1)}, u32[]{:S(2)}, u32[]{:S(2)}) collective-permute-start(bf16[4,1024]{1,0:T(4,128)(2,1)S(1)} %get-tuple-element.58), channel_id=1, source_target_pairs={{0,32},{2,34},{4,36},{6,38},{8,40},{10,42},{12,44},{14,46},{16,48}... | collective-permute-start | bytes 24584 | tf_op jit(solution)/shard_map/ppermute | solution.py:445
  175.6 1.6 copy-start.5

commit v3 on v2

--- a/solution.py
+++ b/solution.py
@@ -73,43 +73,82 @@
     )
 
 
+IN_HBM = pl.BlockSpec(memory_space=pltpu.HBM)
+
+
+def in_hbm(array):
+    return pltpu.with_memory_space_constraint(array, pltpu.HBM)
+
+
+def copy_all(pairs, sems):
+    copies = [
+        pltpu.make_async_copy(source, target, sems.at[n]) for n, (source, target) in enumerate(pairs)
+    ]
+    for copy in copies:
+        copy.start()
+    return copies
+
+
 def spec(block, *index):
     return pl.BlockSpec(block, lambda i: tuple(i if at == "i" else at for at in index))
 
 
-def pack_strided_kernel(q_ref, k_ref, v_ref, c_ref, send_ref, pick_ref):
-    @pl.when(pl.program_id(0) == 0)
-    def _():
-        row, col = iotas((128, 256))
-        home, head, array, offset = row >> 6, (row >> 4) & 3, (row >> 2) & 3, row & 3
-        pick_ref[...] = one_hot(col == array * 64 + ((home * OFFS + offset) * HEADS + head) * 2)
-
-    pick = pick_ref[...]
-    for at in range(0, 32, 2):
-        pair = [
-            jnp.concatenate([ref[64 * n : 64 * (n + 1)] for n in (at, at + 1)], 1)
-            for ref in (q_ref, k_ref, v_ref, c_ref)
-        ]
-        picked = dot(pick, jnp.concatenate(pair, 0)).astype(BF16)
-        for n in range(2):
-            for home in range(2):
-                for head in range(HEADS):
-                    row = home * 64 + head * 16
-                    send_ref[2 * (at + n) + home, :, head * HD : (head + 1) * HD] = picked[
-                        row : row + 16, n * HD : (n + 1) * HD
-                    ]
+def pack_strided_kernel(q_ref, k_ref, v_ref, c_ref, send_ref, rows_ref, out_ref, in_sem, out_sem):
+    parts = 4
+    size = BLOCK * 8 // parts
+    copies = copy_all(
+        [
+            (ref.at[pl.ds(part * size, size)], rows_ref.at[array, pl.ds(part * size, size)])
+            for part in range(parts)
+            for array, ref in enumerate((q_ref, k_ref, v_ref, c_ref))
+        ],
+        in_sem,
+    )
+    row, col = iotas((128, 256))
+    home, head, array, offset = row >> 6, (row >> 4) & 3, (row >> 2) & 3, row & 3
+    pick = one_hot(col == array * 64 + ((home * OFFS + offset) * HEADS + head) * 2)
+    sent = []
+    for part in range(parts):
+        for copy in copies[4 * part : 4 * part + 4]:
+            copy.wait()
+        for at in range(part * 64 // parts, (part + 1) * 64 // parts, 2):
+            pair = [
+                jnp.concatenate(
+                    [rows_ref[array, 64 * n : 64 * (n + 1)] for n in (at, at + 1)], 1
+                )
+                for array in range(4)
+            ]
+            picked = dot(pick, jnp.concatenate(pair, 0)).astype(BF16)
+            for n in range(2):
+                for home in range(2):
+                    for head in range(HEADS):
+                        row = home * 64 + head * 16
+                        out_ref[2 * (at + n) + home, :, head * HD : (head + 1) * HD] = picked[
+                            row : row + 16, n * HD : (n + 1) * HD
+                        ]
+        where = pl.ds(part * NB // parts, NB // parts)
+        copy = pltpu.make_async_copy(out_ref.at[where], send_ref.at[where], out_sem.at[part])
+        copy.start()
+        sent.append(copy)
+    for copy in sent:
+        copy.wait()
 
 
 def pack_strided(arrays):
     return call(
         pack_strided_kernel,
-        2,
-        [spec((2048, HD), "i", 0)] * 4,
-        spec((64, 16, WIDTH), "i", 0, 0),
+        1,
+        [IN_HBM] * 4,
+        IN_HBM,
         jax.ShapeDtypeStruct((NB, 16, WIDTH), BF16),
         10**9,
         6 * 2**20,
-        [pltpu.VMEM((128, 256), BF16)],
+        [
+            pltpu.VMEM((4, BLOCK * 8, HD), BF16),
+            pltpu.VMEM((NB, 16, WIDTH), BF16),
+            pltpu.SemaphoreType.DMA((16,)),
+            pltpu.SemaphoreType.DMA((4,)),
+        ],
     )(*arrays)
 
 
@@ -197,7 +236,10 @@
     return one_hot(col == ((row & 15) << 4) + (row >> 4))
 
 
-def strided_forward_kernel(recv_ref, fixed_ref, grp_ref, attn_ref, prob_ref, sums_ref, send_ref):
+def strided_forward_kernel(
+    recv_ref, fixed_ref, grp_out, attn_out, prob_out, sums_ref, send_ref,
+    grp_ref, attn_ref, prob_ref, sem,
+):
     swap = swap_matrix()
     for at in range(0, NB, 16):
         rows = dot(swap, recv_ref[at : at + 16].reshape(256, WIDTH)).astype(BF16)
@@ -205,6 +247,7 @@
             grp_ref[head, :, :, at : at + 16, :] = rows[:, head * HD : (head + 1) * HD].reshape(
                 4, OFFS, 16, HD
             )
+    copies = copy_all([(grp_ref, grp_out)], sem.at[0])
     row, col = iotas((NB, NB))
     square, cross = 0.0, 0.0
     for head in range(HEADS):
@@ -218,6 +261,10 @@
         wide = attn.astype(F32)
         square += wide * wide
         cross += wide * grp_ref[head, 3].astype(F32)
+        copies += copy_all(
+            [(prob_ref.at[head], prob_out.at[head]), (attn_ref.at[head], attn_out.at[head])],
+            sem.at[head + 1],
+        )
     square = jnp.sum(square, axis=-1, keepdims=True)
     cross = jnp.sum(cross, axis=-1, keepdims=True)
     lane = lax.broadcasted_iota(jnp.int32, (NB, HD), 1)
@@ -227,6 +274,8 @@
     sums_ref[...] = part
     for head in range(2):
         send_ref[head * NB : (head + 1) * NB] = part.reshape(NB, 1, HD)
+    for copy in copies:
+        copy.wait()
 
 
 def strided_forward(recv, fixed_sums):
@@ -235,21 +284,27 @@
         1,
         [spec((NB, 16, WIDTH), 0, 0, 0), spec((NB, HD), 0, 0)],
         [
-            spec((HEADS, 4, OFFS, NB, HD), 0, 0, 0, 0, 0),
-            spec((HEADS, OFFS, NB, HD), 0, 0, 0, 0),
-            spec((HEADS, OFFS, NB, NB), 0, 0, 0, 0),
+            IN_HBM,
+            IN_HBM,
+            IN_HBM,
             spec((NB, HD), 0, 0),
             spec((2 * NB, 1, HD), 0, 0, 0),
         ],
         [
-            jax.ShapeDtypeStruct((HEADS, 4, OFFS, NB, HD), BF16),
-            jax.ShapeDtypeStruct((HEADS, OFFS, NB, HD), BF16),
-            jax.ShapeDtypeStruct((HEADS, OFFS, NB, NB), F32),
+            pltpu.HBM((HEADS, 4, OFFS, NB, HD), BF16),
+            pltpu.HBM((HEADS, OFFS, NB, HD), BF16),
+            pltpu.HBM((HEADS, OFFS, NB, NB), F32),
             jax.ShapeDtypeStruct((NB, HD), F32),
             jax.ShapeDtypeStruct((2 * NB, 1, HD), F32),
         ],
         10**9,
         6 * 2**20,
+        [
+            pltpu.VMEM((HEADS, 4, OFFS, NB, HD), BF16),
+            pltpu.VMEM((HEADS, OFFS, NB, HD), BF16),
+            pltpu.VMEM((HEADS, OFFS, NB, NB), F32),
+            pltpu.SemaphoreType.DMA((HEADS + 1, 2)),
+        ],
         vmem=VMEM3,
     )(recv, fixed_sums)
 
@@ -264,8 +319,20 @@
 
 
 def strided_backward_kernel(
-    grp_ref, attn_ref, prob_ref, sums_ref, other_ref, recv_ref, send_ref, block_ref, out_ref
+    grp_in, attn_in, prob_in, sums_ref, other_ref, recv_ref, send_out, block_ref,
+    grp_ref, attn_ref, prob_ref, out_ref, send_ref, in_sem, out_sem,
 ):
+    copies = [
+        copy_all(
+            [
+                (attn_in.at[head], attn_ref.at[head]),
+                (grp_in.at[head], grp_ref.at[head]),
+                (prob_in.at[head], prob_ref.at[head]),
+            ],
+            in_sem.at[head],
+        )
+        for head in range(HEADS)
+    ]
     both = sums_ref[:, :16] + other_ref[...]
     moved = (recv_ref[:NB] + recv_ref[NB:]).reshape(NB, HD)
     block_ref[...] = both[:, :8] + moved[:, 8:16]
@@ -273,6 +340,8 @@
     square = jnp.stack([total[:, at : at + 1] for at in range(OFFS)])
     cross = jnp.stack([total[:, OFFS + at : OFFS + at + 1] for at in range(OFFS)])
     for head in range(HEADS):
+        for copy in copies[head]:
+            copy.wait()
         wide = attn_ref[head].astype(F32)
         normed, grad, row_dot = normalize(wide, grp_ref[head, 3], square, cross)
         prob = prob_ref[head]
@@ -283,10 +352,15 @@
         out_ref[head, 2] = batch_dot(grad_score, grp_ref[head, 0], 1, 1).astype(BF16)
         out_ref[head, 3] = batch_dot(prob.astype(BF16), grad, 1, 1).astype(BF16)
     swap = swap_matrix()
+    copies = []
     for at in range(0, NB, 16):
         rows = [out_ref[head, :, :, at : at + 16, :].reshape(256, HD) for head in range(HEADS)]
         moved = dot(swap, jnp.concatenate(rows, 1)).astype(BF16)
         send_ref[at : at + 16] = moved.reshape(16, 16, WIDTH)
+        where = pl.ds(at, 16)
+        copies += copy_all([(send_ref.at[where], send_out.at[where])], out_sem.at[at // 16])
+    for copy in copies:
+        copy.wait()
 
 
 def strided_backward(grp, attn, prob, sums, other, recv):
@@ -294,23 +368,31 @@
         strided_backward_kernel,
         1,
         [
-            spec((HEADS, 4, OFFS, NB, HD), 0, 0, 0, 0, 0),
-            spec((HEADS, OFFS, NB, HD), 0, 0, 0, 0),
-            spec((HEADS, OFFS, NB, NB), 0, 0, 0, 0),
+            IN_HBM,
+            IN_HBM,
+            IN_HBM,
             spec((NB, HD), 0, 0),
             spec((NB, 16), 0, 0),
             spec((2 * NB, 1, HD), 0, 0, 0),
         ],
-        [spec((NB, 16, WIDTH), 0, 0, 0), spec((NB, 8), 0, 0)],
-        [
-            jax.ShapeDtypeStruct((NB, 16, WIDTH), BF16),
+        [IN_HBM, spec((NB, 8), 0, 0)],
+        [
+            pltpu.HBM((NB, 16, WIDTH), BF16),
             jax.ShapeDtypeStruct((NB, 8), F32),
         ],
         10**9,
         6 * 2**20,
-        [pltpu.VMEM((HEADS, 4, OFFS, NB, HD), BF16)],
+        [
+            pltpu.VMEM((HEADS, 4, OFFS, NB, HD), BF16),
+            pltpu.VMEM((HEADS, OFFS, NB, HD), BF16),
+            pltpu.VMEM((HEADS, OFFS, NB, NB), F32),
+            pltpu.VMEM((HEADS, 4, OFFS, NB, HD), BF16),
+            pltpu.VMEM((NB, 16, WIDTH), BF16),
+            pltpu.SemaphoreType.DMA((HEADS, 3)),
+            pltpu.SemaphoreType.DMA((NB // 16, 1)),
+        ],
         vmem=VMEM4,
-    )(grp, attn, prob, sums, other, recv)
+    )(*[in_hbm(array) for array in (grp, attn, prob)], sums, other, recv)
 
 
 def fixed_backward_kernel(rows_ref, summ_ref, seen_ref, attn_ref, sums_ref, out_ref, part_ref):
@@ -348,7 +430,7 @@
         ],
         [spec((4, BLOCK, HD), 0, 0, "i"), spec((BLOCK, 2 * HD), 0, "i")],
         [
-            jax.ShapeDtypeStruct((4, BLOCK, WIDTH), BF16),
+            pltpu.HBM((4, BLOCK, WIDTH), BF16),
             jax.ShapeDtypeStruct((BLOCK, 2 * WIDTH), F32),
         ],
         8 * 10**9,
@@ -356,22 +438,29 @@
     )(rows, summ, seen, attn, sums)
 
 
-def unpack_kernel(recv_ref, fixed_ref, tail_ref, *refs):
-    out_refs, strided_ref, own_ref = refs[:4], refs[4], refs[5]
-
-    @pl.when(pl.program_id(0) == 0)
-    def _():
-        row, col = iotas((512, 256))
-        array, token, head, kind = row >> 7, (row >> 3) & 15, (row >> 1) & 3, row & 1
-        source = (token >> 2) * 64 + head * 16 + array * OFFS + (token & 3)
-        strided_ref[...] = one_hot((kind == 0) & (col == source))
-        row, col = iotas((128, 64))
-        token, head, kind = row >> 3, (row >> 1) & 3, row & 1
-        own_ref[...] = one_hot((kind == 1) & (col == head * 16 + token))
-
-    last = pl.program_id(0) == 1
+def unpack_kernel(recv_ref, fixed_in, tail_ref, *refs):
+    outs, fixed_ref, out_ref, in_sem, out_sem = refs[:4], refs[4], refs[5], refs[6], refs[7]
+    parts = 4
+    size = BLOCK // parts
+    copies = copy_all(
+        [
+            (fixed_in.at[:, pl.ds(part * size, size)], fixed_ref.at[:, pl.ds(part * size, size)])
+            for part in range(parts)
+        ],
+        in_sem,
+    )
+    sent = []
+    row, col = iotas((512, 256))
+    array, token, head, kind = row >> 7, (row >> 3) & 15, (row >> 1) & 3, row & 1
+    source = (token >> 2) * 64 + head * 16 + array * OFFS + (token & 3)
+    strided_pick = one_hot((kind == 0) & (col == source))
+    row, col = iotas((128, 64))
+    token, head, kind = row >> 3, (row >> 1) & 3, row & 1
+    own_pick = one_hot((kind == 1) & (col == head * 16 + token))
     end = lax.broadcasted_iota(jnp.int32, (16, WIDTH), 0) >= 16 - SUMM
-    for at in range(0, 16, 2):
+    for at in range(0, 32, 2):
+        if at * 16 % size == 0:
+            copies[at * 16 // size].wait()
         rows = [
             jnp.concatenate(
                 [
@@ -383,41 +472,51 @@
             )
             for n in (at, at + 1)
         ]
-        strided = dot(strided_ref[...], jnp.concatenate(rows, 1))
+        strided = dot(strided_pick, jnp.concatenate(rows, 1))
         for n in range(2):
             tile = 16 * (at + n)
             fixed = [fixed_ref[array, tile : tile + 16] for array in range(4)]
-            if tile == BLOCK // 2 - 16:
+            if tile == BLOCK - 16:
                 for array in (2, 3):
-                    fixed[array] = jnp.where(end & last, tail_ref[array - 2], fixed[array])
+                    fixed[array] = jnp.where(end, tail_ref[array - 2], fixed[array])
             rows = [
                 jnp.concatenate([part[:, head * HD : (head + 1) * HD] for part in fixed], 1)
                 for head in range(HEADS)
             ]
-            own = dot(own_ref[...], jnp.concatenate(rows, 0))
+            own = dot(own_pick, jnp.concatenate(rows, 0))
             for array in range(4):
-                out_refs[array][8 * tile : 8 * tile + 128] = (
+                out_ref[array, 8 * tile : 8 * tile + 128] = (
                     strided[array * 128 : (array + 1) * 128, n * HD : (n + 1) * HD]
                     + own[:, array * HD : (array + 1) * HD]
                 ).astype(BF16)
+        if (at + 2) * 16 % size == 0:
+            part = at * 16 // size
+            where = pl.ds(part * size * 8, size * 8)
+            sent += copy_all(
+                [(out_ref.at[array, where], outs[array].at[where]) for array in range(4)],
+                out_sem.at[part],
+            )
+    for copy in sent:
+        copy.wait()
 
 
 def unpack(recv, fixed, tail):
     rows = call(
         unpack_kernel,
-        2,
-        [
-            spec((NB // 2, 16, WIDTH), "i", 0, 0),
-            spec((4, BLOCK // 2, WIDTH), 0, "i", 0),
-            spec((2, 16, WIDTH), 0, 0, 0),
-        ],
-        [spec((BLOCK * 4, HD), "i", 0)] * 4,
+        1,
+        [spec((NB, 16, WIDTH), 0, 0, 0), IN_HBM, spec((2, 16, WIDTH), 0, 0, 0)],
+        [IN_HBM] * 4,
         [jax.ShapeDtypeStruct((BLOCK * 8, HD), BF16)] * 4,
         2 * 10**9,
         8 * 2**20,
-        [pltpu.VMEM((512, 256), BF16), pltpu.VMEM((128, 64), BF16)],
+        [
+            pltpu.VMEM((4, BLOCK, WIDTH), BF16),
+            pltpu.VMEM((4, BLOCK * 8, HD), BF16),
+            pltpu.SemaphoreType.DMA((4,)),
+            pltpu.SemaphoreType.DMA((4, 4)),
+        ],
         vmem=VMEM6,
-    )(recv, fixed, tail)
+    )(recv, in_hbm(fixed), tail)
     return tuple(unflat(array) for array in rows)
 
 
@@ -446,8 +545,8 @@
 
 
 ROUNDS = (
-    ((0, 1, 1), (0, -1, 1)),
-    ((0, 3, 3), (0, -3, 2)),
+    ((0, 1, 1),),
+    ((0, 2, 2), (0, -2, 2), (0, 4, 2)),
     ((2, 1, 8), (2, -1, 8), (2, 2, 8)),
     ((1, 1, 32),),
     ((3, 1, 64),),
@@ -493,7 +592,9 @@
     send = pack_strided(arrays)
     tails = [a[BLOCK - SUMM :, 1].reshape(SUMM, HEADS, 1, HD) for a in (key_rows, value_rows)]
     own_summ = jnp.concatenate(tails, 2).reshape(SUMM, 2 * WIDTH)
-    summ = gather_summaries(own_summ, ROUNDS[:2])
+    summ = gather_summaries(own_summ, ROUNDS[:1])
+    send, summ = lax.optimization_barrier((send, summ))
+    summ = gather_summaries(summ, ROUNDS[1:2])
     send, summ = lax.optimization_barrier((send, summ))
     recv = lax.all_to_all(send, "seq", 0, 0, tiled=True)
     summ = gather_summaries(summ, ROUNDS[2:])

time: 183 us -> 183 us (level); the launches traced: 181 us -> 179 us
  local copies, waits for them, and re-layouts: 14.6 us -> 6.68 us
  Pallas kernels: 36 us -> 40.1 us
  starting transfers between devices: 62 us -> 64 us
    unnamed x26 -> x14, local copies, waits for them, and re-layouts: 7.74 us -> 0.08 us
    pallas_call x3, Pallas kernels: 10.2 us -> 13.5 us  [the longest x1 5.04 us: strided_backward(): call(strided_backward_kernel, 1, [IN_HBM, IN_HBM, IN_HBM, spec((NB, HD),...]
  transfers between devices with their start and end apart: 22 -> 22, of which waited for: 17 -> 17; matrix products, arithmetic and copies ran while one was open for 4% -> 4% of each run, Pallas kernels for 14% -> 15%
where the time goes in v3:
time: 183 us; the launch traced here: 179 us
  waiting for transfers between devices  65.9 us (36%)
  starting transfers between devices  64 us (35%)
  Pallas kernels  40.1 us (22%)
  local copies, waits for them, and re-layouts  6.68 us (4%)
    ppermute x18, waiting for transfers between devices, shift(): return lax.ppermute(array, 'seq', perm)  45 us
    ppermute x18, starting transfers between devices, shift(): return lax.ppermute(array, 'seq', perm)  33.1 us
    all_to_all x1, starting transfers between devices, shards(): recv = lax.all_to_all(send, 'seq', 0, 0, tiled=True)  13.3 us
    all_to_all x1, waiting for transfers between devices, shards(): recv = lax.all_to_all(send, 'seq', 0, 0, tiled=True)  11.3 us
    pallas_call x1, Pallas kernels, fixed_backward(): call(fixed_backward_kernel, HEADS, [spec((4, BLOCK, HD), 0, 0, 'i'), spec...  10.5 us
    pallas_call x1, Pallas kernels, fixed_forward(): call(fixed_forward_kernel, HEADS, [spec((4, BLOCK, HD), 0, 0, 'i'), spec(...  8.64 us
    all_to_all x1, starting transfers between devices, shards(): sums_in = lax.all_to_all(sums_both, ('head', 'seq'), 0, 0, tiled=True)  8.25 us
    all_to_all x1, waiting for transfers between devices, shards(): sums_in = lax.all_to_all(sums_both, ('head', 'seq'), 0, 0, tiled=True)  7.49 us
  transfers between devices with their start and end apart: 22, of which 17 were waited for; matrix products, arithmetic and copies ran while one was open for 4% of the time, Pallas kernels for 15%

profile of v3, /device:TPU:1, one launch (start us, length us, event | category | flops | bytes accessed | tf_op | source)
XLA Modules:
  0.0 179.3 jit_solution(5198481740709068462)
XLA Ops:
  0.6 0.7 slice_reduce_fusion.1
  1.4 0.7 slice_reduce_fusion
  2.2 2.5 %collective-permute-start = (bf16[4,1024]{1,0:T(4,128)(2,1)S(1)}, bf16[4,1024]{1,0:T(4,128)(2,1)S(1)}, u32[]{:S(2)}, u32[]{:S(2)}) collective-permute-start(bf16[4,1024]{1,0:T(4,128)(2,1)S(1)} %reshape.93), channel_id=1, source_target_pairs={{0,32},{2,34},{4,36},{6,38},{8,40},{10,42},{12,44},{14,46},{16,48}... | collective-permute-start | bytes 24584 | tf_op jit(solution)/shard_map/ppermute | solution.py:544
  4.7 3.4 %shard_map.84 = bf16[128,16,512]{2,1,0:T(8,128)(2,1)} custom-call(bf16[4096,128]{1,0:T(8,128)(2,1)} %bitcast.80, bf16[4096,128]{1,0:T(8,128)(2,1)} %bitcast.76, bf16[4096,128]{1,0:T(8,128)(2,1)} %bitcast.78, bf16[4096,128]{1,0:T(8,128)(2,1)} %bitcast.82), custom_call_target="tpu_custom_call" | custom-call | flops 1000000000 | bytes 6291456 | tf_op jit(solution)/shard_map/pallas_call | solution.py:138
  8.2 1.5 collective-permute-done
  9.7 4.6 %collective-permute-start.3 = (bf16[8,1024]{1,0:T(8,128)(2,1)S(1)}, bf16[8,1024]{1,0:T(8,128)(2,1)S(1)}, u32[]{:S(2)}, u32[]{:S(2)}) collective-permute-start(bf16[8,1024]{1,0:T(8,128)(2,1)S(1)} %pad_maximum_fusion.2), channel_id=1, source_target_pairs={{0,128},{2,130},{4,132},{6,134},{8,136},{10,138},{12,140},{14,142}... | collective-permute-start | bytes 49160 | tf_op jit(solution)/shard_map/ppermute | solution.py:544
  14.3 0.3 collective-permute-start.2
  14.6 2.1 %collective-permute-start.1 = (bf16[8,1024]{1,0:T(8,128)(2,1)S(1)}, bf16[8,1024]{1,0:T(8,128)(2,1)S(1)}, u32[]{:S(2)}, u32[]{:S(2)}) collective-permute-start(bf16[8,1024]{1,0:T(8,128)(2,1)S(1)} %pad_maximum_fusion.2), channel_id=1, source_target_pairs={{0,64},{2,66},{4,68},{6,70},{8,72},{10,74},{12,76},{14,78},{16,80}... | collective-permute-start | bytes 49160 | tf_op jit(solution)/shard_map/ppermute | solution.py:544
  16.7 1.5 collective-permute-done.2
  18.2 1.1 collective-permute-done.1
  19.3 13.3 %all-to-all-start = ((bf16[128,16,512]{2,1,0:T(8,128)(2,1)}), bf16[128,16,512]{2,1,0:T(8,128)(2,1)S(1)}, u32[]{:S(2)}, u32[]{:S(2)}) async-start(bf16[128,16,512]{2,1,0:T(8,128)(2,1)} %shard_map.84), calls=%async_computation | async-start | bytes 4194304 | tf_op jit(solution)/shard_map/all_to_all | solution.py:599
  32.6 0.0 copy-start.1
  32.6 0.0 copy-start.2
  32.6 0.0 copy-start.3
  32.6 0.0 copy-start.4
  32.7 3.0 %collective-permute-start.6 = (bf16[32,1024]{1,0:T(8,128)(2,1)S(1)}, bf16[32,1024]{1,0:T(8,128)(2,1)S(1)}, u32[]{:S(2)}, u32[]{:S(2)}) collective-permute-start(bf16[32,1024]{1,0:T(8,128)(2,1)S(1)} %pad_maximum_fusion.1), channel_id=1, source_target_pairs={{0,8},{2,10},{4,12},{6,14},{8,0},{10,2},{12,4},{14,6},{16,24},{18,... | collective-permute-start | bytes 196616 | tf_op jit(solution)/shard_map/ppermute | solution.py:544
  35.6 0.9 collective-permute-start.5
  36.5 0.6 collective-permute-start.4
  37.1 4.3 %collective-permute-done.6 = bf16[32,1024]{1,0:T(8,128)(2,1)S(1)} collective-permute-done((bf16[32,1024]{1,0:T(8,128)(2,1)S(1)}, bf16[32,1024]{1,0:T(8,128)(2,1)S(1)}, u32[]{:S(2)}, u32[]{:S(2)}) %collective-permute-start.6) | collective-permute-done | bytes 65568 | tf_op jit(solution)/shard_map/ppermute | solution.py:544
  41.4 1.4 collective-permute-done.5
  42.8 1.7 collective-permute-done.4
  44.6 1.1 collective-permute-start.7
  45.7 9.3 %collective-permute-done.7 = bf16[128,1024]{1,0:T(8,128)(2,1)S(1)} collective-permute-done((bf16[128,1024]{1,0:T(8,128)(2,1)S(1)}, bf16[128,1024]{1,0:T(8,128)(2,1)S(1)}, u32[]{:S(2)}, u32[]{:S(2)}) %collective-permute-start.7) | collective-permute-done | bytes 262176 | tf_op jit(solution)/shard_map/ppermute | solution.py:544
  55.0 0.0 copy-start
  55.0 2.6 %collective-permute-start.8 = (bf16[256,1024]{1,0:T(8,128)(2,1)S(1)}, bf16[256,1024]{1,0:T(8,128)(2,1)S(1)}, u32[]{:S(2)}, u32[]{:S(2)}) collective-permute-start(bf16[256,1024]{1,0:T(8,128)(2,1)S(1)} %get-tuple-element.49), channel_id=1, source_target_pairs={{0,2},{2,0},{4,6},{6,4},{8,10},{10,8},{12,14},{14,12},{16,18},{18,... | collective-permute-start | bytes 1572872 | tf_op jit(solution)/shard_map/ppermute | solution.py:544
  57.7 0.1 broadcast_in_dim.3
  57.8 0.7 broadcast_in_dim_reshape.3.seen_ref
  58.4 3.6 %shard_map.85.rows_ref = bf16[4,512,512]{2,1,0:T(8,128)(2,1)} custom-call(bf16[4096,128]{1,0:T(8,128)(2,1)} %bitcast.81, bf16[4096,128]{1,0:T(8,128)(2,1)} %bitcast.77, bf16[4096,128]{1,0:T(8,128)(2,1)} %bitcast.79, bf16[4096,128]{1,0:T(8,128)(2,1)} %bitcast.83), custom_call_target="tpu_custom_call" | custom-call | flops 1000000000 | bytes 6291456 | tf_op jit(solution)/shard_map/pallas_call | solution.py:169
  62.0 0.0 collective-permute-done.8
  62.0 0.8 constant_dynamic-update-slice_fusion.5.summ_ref
  62.8 8.6 %shard_map.86 = (bf16[512,512]{1,0:T(8,128)(2,1)}, f32[512,8]{1,0:T(8,128)}) custom-call(bf16[4,512,512]{2,1,0:T(8,128)(2,1)} %shard_map.85.rows_ref, bf16[512,1024]{1,0:T(8,128)(2,1)} %constant_dynamic-update-slice_fusion.5.summ_ref, s32[1,512]{1,0:T(1,128)} %broadcast_in_dim_reshape.3.seen_ref), custom_call_target="tpu_custom_call" | custom-call | flops 4000000000 | bytes 4194304 | tf_op jit(solution)/shard_map/pallas_call | solution.py:216
  71.5 1.0 copy.27
  72.5 0.1 copy.28
  72.7 11.3 %all-to-all-done.recv_ref = bf16[128,16,512]{2,1,0:T(8,128)(2,1)S(1)} async-done(((bf16[128,16,512]{2,1,0:T(8,128)(2,1)}), bf16[128,16,512]{2,1,0:T(8,128)(2,1)S(1)}, u32[]{:S(2)}, u32[]{:S(2)}) %all-to-all-start) | async-done | bytes 2097184 | tf_op jit(solution)/shard_map/all_to_all | solution.py:599
  83.9 3.8 %shard_map.87 = (bf16[4,4,4,128,128]{4,3,2,1,0:T(8,128)(2,1)}, bf16[4,4,128,128]{3,2,1,0:T(8,128)(2,1)}, f32[4,4,128,128]{3,2,1,0:T(8,128)}, f32[128,128]{1,0:T(8,128)S(1)}, f32[256,1,128]{2,1,0:T(1,128)}) custom-call(bf16[128,16,512]{2,1,0:T(8,128)(2,1)S(1)} %all-to-all-done.recv_ref, f32[128,128]{1,0:T(8,128)S(1)} %pad.8.fixed_ref), custom_call_target="tpu_custom_call" | custom-call | flops 1000000000 | bytes 6291456 | tf_op jit(solution)/shard_map/pallas_call | solution.py:282
  87.8 8.2 %all-to-all-start.1 = ((f32[256,1,128]{2,1,0:T(1,128)}), f32[256,1,128]{2,1,0:T(1,128)S(1)}, u32[]{:S(2)}, u32[]{:S(2)}) async-start(f32[256,1,128]{2,1,0:T(1,128)} %get-tuple-element.32), calls=%async_computation.1 | async-start | bytes 262144 | tf_op jit(solution)/shard_map/all_to_all | solution.py:607
  96.0 3.0 %collective-permute-start.9 = (f32[128,16]{1,0:T(8,128)S(1)}, f32[128,16]{1,0:T(8,128)S(1)}, u32[]{:S(2)}, u32[]{:S(2)}) collective-permute-start(f32[128,16]{1,0:T(8,128)S(1)} %bitcast.75), channel_id=1, source_target_pairs={{0,1},{1,0},{2,3},{3,2},{4,5},{5,4},{6,7},{7,6},{8,9},{9,8},{10,11... | collective-permute-start | bytes 24584 | tf_op jit(solution)/shard_map/ppermute | solution.py:608
  99.0 2.1 %collective-permute-done.9.other_ref = f32[128,16]{1,0:T(8,128)S(1)} collective-permute-done((f32[128,16]{1,0:T(8,128)S(1)}, f32[128,16]{1,0:T(8,128)S(1)}, u32[]{:S(2)}, u32[]{:S(2)}) %collective-permute-start.9) | collective-permute-done | bytes 8224 | tf_op jit(solution)/shard_map/ppermute | solution.py:608
  101.2 7.5 %all-to-all-done.1.recv_ref = f32[256,1,128]{2,1,0:T(1,128)S(1)} async-done(((f32[256,1,128]{2,1,0:T(1,128)}), f32[256,1,128]{2,1,0:T(1,128)S(1)}, u32[]{:S(2)}, u32[]{:S(2)}) %all-to-all-start.1) | async-done | bytes 131104 | tf_op jit(solution)/shard_map/all_to_all | solution.py:607
  108.7 5.0 %shard_map.88 = (bf16[128,16,512]{2,1,0:T(8,128)(2,1)}, f32[128,8]{1,0:T(8,128)S(1)}) custom-call(bf16[4,4,4,128,128]{4,3,2,1,0:T(8,128)(2,1)} %get-tuple-element.28.grp_in, bf16[4,4,128,128]{3,2,1,0:T(8,128)(2,1)} %get-tuple-element.29.attn_in, f32[4,4,128,128]{3,2,1,0:T(8,128)} %get-tuple-element.30.prob_in, f32[128,128]{1,0:T(8,128)S(1)} %get-tuple-element.31.sums_ref, ...), custom_call_target="tpu_custom_call" | custom-call | flops 1000000000 | bytes 6291456 | tf_op jit(solution)/shard_map/pallas_call | solution.py:367
  113.7 6.3 %all-to-all-start.2 = ((bf16[128,16,512]{2,1,0:T(8,128)(2,1)}), bf16[128,16,512]{2,1,0:T(8,128)(2,1)S(1)}, u32[]{:S(2)}, u32[]{:S(2)}) async-start(bf16[128,16,512]{2,1,0:T(8,128)(2,1)} %get-tuple-element.33), calls=%async_computation.2 | async-start | bytes 4194304 | tf_op jit(solution)/shard_map/all_to_all | solution.py:610
  120.1 0.9 copy.30
  121.0 10.5 %shard_map.89 = (bf16[4,512,512]{2,1,0:T(8,128)(2,1)}, f32[512,1024]{1,0:T(8,128)}) custom-call(bf16[4,512,512]{2,1,0:T(8,128)(2,1)} %shard_map.85.rows_ref, bf16[512,1024]{1,0:T(8,128)(2,1)} %constant_dynamic-update-slice_fusion.5.summ_ref, s32[1,512]{1,0:T(1,128)} %broadcast_in_dim_reshape.3.seen_ref, bf16[512,512]{1,0:T(8,128)(2,1)} %get-tuple-element.34.attn_ref, ...), custom_call_target="tpu_custom_call" | custom-call | flops 8000000000 | bytes 8388608 | tf_op jit(solution)/shard_map/pallas_call | solution.py:421
  131.5 1.3 slice.130
  132.8 1.3 collective-permute-start.10
  134.1 1.5 collective-permute-done.10
  135.6 1.4 convert_add_fusion
  137.0 0.7 collective-permute-start.11
  137.7 11.1 %collective-permute-done.11 = bf16[128,1024]{1,0:T(8,128)(2,1)S(1)} collective-permute-done((bf16[128,1024]{1,0:T(8,128)(2,1)S(1)}, bf16[128,1024]{1,0:T(8,128)(2,1)S(1)}, u32[]{:S(2)}, u32[]{:S(2)}) %collective-permute-start.11) | collective-permute-done | bytes 262176 | tf_op jit(solution)/shard_map/ppermute | solution.py:544
  148.9 0.1 fusion.17
  149.0 3.0 %collective-permute-start.12 = (bf16[32,1024]{1,0:T(8,128)(2,1)S(1)}, bf16[32,1024]{1,0:T(8,128)(2,1)S(1)}, u32[]{:S(2)}, u32[]{:S(2)}) collective-permute-start(bf16[32,1024]{1,0:T(8,128)(2,1)S(1)} %get-tuple-element.46), channel_id=1, source_target_pairs={{0,12},{2,14},{4,0},{6,2},{8,4},{10,6},{12,8},{14,10},{16,28},{18,... | collective-permute-start | bytes 196616 | tf_op jit(solution)/shard_map/ppermute | solution.py:544
  151.9 0.0 collective-permute-start.14
  152.0 0.7 collective-permute-start.13
  152.6 1.8 %collective-permute-done.12 = bf16[32,1024]{1,0:T(8,128)(2,1)S(1)} collective-permute-done((bf16[32,1024]{1,0:T(8,128)(2,1)S(1)}, bf16[32,1024]{1,0:T(8,128)(2,1)S(1)}, u32[]{:S(2)}, u32[]{:S(2)}) %collective-permute-start.12) | collective-permute-done | bytes 65568 | tf_op jit(solution)/shard_map/ppermute | solution.py:544
  154.5 2.6 %collective-permute-done.14 = bf16[32,1024]{1,0:T(8,128)(2,1)S(1)} collective-permute-done((bf16[32,1024]{1,0:T(8,128)(2,1)S(1)}, bf16[32,1024]{1,0:T(8,128)(2,1)S(1)}, u32[]{:S(2)}, u32[]{:S(2)}) %collective-permute-start.14) | collective-permute-done | bytes 65568 | tf_op jit(solution)/shard_map/ppermute | solution.py:544
  157.1 0.8 collective-permute-done.13
  158.0 5.6 %collective-permute-start.15 = (bf16[8,1024]{1,0:T(8,128)(2,1)S(1)}, bf16[8,1024]{1,0:T(8,128)(2,1)S(1)}, u32[]{:S(2)}, u32[]{:S(2)}) collective-permute-start(bf16[8,1024]{1,0:T(8,128)(2,1)S(1)} %get-tuple-element.51), channel_id=1, source_target_pairs={{0,192},{2,194},{4,196},{6,198},{8,200},{10,202},{12,204},{14,206}... | collective-permute-start | bytes 49160 | tf_op jit(solution)/shard_map/ppermute | solution.py:544
  163.6 1.9 %collective-permute-start.17 = (bf16[8,1024]{1,0:T(8,128)(2,1)S(1)}, bf16[8,1024]{1,0:T(8,128)(2,1)S(1)}, u32[]{:S(2)}, u32[]{:S(2)}) collective-permute-start(bf16[8,1024]{1,0:T(8,128)(2,1)S(1)} %get-tuple-element.52), channel_id=1, source_target_pairs={{0,128},{2,130},{4,132},{6,134},{8,136},{10,138},{12,140},{14,142}... | collective-permute-start | bytes 49160 | tf_op jit(solution)/shard_map/ppermute | solution.py:544
  165.5 2.3 %collective-permute-start.16 = (bf16[8,1024]{1,0:T(8,128)(2,1)S(1)}, bf16[8,1024]{1,0:T(8,128)(2,1)S(1)}, u32[]{:S(2)}, u32[]{:S(2)}) collective-permute-start(bf16[8,1024]{1,0:T(8,128)(2,1)S(1)} %get-tuple-element.53), channel_id=1, source_target_pairs={{0,64},{2,66},{4,68},{6,70},{8,72},{10,74},{12,76},{14,78},{16,80}... | collective-permute-start | bytes 49160 | tf_op jit(solution)/shard_map/ppermute | solution.py:544
  167.7 0.0 collective-permute-done.15
  167.7 3.7 %collective-permute-done.17 = bf16[8,1024]{1,0:T(8,128)(2,1)S(1)} collective-permute-done((bf16[8,1024]{1,0:T(8,128)(2,1)S(1)}, bf16[8,1024]{1,0:T(8,128)(2,1)S(1)}, u32[]{:S(2)}, u32[]{:S(2)}) %collective-permute-start.17) | collective-permute-done | bytes 16416 | tf_op jit(solution)/shard_map/ppermute | solution.py:544
  171.5 0.1 collective-permute-start.18
  171.6 2.5 %collective-permute-done.18 = bf16[4,1024]{1,0:T(4,128)(2,1)S(1)} collective-permute-done((bf16[4,1024]{1,0:T(4,128)(2,1)S(1)}, bf16[4,1024]{1,0:T(4,128)(2,1)S(1)}, u32[]{:S(2)}, u32[]{:S(2)}) %collective-permute-start.18) | collective-permute-done | bytes 8224 | tf_op jit(solution)/shard_map/ppermute | solution.py:544
  174.1 5.0 %shard_map.90 = (bf16[4096,128]{1,0:T(8,128)(2,1)}, bf16[4096,128]{1,0:T(8,128)(2,1)}, bf16[4096,128]{1,0:T(8,128)(2,1)}, bf16[4096,128]{1,0:T(8,128)(2,1)}) custom-call(bf16[128,16,512]{2,1,0:T(8,128)(2,1)S(1)} %all-to-all-done.2.recv_ref, bf16[4,512,512]{2,1,0:T(8,128)(2,1)} %get-tuple-element.36.fixed_in, bf16[2,16,512]{2,1,0:T(8,128)(2,1)S(1)} %pad.9.tail_ref), custom_call_target="tpu_custom_call" | custom-call | flops 2000000000 | bytes 8388608 | tf_op jit(solution)/shard_map/pallas_call | solution.py:504
  (35 shorter events, 0.4 us)
Async XLA Ops:
  2.2 7.5 %collective-permute-start = (bf16[4,1024]{1,0:T(4,128)(2,1)S(1)}, bf16[4,1024]{1,0:T(4,128)(2,1)S(1)}, u32[]{:S(2)}, u32[]{:S(2)}) collective-permute-start(bf16[4,1024]{1,0:T(4,128)(2,1)S(1)} %reshape.93), channel_id=1, source_target_pairs={{0,32},{2,34},{4,36},{6,38},{8,40},{10,42},{12,44},{14,46},{16,48}... | collective-permute-start | bytes 24584 | tf_op jit(solution)/shard_map/ppermute | solution.py:544
  9.7 6.9 %collective-permute-start.3 = (bf16[8,1024]{1,0:T(8,128)(2,1)S(1)}, bf16[8,1024]{1,0:T(8,128)(2,1)S(1)}, u32[]{:S(2)}, u32[]{:S(2)}) collective-permute-start(bf16[8,1024]{1,0:T(8,128)(2,1)S(1)} %pad_maximum_fusion.2), channel_id=1, source_target_pairs={{0,128},{2,130},{4,132},{6,134},{8,136},{10,138},{12,140},{14,142}... | collective-permute-start | bytes 49160 | tf_op jit(solution)/shard_map/ppermute | solution.py:544
  14.3 3.9 %collective-permute-start.2 = (bf16[8,1024]{1,0:T(8,128)(2,1)S(1)}, bf16[8,1024]{1,0:T(8,128)(2,1)S(1)}, u32[]{:S(2)}, u32[]{:S(2)}) collective-permute-start(bf16[8,1024]{1,0:T(8,128)(2,1)S(1)} %pad_maximum_fusion.2), channel_id=1, source_target_pairs={{0,192},{2,194},{4,196},{6,198},{8,200},{10,202},{12,204},{14,206}... | collective-permute-start | bytes 49160 | tf_op jit(solution)/shard_map/ppermute | solution.py:544
  14.6 4.7 %collective-permute-start.1 = (bf16[8,1024]{1,0:T(8,128)(2,1)S(1)}, bf16[8,1024]{1,0:T(8,128)(2,1)S(1)}, u32[]{:S(2)}, u32[]{:S(2)}) collective-permute-start(bf16[8,1024]{1,0:T(8,128)(2,1)S(1)} %pad_maximum_fusion.2), channel_id=1, source_target_pairs={{0,64},{2,66},{4,68},{6,70},{8,72},{10,74},{12,76},{14,78},{16,80}... | collective-permute-start | bytes 49160 | tf_op jit(solution)/shard_map/ppermute | solution.py:544
  19.3 64.7 %all-to-all-start = ((bf16[128,16,512]{2,1,0:T(8,128)(2,1)}), bf16[128,16,512]{2,1,0:T(8,128)(2,1)S(1)}, u32[]{:S(2)}, u32[]{:S(2)}) async-start(bf16[128,16,512]{2,1,0:T(8,128)(2,1)} %shard_map.84), calls=%async_computation | async-start | bytes 4194304 | tf_op jit(solution)/shard_map/all_to_all | solution.py:599
  32.6 25.0 %copy-start.1 = (s32[128,1]{0,1:T(1,128)S(1)}, s32[128,1]{0,1:T(1,128)}, u32[]{:S(2)}) copy-start(s32[128,1]{0,1:T(1,128)} %constant.113) | copy-start | bytes 1540
  32.6 25.0 %copy-start.2 = (s32[128,1]{0,1:T(1,128)S(1)}, s32[128,1]{0,1:T(1,128)}, u32[]{:S(2)}) copy-start(s32[128,1]{0,1:T(1,128)} %constant.112) | copy-start | bytes 1540
  32.6 25.0 %copy-start.3 = (s32[128,1]{0,1:T(1,128)S(1)}, s32[128,1]{0,1:T(1,128)}, u32[]{:S(2)}) copy-start(s32[128,1]{0,1:T(1,128)} %constant.111) | copy-start | bytes 1540
  32.6 25.0 %copy-start.4 = (s32[128,1]{0,1:T(1,128)S(1)}, s32[128,1]{0,1:T(1,128)}, u32[]{:S(2)}) copy-start(s32[128,1]{0,1:T(1,128)} %constant.110) | copy-start | bytes 1540
  32.7 8.7 %collective-permute-start.6 = (bf16[32,1024]{1,0:T(8,128)(2,1)S(1)}, bf16[32,1024]{1,0:T(8,128)(2,1)S(1)}, u32[]{:S(2)}, u32[]{:S(2)}) collective-permute-start(bf16[32,1024]{1,0:T(8,128)(2,1)S(1)} %pad_maximum_fusion.1), channel_id=1, source_target_pairs={{0,8},{2,10},{4,12},{6,14},{8,0},{10,2},{12,4},{14,6},{16,24},{18,... | collective-permute-start | bytes 196616 | tf_op jit(solution)/shard_map/ppermute | solution.py:544
  35.6 7.2 %collective-permute-start.5 = (bf16[32,1024]{1,0:T(8,128)(2,1)S(1)}, bf16[32,1024]{1,0:T(8,128)(2,1)S(1)}, u32[]{:S(2)}, u32[]{:S(2)}) collective-permute-start(bf16[32,1024]{1,0:T(8,128)(2,1)S(1)} %pad_maximum_fusion.1), channel_id=1, source_target_pairs={{0,12},{2,14},{4,0},{6,2},{8,4},{10,6},{12,8},{14,10},{16,28},{18,... | collective-permute-start | bytes 196616 | tf_op jit(solution)/shard_map/ppermute | solution.py:544
  36.5 8.0 %collective-permute-start.4 = (bf16[32,1024]{1,0:T(8,128)(2,1)S(1)}, bf16[32,1024]{1,0:T(8,128)(2,1)S(1)}, u32[]{:S(2)}, u32[]{:S(2)}) collective-permute-start(bf16[32,1024]{1,0:T(8,128)(2,1)S(1)} %pad_maximum_fusion.1), channel_id=1, source_target_pairs={{0,4},{2,6},{4,8},{6,10},{8,12},{10,14},{12,0},{14,2},{16,20},{18,... | collective-permute-start | bytes 196616 | tf_op jit(solution)/shard_map/ppermute | solution.py:544
  44.6 10.4 %collective-permute-start.7 = (bf16[128,1024]{1,0:T(8,128)(2,1)S(1)}, bf16[128,1024]{1,0:T(8,128)(2,1)S(1)}, u32[]{:S(2)}, u32[]{:S(2)}) collective-permute-start(bf16[128,1024]{1,0:T(8,128)(2,1)S(1)} %pad_maximum_fusion), channel_id=1, source_target_pairs={{0,16},{2,18},{4,20},{6,22},{8,24},{10,26},{12,28},{14,30},{16,0},... | collective-permute-start | bytes 786440 | tf_op jit(solution)/shard_map/ppermute | solution.py:544
  55.0 2.6 %copy-start = (bf16[512,1024]{1,0:T(8,128)(2,1)}, bf16[512,1024]{1,0:T(8,128)(2,1)S(1)}, u32[]{:S(2)}) copy-start(bf16[512,1024]{1,0:T(8,128)(2,1)S(1)} %get-tuple-element.50) | copy-start | bytes 3145732
  55.0 7.0 %collective-permute-start.8 = (bf16[256,1024]{1,0:T(8,128)(2,1)S(1)}, bf16[256,1024]{1,0:T(8,128)(2,1)S(1)}, u32[]{:S(2)}, u32[]{:S(2)}) collective-permute-start(bf16[256,1024]{1,0:T(8,128)(2,1)S(1)} %get-tuple-element.49), channel_id=1, source_target_pairs={{0,2},{2,0},{4,6},{6,4},{8,10},{10,8},{12,14},{14,12},{16,18},{18,... | collective-permute-start | bytes 1572872 | tf_op jit(solution)/shard_map/ppermute | solution.py:544
  87.8 20.9 %all-to-all-start.1 = ((f32[256,1,128]{2,1,0:T(1,128)}), f32[256,1,128]{2,1,0:T(1,128)S(1)}, u32[]{:S(2)}, u32[]{:S(2)}) async-start(f32[256,1,128]{2,1,0:T(1,128)} %get-tuple-element.32), calls=%async_computation.1 | async-start | bytes 262144 | tf_op jit(solution)/shard_map/all_to_all | solution.py:607
  96.0 5.1 %collective-permute-start.9 = (f32[128,16]{1,0:T(8,128)S(1)}, f32[128,16]{1,0:T(8,128)S(1)}, u32[]{:S(2)}, u32[]{:S(2)}) collective-permute-start(f32[128,16]{1,0:T(8,128)S(1)} %bitcast.75), channel_id=1, source_target_pairs={{0,1},{1,0},{2,3},{3,2},{4,5},{5,4},{6,7},{7,6},{8,9},{9,8},{10,11... | collective-permute-start | bytes 24584 | tf_op jit(solution)/shard_map/ppermute | solution.py:608
  113.7 60.4 %all-to-all-start.2 = ((bf16[128,16,512]{2,1,0:T(8,128)(2,1)}), bf16[128,16,512]{2,1,0:T(8,128)(2,1)S(1)}, u32[]{:S(2)}, u32[]{:S(2)}) async-start(bf16[128,16,512]{2,1,0:T(8,128)(2,1)} %get-tuple-element.33), calls=%async_computation.2 | async-start | bytes 4194304 | tf_op jit(solution)/shard_map/all_to_all | solution.py:610
  132.8 2.8 %collective-permute-start.10 = (bf16[256,1024]{1,0:T(8,128)(2,1)S(1)}, bf16[256,1024]{1,0:T(8,128)(2,1)S(1)}, u32[]{:S(2)}, u32[]{:S(2)}) collective-permute-start(bf16[256,1024]{1,0:T(8,128)(2,1)S(1)} %slice.130), channel_id=1, source_target_pairs={{0,2},{2,0},{4,6},{6,4},{8,10},{10,8},{12,14},{14,12},{16,18},{18,... | collective-permute-start | bytes 1572872 | tf_op jit(solution)/shard_map/ppermute | solution.py:544
  137.0 11.8 %collective-permute-start.11 = (bf16[128,1024]{1,0:T(8,128)(2,1)S(1)}, bf16[128,1024]{1,0:T(8,128)(2,1)S(1)}, u32[]{:S(2)}, u32[]{:S(2)}) collective-permute-start(bf16[128,1024]{1,0:T(8,128)(2,1)S(1)} %slice.131), channel_id=1, source_target_pairs={{0,16},{2,18},{4,20},{6,22},{8,24},{10,26},{12,28},{14,30},{16,0},... | collective-permute-start | bytes 786440 | tf_op jit(solution)/shard_map/ppermute | solution.py:544
  149.0 5.5 %collective-permute-start.12 = (bf16[32,1024]{1,0:T(8,128)(2,1)S(1)}, bf16[32,1024]{1,0:T(8,128)(2,1)S(1)}, u32[]{:S(2)}, u32[]{:S(2)}) collective-permute-start(bf16[32,1024]{1,0:T(8,128)(2,1)S(1)} %get-tuple-element.46), channel_id=1, source_target_pairs={{0,12},{2,14},{4,0},{6,2},{8,4},{10,6},{12,8},{14,10},{16,28},{18,... | collective-permute-start | bytes 196616 | tf_op jit(solution)/shard_map/ppermute | solution.py:544
  151.9 5.2 %collective-permute-start.14 = (bf16[32,1024]{1,0:T(8,128)(2,1)S(1)}, bf16[32,1024]{1,0:T(8,128)(2,1)S(1)}, u32[]{:S(2)}, u32[]{:S(2)}) collective-permute-start(bf16[32,1024]{1,0:T(8,128)(2,1)S(1)} %get-tuple-element.47), channel_id=1, source_target_pairs={{0,8},{2,10},{4,12},{6,14},{8,0},{10,2},{12,4},{14,6},{16,24},{18,... | collective-permute-start | bytes 196616 | tf_op jit(solution)/shard_map/ppermute | solution.py:544
  152.0 6.0 %collective-permute-start.13 = (bf16[32,1024]{1,0:T(8,128)(2,1)S(1)}, bf16[32,1024]{1,0:T(8,128)(2,1)S(1)}, u32[]{:S(2)}, u32[]{:S(2)}) collective-permute-start(bf16[32,1024]{1,0:T(8,128)(2,1)S(1)} %get-tuple-element.48), channel_id=1, source_target_pairs={{0,4},{2,6},{4,8},{6,10},{8,12},{10,14},{12,0},{14,2},{16,20},{18,... | collective-permute-start | bytes 196616 | tf_op jit(solution)/shard_map/ppermute | solution.py:544
  158.0 9.8 %collective-permute-start.15 = (bf16[8,1024]{1,0:T(8,128)(2,1)S(1)}, bf16[8,1024]{1,0:T(8,128)(2,1)S(1)}, u32[]{:S(2)}, u32[]{:S(2)}) collective-permute-start(bf16[8,1024]{1,0:T(8,128)(2,1)S(1)} %get-tuple-element.51), channel_id=1, source_target_pairs={{0,192},{2,194},{4,196},{6,198},{8,200},{10,202},{12,204},{14,206}... | collective-permute-start | bytes 49160 | tf_op jit(solution)/shard_map/ppermute | solution.py:544
  163.6 7.8 %collective-permute-start.17 = (bf16[8,1024]{1,0:T(8,128)(2,1)S(1)}, bf16[8,1024]{1,0:T(8,128)(2,1)S(1)}, u32[]{:S(2)}, u32[]{:S(2)}) collective-permute-start(bf16[8,1024]{1,0:T(8,128)(2,1)S(1)} %get-tuple-element.52), channel_id=1, source_target_pairs={{0,128},{2,130},{4,132},{6,134},{8,136},{10,138},{12,140},{14,142}... | collective-permute-start | bytes 49160 | tf_op jit(solution)/shard_map/ppermute | solution.py:544
  165.5 6.0 %collective-permute-start.16 = (bf16[8,1024]{1,0:T(8,128)(2,1)S(1)}, bf16[8,1024]{1,0:T(8,128)(2,1)S(1)}, u32[]{:S(2)}, u32[]{:S(2)}) collective-permute-start(bf16[8,1024]{1,0:T(8,128)(2,1)S(1)} %get-tuple-element.53), channel_id=1, source_target_pairs={{0,64},{2,66},{4,68},{6,70},{8,72},{10,74},{12,76},{14,78},{16,80}... | collective-permute-start | bytes 49160 | tf_op jit(solution)/shard_map/ppermute | solution.py:544
  171.5 2.6 %collective-permute-start.18 = (bf16[4,1024]{1,0:T(4,128)(2,1)S(1)}, bf16[4,1024]{1,0:T(4,128)(2,1)S(1)}, u32[]{:S(2)}, u32[]{:S(2)}) collective-permute-start(bf16[4,1024]{1,0:T(4,128)(2,1)S(1)} %slice.132), channel_id=1, source_target_pairs={{0,224},{2,226},{4,228},{6,230},{8,232},{10,234},{12,236},{14,238}... | collective-permute-start | bytes 24584 | tf_op jit(solution)/shard_map/ppermute | solution.py:544

commit v4 on v3

--- a/solution.py
+++ b/solution.py
@@ -191,8 +191,10 @@
     return own * inverse, far * inverse
 
 
-def fixed_forward_kernel(rows_ref, summ_ref, seen_ref, attn_ref, sums_ref):
+def fixed_forward_kernel(rows_ref, summ_ref, seen_ref, attn_ref, own_ref, far_ref, sums_ref):
     own, far = fixed_probabilities(rows_ref[0], rows_ref[1], summ_ref[:, :HD], seen_ref[...])
+    own_ref[0] = own
+    far_ref[0] = far
     attn = (
         dot(own.astype(BF16), rows_ref[2]) + dot(far.astype(BF16), summ_ref[:, HD:])
     ).astype(BF16)
@@ -221,9 +223,16 @@
             spec((BLOCK, 2 * HD), 0, "i"),
             spec((1, BLOCK), 0, 0),
         ],
-        [spec((BLOCK, HD), 0, "i"), spec((BLOCK, 8), 0, 0)],
+        [
+            spec((BLOCK, HD), 0, "i"),
+            spec((1, BLOCK, BLOCK), "i", 0, 0),
+            spec((1, BLOCK, BLOCK), "i", 0, 0),
+            spec((BLOCK, 8), 0, 0),
+        ],
         [
             jax.ShapeDtypeStruct((BLOCK, WIDTH), BF16),
+            jax.ShapeDtypeStruct((HEADS, BLOCK, BLOCK), F32),
+            jax.ShapeDtypeStruct((HEADS, BLOCK, BLOCK), F32),
             jax.ShapeDtypeStruct((BLOCK, 8), F32),
         ],
         4 * 10**9,
@@ -237,34 +246,30 @@
 
 
 def strided_forward_kernel(
-    recv_ref, fixed_ref, grp_out, attn_out, prob_out, sums_ref, send_ref,
-    grp_ref, attn_ref, prob_ref, sem,
+    recv_ref, fixed_ref, keys_out, prob_out, grp_ref, sums_ref, send_ref, keys_ref, prob_ref, sem
 ):
     swap = swap_matrix()
     for at in range(0, NB, 16):
         rows = dot(swap, recv_ref[at : at + 16].reshape(256, WIDTH)).astype(BF16)
         for head in range(HEADS):
-            grp_ref[head, :, :, at : at + 16, :] = rows[:, head * HD : (head + 1) * HD].reshape(
-                4, OFFS, 16, HD
-            )
-    copies = copy_all([(grp_ref, grp_out)], sem.at[0])
+            tiles = rows[:, head * HD : (head + 1) * HD].reshape(4, OFFS, 16, HD)
+            keys_ref[head, :, :, at : at + 16, :] = tiles[:3]
+            grp_ref[head, 0, :, at : at + 16, :] = tiles[3]
+    copies = copy_all([(keys_ref, keys_out)], sem.at[0])
     row, col = iotas((NB, NB))
     square, cross = 0.0, 0.0
     for head in range(HEADS):
-        scores = batch_dot(grp_ref[head, 0], grp_ref[head, 1], 2, 2) * scale
+        scores = batch_dot(keys_ref[head, 0], keys_ref[head, 1], 2, 2) * scale
         scores = jnp.where((col <= row)[None], scores, -jnp.inf)
         expo = jnp.exp(scores - jnp.max(scores, axis=-1, keepdims=True))
         prob = expo * (1.0 / jnp.sum(expo, axis=-1, keepdims=True))
-        attn = batch_dot(prob.astype(BF16), grp_ref[head, 2], 2, 1).astype(BF16)
+        attn = batch_dot(prob.astype(BF16), keys_ref[head, 2], 2, 1).astype(BF16)
         prob_ref[head] = prob
-        attn_ref[head] = attn
         wide = attn.astype(F32)
         square += wide * wide
-        cross += wide * grp_ref[head, 3].astype(F32)
-        copies += copy_all(
-            [(prob_ref.at[head], prob_out.at[head]), (attn_ref.at[head], attn_out.at[head])],
-            sem.at[head + 1],
-        )
+        cross += wide * grp_ref[head, 0].astype(F32)
+        grp_ref[head, 1] = attn
+        copies += copy_all([(prob_ref.at[head], prob_out.at[head])], sem.at[head + 1])
     square = jnp.sum(square, axis=-1, keepdims=True)
     cross = jnp.sum(cross, axis=-1, keepdims=True)
     lane = lax.broadcasted_iota(jnp.int32, (NB, HD), 1)
@@ -272,8 +277,7 @@
     for at in range(OFFS):
         part += jnp.where(lane == 8 + at, square[at], jnp.where(lane == 12 + at, cross[at], 0.0))
     sums_ref[...] = part
-    for head in range(2):
-        send_ref[head * NB : (head + 1) * NB] = part.reshape(NB, 1, HD)
+    send_ref[...] = part.reshape(NB, 1, HD)
     for copy in copies:
         copy.wait()
 
@@ -286,24 +290,23 @@
         [
             IN_HBM,
             IN_HBM,
-            IN_HBM,
+            spec((HEADS, 2, OFFS, NB, HD), 0, 0, 0, 0, 0),
             spec((NB, HD), 0, 0),
-            spec((2 * NB, 1, HD), 0, 0, 0),
-        ],
-        [
-            pltpu.HBM((HEADS, 4, OFFS, NB, HD), BF16),
-            pltpu.HBM((HEADS, OFFS, NB, HD), BF16),
+            spec((NB, 1, HD), 0, 0, 0),
+        ],
+        [
+            pltpu.HBM((HEADS, 3, OFFS, NB, HD), BF16),
             pltpu.HBM((HEADS, OFFS, NB, NB), F32),
+            jax.ShapeDtypeStruct((HEADS, 2, OFFS, NB, HD), BF16),
             jax.ShapeDtypeStruct((NB, HD), F32),
-            jax.ShapeDtypeStruct((2 * NB, 1, HD), F32),
+            jax.ShapeDtypeStruct((NB, 1, HD), F32),
         ],
         10**9,
         6 * 2**20,
         [
-            pltpu.VMEM((HEADS, 4, OFFS, NB, HD), BF16),
-            pltpu.VMEM((HEADS, OFFS, NB, HD), BF16),
+            pltpu.VMEM((HEADS, 3, OFFS, NB, HD), BF16),
             pltpu.VMEM((HEADS, OFFS, NB, NB), F32),
-            pltpu.SemaphoreType.DMA((HEADS + 1, 2)),
+            pltpu.SemaphoreType.DMA((HEADS + 1, 1)),
         ],
         vmem=VMEM3,
     )(recv, fixed_sums)
@@ -319,37 +322,36 @@
 
 
 def strided_backward_kernel(
-    grp_in, attn_in, prob_in, sums_ref, other_ref, recv_ref, send_out, block_ref,
-    grp_ref, attn_ref, prob_ref, out_ref, send_ref, in_sem, out_sem,
+    keys_in, prob_in, grp_ref, sums_ref, other_ref, recv_ref, send_out, block_ref,
+    keys_ref, prob_ref, out_ref, send_ref, in_sem, out_sem,
 ):
-    copies = [
+    fetched = [
         copy_all(
-            [
-                (attn_in.at[head], attn_ref.at[head]),
-                (grp_in.at[head], grp_ref.at[head]),
-                (prob_in.at[head], prob_ref.at[head]),
-            ],
+            [(keys_in.at[head], keys_ref.at[head]), (prob_in.at[head], prob_ref.at[head])],
             in_sem.at[head],
         )
         for head in range(HEADS)
     ]
-    both = sums_ref[:, :16] + other_ref[...]
-    moved = (recv_ref[:NB] + recv_ref[NB:]).reshape(NB, HD)
-    block_ref[...] = both[:, :8] + moved[:, 8:16]
-    total = both[:, 8:] + moved[:, :8]
+    moved = recv_ref[...].reshape(NB, HD)
+    block_ref[...] = moved[:, 8:16]
+    total = sums_ref[:, 8:16] + other_ref[...] + moved[:, :8]
     square = jnp.stack([total[:, at : at + 1] for at in range(OFFS)])
     cross = jnp.stack([total[:, OFFS + at : OFFS + at + 1] for at in range(OFFS)])
+    grads = []
     for head in range(HEADS):
-        for copy in copies[head]:
+        wide = grp_ref[head, 1].astype(F32)
+        normed, grad, row_dot = normalize(wide, grp_ref[head, 0], square, cross)
+        out_ref[head, 0] = normed
+        grads.append((grad, row_dot))
+    for head in range(HEADS):
+        for copy in fetched[head]:
             copy.wait()
-        wide = attn_ref[head].astype(F32)
-        normed, grad, row_dot = normalize(wide, grp_ref[head, 3], square, cross)
+        grad, row_dot = grads[head]
         prob = prob_ref[head]
-        grad_prob = batch_dot(grad, grp_ref[head, 2], 2, 2)
+        grad_prob = batch_dot(grad, keys_ref[head, 2], 2, 2)
         grad_score = (prob * (grad_prob - row_dot) * scale).astype(BF16)
-        out_ref[head, 0] = normed
-        out_ref[head, 1] = batch_dot(grad_score, grp_ref[head, 1], 2, 1).astype(BF16)
-        out_ref[head, 2] = batch_dot(grad_score, grp_ref[head, 0], 1, 1).astype(BF16)
+        out_ref[head, 1] = batch_dot(grad_score, keys_ref[head, 1], 2, 1).astype(BF16)
+        out_ref[head, 2] = batch_dot(grad_score, keys_ref[head, 0], 1, 1).astype(BF16)
         out_ref[head, 3] = batch_dot(prob.astype(BF16), grad, 1, 1).astype(BF16)
     swap = swap_matrix()
     copies = []
@@ -363,17 +365,17 @@
         copy.wait()
 
 
-def strided_backward(grp, attn, prob, sums, other, recv):
+def strided_backward(keys, prob, grp, sums, other, recv):
     return call(
         strided_backward_kernel,
         1,
         [
             IN_HBM,
             IN_HBM,
-            IN_HBM,
+            spec((HEADS, 2, OFFS, NB, HD), 0, 0, 0, 0, 0),
             spec((NB, HD), 0, 0),
-            spec((NB, 16), 0, 0),
-            spec((2 * NB, 1, HD), 0, 0, 0),
+            spec((NB, 8), 0, 0),
+            spec((NB, 1, HD), 0, 0, 0),
         ],
         [IN_HBM, spec((NB, 8), 0, 0)],
         [
@@ -383,22 +385,23 @@
         10**9,
         6 * 2**20,
         [
-            pltpu.VMEM((HEADS, 4, OFFS, NB, HD), BF16),
-            pltpu.VMEM((HEADS, OFFS, NB, HD), BF16),
+            pltpu.VMEM((HEADS, 3, OFFS, NB, HD), BF16),
             pltpu.VMEM((HEADS, OFFS, NB, NB), F32),
             pltpu.VMEM((HEADS, 4, OFFS, NB, HD), BF16),
             pltpu.VMEM((NB, 16, WIDTH), BF16),
-            pltpu.SemaphoreType.DMA((HEADS, 3)),
+            pltpu.SemaphoreType.DMA((HEADS, 2)),
             pltpu.SemaphoreType.DMA((NB // 16, 1)),
         ],
         vmem=VMEM4,
-    )(*[in_hbm(array) for array in (grp, attn, prob)], sums, other, recv)
-
-
-def fixed_backward_kernel(rows_ref, summ_ref, seen_ref, attn_ref, sums_ref, out_ref, part_ref):
+    )(in_hbm(keys), in_hbm(prob), grp, sums, other, recv)
+
+
+def fixed_backward_kernel(
+    rows_ref, summ_ref, own_ref, far_ref, attn_ref, sums_ref, out_ref, keep_ref, send_ref
+):
     query, key, value = rows_ref[0], rows_ref[1], rows_ref[2]
     summ_key, summ_value = summ_ref[:, :HD], summ_ref[:, HD:]
-    own, far = fixed_probabilities(query, key, summ_key, seen_ref[...])
+    own, far = own_ref[0], far_ref[0]
     wide = attn_ref[...].astype(F32)
     normed, grad, row_dot = normalize(wide, rows_ref[3], sums_ref[:, 0:1], sums_ref[:, 1:2])
     out_ref[0] = normed
@@ -409,33 +412,44 @@
     grad_value = dot_tn(own.astype(BF16), grad)
     out_ref[2] = grad_key.astype(BF16)
     out_ref[3] = grad_value.astype(BF16)
-    part_ref[:, :HD] = dot_tn(far_score, query)
-    part_ref[:, HD:] = dot_tn(far.astype(BF16), grad)
+    far_key = dot_tn(far_score, query)
+    far_value = dot_tn(far.astype(BF16), grad)
+    half = BLOCK // 2
+    send_ref[:, :HD] = far_key[half:].astype(BF16)
+    send_ref[:, HD:] = far_value[half:].astype(BF16)
+    keep_ref[:, :HD] = far_key[:half]
+    keep_ref[:, HD:] = far_value[:half]
     row = lax.broadcasted_iota(jnp.int32, (8, HD), 0)
     for at, grads in ((0, grad_key), (HD, grad_value)):
         tail = pltpu.roll(grads[BLOCK - 8 :], SUMM, 0)
-        part_ref[0:8, at : at + HD] += jnp.where(row < SUMM, tail, 0.0)
-
-
-def fixed_backward(rows, summ, seen, attn, sums):
+        keep_ref[0:8, at : at + HD] += jnp.where(row < SUMM, tail, 0.0)
+
+
+def fixed_backward(rows, summ, own, far, attn, sums):
     return call(
         fixed_backward_kernel,
         HEADS,
         [
             spec((4, BLOCK, HD), 0, 0, "i"),
             spec((BLOCK, 2 * HD), 0, "i"),
-            spec((1, BLOCK), 0, 0),
+            spec((1, BLOCK, BLOCK), "i", 0, 0),
+            spec((1, BLOCK, BLOCK), "i", 0, 0),
             spec((BLOCK, HD), 0, "i"),
             spec((BLOCK, 2), 0, 0),
         ],
-        [spec((4, BLOCK, HD), 0, 0, "i"), spec((BLOCK, 2 * HD), 0, "i")],
+        [
+            spec((4, BLOCK, HD), 0, 0, "i"),
+            spec((BLOCK // 2, 2 * HD), 0, "i"),
+            spec((BLOCK // 2, 2 * HD), 0, "i"),
+        ],
         [
             pltpu.HBM((4, BLOCK, WIDTH), BF16),
-            jax.ShapeDtypeStruct((BLOCK, 2 * WIDTH), F32),
+            jax.ShapeDtypeStruct((BLOCK // 2, 2 * WIDTH), F32),
+            jax.ShapeDtypeStruct((BLOCK // 2, 2 * WIDTH), BF16),
         ],
         8 * 10**9,
         8 * 2**20,
-    )(rows, summ, seen, attn, sums)
+    )(rows, summ, own, far, attn, sums)
 
 
 def unpack_kernel(recv_ref, fixed_in, tail_ref, *refs):
@@ -544,24 +558,41 @@
     return lax.ppermute(array, "seq", perm)
 
 
+def other_head(array):
+    return lax.ppermute(array, "head", [(0, 1), (1, 0)])
+
+
 ROUNDS = (
-    ((0, 1, 1),),
-    ((0, 2, 2), (0, -2, 2), (0, 4, 2)),
-    ((2, 1, 8), (2, -1, 8), (2, 2, 8)),
-    ((1, 1, 32),),
+    ((0, -1, 1),),
+    ((0, -2, 2), (0, -4, 2), (0, 2, 2)),
+    ((1, 1, 8),),
+    ((2, 1, 16), (2, -1, 16), (2, 2, 16)),
     ((3, 1, 64),),
 )
 
 
-def gather_summaries(held, rounds):
-    for steps in rounds:
+def gather_along_z(own, me):
+    size = PARTS[0]
+    step = NB // size
+    groups = [[at + step * z for z in range(size)] for at in range(step)]
+    sent = jnp.broadcast_to(own[None], (size,) + own.shape)
+    held = lax.all_to_all(sent, "seq", 0, 0, axis_index_groups=groups, tiled=True)
+    held = jnp.concatenate([held, held], 0)
+    held = lax.dynamic_slice_in_dim(held, me // step, size, 0)
+    return held.reshape(size * SUMM, 2 * WIDTH)
+
+
+def gather_summaries(held):
+    for steps in ROUNDS[2:]:
         moved = [shift(held[: slots * SUMM], part, step) for part, step, slots in steps]
         held = jnp.concatenate([held] + moved, 0)
     return held
 
 
-def scatter_summaries(parts):
-    for steps in ROUNDS[::-1]:
+def scatter_summaries(total, sent):
+    (part, step, _), = ROUNDS[-1]
+    parts = total + shift(sent, part, -step).astype(F32)
+    for steps in ROUNDS[-2::-1]:
         kept = parts.shape[0] - SUMM * sum(slots for _, _, slots in steps)
         total, at = parts[:kept], kept
         for part, step, slots in steps:
@@ -592,25 +623,24 @@
     send = pack_strided(arrays)
     tails = [a[BLOCK - SUMM :, 1].reshape(SUMM, HEADS, 1, HD) for a in (key_rows, value_rows)]
     own_summ = jnp.concatenate(tails, 2).reshape(SUMM, 2 * WIDTH)
-    summ = gather_summaries(own_summ, ROUNDS[:1])
-    send, summ = lax.optimization_barrier((send, summ))
-    summ = gather_summaries(summ, ROUNDS[1:2])
+    summ = gather_along_z(own_summ, me)
     send, summ = lax.optimization_barrier((send, summ))
     recv = lax.all_to_all(send, "seq", 0, 0, tiled=True)
-    summ = gather_summaries(summ, ROUNDS[2:])
+    summ = gather_summaries(summ)
     seen = jnp.repeat((slot_blocks(me) < me).astype(jnp.int32), SUMM)[None]
     rows = pack_fixed(arrays)
-    fixed_attn, fixed_sums = fixed_forward(rows, summ, seen)
+    fixed_attn, own_prob, far_prob, fixed_sums = fixed_forward(rows, summ, seen)
     fixed_send = fixed_sums[:, :2].reshape(NB, OFFS, 2).transpose(0, 2, 1).reshape(NB, 8)
-    fixed_send = jnp.pad(fixed_send, ((0, 0), (0, HD - 8)))
-    grp, attn, prob, sums, sums_both = strided_forward(recv, fixed_send)
-    sums_in = lax.all_to_all(sums_both, ("head", "seq"), 0, 0, tiled=True)
-    sums_other = lax.ppermute(sums[:, :16], "head", [(0, 1), (1, 0)])
-    send_back, block_sums = strided_backward(grp, attn, prob, sums, sums_other, sums_in)
+    fixed_both = fixed_send + other_head(fixed_send)
+    keys, prob, grp, sums, sums_send = strided_forward(recv, jnp.pad(fixed_both, ((0, 0), (0, HD - 8))))
+    sums_in = lax.all_to_all(sums_send, "seq", 0, 0, tiled=True)
+    sums_other = other_head(sums[:, 8:16])
+    send_back, block_sums = strided_backward(keys, prob, grp, sums, sums_other, sums_in)
+    block_sums = fixed_both + block_sums + other_head(block_sums)
     recv_back = lax.all_to_all(send_back, "seq", 0, 0, tiled=True)
     block_sums = block_sums.reshape(NB, 2, OFFS).transpose(0, 2, 1).reshape(BLOCK, 2)
-    fixed_out, parts = fixed_backward(rows, summ, seen, fixed_attn, block_sums)
-    totals = scatter_summaries(parts).astype(BF16).reshape(SUMM, HEADS, 2, HD)
+    fixed_out, kept, sent = fixed_backward(rows, summ, own_prob, far_prob, fixed_attn, block_sums)
+    totals = scatter_summaries(kept, sent).astype(BF16).reshape(SUMM, HEADS, 2, HD)
     totals = totals.transpose(2, 0, 1, 3).reshape(2, SUMM, WIDTH)
     tail = jnp.pad(totals, ((0, 0), (16 - SUMM, 0), (0, 0)))
     return unpack(recv_back, fixed_out, tail)

time: 183 us -> 184 us (level)
  starting transfers between devices: 64 us -> 68.4 us
  waiting for transfers between devices: 65.9 us -> 62.6 us
    ppermute x1 -> x3, waiting for transfers between devices: 2.15 us -> 11.7 us  [other_head(): return lax.ppermute(array, 'head', [(0, 1), (1, 0)])]
    ppermute x18 -> x14, waiting for transfers between devices: 45 us -> 35.8 us  [shift(): return lax.ppermute(array, 'seq', perm)]
    all_to_all x1 -> x2, starting transfers between devices: 8.25 us -> 17 us  [the longest x1 9.01 us: gather_along_z(): lax.all_to_all(sent, 'seq', 0, 0, axis_index_groups=groups, tiled=True)]
    ppermute x18 -> x14, starting transfers between devices: 33.1 us -> 27.2 us  [shift(): return lax.ppermute(array, 'seq', perm)]
    all_to_all x1, waiting for transfers between devices: 11.3 us -> 5.96 us  [shards(): recv = lax.all_to_all(send, 'seq', 0, 0, tiled=True)]
    ppermute x1 -> x3, starting transfers between devices: 2.98 us -> 7.04 us  [other_head(): return lax.ppermute(array, 'head', [(0, 1), (1, 0)])]
    all_to_all x1, starting transfers between devices: 13.3 us -> 9.44 us  [shards(): recv = lax.all_to_all(send, 'seq', 0, 0, tiled=True)]
    all_to_all x1 -> x2, waiting for transfers between devices: 7.49 us -> 9.18 us  [the longest x1 5.39 us: shards(): sums_in = lax.all_to_all(sums_send, 'seq', 0, 0, tiled=True)]
  transfers between devices with their start and end apart: 22 -> 21, of which waited for: 17 -> 17; matrix products, arithmetic and copies ran while one was open for 4% -> 3% of each run, Pallas kernels for 15% -> 15%
where the time goes in v4:
time: 184 us; the launch traced here: 181 us
  starting transfers between devices  68.4 us (37%)
  waiting for transfers between devices  62.6 us (34%)
  Pallas kernels  40.4 us (22%)
  local copies, waits for them, and re-layouts  7.13 us (4%)
    ppermute x14, waiting for transfers between devices, shift(): return lax.ppermute(array, 'seq', perm)  35.8 us
    ppermute x14, starting transfers between devices, shift(): return lax.ppermute(array, 'seq', perm)  27.2 us
    ppermute x3, waiting for transfers between devices, other_head(): return lax.ppermute(array, 'head', [(0, 1), (1, 0)])  11.7 us
    pallas_call x1, Pallas kernels, fixed_forward(): call(fixed_forward_kernel, HEADS, [spec((4, BLOCK, HD), 0, 0, 'i'), spec(...  9.75 us
    pallas_call x1, Pallas kernels, fixed_backward(): call(fixed_backward_kernel, HEADS, [spec((4, BLOCK, HD), 0, 0, 'i'), spec...  9.61 us
    all_to_all x1, starting transfers between devices, shards(): recv = lax.all_to_all(send, 'seq', 0, 0, tiled=True)  9.44 us
    all_to_all x1, starting transfers between devices, gather_along_z(): lax.all_to_all(sent, 'seq', 0, 0, axis_index_groups=groups, tiled=True)  9.01 us
    all_to_all x1, starting transfers between devices, shards(): sums_in = lax.all_to_all(sums_send, 'seq', 0, 0, tiled=True)  8.01 us
  transfers between devices with their start and end apart: 21, of which 17 were waited for; matrix products, arithmetic and copies ran while one was open for 3% of the time, Pallas kernels for 15%

profile of v4, /device:TPU:1, one launch (start us, length us, event | category | flops | bytes accessed | tf_op | source)
XLA Modules:
  0.0 181.2 jit_solution(805055891412481443)
XLA Ops:
  0.6 0.7 slice_reduce_fusion.1
  1.4 0.7 slice_reduce_fusion
  2.2 0.6 broadcast_in_dim.11
  2.8 9.0 %all-to-all-start = ((bf16[8,4,1024]{2,1,0:T(4,128)(2,1)}), bf16[8,4,1024]{2,1,0:T(4,128)(2,1)S(1)}, u32[]{:S(2)}, u32[]{:S(2)}) async-start(bf16[8,4,1024]{2,1,0:T(4,128)(2,1)} %broadcast_in_dim.11), calls=%async_computation | async-start | bytes 131072 | tf_op jit(solution)/shard_map/all_to_all | solution.py:579
  11.8 3.4 %shard_map.84 = bf16[128,16,512]{2,1,0:T(8,128)(2,1)} custom-call(bf16[4096,128]{1,0:T(8,128)(2,1)} %bitcast.78, bf16[4096,128]{1,0:T(8,128)(2,1)} %bitcast.74, bf16[4096,128]{1,0:T(8,128)(2,1)} %bitcast.76, bf16[4096,128]{1,0:T(8,128)(2,1)} %bitcast.80), custom_call_target="tpu_custom_call" | custom-call | flops 1000000000 | bytes 6291456 | tf_op jit(solution)/shard_map/pallas_call | solution.py:138
  15.3 3.8 %all-to-all-done = bf16[8,4,1024]{2,1,0:T(4,128)(2,1)S(1)} async-done(((bf16[8,4,1024]{2,1,0:T(4,128)(2,1)}), bf16[8,4,1024]{2,1,0:T(4,128)(2,1)S(1)}, u32[]{:S(2)}, u32[]{:S(2)}) %all-to-all-start) | async-done | bytes 65568 | tf_op jit(solution)/shard_map/all_to_all | solution.py:579
  19.1 0.1 fusion.2
  19.2 0.0 copy-start.1
  19.2 0.0 copy-start.2
  19.2 0.0 copy-start.3
  19.2 0.0 copy-start.4
  19.2 9.4 %all-to-all-start.1 = ((bf16[128,16,512]{2,1,0:T(8,128)(2,1)}), bf16[128,16,512]{2,1,0:T(8,128)(2,1)S(1)}, u32[]{:S(2)}, u32[]{:S(2)}) async-start(bf16[128,16,512]{2,1,0:T(8,128)(2,1)} %shard_map.84), calls=%async_computation.1 | async-start | bytes 4194304 | tf_op jit(solution)/shard_map/all_to_all | solution.py:628
  28.7 1.5 collective-permute-start
  30.2 5.6 %collective-permute-done = bf16[32,1024]{1,0:T(8,128)(2,1)S(1)} collective-permute-done((bf16[32,1024]{1,0:T(8,128)(2,1)S(1)}, bf16[32,1024]{1,0:T(8,128)(2,1)S(1)}, u32[]{:S(2)}, u32[]{:S(2)}) %collective-permute-start) | collective-permute-done | bytes 65568 | tf_op jit(solution)/shard_map/ppermute | solution.py:558
  35.8 0.6 collective-permute-start.1
  36.4 2.1 %collective-permute-start.2 = (bf16[64,1024]{1,0:T(8,128)(2,1)S(1)}, bf16[64,1024]{1,0:T(8,128)(2,1)S(1)}, u32[]{:S(2)}, u32[]{:S(2)}) collective-permute-start(bf16[64,1024]{1,0:T(8,128)(2,1)S(1)} %get-tuple-element.62), channel_id=1, source_target_pairs={{0,12},{2,14},{4,0},{6,2},{8,4},{10,6},{12,8},{14,10},{16,28},{18,... | collective-permute-start | bytes 393224 | tf_op jit(solution)/shard_map/ppermute | solution.py:558
  38.5 0.8 collective-permute-start.3
  39.4 3.7 %collective-permute-done.1 = bf16[64,1024]{1,0:T(8,128)(2,1)S(1)} collective-permute-done((bf16[64,1024]{1,0:T(8,128)(2,1)S(1)}, bf16[64,1024]{1,0:T(8,128)(2,1)S(1)}, u32[]{:S(2)}, u32[]{:S(2)}) %collective-permute-start.1) | collective-permute-done | bytes 131104 | tf_op jit(solution)/shard_map/ppermute | solution.py:558
  43.1 0.6 collective-permute-done.2
  43.7 5.3 %collective-permute-done.3 = bf16[64,1024]{1,0:T(8,128)(2,1)S(1)} collective-permute-done((bf16[64,1024]{1,0:T(8,128)(2,1)S(1)}, bf16[64,1024]{1,0:T(8,128)(2,1)S(1)}, u32[]{:S(2)}, u32[]{:S(2)}) %collective-permute-start.3) | collective-permute-done | bytes 131104 | tf_op jit(solution)/shard_map/ppermute | solution.py:558
  49.0 0.0 copy-start
  49.0 1.0 copy-done
  50.0 1.2 collective-permute-start.4
  51.2 0.1 broadcast_in_dim.12
  51.3 0.7 broadcast_in_dim_reshape.4.seen_ref
  52.0 3.6 %shard_map.85.rows_ref = bf16[4,512,512]{2,1,0:T(8,128)(2,1)} custom-call(bf16[4096,128]{1,0:T(8,128)(2,1)} %bitcast.79, bf16[4096,128]{1,0:T(8,128)(2,1)} %bitcast.75, bf16[4096,128]{1,0:T(8,128)(2,1)} %bitcast.77, bf16[4096,128]{1,0:T(8,128)(2,1)} %bitcast.81), custom_call_target="tpu_custom_call" | custom-call | flops 1000000000 | bytes 6291456 | tf_op jit(solution)/shard_map/pallas_call | solution.py:169
  55.6 0.8 constant_dynamic-update-slice_fusion.7.summ_ref
  56.4 9.7 %shard_map.86 = (bf16[512,512]{1,0:T(8,128)(2,1)}, f32[4,512,512]{2,1,0:T(8,128)}, f32[4,512,512]{2,1,0:T(8,128)}, f32[512,8]{1,0:T(8,128)}) custom-call(bf16[4,512,512]{2,1,0:T(8,128)(2,1)} %shard_map.85.rows_ref, bf16[512,1024]{1,0:T(8,128)(2,1)} %constant_dynamic-update-slice_fusion.7.summ_ref, s32[1,512]{1,0:T(1,128)} %broadcast_in_dim_reshape.4.seen_ref), custom_call_target="tpu_custom_call" | custom-call | flops 4000000000 | bytes 4194304 | tf_op jit(solution)/shard_map/pallas_call | solution.py:218
  66.2 1.0 copy.25
  67.2 0.1 copy.27
  67.3 2.5 %collective-permute-start.5 = (f32[128,8]{1,0:T(8,128)S(1)}, f32[128,8]{1,0:T(8,128)S(1)}, u32[]{:S(2)}, u32[]{:S(2)}) collective-permute-start(f32[128,8]{1,0:T(8,128)S(1)} %copy.27), channel_id=1, source_target_pairs={{0,1},{1,0},{2,3},{3,2},{4,5},{5,4},{6,7},{7,6},{8,9},{9,8},{10,11... | collective-permute-start | bytes 12296 | tf_op jit(solution)/shard_map/ppermute | solution.py:562
  69.9 4.2 %collective-permute-done.5 = f32[128,8]{1,0:T(8,128)S(1)} collective-permute-done((f32[128,8]{1,0:T(8,128)S(1)}, f32[128,8]{1,0:T(8,128)S(1)}, u32[]{:S(2)}, u32[]{:S(2)}) %collective-permute-start.5) | collective-permute-done | bytes 4128 | tf_op jit(solution)/shard_map/ppermute | solution.py:562
  74.1 6.0 %all-to-all-done.1.recv_ref = bf16[128,16,512]{2,1,0:T(8,128)(2,1)S(1)} async-done(((bf16[128,16,512]{2,1,0:T(8,128)(2,1)}), bf16[128,16,512]{2,1,0:T(8,128)(2,1)S(1)}, u32[]{:S(2)}, u32[]{:S(2)}) %all-to-all-start.1) | async-done | bytes 2097184 | tf_op jit(solution)/shard_map/all_to_all | solution.py:628
  80.0 3.7 %shard_map.87 = (bf16[4,3,4,128,128]{4,3,2,1,0:T(8,128)(2,1)}, f32[4,4,128,128]{3,2,1,0:T(8,128)}, bf16[4,2,4,128,128]{4,3,2,1,0:T(8,128)(2,1)S(1)}, f32[128,128]{1,0:T(8,128)S(1)}, f32[128,1,128]{2,1,0:T(1,128)}) custom-call(bf16[128,16,512]{2,1,0:T(8,128)(2,1)S(1)} %all-to-all-done.1.recv_ref, f32[128,128]{1,0:T(8,128)S(1)} %pad.8.fixed_ref), custom_call_target="tpu_custom_call" | custom-call | flops 1000000000 | bytes 6291456 | tf_op jit(solution)/shard_map/pallas_call | solution.py:286
  83.8 8.0 %all-to-all-start.2 = ((f32[128,1,128]{2,1,0:T(1,128)}), f32[128,1,128]{2,1,0:T(1,128)S(1)}, u32[]{:S(2)}, u32[]{:S(2)}) async-start(f32[128,1,128]{2,1,0:T(1,128)} %get-tuple-element.31), calls=%async_computation.2 | async-start | bytes 131072 | tf_op jit(solution)/shard_map/all_to_all | solution.py:636
  91.8 0.1 slice.75
  91.9 2.2 %collective-permute-start.6 = (f32[128,8]{1,0:T(8,128)S(1)}, f32[128,8]{1,0:T(8,128)S(1)}, u32[]{:S(2)}, u32[]{:S(2)}) collective-permute-start(f32[128,8]{1,0:T(8,128)S(1)} %slice.75), channel_id=1, source_target_pairs={{0,1},{1,0},{2,3},{3,2},{4,5},{5,4},{6,7},{7,6},{8,9},{9,8},{10,11... | collective-permute-start | bytes 12296 | tf_op jit(solution)/shard_map/ppermute | solution.py:562
  94.1 2.8 %collective-permute-done.6.other_ref = f32[128,8]{1,0:T(8,128)S(1)} collective-permute-done((f32[128,8]{1,0:T(8,128)S(1)}, f32[128,8]{1,0:T(8,128)S(1)}, u32[]{:S(2)}, u32[]{:S(2)}) %collective-permute-start.6) | collective-permute-done | bytes 4128 | tf_op jit(solution)/shard_map/ppermute | solution.py:562
  96.9 5.4 %all-to-all-done.2.recv_ref = f32[128,1,128]{2,1,0:T(1,128)S(1)} async-done(((f32[128,1,128]{2,1,0:T(1,128)}), f32[128,1,128]{2,1,0:T(1,128)S(1)}, u32[]{:S(2)}, u32[]{:S(2)}) %all-to-all-start.2) | async-done | bytes 65568 | tf_op jit(solution)/shard_map/all_to_all | solution.py:636
  102.3 5.3 %shard_map.88 = (bf16[128,16,512]{2,1,0:T(8,128)(2,1)}, f32[128,8]{1,0:T(8,128)S(1)}) custom-call(bf16[4,3,4,128,128]{4,3,2,1,0:T(8,128)(2,1)} %get-tuple-element.27.keys_in, f32[4,4,128,128]{3,2,1,0:T(8,128)} %get-tuple-element.28.prob_in, bf16[4,2,4,128,128]{4,3,2,1,0:T(8,128)(2,1)S(1)} %get-tuple-element.29.grp_ref, ...), custom_call_target="tpu_custom_call" | custom-call | flops 1000000000 | bytes 6291456 | tf_op jit(solution)/shard_map/pallas_call | solution.py:369
  107.6 7.7 %all-to-all-start.3 = ((bf16[128,16,512]{2,1,0:T(8,128)(2,1)}), bf16[128,16,512]{2,1,0:T(8,128)(2,1)S(1)}, u32[]{:S(2)}, u32[]{:S(2)}) async-start(bf16[128,16,512]{2,1,0:T(8,128)(2,1)} %get-tuple-element.32), calls=%async_computation.3 | async-start | bytes 4194304 | tf_op jit(solution)/shard_map/all_to_all | solution.py:640
  115.2 2.3 %collective-permute-start.7 = (f32[128,8]{1,0:T(8,128)S(1)}, f32[128,8]{1,0:T(8,128)S(1)}, u32[]{:S(2)}, u32[]{:S(2)}) collective-permute-start(f32[128,8]{1,0:T(8,128)S(1)} %get-tuple-element.36), channel_id=1, source_target_pairs={{0,1},{1,0},{2,3},{3,2},{4,5},{5,4},{6,7},{7,6},{8,9},{9,8},{10,11... | collective-permute-start | bytes 12296 | tf_op jit(solution)/shard_map/ppermute | solution.py:562
  117.5 4.7 %collective-permute-done.7 = f32[128,8]{1,0:T(8,128)S(1)} collective-permute-done((f32[128,8]{1,0:T(8,128)S(1)}, f32[128,8]{1,0:T(8,128)S(1)}, u32[]{:S(2)}, u32[]{:S(2)}) %collective-permute-start.7) | collective-permute-done | bytes 4128 | tf_op jit(solution)/shard_map/ppermute | solution.py:562
  122.3 0.9 copy.29
  123.1 9.6 %shard_map.89 = (bf16[4,512,512]{2,1,0:T(8,128)(2,1)}, f32[256,1024]{1,0:T(8,128)}, bf16[256,1024]{1,0:T(8,128)(2,1)}) custom-call(bf16[4,512,512]{2,1,0:T(8,128)(2,1)} %shard_map.85.rows_ref, bf16[512,1024]{1,0:T(8,128)(2,1)} %constant_dynamic-update-slice_fusion.7.summ_ref, f32[4,512,512]{2,1,0:T(8,128)} %get-tuple-element.33.own_ref, ...), custom_call_target="tpu_custom_call" | custom-call | flops 8000000000 | bytes 8388608 | tf_op jit(solution)/shard_map/pallas_call | solution.py:429
  132.8 2.9 %collective-permute-start.8 = (bf16[256,1024]{1,0:T(8,128)(2,1)}, bf16[256,1024]{1,0:T(8,128)(2,1)S(1)}, u32[]{:S(2)}, u32[]{:S(2)}) collective-permute-start(bf16[256,1024]{1,0:T(8,128)(2,1)} %get-tuple-element.39), channel_id=1, source_target_pairs={{0,2},{2,0},{4,6},{6,4},{8,10},{10,8},{12,14},{14,12},{16,18},{18,... | collective-permute-start | bytes 1572872 | tf_op jit(solution)/shard_map/ppermute | solution.py:558
  135.6 1.7 collective-permute-done.8
  137.4 1.4 fusion.17
  138.8 1.5 collective-permute-start.9
  140.3 1.2 collective-permute-start.11
  141.6 0.0 collective-permute-start.10
  141.6 4.0 %collective-permute-done.9 = bf16[64,1024]{1,0:T(8,128)(2,1)S(1)} collective-permute-done((bf16[64,1024]{1,0:T(8,128)(2,1)S(1)}, bf16[64,1024]{1,0:T(8,128)(2,1)S(1)}, u32[]{:S(2)}, u32[]{:S(2)}) %collective-permute-start.9) | collective-permute-done | bytes 131104 | tf_op jit(solution)/shard_map/ppermute | solution.py:558
  145.5 3.1 %collective-permute-done.11 = bf16[64,1024]{1,0:T(8,128)(2,1)S(1)} collective-permute-done((bf16[64,1024]{1,0:T(8,128)(2,1)S(1)}, bf16[64,1024]{1,0:T(8,128)(2,1)S(1)}, u32[]{:S(2)}, u32[]{:S(2)}) %collective-permute-start.11) | collective-permute-done | bytes 131104 | tf_op jit(solution)/shard_map/ppermute | solution.py:558
  148.6 4.6 %collective-permute-done.10 = bf16[64,1024]{1,0:T(8,128)(2,1)S(1)} collective-permute-done((bf16[64,1024]{1,0:T(8,128)(2,1)S(1)}, bf16[64,1024]{1,0:T(8,128)(2,1)S(1)}, u32[]{:S(2)}, u32[]{:S(2)}) %collective-permute-start.10) | collective-permute-done | bytes 131104 | tf_op jit(solution)/shard_map/ppermute | solution.py:558
  153.2 0.1 fusion.1
  153.3 2.1 %collective-permute-start.12 = (bf16[32,1024]{1,0:T(8,128)(2,1)S(1)}, bf16[32,1024]{1,0:T(8,128)(2,1)S(1)}, u32[]{:S(2)}, u32[]{:S(2)}) collective-permute-start(bf16[32,1024]{1,0:T(8,128)(2,1)S(1)} %slice.118), channel_id=1, source_target_pairs={{0,16},{2,18},{4,20},{6,22},{8,24},{10,26},{12,28},{14,30},{16,0},... | collective-permute-start | bytes 196616 | tf_op jit(solution)/shard_map/ppermute | solution.py:558
  155.4 2.4 %collective-permute-done.12 = bf16[32,1024]{1,0:T(8,128)(2,1)S(1)} collective-permute-done((bf16[32,1024]{1,0:T(8,128)(2,1)S(1)}, bf16[32,1024]{1,0:T(8,128)(2,1)S(1)}, u32[]{:S(2)}, u32[]{:S(2)}) %collective-permute-start.12) | collective-permute-done | bytes 65568 | tf_op jit(solution)/shard_map/ppermute | solution.py:558
  157.9 5.2 %collective-permute-start.13 = (bf16[8,1024]{1,0:T(8,128)(2,1)S(1)}, bf16[8,1024]{1,0:T(8,128)(2,1)S(1)}, u32[]{:S(2)}, u32[]{:S(2)}) collective-permute-start(bf16[8,1024]{1,0:T(8,128)(2,1)S(1)} %get-tuple-element.57), channel_id=1, source_target_pairs={{0,64},{2,66},{4,68},{6,70},{8,72},{10,74},{12,76},{14,78},{16,80}... | collective-permute-start | bytes 49160 | tf_op jit(solution)/shard_map/ppermute | solution.py:558
  163.1 1.9 %collective-permute-start.15 = (bf16[8,1024]{1,0:T(8,128)(2,1)S(1)}, bf16[8,1024]{1,0:T(8,128)(2,1)S(1)}, u32[]{:S(2)}, u32[]{:S(2)}) collective-permute-start(bf16[8,1024]{1,0:T(8,128)(2,1)S(1)} %get-tuple-element.58), channel_id=1, source_target_pairs={{0,192},{2,194},{4,196},{6,198},{8,200},{10,202},{12,204},{14,206}... | collective-permute-start | bytes 49160 | tf_op jit(solution)/shard_map/ppermute | solution.py:558
  165.0 6.0 %collective-permute-start.14 = (bf16[8,1024]{1,0:T(8,128)(2,1)S(1)}, bf16[8,1024]{1,0:T(8,128)(2,1)S(1)}, u32[]{:S(2)}, u32[]{:S(2)}) collective-permute-start(bf16[8,1024]{1,0:T(8,128)(2,1)S(1)} %get-tuple-element.59), channel_id=1, source_target_pairs={{0,128},{2,130},{4,132},{6,134},{8,136},{10,138},{12,140},{14,142}... | collective-permute-start | bytes 49160 | tf_op jit(solution)/shard_map/ppermute | solution.py:558
  171.0 1.1 collective-permute-done.14
  172.2 0.1 collective-permute-start.16
  172.3 3.7 %collective-permute-done.16 = bf16[4,1024]{1,0:T(4,128)(2,1)S(1)} collective-permute-done((bf16[4,1024]{1,0:T(4,128)(2,1)S(1)}, bf16[4,1024]{1,0:T(4,128)(2,1)S(1)}, u32[]{:S(2)}, u32[]{:S(2)}) %collective-permute-start.16) | collective-permute-done | bytes 8224 | tf_op jit(solution)/shard_map/ppermute | solution.py:558
  176.0 5.0 %shard_map.90 = (bf16[4096,128]{1,0:T(8,128)(2,1)}, bf16[4096,128]{1,0:T(8,128)(2,1)}, bf16[4096,128]{1,0:T(8,128)(2,1)}, bf16[4096,128]{1,0:T(8,128)(2,1)}) custom-call(bf16[128,16,512]{2,1,0:T(8,128)(2,1)S(1)} %all-to-all-done.3.recv_ref, bf16[4,512,512]{2,1,0:T(8,128)(2,1)} %get-tuple-element.37.fixed_in, bf16[2,16,512]{2,1,0:T(8,128)(2,1)S(1)} %pad.9.tail_ref), custom_call_target="tpu_custom_call" | custom-call | flops 2000000000 | bytes 8388608 | tf_op jit(solution)/shard_map/pallas_call | solution.py:518
  (35 shorter events, 0.4 us)
Async XLA Ops:
  2.8 16.3 %all-to-all-start = ((bf16[8,4,1024]{2,1,0:T(4,128)(2,1)}), bf16[8,4,1024]{2,1,0:T(4,128)(2,1)S(1)}, u32[]{:S(2)}, u32[]{:S(2)}) async-start(bf16[8,4,1024]{2,1,0:T(4,128)(2,1)} %broadcast_in_dim.11), calls=%async_computation | async-start | bytes 131072 | tf_op jit(solution)/shard_map/all_to_all | solution.py:579
  19.2 32.0 %copy-start.1 = (s32[128,1]{0,1:T(1,128)S(1)}, s32[128,1]{0,1:T(1,128)}, u32[]{:S(2)}) copy-start(s32[128,1]{0,1:T(1,128)} %constant.124) | copy-start | bytes 1540
  19.2 32.0 %copy-start.2 = (s32[128,1]{0,1:T(1,128)S(1)}, s32[128,1]{0,1:T(1,128)}, u32[]{:S(2)}) copy-start(s32[128,1]{0,1:T(1,128)} %constant.123) | copy-start | bytes 1540
  19.2 32.0 %copy-start.3 = (s32[128,1]{0,1:T(1,128)S(1)}, s32[128,1]{0,1:T(1,128)}, u32[]{:S(2)}) copy-start(s32[128,1]{0,1:T(1,128)} %constant.122) | copy-start | bytes 1540
  19.2 32.0 %copy-start.4 = (s32[128,1]{0,1:T(1,128)S(1)}, s32[128,1]{0,1:T(1,128)}, u32[]{:S(2)}) copy-start(s32[128,1]{0,1:T(1,128)} %constant.121) | copy-start | bytes 1540
  19.2 60.8 %all-to-all-start.1 = ((bf16[128,16,512]{2,1,0:T(8,128)(2,1)}), bf16[128,16,512]{2,1,0:T(8,128)(2,1)S(1)}, u32[]{:S(2)}, u32[]{:S(2)}) async-start(bf16[128,16,512]{2,1,0:T(8,128)(2,1)} %shard_map.84), calls=%async_computation.1 | async-start | bytes 4194304 | tf_op jit(solution)/shard_map/all_to_all | solution.py:628
  28.7 7.1 %collective-permute-start = (bf16[32,1024]{1,0:T(8,128)(2,1)S(1)}, bf16[32,1024]{1,0:T(8,128)(2,1)S(1)}, u32[]{:S(2)}, u32[]{:S(2)}) collective-permute-start(bf16[32,1024]{1,0:T(8,128)(2,1)S(1)} %reshape.94), channel_id=1, source_target_pairs={{0,16},{2,18},{4,20},{6,22},{8,24},{10,26},{12,28},{14,30},{16,0},... | collective-permute-start | bytes 196616 | tf_op jit(solution)/shard_map/ppermute | solution.py:558
  35.8 7.3 %collective-permute-start.1 = (bf16[64,1024]{1,0:T(8,128)(2,1)S(1)}, bf16[64,1024]{1,0:T(8,128)(2,1)S(1)}, u32[]{:S(2)}, u32[]{:S(2)}) collective-permute-start(bf16[64,1024]{1,0:T(8,128)(2,1)S(1)} %get-tuple-element.62), channel_id=1, source_target_pairs={{0,4},{2,6},{4,8},{6,10},{8,12},{10,14},{12,0},{14,2},{16,20},{18,... | collective-permute-start | bytes 393224 | tf_op jit(solution)/shard_map/ppermute | solution.py:558
  36.4 7.3 %collective-permute-start.2 = (bf16[64,1024]{1,0:T(8,128)(2,1)S(1)}, bf16[64,1024]{1,0:T(8,128)(2,1)S(1)}, u32[]{:S(2)}, u32[]{:S(2)}) collective-permute-start(bf16[64,1024]{1,0:T(8,128)(2,1)S(1)} %get-tuple-element.62), channel_id=1, source_target_pairs={{0,12},{2,14},{4,0},{6,2},{8,4},{10,6},{12,8},{14,10},{16,28},{18,... | collective-permute-start | bytes 393224 | tf_op jit(solution)/shard_map/ppermute | solution.py:558
  38.5 10.5 %collective-permute-start.3 = (bf16[64,1024]{1,0:T(8,128)(2,1)S(1)}, bf16[64,1024]{1,0:T(8,128)(2,1)S(1)}, u32[]{:S(2)}, u32[]{:S(2)}) collective-permute-start(bf16[64,1024]{1,0:T(8,128)(2,1)S(1)} %get-tuple-element.62), channel_id=1, source_target_pairs={{0,8},{2,10},{4,12},{6,14},{8,0},{10,2},{12,4},{14,6},{16,24},{18,... | collective-permute-start | bytes 393224 | tf_op jit(solution)/shard_map/ppermute | solution.py:558
  49.0 1.0 copy-start
  50.0 5.6 %collective-permute-start.4 = (bf16[256,1024]{1,0:T(8,128)(2,1)S(1)}, bf16[256,1024]{1,0:T(8,128)(2,1)S(1)}, u32[]{:S(2)}, u32[]{:S(2)}) collective-permute-start(bf16[256,1024]{1,0:T(8,128)(2,1)S(1)} %get-tuple-element.51), channel_id=1, source_target_pairs={{0,2},{2,0},{4,6},{6,4},{8,10},{10,8},{12,14},{14,12},{16,18},{18,... | collective-permute-start | bytes 1572872 | tf_op jit(solution)/shard_map/ppermute | solution.py:558
  67.3 6.7 %collective-permute-start.5 = (f32[128,8]{1,0:T(8,128)S(1)}, f32[128,8]{1,0:T(8,128)S(1)}, u32[]{:S(2)}, u32[]{:S(2)}) collective-permute-start(f32[128,8]{1,0:T(8,128)S(1)} %copy.27), channel_id=1, source_target_pairs={{0,1},{1,0},{2,3},{3,2},{4,5},{5,4},{6,7},{7,6},{8,9},{9,8},{10,11... | collective-permute-start | bytes 12296 | tf_op jit(solution)/shard_map/ppermute | solution.py:562
  83.8 18.5 %all-to-all-start.2 = ((f32[128,1,128]{2,1,0:T(1,128)}), f32[128,1,128]{2,1,0:T(1,128)S(1)}, u32[]{:S(2)}, u32[]{:S(2)}) async-start(f32[128,1,128]{2,1,0:T(1,128)} %get-tuple-element.31), calls=%async_computation.2 | async-start | bytes 131072 | tf_op jit(solution)/shard_map/all_to_all | solution.py:636
  91.9 5.1 %collective-permute-start.6 = (f32[128,8]{1,0:T(8,128)S(1)}, f32[128,8]{1,0:T(8,128)S(1)}, u32[]{:S(2)}, u32[]{:S(2)}) collective-permute-start(f32[128,8]{1,0:T(8,128)S(1)} %slice.75), channel_id=1, source_target_pairs={{0,1},{1,0},{2,3},{3,2},{4,5},{5,4},{6,7},{7,6},{8,9},{9,8},{10,11... | collective-permute-start | bytes 12296 | tf_op jit(solution)/shard_map/ppermute | solution.py:562
  107.6 68.5 %all-to-all-start.3 = ((bf16[128,16,512]{2,1,0:T(8,128)(2,1)}), bf16[128,16,512]{2,1,0:T(8,128)(2,1)S(1)}, u32[]{:S(2)}, u32[]{:S(2)}) async-start(bf16[128,16,512]{2,1,0:T(8,128)(2,1)} %get-tuple-element.32), calls=%async_computation.3 | async-start | bytes 4194304 | tf_op jit(solution)/shard_map/all_to_all | solution.py:640
  115.2 6.9 %collective-permute-start.7 = (f32[128,8]{1,0:T(8,128)S(1)}, f32[128,8]{1,0:T(8,128)S(1)}, u32[]{:S(2)}, u32[]{:S(2)}) collective-permute-start(f32[128,8]{1,0:T(8,128)S(1)} %get-tuple-element.36), channel_id=1, source_target_pairs={{0,1},{1,0},{2,3},{3,2},{4,5},{5,4},{6,7},{7,6},{8,9},{9,8},{10,11... | collective-permute-start | bytes 12296 | tf_op jit(solution)/shard_map/ppermute | solution.py:562
  132.8 4.6 %collective-permute-start.8 = (bf16[256,1024]{1,0:T(8,128)(2,1)}, bf16[256,1024]{1,0:T(8,128)(2,1)S(1)}, u32[]{:S(2)}, u32[]{:S(2)}) collective-permute-start(bf16[256,1024]{1,0:T(8,128)(2,1)} %get-tuple-element.39), channel_id=1, source_target_pairs={{0,2},{2,0},{4,6},{6,4},{8,10},{10,8},{12,14},{14,12},{16,18},{18,... | collective-permute-start | bytes 1572872 | tf_op jit(solution)/shard_map/ppermute | solution.py:558
  138.8 6.7 %collective-permute-start.9 = (bf16[64,1024]{1,0:T(8,128)(2,1)S(1)}, bf16[64,1024]{1,0:T(8,128)(2,1)S(1)}, u32[]{:S(2)}, u32[]{:S(2)}) collective-permute-start(bf16[64,1024]{1,0:T(8,128)(2,1)S(1)} %get-tuple-element.48), channel_id=1, source_target_pairs={{0,12},{2,14},{4,0},{6,2},{8,4},{10,6},{12,8},{14,10},{16,28},{18,... | collective-permute-start | bytes 393224 | tf_op jit(solution)/shard_map/ppermute | solution.py:558
  140.3 8.3 %collective-permute-start.11 = (bf16[64,1024]{1,0:T(8,128)(2,1)S(1)}, bf16[64,1024]{1,0:T(8,128)(2,1)S(1)}, u32[]{:S(2)}, u32[]{:S(2)}) collective-permute-start(bf16[64,1024]{1,0:T(8,128)(2,1)S(1)} %get-tuple-element.49), channel_id=1, source_target_pairs={{0,8},{2,10},{4,12},{6,14},{8,0},{10,2},{12,4},{14,6},{16,24},{18,... | collective-permute-start | bytes 393224 | tf_op jit(solution)/shard_map/ppermute | solution.py:558
  141.6 11.7 %collective-permute-start.10 = (bf16[64,1024]{1,0:T(8,128)(2,1)S(1)}, bf16[64,1024]{1,0:T(8,128)(2,1)S(1)}, u32[]{:S(2)}, u32[]{:S(2)}) collective-permute-start(bf16[64,1024]{1,0:T(8,128)(2,1)S(1)} %get-tuple-element.50), channel_id=1, source_target_pairs={{0,4},{2,6},{4,8},{6,10},{8,12},{10,14},{12,0},{14,2},{16,20},{18,... | collective-permute-start | bytes 393224 | tf_op jit(solution)/shard_map/ppermute | solution.py:558
  153.3 4.5 %collective-permute-start.12 = (bf16[32,1024]{1,0:T(8,128)(2,1)S(1)}, bf16[32,1024]{1,0:T(8,128)(2,1)S(1)}, u32[]{:S(2)}, u32[]{:S(2)}) collective-permute-start(bf16[32,1024]{1,0:T(8,128)(2,1)S(1)} %slice.118), channel_id=1, source_target_pairs={{0,16},{2,18},{4,20},{6,22},{8,24},{10,26},{12,28},{14,30},{16,0},... | collective-permute-start | bytes 196616 | tf_op jit(solution)/shard_map/ppermute | solution.py:558
  157.9 13.1 %collective-permute-start.13 = (bf16[8,1024]{1,0:T(8,128)(2,1)S(1)}, bf16[8,1024]{1,0:T(8,128)(2,1)S(1)}, u32[]{:S(2)}, u32[]{:S(2)}) collective-permute-start(bf16[8,1024]{1,0:T(8,128)(2,1)S(1)} %get-tuple-element.57), channel_id=1, source_target_pairs={{0,64},{2,66},{4,68},{6,70},{8,72},{10,74},{12,76},{14,78},{16,80}... | collective-permute-start | bytes 49160 | tf_op jit(solution)/shard_map/ppermute | solution.py:558
  163.1 7.9 %collective-permute-start.15 = (bf16[8,1024]{1,0:T(8,128)(2,1)S(1)}, bf16[8,1024]{1,0:T(8,128)(2,1)S(1)}, u32[]{:S(2)}, u32[]{:S(2)}) collective-permute-start(bf16[8,1024]{1,0:T(8,128)(2,1)S(1)} %get-tuple-element.58), channel_id=1, source_target_pairs={{0,192},{2,194},{4,196},{6,198},{8,200},{10,202},{12,204},{14,206}... | collective-permute-start | bytes 49160 | tf_op jit(solution)/shard_map/ppermute | solution.py:558
  165.0 7.1 %collective-permute-start.14 = (bf16[8,1024]{1,0:T(8,128)(2,1)S(1)}, bf16[8,1024]{1,0:T(8,128)(2,1)S(1)}, u32[]{:S(2)}, u32[]{:S(2)}) collective-permute-start(bf16[8,1024]{1,0:T(8,128)(2,1)S(1)} %get-tuple-element.59), channel_id=1, source_target_pairs={{0,128},{2,130},{4,132},{6,134},{8,136},{10,138},{12,140},{14,142}... | collective-permute-start | bytes 49160 | tf_op jit(solution)/shard_map/ppermute | solution.py:558
  172.2 3.8 %collective-permute-start.16 = (bf16[4,1024]{1,0:T(4,128)(2,1)S(1)}, bf16[4,1024]{1,0:T(4,128)(2,1)S(1)}, u32[]{:S(2)}, u32[]{:S(2)}) collective-permute-start(bf16[4,1024]{1,0:T(4,128)(2,1)S(1)} %slice.119), channel_id=1, source_target_pairs={{0,32},{2,34},{4,36},{6,38},{8,40},{10,42},{12,44},{14,46},{16,48}... | collective-permute-start | bytes 24584 | tf_op jit(solution)/shard_map/ppermute | solution.py:558

commit v5 on v4

--- a/solution.py
+++ b/solution.py
@@ -43,6 +43,10 @@
 
 def dot_tn(a, b):
     return lax.dot_general(a, b, (((0,), (0,)), ((), ())), preferred_element_type=F32)
+
+
+def dot_rows(a, b):
+    return dot_tn(b, a).T
 
 
 def batch_dot(a, b, left, right):
@@ -322,7 +326,7 @@
 
 
 def strided_backward_kernel(
-    keys_in, prob_in, grp_ref, sums_ref, other_ref, recv_ref, send_out, block_ref,
+    keys_in, prob_in, grp_ref, sums_ref, other_ref, recv_ref, send_out,
     keys_ref, prob_ref, out_ref, send_ref, in_sem, out_sem,
 ):
     fetched = [
@@ -333,7 +337,6 @@
         for head in range(HEADS)
     ]
     moved = recv_ref[...].reshape(NB, HD)
-    block_ref[...] = moved[:, 8:16]
     total = sums_ref[:, 8:16] + other_ref[...] + moved[:, :8]
     square = jnp.stack([total[:, at : at + 1] for at in range(OFFS)])
     cross = jnp.stack([total[:, OFFS + at : OFFS + at + 1] for at in range(OFFS)])
@@ -377,11 +380,8 @@
             spec((NB, 8), 0, 0),
             spec((NB, 1, HD), 0, 0, 0),
         ],
-        [IN_HBM, spec((NB, 8), 0, 0)],
-        [
-            pltpu.HBM((NB, 16, WIDTH), BF16),
-            jax.ShapeDtypeStruct((NB, 8), F32),
-        ],
+        IN_HBM,
+        pltpu.HBM((NB, 16, WIDTH), BF16),
         10**9,
         6 * 2**20,
         [
@@ -396,60 +396,81 @@
     )(in_hbm(keys), in_hbm(prob), grp, sums, other, recv)
 
 
-def fixed_backward_kernel(
-    rows_ref, summ_ref, own_ref, far_ref, attn_ref, sums_ref, out_ref, keep_ref, send_ref
+def summary_backward_kernel(
+    rows_ref, summ_ref, far_ref, attn_ref, sums_ref, query_ref, keep_ref, send_ref
 ):
+    wide = attn_ref[...].astype(F32)
+    _, grad, row_dot = normalize(wide, rows_ref[3], sums_ref[:, 0:1], sums_ref[:, 1:2])
+    far = far_ref[0]
+    score = (far * (dot_nt(grad, summ_ref[:, HD:]) - row_dot) * scale).astype(BF16)
+    query_ref[...] = dot(score, summ_ref[:, :HD])
+    key = dot_rows(score, rows_ref[0])
+    value = dot_rows(far.astype(BF16), grad)
+    half = BLOCK // 2
+    send_ref[:, :HD] = key[half:].astype(BF16)
+    send_ref[:, HD:] = value[half:].astype(BF16)
+    keep_ref[:, :HD] = key[:half]
+    keep_ref[:, HD:] = value[:half]
+
+
+def summary_backward(rows, summ, far, attn, sums):
+    return call(
+        summary_backward_kernel,
+        HEADS,
+        [
+            spec((4, BLOCK, HD), 0, 0, "i"),
+            spec((BLOCK, 2 * HD), 0, "i"),
+            spec((1, BLOCK, BLOCK), "i", 0, 0),
+            spec((BLOCK, HD), 0, "i"),
+            spec((BLOCK, 2), 0, 0),
+        ],
+        [
+            spec((BLOCK, HD), 0, "i"),
+            spec((BLOCK // 2, 2 * HD), 0, "i"),
+            spec((BLOCK // 2, 2 * HD), 0, "i"),
+        ],
+        [
+            jax.ShapeDtypeStruct((BLOCK, WIDTH), F32),
+            jax.ShapeDtypeStruct((BLOCK // 2, 2 * WIDTH), F32),
+            jax.ShapeDtypeStruct((BLOCK // 2, 2 * WIDTH), BF16),
+        ],
+        3 * 10**9,
+        8 * 2**20,
+    )(rows, summ, far, attn, sums)
+
+
+def fixed_backward_kernel(rows_ref, own_ref, attn_ref, sums_ref, query_ref, out_ref, tail_ref):
     query, key, value = rows_ref[0], rows_ref[1], rows_ref[2]
-    summ_key, summ_value = summ_ref[:, :HD], summ_ref[:, HD:]
-    own, far = own_ref[0], far_ref[0]
+    own = own_ref[0]
     wide = attn_ref[...].astype(F32)
     normed, grad, row_dot = normalize(wide, rows_ref[3], sums_ref[:, 0:1], sums_ref[:, 1:2])
     out_ref[0] = normed
-    own_score = (own * (dot_nt(grad, value) - row_dot) * scale).astype(BF16)
-    far_score = (far * (dot_nt(grad, summ_value) - row_dot) * scale).astype(BF16)
-    out_ref[1] = (dot(own_score, key) + dot(far_score, summ_key)).astype(BF16)
-    grad_key = dot_tn(own_score, query)
-    grad_value = dot_tn(own.astype(BF16), grad)
-    out_ref[2] = grad_key.astype(BF16)
-    out_ref[3] = grad_value.astype(BF16)
-    far_key = dot_tn(far_score, query)
-    far_value = dot_tn(far.astype(BF16), grad)
-    half = BLOCK // 2
-    send_ref[:, :HD] = far_key[half:].astype(BF16)
-    send_ref[:, HD:] = far_value[half:].astype(BF16)
-    keep_ref[:, :HD] = far_key[:half]
-    keep_ref[:, HD:] = far_value[:half]
-    row = lax.broadcasted_iota(jnp.int32, (8, HD), 0)
-    for at, grads in ((0, grad_key), (HD, grad_value)):
-        tail = pltpu.roll(grads[BLOCK - 8 :], SUMM, 0)
-        keep_ref[0:8, at : at + HD] += jnp.where(row < SUMM, tail, 0.0)
-
-
-def fixed_backward(rows, summ, own, far, attn, sums):
+    score = (own * (dot_nt(grad, value) - row_dot) * scale).astype(BF16)
+    out_ref[1] = (dot(score, key) + query_ref[...]).astype(BF16)
+    for at, grads in enumerate((dot_rows(score, query), dot_rows(own.astype(BF16), grad))):
+        out_ref[2 + at] = grads.astype(BF16)
+        tail_ref[at] = grads[BLOCK - 8 :]
+
+
+def fixed_backward(rows, own, attn, sums, far_query):
     return call(
         fixed_backward_kernel,
         HEADS,
         [
             spec((4, BLOCK, HD), 0, 0, "i"),
-            spec((BLOCK, 2 * HD), 0, "i"),
-            spec((1, BLOCK, BLOCK), "i", 0, 0),
             spec((1, BLOCK, BLOCK), "i", 0, 0),
             spec((BLOCK, HD), 0, "i"),
             spec((BLOCK, 2), 0, 0),
-        ],
-        [
-            spec((4, BLOCK, HD), 0, 0, "i"),
-            spec((BLOCK // 2, 2 * HD), 0, "i"),
-            spec((BLOCK // 2, 2 * HD), 0, "i"),
-        ],
+            spec((BLOCK, HD), 0, "i"),
+        ],
+        [spec((4, BLOCK, HD), 0, 0, "i"), spec((2, 8, HD), 0, 0, "i")],
         [
             pltpu.HBM((4, BLOCK, WIDTH), BF16),
-            jax.ShapeDtypeStruct((BLOCK // 2, 2 * WIDTH), F32),
-            jax.ShapeDtypeStruct((BLOCK // 2, 2 * WIDTH), BF16),
-        ],
-        8 * 10**9,
+            jax.ShapeDtypeStruct((2, 8, WIDTH), F32),
+        ],
+        5 * 10**9,
         8 * 2**20,
-    )(rows, summ, own, far, attn, sums)
+    )(rows, own, attn, sums, far_query)
 
 
 def unpack_kernel(recv_ref, fixed_in, tail_ref, *refs):
@@ -589,10 +610,13 @@
     return held
 
 
-def scatter_summaries(total, sent):
-    (part, step, _), = ROUNDS[-1]
-    parts = total + shift(sent, part, -step).astype(F32)
-    for steps in ROUNDS[-2::-1]:
+def scatter_first(total, sent):
+    ((part, step, _),) = ROUNDS[-1]
+    return total + shift(sent, part, -step).astype(F32)
+
+
+def scatter_summaries(parts, rounds):
+    for steps in rounds[::-1]:
         kept = parts.shape[0] - SUMM * sum(slots for _, _, slots in steps)
         total, at = parts[:kept], kept
         for part, step, slots in steps:
@@ -635,13 +659,19 @@
     keys, prob, grp, sums, sums_send = strided_forward(recv, jnp.pad(fixed_both, ((0, 0), (0, HD - 8))))
     sums_in = lax.all_to_all(sums_send, "seq", 0, 0, tiled=True)
     sums_other = other_head(sums[:, 8:16])
-    send_back, block_sums = strided_backward(keys, prob, grp, sums, sums_other, sums_in)
-    block_sums = fixed_both + block_sums + other_head(block_sums)
+    own_sums = sums_in[:, 0, 8:16]
+    block_sums = fixed_both + own_sums + other_head(own_sums)
+    send_back = strided_backward(keys, prob, grp, sums, sums_other, sums_in)
+    send_back, block_sums = lax.optimization_barrier((send_back, block_sums))
     recv_back = lax.all_to_all(send_back, "seq", 0, 0, tiled=True)
     block_sums = block_sums.reshape(NB, 2, OFFS).transpose(0, 2, 1).reshape(BLOCK, 2)
-    fixed_out, kept, sent = fixed_backward(rows, summ, own_prob, far_prob, fixed_attn, block_sums)
-    totals = scatter_summaries(kept, sent).astype(BF16).reshape(SUMM, HEADS, 2, HD)
+    far_query, kept, sent = summary_backward(rows, summ, far_prob, fixed_attn, block_sums)
+    fixed_out, tails = fixed_backward(rows, own_prob, fixed_attn, block_sums, far_query)
+    parts = scatter_summaries(scatter_first(kept, sent), ROUNDS[3:4])
+    parts, fixed_out, tails = lax.optimization_barrier((parts, fixed_out, tails))
+    totals = scatter_summaries(parts, ROUNDS[:3]).reshape(SUMM, HEADS, 2, HD)
     totals = totals.transpose(2, 0, 1, 3).reshape(2, SUMM, WIDTH)
+    totals = (tails[:, 8 - SUMM :] + totals).astype(BF16)
     tail = jnp.pad(totals, ((0, 0), (16 - SUMM, 0), (0, 0)))
     return unpack(recv_back, fixed_out, tail)
 

time: 184 us -> 180 us (0.978)
  starting transfers between devices: 68.4 us -> 62.3 us
  Pallas kernels: 40.4 us -> 45.7 us
  waiting for transfers between devices: 62.6 us -> 59.8 us
    ppermute x3, waiting for transfers between devices: 11.7 us -> 4.18 us  [other_head(): return lax.ppermute(array, 'head', [(0, 1), (1, 0)])]
    pallas_call x0 -> x1, Pallas kernels: none -> 7.1 us  [summary_backward(): call(summary_backward_kernel, HEADS, [spec((4, BLOCK, HD), 0, 0, 'i'), sp...]
    ppermute x14, starting transfers between devices: 27.2 us -> 22.6 us  [shift(): return lax.ppermute(array, 'seq', perm)]
    all_to_all x1, waiting for transfers between devices: 5.39 us -> 8.2 us  [shards(): sums_in = lax.all_to_all(sums_send, 'seq', 0, 0, tiled=True)]
    ppermute x14, waiting for transfers between devices: 35.8 us -> 37.7 us  [shift(): return lax.ppermute(array, 'seq', perm)]
  transfers between devices with their start and end apart: 21 -> 21, of which waited for: 17 -> 15; matrix products, arithmetic and copies ran while one was open for 3% -> 4% of each run, Pallas kernels for 15% -> 21%
where the time goes in v5:
time: 180 us; the launch traced here: 179 us
  starting transfers between devices  62.3 us (35%)
  waiting for transfers between devices  59.8 us (33%)
  Pallas kernels  45.7 us (25%)
  local copies, waits for them, and re-layouts  7.35 us (4%)
  other arithmetic  2.41 us (1%)
    ppermute x14, waiting for transfers between devices, shift(): return lax.ppermute(array, 'seq', perm)  37.7 us
    ppermute x14, starting transfers between devices, shift(): return lax.ppermute(array, 'seq', perm)  22.6 us
    pallas_call x1, Pallas kernels, fixed_forward(): call(fixed_forward_kernel, HEADS, [spec((4, BLOCK, HD), 0, 0, 'i'), spec(...  9.74 us
    all_to_all x1, starting transfers between devices, shards(): recv = lax.all_to_all(send, 'seq', 0, 0, tiled=True)  9.51 us
    all_to_all x1, starting transfers between devices, gather_along_z(): lax.all_to_all(sent, 'seq', 0, 0, axis_index_groups=groups, tiled=True)  9.01 us
    all_to_all x1, waiting for transfers between devices, shards(): sums_in = lax.all_to_all(sums_send, 'seq', 0, 0, tiled=True)  8.2 us
    all_to_all x1, starting transfers between devices, shards(): sums_in = lax.all_to_all(sums_send, 'seq', 0, 0, tiled=True)  8.01 us
    pallas_call x1, Pallas kernels, fixed_backward(): call(fixed_backward_kernel, HEADS, [spec((4, BLOCK, HD), 0, 0, 'i'), spec...  7.78 us
  transfers between devices with their start and end apart: 21, of which 15 were waited for; matrix products, arithmetic and copies ran while one was open for 4% of the time, Pallas kernels for 21%

profile of v5, /device:TPU:1, one launch (start us, length us, event | category | flops | bytes accessed | tf_op | source)
XLA Modules:
  0.0 178.6 jit_solution(10788407751253389328)
XLA Ops:
  0.6 0.7 slice_reduce_fusion.1
  1.4 0.7 slice_reduce_fusion
  2.2 0.6 broadcast_in_dim.11
  2.8 9.0 %all-to-all-start = ((bf16[8,4,1024]{2,1,0:T(4,128)(2,1)}), bf16[8,4,1024]{2,1,0:T(4,128)(2,1)S(1)}, u32[]{:S(2)}, u32[]{:S(2)}) async-start(bf16[8,4,1024]{2,1,0:T(4,128)(2,1)} %broadcast_in_dim.11), calls=%async_computation | async-start | bytes 131072 | tf_op jit(solution)/shard_map/all_to_all | solution.py:600
  11.8 3.5 %shard_map.84 = bf16[128,16,512]{2,1,0:T(8,128)(2,1)} custom-call(bf16[4096,128]{1,0:T(8,128)(2,1)} %bitcast.79, bf16[4096,128]{1,0:T(8,128)(2,1)} %bitcast.75, bf16[4096,128]{1,0:T(8,128)(2,1)} %bitcast.77, bf16[4096,128]{1,0:T(8,128)(2,1)} %bitcast.81), custom_call_target="tpu_custom_call" | custom-call | flops 1000000000 | bytes 6291456 | tf_op jit(solution)/shard_map/pallas_call | solution.py:142
  15.4 3.7 %all-to-all-done = bf16[8,4,1024]{2,1,0:T(4,128)(2,1)S(1)} async-done(((bf16[8,4,1024]{2,1,0:T(4,128)(2,1)}), bf16[8,4,1024]{2,1,0:T(4,128)(2,1)S(1)}, u32[]{:S(2)}, u32[]{:S(2)}) %all-to-all-start) | async-done | bytes 65568 | tf_op jit(solution)/shard_map/all_to_all | solution.py:600
  19.1 0.1 fusion.2
  19.2 0.0 copy-start.1
  19.2 0.0 copy-start.2
  19.2 0.0 copy-start.3
  19.2 0.0 copy-start.4
  19.2 9.5 %all-to-all-start.1 = ((bf16[128,16,512]{2,1,0:T(8,128)(2,1)}), bf16[128,16,512]{2,1,0:T(8,128)(2,1)S(1)}, u32[]{:S(2)}, u32[]{:S(2)}) async-start(bf16[128,16,512]{2,1,0:T(8,128)(2,1)} %shard_map.84), calls=%async_computation.1 | async-start | bytes 4194304 | tf_op jit(solution)/shard_map/all_to_all | solution.py:652
  28.8 1.5 collective-permute-start
  30.3 5.6 %collective-permute-done = bf16[32,1024]{1,0:T(8,128)(2,1)S(1)} collective-permute-done((bf16[32,1024]{1,0:T(8,128)(2,1)S(1)}, bf16[32,1024]{1,0:T(8,128)(2,1)S(1)}, u32[]{:S(2)}, u32[]{:S(2)}) %collective-permute-start) | collective-permute-done | bytes 65568 | tf_op jit(solution)/shard_map/ppermute | solution.py:579
  35.8 0.6 collective-permute-start.1
  36.5 2.1 %collective-permute-start.2 = (bf16[64,1024]{1,0:T(8,128)(2,1)S(1)}, bf16[64,1024]{1,0:T(8,128)(2,1)S(1)}, u32[]{:S(2)}, u32[]{:S(2)}) collective-permute-start(bf16[64,1024]{1,0:T(8,128)(2,1)S(1)} %get-tuple-element.72), channel_id=1, source_target_pairs={{0,12},{2,14},{4,0},{6,2},{8,4},{10,6},{12,8},{14,10},{16,28},{18,... | collective-permute-start | bytes 393224 | tf_op jit(solution)/shard_map/ppermute | solution.py:579
  38.6 0.8 collective-permute-start.3
  39.4 3.7 %collective-permute-done.1 = bf16[64,1024]{1,0:T(8,128)(2,1)S(1)} collective-permute-done((bf16[64,1024]{1,0:T(8,128)(2,1)S(1)}, bf16[64,1024]{1,0:T(8,128)(2,1)S(1)}, u32[]{:S(2)}, u32[]{:S(2)}) %collective-permute-start.1) | collective-permute-done | bytes 131104 | tf_op jit(solution)/shard_map/ppermute | solution.py:579
  43.1 0.6 collective-permute-done.2
  43.7 5.3 %collective-permute-done.3 = bf16[64,1024]{1,0:T(8,128)(2,1)S(1)} collective-permute-done((bf16[64,1024]{1,0:T(8,128)(2,1)S(1)}, bf16[64,1024]{1,0:T(8,128)(2,1)S(1)}, u32[]{:S(2)}, u32[]{:S(2)}) %collective-permute-start.3) | collective-permute-done | bytes 131104 | tf_op jit(solution)/shard_map/ppermute | solution.py:579
  49.1 1.0 copy-done
  50.1 1.2 collective-permute-start.4
  51.3 0.1 broadcast_in_dim.12
  51.4 0.7 broadcast_in_dim_reshape.4.seen_ref
  52.1 3.6 %shard_map.85.rows_ref = bf16[4,512,512]{2,1,0:T(8,128)(2,1)} custom-call(bf16[4096,128]{1,0:T(8,128)(2,1)} %bitcast.80, bf16[4096,128]{1,0:T(8,128)(2,1)} %bitcast.76, bf16[4096,128]{1,0:T(8,128)(2,1)} %bitcast.78, bf16[4096,128]{1,0:T(8,128)(2,1)} %bitcast.82), custom_call_target="tpu_custom_call" | custom-call | flops 1000000000 | bytes 6291456 | tf_op jit(solution)/shard_map/pallas_call | solution.py:173
  55.7 0.8 constant_dynamic-update-slice_fusion.7.summ_ref
  56.5 9.7 %shard_map.86 = (bf16[512,512]{1,0:T(8,128)(2,1)}, f32[4,512,512]{2,1,0:T(8,128)}, f32[4,512,512]{2,1,0:T(8,128)}, f32[512,8]{1,0:T(8,128)}) custom-call(bf16[4,512,512]{2,1,0:T(8,128)(2,1)} %shard_map.85.rows_ref, bf16[512,1024]{1,0:T(8,128)(2,1)} %constant_dynamic-update-slice_fusion.7.summ_ref, s32[1,512]{1,0:T(1,128)} %broadcast_in_dim_reshape.4.seen_ref), custom_call_target="tpu_custom_call" | custom-call | flops 4000000000 | bytes 4194304 | tf_op jit(solution)/shard_map/pallas_call | solution.py:222
  66.2 1.0 copy.25
  67.3 0.1 copy.27
  67.4 2.5 %collective-permute-start.5 = (f32[128,8]{1,0:T(8,128)S(1)}, f32[128,8]{1,0:T(8,128)S(1)}, u32[]{:S(2)}, u32[]{:S(2)}) collective-permute-start(f32[128,8]{1,0:T(8,128)S(1)} %copy.27), channel_id=1, source_target_pairs={{0,1},{1,0},{2,3},{3,2},{4,5},{5,4},{6,7},{7,6},{8,9},{9,8},{10,11... | collective-permute-start | bytes 12296 | tf_op jit(solution)/shard_map/ppermute | solution.py:583
  69.9 4.2 %collective-permute-done.5 = f32[128,8]{1,0:T(8,128)S(1)} collective-permute-done((f32[128,8]{1,0:T(8,128)S(1)}, f32[128,8]{1,0:T(8,128)S(1)}, u32[]{:S(2)}, u32[]{:S(2)}) %collective-permute-start.5) | collective-permute-done | bytes 4128 | tf_op jit(solution)/shard_map/ppermute | solution.py:583
  74.1 6.0 %all-to-all-done.1.recv_ref = bf16[128,16,512]{2,1,0:T(8,128)(2,1)S(1)} async-done(((bf16[128,16,512]{2,1,0:T(8,128)(2,1)}), bf16[128,16,512]{2,1,0:T(8,128)(2,1)S(1)}, u32[]{:S(2)}, u32[]{:S(2)}) %all-to-all-start.1) | async-done | bytes 2097184 | tf_op jit(solution)/shard_map/all_to_all | solution.py:652
  80.1 3.7 %shard_map.87 = (bf16[4,3,4,128,128]{4,3,2,1,0:T(8,128)(2,1)}, f32[4,4,128,128]{3,2,1,0:T(8,128)}, bf16[4,2,4,128,128]{4,3,2,1,0:T(8,128)(2,1)S(1)}, f32[128,128]{1,0:T(8,128)S(1)}, f32[128,1,128]{2,1,0:T(1,128)}) custom-call(bf16[128,16,512]{2,1,0:T(8,128)(2,1)S(1)} %all-to-all-done.1.recv_ref, f32[128,128]{1,0:T(8,128)S(1)} %pad.8.fixed_ref), custom_call_target="tpu_custom_call" | custom-call | flops 1000000000 | bytes 6291456 | tf_op jit(solution)/shard_map/pallas_call | solution.py:290
  83.8 8.0 %all-to-all-start.2 = ((f32[128,1,128]{2,1,0:T(1,128)}), f32[128,1,128]{2,1,0:T(1,128)S(1)}, u32[]{:S(2)}, u32[]{:S(2)}) async-start(f32[128,1,128]{2,1,0:T(1,128)} %get-tuple-element.36), calls=%async_computation.2 | async-start | bytes 131072 | tf_op jit(solution)/shard_map/all_to_all | solution.py:660
  91.9 0.1 slice.81
  91.9 2.2 %collective-permute-start.6 = (f32[128,8]{1,0:T(8,128)S(1)}, f32[128,8]{1,0:T(8,128)S(1)}, u32[]{:S(2)}, u32[]{:S(2)}) collective-permute-start(f32[128,8]{1,0:T(8,128)S(1)} %slice.81), channel_id=1, source_target_pairs={{0,1},{1,0},{2,3},{3,2},{4,5},{5,4},{6,7},{7,6},{8,9},{9,8},{10,11... | collective-permute-start | bytes 12296 | tf_op jit(solution)/shard_map/ppermute | solution.py:583
  94.2 8.2 %all-to-all-done.2.recv_ref = f32[128,1,128]{2,1,0:T(1,128)S(1)} async-done(((f32[128,1,128]{2,1,0:T(1,128)}), f32[128,1,128]{2,1,0:T(1,128)S(1)}, u32[]{:S(2)}, u32[]{:S(2)}) %all-to-all-start.2) | async-done | bytes 65568 | tf_op jit(solution)/shard_map/all_to_all | solution.py:660
  102.4 0.2 slice.96
  102.6 2.3 %collective-permute-start.7 = (f32[128,8]{1,0:T(8,128)S(1)}, f32[128,8]{1,0:T(8,128)S(1)}, u32[]{:S(2)}, u32[]{:S(2)}) collective-permute-start(f32[128,8]{1,0:T(8,128)S(1)} %bitcast.86), channel_id=1, source_target_pairs={{0,1},{1,0},{2,3},{3,2},{4,5},{5,4},{6,7},{7,6},{8,9},{9,8},{10,11... | collective-permute-start | bytes 12296 | tf_op jit(solution)/shard_map/ppermute | solution.py:583
  104.8 5.2 %shard_map.88 = bf16[128,16,512]{2,1,0:T(8,128)(2,1)} custom-call(bf16[4,3,4,128,128]{4,3,2,1,0:T(8,128)(2,1)} %get-tuple-element.32.keys_in, f32[4,4,128,128]{3,2,1,0:T(8,128)} %get-tuple-element.33.prob_in, bf16[4,2,4,128,128]{4,3,2,1,0:T(8,128)(2,1)S(1)} %get-tuple-element.34.grp_ref, f32[128,128]{1,0:T(8,128)S(1)} %get-tuple-element.35.sums_ref, ...), custom_call_target="tpu_custom_call" | custom-call | flops 1000000000 | bytes 6291456 | tf_op jit(solution)/shard_map/pallas_call | solution.py:372
  110.1 6.2 %all-to-all-start.3 = ((bf16[128,16,512]{2,1,0:T(8,128)(2,1)}), bf16[128,16,512]{2,1,0:T(8,128)(2,1)S(1)}, u32[]{:S(2)}, u32[]{:S(2)}) async-start(bf16[128,16,512]{2,1,0:T(8,128)(2,1)} %shard_map.88), calls=%async_computation.3 | async-start | bytes 4194304 | tf_op jit(solution)/shard_map/all_to_all | solution.py:666
  116.3 0.9 copy.29
  117.2 7.1 %shard_map.89 = (f32[512,512]{1,0:T(8,128)}, f32[256,1024]{1,0:T(8,128)}, bf16[256,1024]{1,0:T(8,128)(2,1)}) custom-call(bf16[4,512,512]{2,1,0:T(8,128)(2,1)} %shard_map.85.rows_ref, bf16[512,1024]{1,0:T(8,128)(2,1)} %constant_dynamic-update-slice_fusion.7.summ_ref, f32[4,512,512]{2,1,0:T(8,128)} %get-tuple-element.38.far_ref, ...), custom_call_target="tpu_custom_call" | custom-call | flops 3000000000 | bytes 8388608 | tf_op jit(solution)/shard_map/pallas_call | solution.py:417
  124.3 1.0 collective-permute-start.8
  125.3 1.7 collective-permute-done.8
  127.1 1.4 fusion.16
  128.5 0.8 collective-permute-start.10
  129.3 2.4 %collective-permute-start.11 = (bf16[64,1024]{1,0:T(8,128)(2,1)S(1)}, bf16[64,1024]{1,0:T(8,128)(2,1)S(1)}, u32[]{:S(2)}, u32[]{:S(2)}) collective-permute-start(bf16[64,1024]{1,0:T(8,128)(2,1)S(1)} %get-tuple-element.59), channel_id=1, source_target_pairs={{0,8},{2,10},{4,12},{6,14},{8,0},{10,2},{12,4},{14,6},{16,24},{18,... | collective-permute-start | bytes 393224 | tf_op jit(solution)/shard_map/ppermute | solution.py:579
  131.8 1.2 collective-permute-start.9
  132.9 7.8 %shard_map.90 = (bf16[4,512,512]{2,1,0:T(8,128)(2,1)}, f32[2,8,512]{2,1,0:T(8,128)}) custom-call(bf16[4,512,512]{2,1,0:T(8,128)(2,1)} %shard_map.85.rows_ref, f32[4,512,512]{2,1,0:T(8,128)} %get-tuple-element.43.own_ref, bf16[512,512]{1,0:T(8,128)(2,1)} %get-tuple-element.39.attn_ref, f32[512,2]{1,0:T(8,128)} %bitcast.84, f32[512,512]{1,0:T(8,128)} %get-tuple-element.44.query_ref), custom_call_target="tpu_custom_call" | custom-call | flops 5000000000 | bytes 8388608 | tf_op jit(solution)/shard_map/pallas_call | solution.py:456
  140.7 0.1 collective-permute-done.11
  140.8 1.9 %collective-permute-done.9 = bf16[64,1024]{1,0:T(8,128)(2,1)S(1)} collective-permute-done((bf16[64,1024]{1,0:T(8,128)(2,1)S(1)}, bf16[64,1024]{1,0:T(8,128)(2,1)S(1)}, u32[]{:S(2)}, u32[]{:S(2)}) %collective-permute-start.9) | collective-permute-done | bytes 131104 | tf_op jit(solution)/shard_map/ppermute | solution.py:579
  142.6 0.1 fusion.1
  142.7 1.4 collective-permute-start.12
  144.1 2.7 %collective-permute-done.12 = bf16[32,1024]{1,0:T(8,128)(2,1)S(1)} collective-permute-done((bf16[32,1024]{1,0:T(8,128)(2,1)S(1)}, bf16[32,1024]{1,0:T(8,128)(2,1)S(1)}, u32[]{:S(2)}, u32[]{:S(2)}) %collective-permute-start.12) | collective-permute-done | bytes 65568 | tf_op jit(solution)/shard_map/ppermute | solution.py:579
  146.8 3.3 %collective-permute-start.13 = (bf16[8,1024]{1,0:T(8,128)(2,1)S(1)}, bf16[8,1024]{1,0:T(8,128)(2,1)S(1)}, u32[]{:S(2)}, u32[]{:S(2)}) collective-permute-start(bf16[8,1024]{1,0:T(8,128)(2,1)S(1)} %get-tuple-element.67), channel_id=1, source_target_pairs={{0,64},{2,66},{4,68},{6,70},{8,72},{10,74},{12,76},{14,78},{16,80}... | collective-permute-start | bytes 49160 | tf_op jit(solution)/shard_map/ppermute | solution.py:579
  150.1 2.7 %collective-permute-start.14 = (bf16[8,1024]{1,0:T(8,128)(2,1)S(1)}, bf16[8,1024]{1,0:T(8,128)(2,1)S(1)}, u32[]{:S(2)}, u32[]{:S(2)}) collective-permute-start(bf16[8,1024]{1,0:T(8,128)(2,1)S(1)} %get-tuple-element.69), channel_id=1, source_target_pairs={{0,128},{2,130},{4,132},{6,134},{8,136},{10,138},{12,140},{14,142}... | collective-permute-start | bytes 49160 | tf_op jit(solution)/shard_map/ppermute | solution.py:579
  152.8 3.5 %collective-permute-start.15 = (bf16[8,1024]{1,0:T(8,128)(2,1)S(1)}, bf16[8,1024]{1,0:T(8,128)(2,1)S(1)}, u32[]{:S(2)}, u32[]{:S(2)}) collective-permute-start(bf16[8,1024]{1,0:T(8,128)(2,1)S(1)} %get-tuple-element.68), channel_id=1, source_target_pairs={{0,192},{2,194},{4,196},{6,198},{8,200},{10,202},{12,204},{14,206}... | collective-permute-start | bytes 49160 | tf_op jit(solution)/shard_map/ppermute | solution.py:579
  156.3 9.2 %collective-permute-done.13 = bf16[8,1024]{1,0:T(8,128)(2,1)S(1)} collective-permute-done((bf16[8,1024]{1,0:T(8,128)(2,1)S(1)}, bf16[8,1024]{1,0:T(8,128)(2,1)S(1)}, u32[]{:S(2)}, u32[]{:S(2)}) %collective-permute-start.13) | collective-permute-done | bytes 16416 | tf_op jit(solution)/shard_map/ppermute | solution.py:579
  165.5 3.2 %collective-permute-done.14 = bf16[8,1024]{1,0:T(8,128)(2,1)S(1)} collective-permute-done((bf16[8,1024]{1,0:T(8,128)(2,1)S(1)}, bf16[8,1024]{1,0:T(8,128)(2,1)S(1)}, u32[]{:S(2)}, u32[]{:S(2)}) %collective-permute-start.14) | collective-permute-done | bytes 16416 | tf_op jit(solution)/shard_map/ppermute | solution.py:579
  168.8 0.1 collective-permute-start.16
  168.9 3.7 %collective-permute-done.16 = bf16[4,1024]{1,0:T(4,128)(2,1)S(1)} collective-permute-done((bf16[4,1024]{1,0:T(4,128)(2,1)S(1)}, bf16[4,1024]{1,0:T(4,128)(2,1)S(1)}, u32[]{:S(2)}, u32[]{:S(2)}) %collective-permute-start.16) | collective-permute-done | bytes 8224 | tf_op jit(solution)/shard_map/ppermute | solution.py:579
  172.6 0.8 add_convert_fusion
  173.4 5.0 %shard_map.91 = (bf16[4096,128]{1,0:T(8,128)(2,1)}, bf16[4096,128]{1,0:T(8,128)(2,1)}, bf16[4096,128]{1,0:T(8,128)(2,1)}, bf16[4096,128]{1,0:T(8,128)(2,1)}) custom-call(bf16[128,16,512]{2,1,0:T(8,128)(2,1)S(1)} %all-to-all-done.3.recv_ref, bf16[4,512,512]{2,1,0:T(8,128)(2,1)} %get-tuple-element.47.fixed_in, bf16[2,16,512]{2,1,0:T(8,128)(2,1)S(1)} %pad.9.tail_ref), custom_call_target="tpu_custom_call" | custom-call | flops 2000000000 | bytes 8388608 | tf_op jit(solution)/shard_map/pallas_call | solution.py:539
  (38 shorter events, 0.4 us)
Async XLA Ops:
  2.8 16.3 %all-to-all-start = ((bf16[8,4,1024]{2,1,0:T(4,128)(2,1)}), bf16[8,4,1024]{2,1,0:T(4,128)(2,1)S(1)}, u32[]{:S(2)}, u32[]{:S(2)}) async-start(bf16[8,4,1024]{2,1,0:T(4,128)(2,1)} %broadcast_in_dim.11), calls=%async_computation | async-start | bytes 131072 | tf_op jit(solution)/shard_map/all_to_all | solution.py:600
  19.2 32.1 %copy-start.1 = (s32[128,1]{0,1:T(1,128)S(1)}, s32[128,1]{0,1:T(1,128)}, u32[]{:S(2)}) copy-start(s32[128,1]{0,1:T(1,128)} %constant.121) | copy-start | bytes 1540
  19.2 32.1 %copy-start.2 = (s32[128,1]{0,1:T(1,128)S(1)}, s32[128,1]{0,1:T(1,128)}, u32[]{:S(2)}) copy-start(s32[128,1]{0,1:T(1,128)} %constant.122) | copy-start | bytes 1540
  19.2 32.0 %copy-start.3 = (s32[128,1]{0,1:T(1,128)S(1)}, s32[128,1]{0,1:T(1,128)}, u32[]{:S(2)}) copy-start(s32[128,1]{0,1:T(1,128)} %constant.123) | copy-start | bytes 1540
  19.2 32.0 %copy-start.4 = (s32[128,1]{0,1:T(1,128)S(1)}, s32[128,1]{0,1:T(1,128)}, u32[]{:S(2)}) copy-start(s32[128,1]{0,1:T(1,128)} %constant.124) | copy-start | bytes 1540
  19.2 60.9 %all-to-all-start.1 = ((bf16[128,16,512]{2,1,0:T(8,128)(2,1)}), bf16[128,16,512]{2,1,0:T(8,128)(2,1)S(1)}, u32[]{:S(2)}, u32[]{:S(2)}) async-start(bf16[128,16,512]{2,1,0:T(8,128)(2,1)} %shard_map.84), calls=%async_computation.1 | async-start | bytes 4194304 | tf_op jit(solution)/shard_map/all_to_all | solution.py:652
  28.8 7.1 %collective-permute-start = (bf16[32,1024]{1,0:T(8,128)(2,1)S(1)}, bf16[32,1024]{1,0:T(8,128)(2,1)S(1)}, u32[]{:S(2)}, u32[]{:S(2)}) collective-permute-start(bf16[32,1024]{1,0:T(8,128)(2,1)S(1)} %reshape.94), channel_id=1, source_target_pairs={{0,16},{2,18},{4,20},{6,22},{8,24},{10,26},{12,28},{14,30},{16,0},... | collective-permute-start | bytes 196616 | tf_op jit(solution)/shard_map/ppermute | solution.py:579
  35.8 7.3 %collective-permute-start.1 = (bf16[64,1024]{1,0:T(8,128)(2,1)S(1)}, bf16[64,1024]{1,0:T(8,128)(2,1)S(1)}, u32[]{:S(2)}, u32[]{:S(2)}) collective-permute-start(bf16[64,1024]{1,0:T(8,128)(2,1)S(1)} %get-tuple-element.72), channel_id=1, source_target_pairs={{0,4},{2,6},{4,8},{6,10},{8,12},{10,14},{12,0},{14,2},{16,20},{18,... | collective-permute-start | bytes 393224 | tf_op jit(solution)/shard_map/ppermute | solution.py:579
  36.5 7.3 %collective-permute-start.2 = (bf16[64,1024]{1,0:T(8,128)(2,1)S(1)}, bf16[64,1024]{1,0:T(8,128)(2,1)S(1)}, u32[]{:S(2)}, u32[]{:S(2)}) collective-permute-start(bf16[64,1024]{1,0:T(8,128)(2,1)S(1)} %get-tuple-element.72), channel_id=1, source_target_pairs={{0,12},{2,14},{4,0},{6,2},{8,4},{10,6},{12,8},{14,10},{16,28},{18,... | collective-permute-start | bytes 393224 | tf_op jit(solution)/shard_map/ppermute | solution.py:579
  38.6 10.5 %collective-permute-start.3 = (bf16[64,1024]{1,0:T(8,128)(2,1)S(1)}, bf16[64,1024]{1,0:T(8,128)(2,1)S(1)}, u32[]{:S(2)}, u32[]{:S(2)}) collective-permute-start(bf16[64,1024]{1,0:T(8,128)(2,1)S(1)} %get-tuple-element.72), channel_id=1, source_target_pairs={{0,8},{2,10},{4,12},{6,14},{8,0},{10,2},{12,4},{14,6},{16,24},{18,... | collective-permute-start | bytes 393224 | tf_op jit(solution)/shard_map/ppermute | solution.py:579
  49.1 1.0 copy-start
  50.1 5.6 %collective-permute-start.4 = (bf16[256,1024]{1,0:T(8,128)(2,1)S(1)}, bf16[256,1024]{1,0:T(8,128)(2,1)S(1)}, u32[]{:S(2)}, u32[]{:S(2)}) collective-permute-start(bf16[256,1024]{1,0:T(8,128)(2,1)S(1)} %get-tuple-element.61), channel_id=1, source_target_pairs={{0,2},{2,0},{4,6},{6,4},{8,10},{10,8},{12,14},{14,12},{16,18},{18,... | collective-permute-start | bytes 1572872 | tf_op jit(solution)/shard_map/ppermute | solution.py:579
  67.4 6.7 %collective-permute-start.5 = (f32[128,8]{1,0:T(8,128)S(1)}, f32[128,8]{1,0:T(8,128)S(1)}, u32[]{:S(2)}, u32[]{:S(2)}) collective-permute-start(f32[128,8]{1,0:T(8,128)S(1)} %copy.27), channel_id=1, source_target_pairs={{0,1},{1,0},{2,3},{3,2},{4,5},{5,4},{6,7},{7,6},{8,9},{9,8},{10,11... | collective-permute-start | bytes 12296 | tf_op jit(solution)/shard_map/ppermute | solution.py:583
  83.8 18.5 %all-to-all-start.2 = ((f32[128,1,128]{2,1,0:T(1,128)}), f32[128,1,128]{2,1,0:T(1,128)S(1)}, u32[]{:S(2)}, u32[]{:S(2)}) async-start(f32[128,1,128]{2,1,0:T(1,128)} %get-tuple-element.36), calls=%async_computation.2 | async-start | bytes 131072 | tf_op jit(solution)/shard_map/all_to_all | solution.py:660
  91.9 12.9 %collective-permute-start.6 = (f32[128,8]{1,0:T(8,128)S(1)}, f32[128,8]{1,0:T(8,128)S(1)}, u32[]{:S(2)}, u32[]{:S(2)}) collective-permute-start(f32[128,8]{1,0:T(8,128)S(1)} %slice.81), channel_id=1, source_target_pairs={{0,1},{1,0},{2,3},{3,2},{4,5},{5,4},{6,7},{7,6},{8,9},{9,8},{10,11... | collective-permute-start | bytes 12296 | tf_op jit(solution)/shard_map/ppermute | solution.py:583
  102.6 7.5 %collective-permute-start.7 = (f32[128,8]{1,0:T(8,128)S(1)}, f32[128,8]{1,0:T(8,128)S(1)}, u32[]{:S(2)}, u32[]{:S(2)}) collective-permute-start(f32[128,8]{1,0:T(8,128)S(1)} %bitcast.86), channel_id=1, source_target_pairs={{0,1},{1,0},{2,3},{3,2},{4,5},{5,4},{6,7},{7,6},{8,9},{9,8},{10,11... | collective-permute-start | bytes 12296 | tf_op jit(solution)/shard_map/ppermute | solution.py:583
  110.1 63.3 %all-to-all-start.3 = ((bf16[128,16,512]{2,1,0:T(8,128)(2,1)}), bf16[128,16,512]{2,1,0:T(8,128)(2,1)S(1)}, u32[]{:S(2)}, u32[]{:S(2)}) async-start(bf16[128,16,512]{2,1,0:T(8,128)(2,1)} %shard_map.88), calls=%async_computation.3 | async-start | bytes 4194304 | tf_op jit(solution)/shard_map/all_to_all | solution.py:666
  124.3 2.7 %collective-permute-start.8 = (bf16[256,1024]{1,0:T(8,128)(2,1)}, bf16[256,1024]{1,0:T(8,128)(2,1)S(1)}, u32[]{:S(2)}, u32[]{:S(2)}) collective-permute-start(bf16[256,1024]{1,0:T(8,128)(2,1)} %get-tuple-element.42), channel_id=1, source_target_pairs={{0,2},{2,0},{4,6},{6,4},{8,10},{10,8},{12,14},{14,12},{16,18},{18,... | collective-permute-start | bytes 1572872 | tf_op jit(solution)/shard_map/ppermute | solution.py:579
  128.5 12.2 %collective-permute-start.10 = (bf16[64,1024]{1,0:T(8,128)(2,1)S(1)}, bf16[64,1024]{1,0:T(8,128)(2,1)S(1)}, u32[]{:S(2)}, u32[]{:S(2)}) collective-permute-start(bf16[64,1024]{1,0:T(8,128)(2,1)S(1)} %get-tuple-element.60), channel_id=1, source_target_pairs={{0,4},{2,6},{4,8},{6,10},{8,12},{10,14},{12,0},{14,2},{16,20},{18,... | collective-permute-start | bytes 393224 | tf_op jit(solution)/shard_map/ppermute | solution.py:579
  129.3 11.4 %collective-permute-start.11 = (bf16[64,1024]{1,0:T(8,128)(2,1)S(1)}, bf16[64,1024]{1,0:T(8,128)(2,1)S(1)}, u32[]{:S(2)}, u32[]{:S(2)}) collective-permute-start(bf16[64,1024]{1,0:T(8,128)(2,1)S(1)} %get-tuple-element.59), channel_id=1, source_target_pairs={{0,8},{2,10},{4,12},{6,14},{8,0},{10,2},{12,4},{14,6},{16,24},{18,... | collective-permute-start | bytes 393224 | tf_op jit(solution)/shard_map/ppermute | solution.py:579
  131.8 10.9 %collective-permute-start.9 = (bf16[64,1024]{1,0:T(8,128)(2,1)S(1)}, bf16[64,1024]{1,0:T(8,128)(2,1)S(1)}, u32[]{:S(2)}, u32[]{:S(2)}) collective-permute-start(bf16[64,1024]{1,0:T(8,128)(2,1)S(1)} %get-tuple-element.58), channel_id=1, source_target_pairs={{0,12},{2,14},{4,0},{6,2},{8,4},{10,6},{12,8},{14,10},{16,28},{18,... | collective-permute-start | bytes 393224 | tf_op jit(solution)/shard_map/ppermute | solution.py:579
  142.7 4.1 %collective-permute-start.12 = (bf16[32,1024]{1,0:T(8,128)(2,1)S(1)}, bf16[32,1024]{1,0:T(8,128)(2,1)S(1)}, u32[]{:S(2)}, u32[]{:S(2)}) collective-permute-start(bf16[32,1024]{1,0:T(8,128)(2,1)S(1)} %slice.125), channel_id=1, source_target_pairs={{0,16},{2,18},{4,20},{6,22},{8,24},{10,26},{12,28},{14,30},{16,0},... | collective-permute-start | bytes 196616 | tf_op jit(solution)/shard_map/ppermute | solution.py:579
  146.8 18.7 %collective-permute-start.13 = (bf16[8,1024]{1,0:T(8,128)(2,1)S(1)}, bf16[8,1024]{1,0:T(8,128)(2,1)S(1)}, u32[]{:S(2)}, u32[]{:S(2)}) collective-permute-start(bf16[8,1024]{1,0:T(8,128)(2,1)S(1)} %get-tuple-element.67), channel_id=1, source_target_pairs={{0,64},{2,66},{4,68},{6,70},{8,72},{10,74},{12,76},{14,78},{16,80}... | collective-permute-start | bytes 49160 | tf_op jit(solution)/shard_map/ppermute | solution.py:579
  150.1 18.7 %collective-permute-start.14 = (bf16[8,1024]{1,0:T(8,128)(2,1)S(1)}, bf16[8,1024]{1,0:T(8,128)(2,1)S(1)}, u32[]{:S(2)}, u32[]{:S(2)}) collective-permute-start(bf16[8,1024]{1,0:T(8,128)(2,1)S(1)} %get-tuple-element.69), channel_id=1, source_target_pairs={{0,128},{2,130},{4,132},{6,134},{8,136},{10,138},{12,140},{14,142}... | collective-permute-start | bytes 49160 | tf_op jit(solution)/shard_map/ppermute | solution.py:579
  152.8 16.0 %collective-permute-start.15 = (bf16[8,1024]{1,0:T(8,128)(2,1)S(1)}, bf16[8,1024]{1,0:T(8,128)(2,1)S(1)}, u32[]{:S(2)}, u32[]{:S(2)}) collective-permute-start(bf16[8,1024]{1,0:T(8,128)(2,1)S(1)} %get-tuple-element.68), channel_id=1, source_target_pairs={{0,192},{2,194},{4,196},{6,198},{8,200},{10,202},{12,204},{14,206}... | collective-permute-start | bytes 49160 | tf_op jit(solution)/shard_map/ppermute | solution.py:579
  168.8 3.8 %collective-permute-start.16 = (bf16[4,1024]{1,0:T(4,128)(2,1)S(1)}, bf16[4,1024]{1,0:T(4,128)(2,1)S(1)}, u32[]{:S(2)}, u32[]{:S(2)}) collective-permute-start(bf16[4,1024]{1,0:T(4,128)(2,1)S(1)} %slice.126), channel_id=1, source_target_pairs={{0,32},{2,34},{4,36},{6,38},{8,40},{10,42},{12,44},{14,46},{16,48}... | collective-permute-start | bytes 24584 | tf_op jit(solution)/shard_map/ppermute | solution.py:579

commit v6 on v5

--- a/solution.py
+++ b/solution.py
@@ -14,7 +14,7 @@
 OFFS = 4
 WIDTH = HEADS * HD
 PARTS = (8, 2, 4, 2)
-VMEM3, VMEM4, VMEM6 = 32, 32, 32
+VMEM3, VMEM4, VMEM5, VMEM6 = 32, 32, 48, 32
 
 epsilon = 1e-06
 scale = HD ** (-0.5)
@@ -197,11 +197,9 @@
 
 def fixed_forward_kernel(rows_ref, summ_ref, seen_ref, attn_ref, own_ref, far_ref, sums_ref):
     own, far = fixed_probabilities(rows_ref[0], rows_ref[1], summ_ref[:, :HD], seen_ref[...])
-    own_ref[0] = own
-    far_ref[0] = far
-    attn = (
-        dot(own.astype(BF16), rows_ref[2]) + dot(far.astype(BF16), summ_ref[:, HD:])
-    ).astype(BF16)
+    own_ref[0] = own.astype(BF16)
+    far_ref[0] = far.astype(BF16)
+    attn = (dot(own_ref[0], rows_ref[2]) + dot(far_ref[0], summ_ref[:, HD:])).astype(BF16)
     attn_ref[...] = attn
     wide = attn.astype(F32)
     square = jnp.sum(wide * wide, axis=-1, keepdims=True)
@@ -235,8 +233,8 @@
         ],
         [
             jax.ShapeDtypeStruct((BLOCK, WIDTH), BF16),
-            jax.ShapeDtypeStruct((HEADS, BLOCK, BLOCK), F32),
-            jax.ShapeDtypeStruct((HEADS, BLOCK, BLOCK), F32),
+            pltpu.HBM((HEADS, BLOCK, BLOCK), BF16),
+            pltpu.HBM((HEADS, BLOCK, BLOCK), BF16),
             jax.ShapeDtypeStruct((BLOCK, 8), F32),
         ],
         4 * 10**9,
@@ -266,14 +264,14 @@
         scores = batch_dot(keys_ref[head, 0], keys_ref[head, 1], 2, 2) * scale
         scores = jnp.where((col <= row)[None], scores, -jnp.inf)
         expo = jnp.exp(scores - jnp.max(scores, axis=-1, keepdims=True))
-        prob = expo * (1.0 / jnp.sum(expo, axis=-1, keepdims=True))
-        attn = batch_dot(prob.astype(BF16), keys_ref[head, 2], 2, 1).astype(BF16)
+        prob = (expo * (1.0 / jnp.sum(expo, axis=-1, keepdims=True))).astype(BF16)
+        attn = batch_dot(prob, keys_ref[head, 2], 2, 1).astype(BF16)
         prob_ref[head] = prob
+        copies += copy_all([(prob_ref.at[head], prob_out.at[head])], sem.at[head + 1])
         wide = attn.astype(F32)
         square += wide * wide
         cross += wide * grp_ref[head, 0].astype(F32)
         grp_ref[head, 1] = attn
-        copies += copy_all([(prob_ref.at[head], prob_out.at[head])], sem.at[head + 1])
     square = jnp.sum(square, axis=-1, keepdims=True)
     cross = jnp.sum(cross, axis=-1, keepdims=True)
     lane = lax.broadcasted_iota(jnp.int32, (NB, HD), 1)
@@ -300,7 +298,7 @@
         ],
         [
             pltpu.HBM((HEADS, 3, OFFS, NB, HD), BF16),
-            pltpu.HBM((HEADS, OFFS, NB, NB), F32),
+            pltpu.HBM((HEADS, OFFS, NB, NB), BF16),
             jax.ShapeDtypeStruct((HEADS, 2, OFFS, NB, HD), BF16),
             jax.ShapeDtypeStruct((NB, HD), F32),
             jax.ShapeDtypeStruct((NB, 1, HD), F32),
@@ -309,7 +307,7 @@
         6 * 2**20,
         [
             pltpu.VMEM((HEADS, 3, OFFS, NB, HD), BF16),
-            pltpu.VMEM((HEADS, OFFS, NB, NB), F32),
+            pltpu.VMEM((HEADS, OFFS, NB, NB), BF16),
             pltpu.SemaphoreType.DMA((HEADS + 1, 1)),
         ],
         vmem=VMEM3,
@@ -352,10 +350,10 @@
         grad, row_dot = grads[head]
         prob = prob_ref[head]
         grad_prob = batch_dot(grad, keys_ref[head, 2], 2, 2)
-        grad_score = (prob * (grad_prob - row_dot) * scale).astype(BF16)
+        grad_score = (prob.astype(F32) * (grad_prob - row_dot) * scale).astype(BF16)
         out_ref[head, 1] = batch_dot(grad_score, keys_ref[head, 1], 2, 1).astype(BF16)
         out_ref[head, 2] = batch_dot(grad_score, keys_ref[head, 0], 1, 1).astype(BF16)
-        out_ref[head, 3] = batch_dot(prob.astype(BF16), grad, 1, 1).astype(BF16)
+        out_ref[head, 3] = batch_dot(prob, grad, 1, 1).astype(BF16)
     swap = swap_matrix()
     copies = []
     for at in range(0, NB, 16):
@@ -386,7 +384,7 @@
         6 * 2**20,
         [
             pltpu.VMEM((HEADS, 3, OFFS, NB, HD), BF16),
-            pltpu.VMEM((HEADS, OFFS, NB, NB), F32),
+            pltpu.VMEM((HEADS, OFFS, NB, NB), BF16),
             pltpu.VMEM((HEADS, 4, OFFS, NB, HD), BF16),
             pltpu.VMEM((NB, 16, WIDTH), BF16),
             pltpu.SemaphoreType.DMA((HEADS, 2)),
@@ -397,46 +395,68 @@
 
 
 def summary_backward_kernel(
-    rows_ref, summ_ref, far_ref, attn_ref, sums_ref, query_ref, keep_ref, send_ref
+    rows_in, summ_in, far_in, attn_in, sums_ref, query_ref, keep_ref, send_ref,
+    attn_ref, cot_ref, summ_ref, rows_ref, far_ref, sem,
 ):
-    wide = attn_ref[...].astype(F32)
-    _, grad, row_dot = normalize(wide, rows_ref[3], sums_ref[:, 0:1], sums_ref[:, 1:2])
-    far = far_ref[0]
-    score = (far * (dot_nt(grad, summ_ref[:, HD:]) - row_dot) * scale).astype(BF16)
-    query_ref[...] = dot(score, summ_ref[:, :HD])
-    key = dot_rows(score, rows_ref[0])
-    value = dot_rows(far.astype(BF16), grad)
-    half = BLOCK // 2
-    send_ref[:, :HD] = key[half:].astype(BF16)
-    send_ref[:, HD:] = value[half:].astype(BF16)
-    keep_ref[:, :HD] = key[:half]
-    keep_ref[:, HD:] = value[:half]
+    copies = copy_all(
+        [
+            (attn_in, attn_ref),
+            (rows_in.at[3], cot_ref),
+            (summ_in, summ_ref),
+            (rows_in.at[0], rows_ref),
+        ]
+        + [(far_in.at[head], far_ref.at[head]) for head in range(HEADS)],
+        sem,
+    )
+    for copy in copies[:4]:
+        copy.wait()
+    for head in range(HEADS):
+        copies[4 + head].wait()
+        at = slice(head * HD, (head + 1) * HD)
+        to_key = slice(2 * head * HD, (2 * head + 1) * HD)
+        to_value = slice((2 * head + 1) * HD, (2 * head + 2) * HD)
+        _, grad, row_dot = normalize(
+            attn_ref[:, at].astype(F32), cot_ref[:, at], sums_ref[:, 0:1], sums_ref[:, 1:2]
+        )
+        far = far_ref[head]
+        score = far.astype(F32) * (dot_nt(grad, summ_ref[:, to_value]) - row_dot) * scale
+        score = score.astype(BF16)
+        query_ref[:, at] = dot(score, summ_ref[:, to_key])
+        for to, grads in ((to_key, dot_rows(score, rows_ref[:, at])), (to_value, dot_rows(far, grad))):
+            grads = grads.reshape(2, 8, 2, 16, HD)
+            keep = jnp.stack([grads[0, :, 0], grads[1, :, 1]], 1)
+            send = jnp.stack([grads[1, :, 0], grads[0, :, 1]], 1)
+            keep_ref[:, to] = keep.reshape(BLOCK // 2, HD)
+            send_ref[:, to] = send.reshape(BLOCK // 2, HD).astype(BF16)
 
 
 def summary_backward(rows, summ, far, attn, sums):
     return call(
         summary_backward_kernel,
-        HEADS,
-        [
-            spec((4, BLOCK, HD), 0, 0, "i"),
-            spec((BLOCK, 2 * HD), 0, "i"),
-            spec((1, BLOCK, BLOCK), "i", 0, 0),
-            spec((BLOCK, HD), 0, "i"),
-            spec((BLOCK, 2), 0, 0),
-        ],
-        [
-            spec((BLOCK, HD), 0, "i"),
-            spec((BLOCK // 2, 2 * HD), 0, "i"),
-            spec((BLOCK // 2, 2 * HD), 0, "i"),
-        ],
-        [
-            jax.ShapeDtypeStruct((BLOCK, WIDTH), F32),
+        1,
+        [IN_HBM] * 4 + [spec((BLOCK, 2), 0, 0)],
+        [
+            spec((BLOCK, WIDTH), 0, 0),
+            spec((BLOCK // 2, 2 * WIDTH), 0, 0),
+            spec((BLOCK // 2, 2 * WIDTH), 0, 0),
+        ],
+        [
+            pltpu.HBM((BLOCK, WIDTH), F32),
             jax.ShapeDtypeStruct((BLOCK // 2, 2 * WIDTH), F32),
             jax.ShapeDtypeStruct((BLOCK // 2, 2 * WIDTH), BF16),
         ],
         3 * 10**9,
         8 * 2**20,
-    )(rows, summ, far, attn, sums)
+        [
+            pltpu.VMEM((BLOCK, WIDTH), BF16),
+            pltpu.VMEM((BLOCK, WIDTH), BF16),
+            pltpu.VMEM((BLOCK, 2 * WIDTH), BF16),
+            pltpu.VMEM((BLOCK, WIDTH), BF16),
+            pltpu.VMEM((HEADS, BLOCK, BLOCK), BF16),
+            pltpu.SemaphoreType.DMA((8,)),
+        ],
+        vmem=VMEM5,
+    )(*[in_hbm(array) for array in (rows, summ, far, attn)], sums)
 
 
 def fixed_backward_kernel(rows_ref, own_ref, attn_ref, sums_ref, query_ref, out_ref, tail_ref):
@@ -445,9 +465,9 @@
     wide = attn_ref[...].astype(F32)
     normed, grad, row_dot = normalize(wide, rows_ref[3], sums_ref[:, 0:1], sums_ref[:, 1:2])
     out_ref[0] = normed
-    score = (own * (dot_nt(grad, value) - row_dot) * scale).astype(BF16)
+    score = (own.astype(F32) * (dot_nt(grad, value) - row_dot) * scale).astype(BF16)
     out_ref[1] = (dot(score, key) + query_ref[...]).astype(BF16)
-    for at, grads in enumerate((dot_rows(score, query), dot_rows(own.astype(BF16), grad))):
+    for at, grads in enumerate((dot_rows(score, query), dot_rows(own, grad))):
         out_ref[2 + at] = grads.astype(BF16)
         tail_ref[at] = grads[BLOCK - 8 :]
 
@@ -583,62 +603,66 @@
     return lax.ppermute(array, "head", [(0, 1), (1, 0)])
 
 
-ROUNDS = (
-    ((0, -1, 1),),
-    ((0, -2, 2), (0, -4, 2), (0, 2, 2)),
-    ((1, 1, 8),),
-    ((2, 1, 16), (2, -1, 16), (2, 2, 16)),
-    ((3, 1, 64),),
-)
+Z, X, Y, CORE = range(4)
+Y_BACK = (0, 1, -1, 2)
+SLAB = 2 * WIDTH
 
 
 def gather_along_z(own, me):
-    size = PARTS[0]
+    size = PARTS[Z]
     step = NB // size
     groups = [[at + step * z for z in range(size)] for at in range(step)]
     sent = jnp.broadcast_to(own[None], (size,) + own.shape)
     held = lax.all_to_all(sent, "seq", 0, 0, axis_index_groups=groups, tiled=True)
     held = jnp.concatenate([held, held], 0)
-    held = lax.dynamic_slice_in_dim(held, me // step, size, 0)
-    return held.reshape(size * SUMM, 2 * WIDTH)
+    first = (me // step + 4 * (me % 2)) % size
+    return lax.dynamic_slice_in_dim(held, first, size, 0).reshape(size * SUMM, SLAB)
 
 
 def gather_summaries(held):
-    for steps in ROUNDS[2:]:
-        moved = [shift(held[: slots * SUMM], part, step) for part, step, slots in steps]
-        held = jnp.concatenate([held] + moved, 0)
-    return held
-
-
-def scatter_first(total, sent):
-    ((part, step, _),) = ROUNDS[-1]
-    return total + shift(sent, part, -step).astype(F32)
-
-
-def scatter_summaries(parts, rounds):
-    for steps in rounds[::-1]:
-        kept = parts.shape[0] - SUMM * sum(slots for _, _, slots in steps)
-        total, at = parts[:kept], kept
-        for part, step, slots in steps:
-            rows = slots * SUMM
-            moved = shift(parts[at : at + rows].astype(BF16), part, -step).astype(F32)
-            total = total + jnp.pad(moved, ((0, kept - rows), (0, 0)))
-            at += rows
-        parts = total
-    return parts
+    held = jnp.concatenate([held, shift(held, X, 1)], 0)
+    held = jnp.concatenate([held] + [shift(held, Y, back) for back in Y_BACK[1:]], 0)
+    return jnp.concatenate([held, shift(held, CORE, 1)], 0)
+
+
+def add_up(own, moved):
+    return sum((part.astype(F32) for part in moved), own)
+
+
+def scatter_along_core(kept, sent):
+    return add_up(kept, [shift(sent, CORE, 1)])
+
+
+def scatter_along_y(parts):
+    parts = parts.reshape(4, -1, SLAB)
+    sent = parts.astype(BF16)
+    return add_up(parts[0], [shift(sent[n], Y, -Y_BACK[n]) for n in range(1, 4)])
+
+
+def scatter_summaries(parts):
+    parts = parts.reshape(2, -1, SLAB)
+    parts = add_up(parts[0], [shift(parts[1].astype(BF16), X, -1)])
+    sent = parts.astype(BF16).reshape(2, 4, SUMM, SLAB)
+    moved = []
+    for n in range(4):
+        perm = []
+        for source in range(NB):
+            coords = place(source)
+            coords[Z] = (coords[Z] + 4 * coords[CORE] + n) % PARTS[Z]
+            perm.append((source, joined(coords)))
+        moved.append(lax.ppermute(sent[:, n].reshape(2 * SUMM, SLAB), "seq", perm))
+    parts = add_up(0.0, moved)
+    return add_up(parts[:SUMM], [shift(parts[SUMM:].astype(BF16), CORE, 1)])
 
 
 def slot_blocks(me):
-    back = [(0,) * len(PARTS)]
-    for steps in ROUNDS:
-        back = back + [
-            tuple(by + step * (at == part) for at, by in enumerate(slot))
-            for part, step, slots in steps
-            for slot in back[:slots]
-        ]
-    back = jnp.array(back, jnp.int32)
-    coords = [(at - back[:, n]) % size for n, (at, size) in enumerate(zip(place(me), PARTS))]
-    return joined(coords)
+    slots = jnp.arange(NB, dtype=jnp.int32)
+    z, x, y, core = place(me)
+    core_of = (core - (slots >> 6)) % 2
+    y_of = (y - jnp.array(Y_BACK, jnp.int32)[(slots >> 4) & 3]) % PARTS[Y]
+    x_of = (x - ((slots >> 3) & 1)) % PARTS[X]
+    z_of = (z + 4 * core_of + (slots & 7)) % PARTS[Z]
+    return joined((z_of, x_of, y_of, core_of))
 
 
 def shards(queries, key_rows, value_rows, cotangent):
@@ -667,9 +691,9 @@
     block_sums = block_sums.reshape(NB, 2, OFFS).transpose(0, 2, 1).reshape(BLOCK, 2)
     far_query, kept, sent = summary_backward(rows, summ, far_prob, fixed_attn, block_sums)
     fixed_out, tails = fixed_backward(rows, own_prob, fixed_attn, block_sums, far_query)
-    parts = scatter_summaries(scatter_first(kept, sent), ROUNDS[3:4])
+    parts = scatter_along_y(scatter_along_core(kept, sent))
     parts, fixed_out, tails = lax.optimization_barrier((parts, fixed_out, tails))
-    totals = scatter_summaries(parts, ROUNDS[:3]).reshape(SUMM, HEADS, 2, HD)
+    totals = scatter_summaries(parts).reshape(SUMM, HEADS, 2, HD)
     totals = totals.transpose(2, 0, 1, 3).reshape(2, SUMM, WIDTH)
     totals = (tails[:, 8 - SUMM :] + totals).astype(BF16)
     tail = jnp.pad(totals, ((0, 0), (16 - SUMM, 0), (0, 0)))

time: 180 us -> 175 us (0.972)
  waiting for transfers between devices: 59.8 us -> 53.9 us
  starting transfers between devices: 62.3 us -> 67.4 us
    ppermute x14 -> x11, waiting for transfers between devices: 37.7 us -> 21.4 us  [shift(): return lax.ppermute(array, 'seq', perm)]
    ppermute x0 -> x4, starting transfers between devices: none -> 12.8 us  [scatter_summaries(): moved.append(lax.ppermute(sent[:, n].reshape(2 * SUMM, SLAB), 'seq', perm))]
    ppermute x0 -> x4, waiting for transfers between devices: none -> 10.5 us  [scatter_summaries(): moved.append(lax.ppermute(sent[:, n].reshape(2 * SUMM, SLAB), 'seq', perm))]
    ppermute x14 -> x11, starting transfers between devices: 22.6 us -> 14.8 us  [shift(): return lax.ppermute(array, 'seq', perm)]
  transfers between devices with their start and end apart: 21 -> 22, of which waited for: 15 -> 14; matrix products, arithmetic and copies ran while one was open for 4% -> 3% of each run, Pallas kernels for 21% -> 20%
where the time goes in v6:
time: 175 us
  starting transfers between devices  67.4 us (39%)
  waiting for transfers between devices  53.9 us (31%)
  Pallas kernels  44.1 us (25%)
  local copies, waits for them, and re-layouts  6.75 us (4%)
    ppermute x11, waiting for transfers between devices, shift(): return lax.ppermute(array, 'seq', perm)  21.4 us
    ppermute x11, starting transfers between devices, shift(): return lax.ppermute(array, 'seq', perm)  14.8 us
    ppermute x4, starting transfers between devices, scatter_summaries(): moved.append(lax.ppermute(sent[:, n].reshape(2 * SUMM, SLAB), 'seq', perm))  12.8 us
    ppermute x4, waiting for transfers between devices, scatter_summaries(): moved.append(lax.ppermute(sent[:, n].reshape(2 * SUMM, SLAB), 'seq', perm))  10.5 us
    all_to_all x1, starting transfers between devices, shards(): recv = lax.all_to_all(send, 'seq', 0, 0, tiled=True)  9.33 us
    pallas_call x1, Pallas kernels, fixed_forward(): call(fixed_forward_kernel, HEADS, [spec((4, BLOCK, HD), 0, 0, 'i'), spec(...  9.18 us
    all_to_all x1, starting transfers between devices, gather_along_z(): lax.all_to_all(sent, 'seq', 0, 0, axis_index_groups=groups, tiled=True)  9.01 us
    ppermute x3, starting transfers between devices, other_head(): return lax.ppermute(array, 'head', [(0, 1), (1, 0)])  8.27 us
  transfers between devices with their start and end apart: 22, of which 14 were waited for; matrix products, arithmetic and copies ran while one was open for 3% of the time, Pallas kernels for 20%

profile of v6, /device:TPU:1, one launch (start us, length us, event | category | flops | bytes accessed | tf_op | source)
XLA Modules:
  0.0 174.5 jit_solution(8722535628675175917)
XLA Ops:
  0.6 0.7 slice_reduce_fusion.1
  1.4 0.7 slice_reduce_fusion
  2.2 0.6 broadcast_in_dim.12
  2.8 9.0 %all-to-all-start = ((bf16[8,4,1024]{2,1,0:T(4,128)(2,1)}), bf16[8,4,1024]{2,1,0:T(4,128)(2,1)S(1)}, u32[]{:S(2)}, u32[]{:S(2)}) async-start(bf16[8,4,1024]{2,1,0:T(4,128)(2,1)} %broadcast_in_dim.12), calls=%async_computation | async-start | bytes 131072 | tf_op jit(solution)/shard_map/all_to_all | solution.py:616
  11.8 3.5 %shard_map.84 = bf16[128,16,512]{2,1,0:T(8,128)(2,1)} custom-call(bf16[4096,128]{1,0:T(8,128)(2,1)} %bitcast.63, bf16[4096,128]{1,0:T(8,128)(2,1)} %bitcast.59, bf16[4096,128]{1,0:T(8,128)(2,1)} %bitcast.61, bf16[4096,128]{1,0:T(8,128)(2,1)} %bitcast.65), custom_call_target="tpu_custom_call" | custom-call | flops 1000000000 | bytes 6291456 | tf_op jit(solution)/shard_map/pallas_call | solution.py:142
  15.3 3.8 %all-to-all-done = bf16[8,4,1024]{2,1,0:T(4,128)(2,1)S(1)} async-done(((bf16[8,4,1024]{2,1,0:T(4,128)(2,1)}), bf16[8,4,1024]{2,1,0:T(4,128)(2,1)S(1)}, u32[]{:S(2)}, u32[]{:S(2)}) %all-to-all-start) | async-done | bytes 65568 | tf_op jit(solution)/shard_map/all_to_all | solution.py:616
  19.1 0.1 fusion.2
  19.2 9.3 %all-to-all-start.1 = ((bf16[128,16,512]{2,1,0:T(8,128)(2,1)}), bf16[128,16,512]{2,1,0:T(8,128)(2,1)S(1)}, u32[]{:S(2)}, u32[]{:S(2)}) async-start(bf16[128,16,512]{2,1,0:T(8,128)(2,1)} %shard_map.84), calls=%async_computation.1 | async-start | bytes 4194304 | tf_op jit(solution)/shard_map/all_to_all | solution.py:676
  28.5 1.5 collective-permute-start
  30.0 5.6 %collective-permute-done = bf16[32,1024]{1,0:T(8,128)(2,1)S(1)} collective-permute-done((bf16[32,1024]{1,0:T(8,128)(2,1)S(1)}, bf16[32,1024]{1,0:T(8,128)(2,1)S(1)}, u32[]{:S(2)}, u32[]{:S(2)}) %collective-permute-start) | collective-permute-done | bytes 65568 | tf_op jit(solution)/shard_map/ppermute | solution.py:599
  35.6 0.6 collective-permute-start.1
  36.2 2.1 %collective-permute-start.2 = (bf16[64,1024]{1,0:T(8,128)(2,1)S(1)}, bf16[64,1024]{1,0:T(8,128)(2,1)S(1)}, u32[]{:S(2)}, u32[]{:S(2)}) collective-permute-start(bf16[64,1024]{1,0:T(8,128)(2,1)S(1)} %get-tuple-element.71), channel_id=1, source_target_pairs={{0,12},{2,14},{4,0},{6,2},{8,4},{10,6},{12,8},{14,10},{16,28},{18,... | collective-permute-start | bytes 393224 | tf_op jit(solution)/shard_map/ppermute | solution.py:599
  38.4 0.8 collective-permute-start.3
  39.2 3.7 %collective-permute-done.1 = bf16[64,1024]{1,0:T(8,128)(2,1)S(1)} collective-permute-done((bf16[64,1024]{1,0:T(8,128)(2,1)S(1)}, bf16[64,1024]{1,0:T(8,128)(2,1)S(1)}, u32[]{:S(2)}, u32[]{:S(2)}) %collective-permute-start.1) | collective-permute-done | bytes 131104 | tf_op jit(solution)/shard_map/ppermute | solution.py:599
  42.9 0.6 collective-permute-done.2
  43.5 5.3 %collective-permute-done.3 = bf16[64,1024]{1,0:T(8,128)(2,1)S(1)} collective-permute-done((bf16[64,1024]{1,0:T(8,128)(2,1)S(1)}, bf16[64,1024]{1,0:T(8,128)(2,1)S(1)}, u32[]{:S(2)}, u32[]{:S(2)}) %collective-permute-start.3) | collective-permute-done | bytes 131104 | tf_op jit(solution)/shard_map/ppermute | solution.py:599
  48.9 0.0 copy-start.1
  48.9 1.0 copy-done.1
  49.8 1.2 collective-permute-start.4
  51.1 0.1 broadcast_in_dim.13
  51.1 0.7 broadcast_in_dim_reshape.4.seen_ref
  51.8 3.6 %shard_map.85.rows_ref.rows_in = bf16[4,512,512]{2,1,0:T(8,128)(2,1)} custom-call(bf16[4096,128]{1,0:T(8,128)(2,1)} %bitcast.64, bf16[4096,128]{1,0:T(8,128)(2,1)} %bitcast.60, bf16[4096,128]{1,0:T(8,128)(2,1)} %bitcast.62, bf16[4096,128]{1,0:T(8,128)(2,1)} %bitcast.66), custom_call_target="tpu_custom_call" | custom-call | flops 1000000000 | bytes 6291456 | tf_op jit(solution)/shard_map/pallas_call | solution.py:173
  55.4 0.0 collective-permute-done.4
  55.4 0.8 constant_dynamic-update-slice_fusion.7.summ_ref.summ_in
  56.2 9.2 %shard_map.86 = (bf16[512,512]{1,0:T(8,128)(2,1)}, bf16[4,512,512]{2,1,0:T(8,128)(2,1)}, bf16[4,512,512]{2,1,0:T(8,128)(2,1)}, f32[512,8]{1,0:T(8,128)}) custom-call(bf16[4,512,512]{2,1,0:T(8,128)(2,1)} %shard_map.85.rows_ref.rows_in, bf16[512,1024]{1,0:T(8,128)(2,1)} %constant_dynamic-update-slice_fusion.7.summ_ref.summ_in, ...), custom_call_target="tpu_custom_call" | custom-call | flops 4000000000 | bytes 4194304 | tf_op jit(solution)/shard_map/pallas_call | solution.py:220
  65.4 1.0 copy.24
  66.5 0.1 copy.26
  66.6 2.5 %collective-permute-start.5 = (f32[128,8]{1,0:T(8,128)S(1)}, f32[128,8]{1,0:T(8,128)S(1)}, u32[]{:S(2)}, u32[]{:S(2)}) collective-permute-start(f32[128,8]{1,0:T(8,128)S(1)} %copy.26), channel_id=1, source_target_pairs={{0,1},{1,0},{2,3},{3,2},{4,5},{5,4},{6,7},{7,6},{8,9},{9,8},{10,11... | collective-permute-start | bytes 12296 | tf_op jit(solution)/shard_map/ppermute | solution.py:603
  69.1 3.7 %collective-permute-done.5 = f32[128,8]{1,0:T(8,128)S(1)} collective-permute-done((f32[128,8]{1,0:T(8,128)S(1)}, f32[128,8]{1,0:T(8,128)S(1)}, u32[]{:S(2)}, u32[]{:S(2)}) %collective-permute-start.5) | collective-permute-done | bytes 4128 | tf_op jit(solution)/shard_map/ppermute | solution.py:603
  72.9 7.0 %all-to-all-done.1.recv_ref = bf16[128,16,512]{2,1,0:T(8,128)(2,1)S(1)} async-done(((bf16[128,16,512]{2,1,0:T(8,128)(2,1)}), bf16[128,16,512]{2,1,0:T(8,128)(2,1)S(1)}, u32[]{:S(2)}, u32[]{:S(2)}) %all-to-all-start.1) | async-done | bytes 2097184 | tf_op jit(solution)/shard_map/all_to_all | solution.py:676
  79.9 3.7 %shard_map.87 = (bf16[4,3,4,128,128]{4,3,2,1,0:T(8,128)(2,1)}, bf16[4,4,128,128]{3,2,1,0:T(8,128)(2,1)}, bf16[4,2,4,128,128]{4,3,2,1,0:T(8,128)(2,1)S(1)}, f32[128,128]{1,0:T(8,128)S(1)}, f32[128,1,128]{2,1,0:T(1,128)}) custom-call(bf16[128,16,512]{2,1,0:T(8,128)(2,1)S(1)} %all-to-all-done.1.recv_ref, f32[128,128]{1,0:T(8,128)S(1)} %pad.8.fixed_ref), custom_call_target="tpu_custom_call" | custom-call | flops 1000000000 | bytes 6291456 | tf_op jit(solution)/shard_map/pallas_call | solution.py:288
  83.6 7.0 %all-to-all-start.2 = ((f32[128,1,128]{2,1,0:T(1,128)}), f32[128,1,128]{2,1,0:T(1,128)S(1)}, u32[]{:S(2)}, u32[]{:S(2)}) async-start(f32[128,1,128]{2,1,0:T(1,128)} %get-tuple-element.36), calls=%async_computation.2 | async-start | bytes 131072 | tf_op jit(solution)/shard_map/all_to_all | solution.py:684
  90.6 0.1 slice.65
  90.7 2.9 %collective-permute-start.6 = (f32[128,8]{1,0:T(8,128)S(1)}, f32[128,8]{1,0:T(8,128)S(1)}, u32[]{:S(2)}, u32[]{:S(2)}) collective-permute-start(f32[128,8]{1,0:T(8,128)S(1)} %slice.65), channel_id=1, source_target_pairs={{0,1},{1,0},{2,3},{3,2},{4,5},{5,4},{6,7},{7,6},{8,9},{9,8},{10,11... | collective-permute-start | bytes 12296 | tf_op jit(solution)/shard_map/ppermute | solution.py:603
  93.5 7.6 %all-to-all-done.2.recv_ref = f32[128,1,128]{2,1,0:T(1,128)S(1)} async-done(((f32[128,1,128]{2,1,0:T(1,128)}), f32[128,1,128]{2,1,0:T(1,128)S(1)}, u32[]{:S(2)}, u32[]{:S(2)}) %all-to-all-start.2) | async-done | bytes 65568 | tf_op jit(solution)/shard_map/all_to_all | solution.py:684
  101.1 0.2 slice.85
  101.3 2.9 %collective-permute-start.7 = (f32[128,8]{1,0:T(8,128)S(1)}, f32[128,8]{1,0:T(8,128)S(1)}, u32[]{:S(2)}, u32[]{:S(2)}) collective-permute-start(f32[128,8]{1,0:T(8,128)S(1)} %bitcast.68), channel_id=1, source_target_pairs={{0,1},{1,0},{2,3},{3,2},{4,5},{5,4},{6,7},{7,6},{8,9},{9,8},{10,11... | collective-permute-start | bytes 12296 | tf_op jit(solution)/shard_map/ppermute | solution.py:603
  104.2 5.2 %shard_map.88 = bf16[128,16,512]{2,1,0:T(8,128)(2,1)} custom-call(bf16[4,3,4,128,128]{4,3,2,1,0:T(8,128)(2,1)} %get-tuple-element.32.keys_in, bf16[4,4,128,128]{3,2,1,0:T(8,128)(2,1)} %get-tuple-element.33.prob_in, bf16[4,2,4,128,128]{4,3,2,1,0:T(8,128)(2,1)S(1)} %get-tuple-element.34.grp_ref, f32[128,128]{1,0:T(8,128)S(1)} %get-tuple-element.35.sums_ref, ...), custom_call_target="tpu_custom_call" | custom-call | flops 1000000000 | bytes 6291456 | tf_op jit(solution)/shard_map/pallas_call | solution.py:370
  109.4 0.0 collective-permute-done.7
  109.5 6.2 %all-to-all-start.3 = ((bf16[128,16,512]{2,1,0:T(8,128)(2,1)}), bf16[128,16,512]{2,1,0:T(8,128)(2,1)S(1)}, u32[]{:S(2)}, u32[]{:S(2)}) async-start(bf16[128,16,512]{2,1,0:T(8,128)(2,1)} %shard_map.88), calls=%async_computation.3 | async-start | bytes 4194304 | tf_op jit(solution)/shard_map/all_to_all | solution.py:690
  115.7 0.2 copy.28
  115.9 0.0 copy-start
  115.9 6.8 %shard_map.89 = (f32[512,512]{1,0:T(8,128)}, f32[256,1024]{1,0:T(8,128)S(1)}, bf16[256,1024]{1,0:T(8,128)(2,1)S(1)}) custom-call(bf16[4,512,512]{2,1,0:T(8,128)(2,1)} %shard_map.85.rows_ref.rows_in, bf16[512,1024]{1,0:T(8,128)(2,1)} %constant_dynamic-update-slice_fusion.7.summ_ref.summ_in, bf16[4,512,512]{2,1,0:T(8,128)(2,1)} %get-tuple-element.38.far_in, ...), custom_call_target="tpu_custom_call" | custom-call | flops 3000000000 | bytes 8388608 | tf_op jit(solution)/shard_map/pallas_call | solution.py:434
  122.7 1.1 collective-permute-start.8
  123.8 1.5 collective-permute-done.8
  125.3 0.2 fusion.12
  125.5 1.1 collective-permute-start.10
  126.6 2.4 %collective-permute-start.11 = (bf16[64,1024]{1,0:T(8,128)(2,1)S(1)}, bf16[64,1024]{1,0:T(8,128)(2,1)S(1)}, u32[]{:S(2)}, u32[]{:S(2)}) collective-permute-start(bf16[64,1024]{1,0:T(8,128)(2,1)S(1)} %get-tuple-element.57), channel_id=1, source_target_pairs={{0,8},{2,10},{4,12},{6,14},{8,0},{10,2},{12,4},{14,6},{16,24},{18,... | collective-permute-start | bytes 393224 | tf_op jit(solution)/shard_map/ppermute | solution.py:599
  129.0 1.2 collective-permute-start.9
  130.2 7.3 %shard_map.90 = (bf16[4,512,512]{2,1,0:T(8,128)(2,1)}, f32[2,8,512]{2,1,0:T(8,128)}) custom-call(bf16[4,512,512]{2,1,0:T(8,128)(2,1)} %shard_map.85.rows_ref.rows_in, bf16[4,512,512]{2,1,0:T(8,128)(2,1)} %get-tuple-element.43.own_ref, bf16[512,512]{1,0:T(8,128)(2,1)} %get-tuple-element.39.attn_in.attn_ref, f32[512,2]{1,0:T(8,128)} %bitcast.58, ...), custom_call_target="tpu_custom_call" | custom-call | flops 5000000000 | bytes 8388608 | tf_op jit(solution)/shard_map/pallas_call | solution.py:476
  137.4 0.9 collective-permute-done.11
  138.4 0.2 collective-permute-done.9
  138.6 0.1 fusion.1
  138.7 2.7 %collective-permute-start.12 = (bf16[32,1024]{1,0:T(8,128)(2,1)S(1)}, bf16[32,1024]{1,0:T(8,128)(2,1)S(1)}, u32[]{:S(2)}, u32[]{:S(2)}) collective-permute-start(bf16[32,1024]{1,0:T(8,128)(2,1)S(1)} %slice.109), channel_id=1, source_target_pairs={{0,16},{2,18},{4,20},{6,22},{8,24},{10,26},{12,28},{14,30},{16,0},... | collective-permute-start | bytes 196616 | tf_op jit(solution)/shard_map/ppermute | solution.py:599
  141.3 2.4 %collective-permute-done.12 = bf16[32,1024]{1,0:T(8,128)(2,1)S(1)} collective-permute-done((bf16[32,1024]{1,0:T(8,128)(2,1)S(1)}, bf16[32,1024]{1,0:T(8,128)(2,1)S(1)}, u32[]{:S(2)}, u32[]{:S(2)}) %collective-permute-start.12) | collective-permute-done | bytes 65568 | tf_op jit(solution)/shard_map/ppermute | solution.py:599
  143.8 7.4 %collective-permute-start.13 = (bf16[8,1024]{1,0:T(8,128)(2,1)S(1)}, bf16[8,1024]{1,0:T(8,128)(2,1)S(1)}, u32[]{:S(2)}, u32[]{:S(2)}) collective-permute-start(bf16[8,1024]{1,0:T(8,128)(2,1)S(1)} %reshape_squeeze.20), channel_id=1, source_target_pairs={{0,0},{2,130},{4,4},{6,134},{8,8},{10,138},{12,12},{14,142},{16,16... | collective-permute-start | bytes 49160 | tf_op jit(solution)/shard_map/ppermute | solution.py:653
  151.3 0.2 collective-permute-start.14
  151.5 3.3 %collective-permute-start.15 = (bf16[8,1024]{1,0:T(8,128)(2,1)S(1)}, bf16[8,1024]{1,0:T(8,128)(2,1)S(1)}, u32[]{:S(2)}, u32[]{:S(2)}) collective-permute-start(bf16[8,1024]{1,0:T(8,128)(2,1)S(1)} %reshape_squeeze.22), channel_id=1, source_target_pairs={{0,64},{2,194},{4,68},{6,198},{8,72},{10,202},{12,76},{14,206},{16... | collective-permute-start | bytes 49160 | tf_op jit(solution)/shard_map/ppermute | solution.py:653
  154.8 1.9 %collective-permute-start.16 = (bf16[8,1024]{1,0:T(8,128)(2,1)S(1)}, bf16[8,1024]{1,0:T(8,128)(2,1)S(1)}, u32[]{:S(2)}, u32[]{:S(2)}) collective-permute-start(bf16[8,1024]{1,0:T(8,128)(2,1)S(1)} %reshape_squeeze.23), channel_id=1, source_target_pairs={{0,96},{2,226},{4,100},{6,230},{8,104},{10,234},{12,108},{14,238},... | collective-permute-start | bytes 49160 | tf_op jit(solution)/shard_map/ppermute | solution.py:653
  156.7 10.5 %collective-permute-done.13 = bf16[8,1024]{1,0:T(8,128)(2,1)S(1)} collective-permute-done((bf16[8,1024]{1,0:T(8,128)(2,1)S(1)}, bf16[8,1024]{1,0:T(8,128)(2,1)S(1)}, u32[]{:S(2)}, u32[]{:S(2)}) %collective-permute-start.13) | collective-permute-done | bytes 16416 | tf_op jit(solution)/shard_map/ppermute | solution.py:653
  167.2 0.1 collective-permute-start.17
  167.3 1.2 collective-permute-done.17
  168.5 0.8 add_convert_fusion.1
  169.3 5.0 %shard_map.91 = (bf16[4096,128]{1,0:T(8,128)(2,1)}, bf16[4096,128]{1,0:T(8,128)(2,1)}, bf16[4096,128]{1,0:T(8,128)(2,1)}, bf16[4096,128]{1,0:T(8,128)(2,1)}) custom-call(bf16[128,16,512]{2,1,0:T(8,128)(2,1)S(1)} %all-to-all-done.3.recv_ref, bf16[4,512,512]{2,1,0:T(8,128)(2,1)} %get-tuple-element.47.fixed_in, bf16[2,16,512]{2,1,0:T(8,128)(2,1)S(1)} %pad.9.tail_ref), custom_call_target="tpu_custom_call" | custom-call | flops 2000000000 | bytes 8388608 | tf_op jit(solution)/shard_map/pallas_call | solution.py:559
  (39 shorter events, 0.5 us)
Async XLA Ops:
  2.8 16.3 %all-to-all-start = ((bf16[8,4,1024]{2,1,0:T(4,128)(2,1)}), bf16[8,4,1024]{2,1,0:T(4,128)(2,1)S(1)}, u32[]{:S(2)}, u32[]{:S(2)}) async-start(bf16[8,4,1024]{2,1,0:T(4,128)(2,1)} %broadcast_in_dim.12), calls=%async_computation | async-start | bytes 131072 | tf_op jit(solution)/shard_map/all_to_all | solution.py:616
  19.2 60.7 %all-to-all-start.1 = ((bf16[128,16,512]{2,1,0:T(8,128)(2,1)}), bf16[128,16,512]{2,1,0:T(8,128)(2,1)S(1)}, u32[]{:S(2)}, u32[]{:S(2)}) async-start(bf16[128,16,512]{2,1,0:T(8,128)(2,1)} %shard_map.84), calls=%async_computation.1 | async-start | bytes 4194304 | tf_op jit(solution)/shard_map/all_to_all | solution.py:676
  28.5 7.1 %collective-permute-start = (bf16[32,1024]{1,0:T(8,128)(2,1)S(1)}, bf16[32,1024]{1,0:T(8,128)(2,1)S(1)}, u32[]{:S(2)}, u32[]{:S(2)}) collective-permute-start(bf16[32,1024]{1,0:T(8,128)(2,1)S(1)} %reshape.123), channel_id=1, source_target_pairs={{0,16},{2,18},{4,20},{6,22},{8,24},{10,26},{12,28},{14,30},{16,0},... | collective-permute-start | bytes 196616 | tf_op jit(solution)/shard_map/ppermute | solution.py:599
  35.6 7.3 %collective-permute-start.1 = (bf16[64,1024]{1,0:T(8,128)(2,1)S(1)}, bf16[64,1024]{1,0:T(8,128)(2,1)S(1)}, u32[]{:S(2)}, u32[]{:S(2)}) collective-permute-start(bf16[64,1024]{1,0:T(8,128)(2,1)S(1)} %get-tuple-element.71), channel_id=1, source_target_pairs={{0,4},{2,6},{4,8},{6,10},{8,12},{10,14},{12,0},{14,2},{16,20},{18,... | collective-permute-start | bytes 393224 | tf_op jit(solution)/shard_map/ppermute | solution.py:599
  36.2 7.3 %collective-permute-start.2 = (bf16[64,1024]{1,0:T(8,128)(2,1)S(1)}, bf16[64,1024]{1,0:T(8,128)(2,1)S(1)}, u32[]{:S(2)}, u32[]{:S(2)}) collective-permute-start(bf16[64,1024]{1,0:T(8,128)(2,1)S(1)} %get-tuple-element.71), channel_id=1, source_target_pairs={{0,12},{2,14},{4,0},{6,2},{8,4},{10,6},{12,8},{14,10},{16,28},{18,... | collective-permute-start | bytes 393224 | tf_op jit(solution)/shard_map/ppermute | solution.py:599
  38.4 10.5 %collective-permute-start.3 = (bf16[64,1024]{1,0:T(8,128)(2,1)S(1)}, bf16[64,1024]{1,0:T(8,128)(2,1)S(1)}, u32[]{:S(2)}, u32[]{:S(2)}) collective-permute-start(bf16[64,1024]{1,0:T(8,128)(2,1)S(1)} %get-tuple-element.71), channel_id=1, source_target_pairs={{0,8},{2,10},{4,12},{6,14},{8,0},{10,2},{12,4},{14,6},{16,24},{18,... | collective-permute-start | bytes 393224 | tf_op jit(solution)/shard_map/ppermute | solution.py:599
  48.9 1.0 copy-start.1
  49.8 5.6 %collective-permute-start.4 = (bf16[256,1024]{1,0:T(8,128)(2,1)S(1)}, bf16[256,1024]{1,0:T(8,128)(2,1)S(1)}, u32[]{:S(2)}, u32[]{:S(2)}) collective-permute-start(bf16[256,1024]{1,0:T(8,128)(2,1)S(1)} %get-tuple-element.59), channel_id=1, source_target_pairs={{0,2},{2,0},{4,6},{6,4},{8,10},{10,8},{12,14},{14,12},{16,18},{18,... | collective-permute-start | bytes 1572872 | tf_op jit(solution)/shard_map/ppermute | solution.py:599
  66.6 6.3 %collective-permute-start.5 = (f32[128,8]{1,0:T(8,128)S(1)}, f32[128,8]{1,0:T(8,128)S(1)}, u32[]{:S(2)}, u32[]{:S(2)}) collective-permute-start(f32[128,8]{1,0:T(8,128)S(1)} %copy.26), channel_id=1, source_target_pairs={{0,1},{1,0},{2,3},{3,2},{4,5},{5,4},{6,7},{7,6},{8,9},{9,8},{10,11... | collective-permute-start | bytes 12296 | tf_op jit(solution)/shard_map/ppermute | solution.py:603
  83.6 17.6 %all-to-all-start.2 = ((f32[128,1,128]{2,1,0:T(1,128)}), f32[128,1,128]{2,1,0:T(1,128)S(1)}, u32[]{:S(2)}, u32[]{:S(2)}) async-start(f32[128,1,128]{2,1,0:T(1,128)} %get-tuple-element.36), calls=%async_computation.2 | async-start | bytes 131072 | tf_op jit(solution)/shard_map/all_to_all | solution.py:684
  90.7 13.5 %collective-permute-start.6 = (f32[128,8]{1,0:T(8,128)S(1)}, f32[128,8]{1,0:T(8,128)S(1)}, u32[]{:S(2)}, u32[]{:S(2)}) collective-permute-start(f32[128,8]{1,0:T(8,128)S(1)} %slice.65), channel_id=1, source_target_pairs={{0,1},{1,0},{2,3},{3,2},{4,5},{5,4},{6,7},{7,6},{8,9},{9,8},{10,11... | collective-permute-start | bytes 12296 | tf_op jit(solution)/shard_map/ppermute | solution.py:603
  101.3 8.1 %collective-permute-start.7 = (f32[128,8]{1,0:T(8,128)S(1)}, f32[128,8]{1,0:T(8,128)S(1)}, u32[]{:S(2)}, u32[]{:S(2)}) collective-permute-start(f32[128,8]{1,0:T(8,128)S(1)} %bitcast.68), channel_id=1, source_target_pairs={{0,1},{1,0},{2,3},{3,2},{4,5},{5,4},{6,7},{7,6},{8,9},{9,8},{10,11... | collective-permute-start | bytes 12296 | tf_op jit(solution)/shard_map/ppermute | solution.py:603
  109.5 59.9 %all-to-all-start.3 = ((bf16[128,16,512]{2,1,0:T(8,128)(2,1)}), bf16[128,16,512]{2,1,0:T(8,128)(2,1)S(1)}, u32[]{:S(2)}, u32[]{:S(2)}) async-start(bf16[128,16,512]{2,1,0:T(8,128)(2,1)} %shard_map.88), calls=%async_computation.3 | async-start | bytes 4194304 | tf_op jit(solution)/shard_map/all_to_all | solution.py:690
  115.9 6.8 %copy-start = (f32[128,4,2]{2,1,0:T(4,128)}, f32[128,4,2]{2,1,0:T(4,128)S(1)}, u32[]{:S(2)}) copy-start(f32[128,4,2]{2,1,0:T(4,128)S(1)} %copy.28) | copy-start | bytes 12292
  122.7 2.6 %collective-permute-start.8 = (bf16[256,1024]{1,0:T(8,128)(2,1)S(1)}, bf16[256,1024]{1,0:T(8,128)(2,1)S(1)}, u32[]{:S(2)}, u32[]{:S(2)}) collective-permute-start(bf16[256,1024]{1,0:T(8,128)(2,1)S(1)} %get-tuple-element.42), channel_id=1, source_target_pairs={{0,2},{2,0},{4,6},{6,4},{8,10},{10,8},{12,14},{14,12},{16,18},{18,... | collective-permute-start | bytes 1572872 | tf_op jit(solution)/shard_map/ppermute | solution.py:599
  125.5 11.9 %collective-permute-start.10 = (bf16[64,1024]{1,0:T(8,128)(2,1)S(1)}, bf16[64,1024]{1,0:T(8,128)(2,1)S(1)}, u32[]{:S(2)}, u32[]{:S(2)}) collective-permute-start(bf16[64,1024]{1,0:T(8,128)(2,1)S(1)} %get-tuple-element.58), channel_id=1, source_target_pairs={{0,4},{2,6},{4,8},{6,10},{8,12},{10,14},{12,0},{14,2},{16,20},{18,... | collective-permute-start | bytes 393224 | tf_op jit(solution)/shard_map/ppermute | solution.py:599
  126.6 11.8 %collective-permute-start.11 = (bf16[64,1024]{1,0:T(8,128)(2,1)S(1)}, bf16[64,1024]{1,0:T(8,128)(2,1)S(1)}, u32[]{:S(2)}, u32[]{:S(2)}) collective-permute-start(bf16[64,1024]{1,0:T(8,128)(2,1)S(1)} %get-tuple-element.57), channel_id=1, source_target_pairs={{0,8},{2,10},{4,12},{6,14},{8,0},{10,2},{12,4},{14,6},{16,24},{18,... | collective-permute-start | bytes 393224 | tf_op jit(solution)/shard_map/ppermute | solution.py:599
  129.0 9.6 %collective-permute-start.9 = (bf16[64,1024]{1,0:T(8,128)(2,1)S(1)}, bf16[64,1024]{1,0:T(8,128)(2,1)S(1)}, u32[]{:S(2)}, u32[]{:S(2)}) collective-permute-start(bf16[64,1024]{1,0:T(8,128)(2,1)S(1)} %get-tuple-element.56), channel_id=1, source_target_pairs={{0,12},{2,14},{4,0},{6,2},{8,4},{10,6},{12,8},{14,10},{16,28},{18,... | collective-permute-start | bytes 393224 | tf_op jit(solution)/shard_map/ppermute | solution.py:599
  138.7 5.1 %collective-permute-start.12 = (bf16[32,1024]{1,0:T(8,128)(2,1)S(1)}, bf16[32,1024]{1,0:T(8,128)(2,1)S(1)}, u32[]{:S(2)}, u32[]{:S(2)}) collective-permute-start(bf16[32,1024]{1,0:T(8,128)(2,1)S(1)} %slice.109), channel_id=1, source_target_pairs={{0,16},{2,18},{4,20},{6,22},{8,24},{10,26},{12,28},{14,30},{16,0},... | collective-permute-start | bytes 196616 | tf_op jit(solution)/shard_map/ppermute | solution.py:599
  143.8 23.3 %collective-permute-start.13 = (bf16[8,1024]{1,0:T(8,128)(2,1)S(1)}, bf16[8,1024]{1,0:T(8,128)(2,1)S(1)}, u32[]{:S(2)}, u32[]{:S(2)}) collective-permute-start(bf16[8,1024]{1,0:T(8,128)(2,1)S(1)} %reshape_squeeze.20), channel_id=1, source_target_pairs={{0,0},{2,130},{4,4},{6,134},{8,8},{10,138},{12,12},{14,142},{16,16... | collective-permute-start | bytes 49160 | tf_op jit(solution)/shard_map/ppermute | solution.py:653
  151.3 15.9 %collective-permute-start.14 = (bf16[8,1024]{1,0:T(8,128)(2,1)S(1)}, bf16[8,1024]{1,0:T(8,128)(2,1)S(1)}, u32[]{:S(2)}, u32[]{:S(2)}) collective-permute-start(bf16[8,1024]{1,0:T(8,128)(2,1)S(1)} %reshape_squeeze.21), channel_id=1, source_target_pairs={{0,32},{2,162},{4,36},{6,166},{8,40},{10,170},{12,44},{14,174},{16... | collective-permute-start | bytes 49160 | tf_op jit(solution)/shard_map/ppermute | solution.py:653
  151.5 15.7 %collective-permute-start.15 = (bf16[8,1024]{1,0:T(8,128)(2,1)S(1)}, bf16[8,1024]{1,0:T(8,128)(2,1)S(1)}, u32[]{:S(2)}, u32[]{:S(2)}) collective-permute-start(bf16[8,1024]{1,0:T(8,128)(2,1)S(1)} %reshape_squeeze.22), channel_id=1, source_target_pairs={{0,64},{2,194},{4,68},{6,198},{8,72},{10,202},{12,76},{14,206},{16... | collective-permute-start | bytes 49160 | tf_op jit(solution)/shard_map/ppermute | solution.py:653
  154.8 12.4 %collective-permute-start.16 = (bf16[8,1024]{1,0:T(8,128)(2,1)S(1)}, bf16[8,1024]{1,0:T(8,128)(2,1)S(1)}, u32[]{:S(2)}, u32[]{:S(2)}) collective-permute-start(bf16[8,1024]{1,0:T(8,128)(2,1)S(1)} %reshape_squeeze.23), channel_id=1, source_target_pairs={{0,96},{2,226},{4,100},{6,230},{8,104},{10,234},{12,108},{14,238},... | collective-permute-start | bytes 49160 | tf_op jit(solution)/shard_map/ppermute | solution.py:653
  167.2 1.3 collective-permute-start.17

commit v7 on v6

--- a/solution.py
+++ b/solution.py
@@ -259,19 +259,22 @@
             grp_ref[head, 0, :, at : at + 16, :] = tiles[3]
     copies = copy_all([(keys_ref, keys_out)], sem.at[0])
     row, col = iotas((NB, NB))
+    heads = range(HEADS)
+    scores = [batch_dot(keys_ref[head, 0], keys_ref[head, 1], 2, 2) * scale for head in heads]
+    scores = [jnp.where((col <= row)[None], score, -jnp.inf) for score in scores]
+    expos = [jnp.exp(score - jnp.max(score, axis=-1, keepdims=True)) for score in scores]
+    probs = [
+        (expo * (1.0 / jnp.sum(expo, axis=-1, keepdims=True))).astype(BF16) for expo in expos
+    ]
+    attns = [batch_dot(probs[head], keys_ref[head, 2], 2, 1).astype(BF16) for head in heads]
     square, cross = 0.0, 0.0
-    for head in range(HEADS):
-        scores = batch_dot(keys_ref[head, 0], keys_ref[head, 1], 2, 2) * scale
-        scores = jnp.where((col <= row)[None], scores, -jnp.inf)
-        expo = jnp.exp(scores - jnp.max(scores, axis=-1, keepdims=True))
-        prob = (expo * (1.0 / jnp.sum(expo, axis=-1, keepdims=True))).astype(BF16)
-        attn = batch_dot(prob, keys_ref[head, 2], 2, 1).astype(BF16)
-        prob_ref[head] = prob
+    for head in heads:
+        prob_ref[head] = probs[head]
         copies += copy_all([(prob_ref.at[head], prob_out.at[head])], sem.at[head + 1])
-        wide = attn.astype(F32)
+        wide = attns[head].astype(F32)
         square += wide * wide
         cross += wide * grp_ref[head, 0].astype(F32)
-        grp_ref[head, 1] = attn
+        grp_ref[head, 1] = attns[head]
     square = jnp.sum(square, axis=-1, keepdims=True)
     cross = jnp.sum(cross, axis=-1, keepdims=True)
     lane = lax.broadcasted_iota(jnp.int32, (NB, HD), 1)
@@ -344,16 +347,22 @@
         normed, grad, row_dot = normalize(wide, grp_ref[head, 0], square, cross)
         out_ref[head, 0] = normed
         grads.append((grad, row_dot))
-    for head in range(HEADS):
+    heads = range(HEADS)
+    for head in heads:
         for copy in fetched[head]:
             copy.wait()
-        grad, row_dot = grads[head]
-        prob = prob_ref[head]
-        grad_prob = batch_dot(grad, keys_ref[head, 2], 2, 2)
-        grad_score = (prob.astype(F32) * (grad_prob - row_dot) * scale).astype(BF16)
-        out_ref[head, 1] = batch_dot(grad_score, keys_ref[head, 1], 2, 1).astype(BF16)
-        out_ref[head, 2] = batch_dot(grad_score, keys_ref[head, 0], 1, 1).astype(BF16)
-        out_ref[head, 3] = batch_dot(prob, grad, 1, 1).astype(BF16)
+    probs = [prob_ref[head] for head in heads]
+    grad_probs = [batch_dot(grads[head][0], keys_ref[head, 2], 2, 2) for head in heads]
+    scores = [
+        (probs[head].astype(F32) * (grad_probs[head] - grads[head][1]) * scale).astype(BF16)
+        for head in heads
+    ]
+    for head in heads:
+        out_ref[head, 3] = batch_dot(probs[head], grads[head][0], 1, 1).astype(BF16)
+    for head in heads:
+        out_ref[head, 1] = batch_dot(scores[head], keys_ref[head, 1], 2, 1).astype(BF16)
+    for head in heads:
+        out_ref[head, 2] = batch_dot(scores[head], keys_ref[head, 0], 1, 1).astype(BF16)
     swap = swap_matrix()
     copies = []
     for at in range(0, NB, 16):
@@ -686,7 +695,6 @@
     own_sums = sums_in[:, 0, 8:16]
     block_sums = fixed_both + own_sums + other_head(own_sums)
     send_back = strided_backward(keys, prob, grp, sums, sums_other, sums_in)
-    send_back, block_sums = lax.optimization_barrier((send_back, block_sums))
     recv_back = lax.all_to_all(send_back, "seq", 0, 0, tiled=True)
     block_sums = block_sums.reshape(NB, 2, OFFS).transpose(0, 2, 1).reshape(BLOCK, 2)
     far_query, kept, sent = summary_backward(rows, summ, far_prob, fixed_attn, block_sums)

time: 175 us -> 176 us (level)
    ppermute x4, waiting for transfers between devices: 10.5 us -> 3.25 us  [scatter_summaries(): moved.append(lax.ppermute(sent[:, n].reshape(2 * SUMM, SLAB), 'seq', perm))]
    ppermute x3, waiting for transfers between devices: 3.71 us -> 10.4 us  [other_head(): return lax.ppermute(array, 'head', [(0, 1), (1, 0)])]
    ppermute x11, waiting for transfers between devices: 21.4 us -> 24.5 us  [shift(): return lax.ppermute(array, 'seq', perm)]
    all_to_all x1, waiting for transfers between devices: 7.59 us -> 5.37 us  [shards(): sums_in = lax.all_to_all(sums_send, 'seq', 0, 0, tiled=True)]
  transfers between devices with their start and end apart: 22 -> 22, of which waited for: 14 -> 15; matrix products, arithmetic and copies ran while one was open for 3% -> 3% of each run, Pallas kernels for 20% -> 17%
where the time goes in v7:
time: 176 us; the launch traced here: 175 us
  starting transfers between devices  68.7 us (39%)
  waiting for transfers between devices  54.3 us (31%)
  Pallas kernels  43 us (24%)
  local copies, waits for them, and re-layouts  6.75 us (4%)
    ppermute x11, waiting for transfers between devices, shift(): return lax.ppermute(array, 'seq', perm)  24.5 us
    ppermute x11, starting transfers between devices, shift(): return lax.ppermute(array, 'seq', perm)  14.8 us
    ppermute x4, starting transfers between devices, scatter_summaries(): moved.append(lax.ppermute(sent[:, n].reshape(2 * SUMM, SLAB), 'seq', perm))  12.6 us
    ppermute x3, waiting for transfers between devices, other_head(): return lax.ppermute(array, 'head', [(0, 1), (1, 0)])  10.4 us
    all_to_all x1, starting transfers between devices, shards(): recv = lax.all_to_all(send, 'seq', 0, 0, tiled=True)  9.33 us
    pallas_call x1, Pallas kernels, fixed_forward(): call(fixed_forward_kernel, HEADS, [spec((4, BLOCK, HD), 0, 0, 'i'), spec(...  9.18 us
    all_to_all x1, starting transfers between devices, gather_along_z(): lax.all_to_all(sent, 'seq', 0, 0, axis_index_groups=groups, tiled=True)  9.01 us
    ppermute x3, starting transfers between devices, other_head(): return lax.ppermute(array, 'head', [(0, 1), (1, 0)])  8.26 us
  transfers between devices with their start and end apart: 22, of which 15 were waited for; matrix products, arithmetic and copies ran while one was open for 3% of the time, Pallas kernels for 17%

profile of v7, /device:TPU:1, one launch (start us, length us, event | category | flops | bytes accessed | tf_op | source)
XLA Modules:
  0.0 175.1 jit_solution(17910568670862985419)
XLA Ops:
  0.6 0.7 slice_reduce_fusion
  1.4 0.7 slice_reduce_fusion.1
  2.2 0.6 broadcast_in_dim.12
  2.8 9.0 %all-to-all-start = ((bf16[8,4,1024]{2,1,0:T(4,128)(2,1)}), bf16[8,4,1024]{2,1,0:T(4,128)(2,1)S(1)}, u32[]{:S(2)}, u32[]{:S(2)}) async-start(bf16[8,4,1024]{2,1,0:T(4,128)(2,1)} %broadcast_in_dim.12), calls=%async_computation | async-start | bytes 131072 | tf_op jit(solution)/shard_map/all_to_all | solution.py:625
  11.8 3.5 %shard_map.84 = bf16[128,16,512]{2,1,0:T(8,128)(2,1)} custom-call(bf16[4096,128]{1,0:T(8,128)(2,1)} %bitcast.63, bf16[4096,128]{1,0:T(8,128)(2,1)} %bitcast.59, bf16[4096,128]{1,0:T(8,128)(2,1)} %bitcast.61, bf16[4096,128]{1,0:T(8,128)(2,1)} %bitcast.65), custom_call_target="tpu_custom_call" | custom-call | flops 1000000000 | bytes 6291456 | tf_op jit(solution)/shard_map/pallas_call | solution.py:142
  15.3 3.8 %all-to-all-done = bf16[8,4,1024]{2,1,0:T(4,128)(2,1)S(1)} async-done(((bf16[8,4,1024]{2,1,0:T(4,128)(2,1)}), bf16[8,4,1024]{2,1,0:T(4,128)(2,1)S(1)}, u32[]{:S(2)}, u32[]{:S(2)}) %all-to-all-start) | async-done | bytes 65568 | tf_op jit(solution)/shard_map/all_to_all | solution.py:625
  19.1 0.1 fusion.2
  19.2 9.3 %all-to-all-start.1 = ((bf16[128,16,512]{2,1,0:T(8,128)(2,1)}), bf16[128,16,512]{2,1,0:T(8,128)(2,1)S(1)}, u32[]{:S(2)}, u32[]{:S(2)}) async-start(bf16[128,16,512]{2,1,0:T(8,128)(2,1)} %shard_map.84), calls=%async_computation.1 | async-start | bytes 4194304 | tf_op jit(solution)/shard_map/all_to_all | solution.py:685
  28.5 1.5 collective-permute-start
  30.0 5.6 %collective-permute-done = bf16[32,1024]{1,0:T(8,128)(2,1)S(1)} collective-permute-done((bf16[32,1024]{1,0:T(8,128)(2,1)S(1)}, bf16[32,1024]{1,0:T(8,128)(2,1)S(1)}, u32[]{:S(2)}, u32[]{:S(2)}) %collective-permute-start) | collective-permute-done | bytes 65568 | tf_op jit(solution)/shard_map/ppermute | solution.py:608
  35.6 0.6 collective-permute-start.1
  36.2 2.1 %collective-permute-start.2 = (bf16[64,1024]{1,0:T(8,128)(2,1)S(1)}, bf16[64,1024]{1,0:T(8,128)(2,1)S(1)}, u32[]{:S(2)}, u32[]{:S(2)}) collective-permute-start(bf16[64,1024]{1,0:T(8,128)(2,1)S(1)} %get-tuple-element.67), channel_id=1, source_target_pairs={{0,12},{2,14},{4,0},{6,2},{8,4},{10,6},{12,8},{14,10},{16,28},{18,... | collective-permute-start | bytes 393224 | tf_op jit(solution)/shard_map/ppermute | solution.py:608
  38.4 0.8 collective-permute-start.3
  39.2 3.7 %collective-permute-done.1 = bf16[64,1024]{1,0:T(8,128)(2,1)S(1)} collective-permute-done((bf16[64,1024]{1,0:T(8,128)(2,1)S(1)}, bf16[64,1024]{1,0:T(8,128)(2,1)S(1)}, u32[]{:S(2)}, u32[]{:S(2)}) %collective-permute-start.1) | collective-permute-done | bytes 131104 | tf_op jit(solution)/shard_map/ppermute | solution.py:608
  42.9 0.6 collective-permute-done.2
  43.5 5.3 %collective-permute-done.3 = bf16[64,1024]{1,0:T(8,128)(2,1)S(1)} collective-permute-done((bf16[64,1024]{1,0:T(8,128)(2,1)S(1)}, bf16[64,1024]{1,0:T(8,128)(2,1)S(1)}, u32[]{:S(2)}, u32[]{:S(2)}) %collective-permute-start.3) | collective-permute-done | bytes 131104 | tf_op jit(solution)/shard_map/ppermute | solution.py:608
  48.9 0.0 copy-start.1
  48.9 1.0 copy-done.1
  49.8 1.2 collective-permute-start.4
  51.1 0.1 broadcast_in_dim.13
  51.1 0.7 broadcast_in_dim_reshape.4.seen_ref
  51.8 3.6 %shard_map.85.rows_ref.rows_in = bf16[4,512,512]{2,1,0:T(8,128)(2,1)} custom-call(bf16[4096,128]{1,0:T(8,128)(2,1)} %bitcast.64, bf16[4096,128]{1,0:T(8,128)(2,1)} %bitcast.60, bf16[4096,128]{1,0:T(8,128)(2,1)} %bitcast.62, bf16[4096,128]{1,0:T(8,128)(2,1)} %bitcast.66), custom_call_target="tpu_custom_call" | custom-call | flops 1000000000 | bytes 6291456 | tf_op jit(solution)/shard_map/pallas_call | solution.py:173
  55.4 0.8 constant_dynamic-update-slice_fusion.7.summ_ref.summ_in
  56.2 9.2 %shard_map.86 = (bf16[512,512]{1,0:T(8,128)(2,1)}, bf16[4,512,512]{2,1,0:T(8,128)(2,1)}, bf16[4,512,512]{2,1,0:T(8,128)(2,1)}, f32[512,8]{1,0:T(8,128)}) custom-call(bf16[4,512,512]{2,1,0:T(8,128)(2,1)} %shard_map.85.rows_ref.rows_in, bf16[512,1024]{1,0:T(8,128)(2,1)} %constant_dynamic-update-slice_fusion.7.summ_ref.summ_in, ...), custom_call_target="tpu_custom_call" | custom-call | flops 4000000000 | bytes 4194304 | tf_op jit(solution)/shard_map/pallas_call | solution.py:220
  65.4 1.0 copy.24
  66.5 0.1 copy.26
  66.6 2.5 %collective-permute-start.5 = (f32[128,8]{1,0:T(8,128)S(1)}, f32[128,8]{1,0:T(8,128)S(1)}, u32[]{:S(2)}, u32[]{:S(2)}) collective-permute-start(f32[128,8]{1,0:T(8,128)S(1)} %copy.26), channel_id=1, source_target_pairs={{0,1},{1,0},{2,3},{3,2},{4,5},{5,4},{6,7},{7,6},{8,9},{9,8},{10,11... | collective-permute-start | bytes 12296 | tf_op jit(solution)/shard_map/ppermute | solution.py:612
  69.1 3.7 %collective-permute-done.5 = f32[128,8]{1,0:T(8,128)S(1)} collective-permute-done((f32[128,8]{1,0:T(8,128)S(1)}, f32[128,8]{1,0:T(8,128)S(1)}, u32[]{:S(2)}, u32[]{:S(2)}) %collective-permute-start.5) | collective-permute-done | bytes 4128 | tf_op jit(solution)/shard_map/ppermute | solution.py:612
  72.9 7.0 %all-to-all-done.1.recv_ref = bf16[128,16,512]{2,1,0:T(8,128)(2,1)S(1)} async-done(((bf16[128,16,512]{2,1,0:T(8,128)(2,1)}), bf16[128,16,512]{2,1,0:T(8,128)(2,1)S(1)}, u32[]{:S(2)}, u32[]{:S(2)}) %all-to-all-start.1) | async-done | bytes 2097184 | tf_op jit(solution)/shard_map/all_to_all | solution.py:685
  79.9 2.9 %shard_map.87 = (bf16[4,3,4,128,128]{4,3,2,1,0:T(8,128)(2,1)}, bf16[4,4,128,128]{3,2,1,0:T(8,128)(2,1)}, bf16[4,2,4,128,128]{4,3,2,1,0:T(8,128)(2,1)S(1)}, f32[128,128]{1,0:T(8,128)S(1)}, f32[128,1,128]{2,1,0:T(1,128)}) custom-call(bf16[128,16,512]{2,1,0:T(8,128)(2,1)S(1)} %all-to-all-done.1.recv_ref, f32[128,128]{1,0:T(8,128)S(1)} %pad.8.fixed_ref), custom_call_target="tpu_custom_call" | custom-call | flops 1000000000 | bytes 6291456 | tf_op jit(solution)/shard_map/pallas_call | solution.py:291
  82.8 7.0 %all-to-all-start.2 = ((f32[128,1,128]{2,1,0:T(1,128)}), f32[128,1,128]{2,1,0:T(1,128)S(1)}, u32[]{:S(2)}, u32[]{:S(2)}) async-start(f32[128,1,128]{2,1,0:T(1,128)} %get-tuple-element.34), calls=%async_computation.2 | async-start | bytes 131072 | tf_op jit(solution)/shard_map/all_to_all | solution.py:693
  89.8 0.1 slice.65
  89.9 2.8 %collective-permute-start.6 = (f32[128,8]{1,0:T(8,128)S(1)}, f32[128,8]{1,0:T(8,128)S(1)}, u32[]{:S(2)}, u32[]{:S(2)}) collective-permute-start(f32[128,8]{1,0:T(8,128)S(1)} %slice.65), channel_id=1, source_target_pairs={{0,1},{1,0},{2,3},{3,2},{4,5},{5,4},{6,7},{7,6},{8,9},{9,8},{10,11... | collective-permute-start | bytes 12296 | tf_op jit(solution)/shard_map/ppermute | solution.py:612
  92.7 2.2 %collective-permute-done.6.other_ref = f32[128,8]{1,0:T(8,128)S(1)} collective-permute-done((f32[128,8]{1,0:T(8,128)S(1)}, f32[128,8]{1,0:T(8,128)S(1)}, u32[]{:S(2)}, u32[]{:S(2)}) %collective-permute-start.6) | collective-permute-done | bytes 4128 | tf_op jit(solution)/shard_map/ppermute | solution.py:612
  95.0 5.4 %all-to-all-done.2.recv_ref = f32[128,1,128]{2,1,0:T(1,128)S(1)} async-done(((f32[128,1,128]{2,1,0:T(1,128)}), f32[128,1,128]{2,1,0:T(1,128)S(1)}, u32[]{:S(2)}, u32[]{:S(2)}) %all-to-all-start.2) | async-done | bytes 65568 | tf_op jit(solution)/shard_map/all_to_all | solution.py:693
  100.3 4.8 %shard_map.88 = bf16[128,16,512]{2,1,0:T(8,128)(2,1)} custom-call(bf16[4,3,4,128,128]{4,3,2,1,0:T(8,128)(2,1)} %get-tuple-element.30.keys_in, bf16[4,4,128,128]{3,2,1,0:T(8,128)(2,1)} %get-tuple-element.31.prob_in, bf16[4,2,4,128,128]{4,3,2,1,0:T(8,128)(2,1)S(1)} %get-tuple-element.32.grp_ref, f32[128,128]{1,0:T(8,128)S(1)} %get-tuple-element.33.sums_ref, ...), custom_call_target="tpu_custom_call" | custom-call | flops 1000000000 | bytes 6291456 | tf_op jit(solution)/shard_map/pallas_call | solution.py:379
  105.2 7.6 %all-to-all-start.3 = ((bf16[128,16,512]{2,1,0:T(8,128)(2,1)}), bf16[128,16,512]{2,1,0:T(8,128)(2,1)S(1)}, u32[]{:S(2)}, u32[]{:S(2)}) async-start(bf16[128,16,512]{2,1,0:T(8,128)(2,1)} %shard_map.88), calls=%async_computation.3 | async-start | bytes 4194304 | tf_op jit(solution)/shard_map/all_to_all | solution.py:698
  112.8 0.2 slice.85
  113.0 2.9 %collective-permute-start.7 = (f32[128,8]{1,0:T(8,128)S(1)}, f32[128,8]{1,0:T(8,128)S(1)}, u32[]{:S(2)}, u32[]{:S(2)}) collective-permute-start(f32[128,8]{1,0:T(8,128)S(1)} %bitcast.68), channel_id=1, source_target_pairs={{0,1},{1,0},{2,3},{3,2},{4,5},{5,4},{6,7},{7,6},{8,9},{9,8},{10,11... | collective-permute-start | bytes 12296 | tf_op jit(solution)/shard_map/ppermute | solution.py:612
  115.9 4.5 %collective-permute-done.7 = f32[128,8]{1,0:T(8,128)S(1)} collective-permute-done((f32[128,8]{1,0:T(8,128)S(1)}, f32[128,8]{1,0:T(8,128)S(1)}, u32[]{:S(2)}, u32[]{:S(2)}) %collective-permute-start.7) | collective-permute-done | bytes 4128 | tf_op jit(solution)/shard_map/ppermute | solution.py:612
  120.5 0.2 copy.28
  120.7 0.0 copy-start
  120.7 6.8 %shard_map.89 = (f32[512,512]{1,0:T(8,128)}, f32[256,1024]{1,0:T(8,128)S(1)}, bf16[256,1024]{1,0:T(8,128)(2,1)S(1)}) custom-call(bf16[4,512,512]{2,1,0:T(8,128)(2,1)} %shard_map.85.rows_ref.rows_in, bf16[512,1024]{1,0:T(8,128)(2,1)} %constant_dynamic-update-slice_fusion.7.summ_ref.summ_in, bf16[4,512,512]{2,1,0:T(8,128)(2,1)} %get-tuple-element.35.far_in, ...), custom_call_target="tpu_custom_call" | custom-call | flops 3000000000 | bytes 8388608 | tf_op jit(solution)/shard_map/pallas_call | solution.py:443
  127.5 3.0 %collective-permute-start.8 = (bf16[256,1024]{1,0:T(8,128)(2,1)S(1)}, bf16[256,1024]{1,0:T(8,128)(2,1)S(1)}, u32[]{:S(2)}, u32[]{:S(2)}) collective-permute-start(bf16[256,1024]{1,0:T(8,128)(2,1)S(1)} %get-tuple-element.38), channel_id=1, source_target_pairs={{0,2},{2,0},{4,6},{6,4},{8,10},{10,8},{12,14},{14,12},{16,18},{18,... | collective-permute-start | bytes 1572872 | tf_op jit(solution)/shard_map/ppermute | solution.py:608
  130.4 1.5 collective-permute-done.8
  131.9 0.2 fusion.12
  132.2 1.6 collective-permute-start.11
  133.8 0.5 collective-permute-start.10
  134.3 2.2 %collective-permute-start.9 = (bf16[64,1024]{1,0:T(8,128)(2,1)S(1)}, bf16[64,1024]{1,0:T(8,128)(2,1)S(1)}, u32[]{:S(2)}, u32[]{:S(2)}) collective-permute-start(bf16[64,1024]{1,0:T(8,128)(2,1)S(1)} %get-tuple-element.52), channel_id=1, source_target_pairs={{0,12},{2,14},{4,0},{6,2},{8,4},{10,6},{12,8},{14,10},{16,28},{18,... | collective-permute-start | bytes 393224 | tf_op jit(solution)/shard_map/ppermute | solution.py:608
  136.5 7.3 %shard_map.90 = (bf16[4,512,512]{2,1,0:T(8,128)(2,1)}, f32[2,8,512]{2,1,0:T(8,128)}) custom-call(bf16[4,512,512]{2,1,0:T(8,128)(2,1)} %shard_map.85.rows_ref.rows_in, bf16[4,512,512]{2,1,0:T(8,128)(2,1)} %get-tuple-element.39.own_ref, bf16[512,512]{1,0:T(8,128)(2,1)} %get-tuple-element.36.attn_in.attn_ref, f32[512,2]{1,0:T(8,128)} %bitcast.58, ...), custom_call_target="tpu_custom_call" | custom-call | flops 5000000000 | bytes 8388608 | tf_op jit(solution)/shard_map/pallas_call | solution.py:485
  143.7 2.4 %collective-permute-done.10 = bf16[64,1024]{1,0:T(8,128)(2,1)S(1)} collective-permute-done((bf16[64,1024]{1,0:T(8,128)(2,1)S(1)}, bf16[64,1024]{1,0:T(8,128)(2,1)S(1)}, u32[]{:S(2)}, u32[]{:S(2)}) %collective-permute-start.10) | collective-permute-done | bytes 131104 | tf_op jit(solution)/shard_map/ppermute | solution.py:608
  146.2 0.0 collective-permute-done.9
  146.2 0.1 fusion.1
  146.3 1.2 collective-permute-start.12
  147.4 4.2 %collective-permute-done.12 = bf16[32,1024]{1,0:T(8,128)(2,1)S(1)} collective-permute-done((bf16[32,1024]{1,0:T(8,128)(2,1)S(1)}, bf16[32,1024]{1,0:T(8,128)(2,1)S(1)}, u32[]{:S(2)}, u32[]{:S(2)}) %collective-permute-start.12) | collective-permute-done | bytes 65568 | tf_op jit(solution)/shard_map/ppermute | solution.py:608
  151.8 4.6 %collective-permute-start.16 = (bf16[8,1024]{1,0:T(8,128)(2,1)S(1)}, bf16[8,1024]{1,0:T(8,128)(2,1)S(1)}, u32[]{:S(2)}, u32[]{:S(2)}) collective-permute-start(bf16[8,1024]{1,0:T(8,128)(2,1)S(1)} %reshape_squeeze.23), channel_id=1, source_target_pairs={{0,96},{2,226},{4,100},{6,230},{8,104},{10,234},{12,108},{14,238},... | collective-permute-start | bytes 49160 | tf_op jit(solution)/shard_map/ppermute | solution.py:662
  156.4 1.0 collective-permute-start.15
  157.3 1.8 %collective-permute-start.14 = (bf16[8,1024]{1,0:T(8,128)(2,1)S(1)}, bf16[8,1024]{1,0:T(8,128)(2,1)S(1)}, u32[]{:S(2)}, u32[]{:S(2)}) collective-permute-start(bf16[8,1024]{1,0:T(8,128)(2,1)S(1)} %reshape_squeeze.21), channel_id=1, source_target_pairs={{0,32},{2,162},{4,36},{6,166},{8,40},{10,170},{12,44},{14,174},{16... | collective-permute-start | bytes 49160 | tf_op jit(solution)/shard_map/ppermute | solution.py:662
  159.2 5.3 %collective-permute-start.13 = (bf16[8,1024]{1,0:T(8,128)(2,1)S(1)}, bf16[8,1024]{1,0:T(8,128)(2,1)S(1)}, u32[]{:S(2)}, u32[]{:S(2)}) collective-permute-start(bf16[8,1024]{1,0:T(8,128)(2,1)S(1)} %reshape_squeeze.20), channel_id=1, source_target_pairs={{0,0},{2,130},{4,4},{6,134},{8,8},{10,138},{12,12},{14,142},{16,16... | collective-permute-start | bytes 49160 | tf_op jit(solution)/shard_map/ppermute | solution.py:662
  164.5 3.2 %collective-permute-done.13 = bf16[8,1024]{1,0:T(8,128)(2,1)S(1)} collective-permute-done((bf16[8,1024]{1,0:T(8,128)(2,1)S(1)}, bf16[8,1024]{1,0:T(8,128)(2,1)S(1)}, u32[]{:S(2)}, u32[]{:S(2)}) %collective-permute-start.13) | collective-permute-done | bytes 16416 | tf_op jit(solution)/shard_map/ppermute | solution.py:662
  167.8 0.1 collective-permute-start.17
  167.9 1.2 collective-permute-done.17
  169.1 0.8 add_convert_fusion.1
  169.9 5.0 %shard_map.91 = (bf16[4096,128]{1,0:T(8,128)(2,1)}, bf16[4096,128]{1,0:T(8,128)(2,1)}, bf16[4096,128]{1,0:T(8,128)(2,1)}, bf16[4096,128]{1,0:T(8,128)(2,1)}) custom-call(bf16[128,16,512]{2,1,0:T(8,128)(2,1)S(1)} %all-to-all-done.3.recv_ref, bf16[4,512,512]{2,1,0:T(8,128)(2,1)} %get-tuple-element.43.fixed_in, bf16[2,16,512]{2,1,0:T(8,128)(2,1)S(1)} %pad.9.tail_ref), custom_call_target="tpu_custom_call" | custom-call | flops 2000000000 | bytes 8388608 | tf_op jit(solution)/shard_map/pallas_call | solution.py:568
  (39 shorter events, 0.5 us)
Async XLA Ops:
  2.8 16.3 %all-to-all-start = ((bf16[8,4,1024]{2,1,0:T(4,128)(2,1)}), bf16[8,4,1024]{2,1,0:T(4,128)(2,1)S(1)}, u32[]{:S(2)}, u32[]{:S(2)}) async-start(bf16[8,4,1024]{2,1,0:T(4,128)(2,1)} %broadcast_in_dim.12), calls=%async_computation | async-start | bytes 131072 | tf_op jit(solution)/shard_map/all_to_all | solution.py:625
  19.2 60.7 %all-to-all-start.1 = ((bf16[128,16,512]{2,1,0:T(8,128)(2,1)}), bf16[128,16,512]{2,1,0:T(8,128)(2,1)S(1)}, u32[]{:S(2)}, u32[]{:S(2)}) async-start(bf16[128,16,512]{2,1,0:T(8,128)(2,1)} %shard_map.84), calls=%async_computation.1 | async-start | bytes 4194304 | tf_op jit(solution)/shard_map/all_to_all | solution.py:685
  28.5 7.1 %collective-permute-start = (bf16[32,1024]{1,0:T(8,128)(2,1)S(1)}, bf16[32,1024]{1,0:T(8,128)(2,1)S(1)}, u32[]{:S(2)}, u32[]{:S(2)}) collective-permute-start(bf16[32,1024]{1,0:T(8,128)(2,1)S(1)} %reshape.123), channel_id=1, source_target_pairs={{0,16},{2,18},{4,20},{6,22},{8,24},{10,26},{12,28},{14,30},{16,0},... | collective-permute-start | bytes 196616 | tf_op jit(solution)/shard_map/ppermute | solution.py:608
  35.6 7.3 %collective-permute-start.1 = (bf16[64,1024]{1,0:T(8,128)(2,1)S(1)}, bf16[64,1024]{1,0:T(8,128)(2,1)S(1)}, u32[]{:S(2)}, u32[]{:S(2)}) collective-permute-start(bf16[64,1024]{1,0:T(8,128)(2,1)S(1)} %get-tuple-element.67), channel_id=1, source_target_pairs={{0,4},{2,6},{4,8},{6,10},{8,12},{10,14},{12,0},{14,2},{16,20},{18,... | collective-permute-start | bytes 393224 | tf_op jit(solution)/shard_map/ppermute | solution.py:608
  36.2 7.3 %collective-permute-start.2 = (bf16[64,1024]{1,0:T(8,128)(2,1)S(1)}, bf16[64,1024]{1,0:T(8,128)(2,1)S(1)}, u32[]{:S(2)}, u32[]{:S(2)}) collective-permute-start(bf16[64,1024]{1,0:T(8,128)(2,1)S(1)} %get-tuple-element.67), channel_id=1, source_target_pairs={{0,12},{2,14},{4,0},{6,2},{8,4},{10,6},{12,8},{14,10},{16,28},{18,... | collective-permute-start | bytes 393224 | tf_op jit(solution)/shard_map/ppermute | solution.py:608
  38.4 10.5 %collective-permute-start.3 = (bf16[64,1024]{1,0:T(8,128)(2,1)S(1)}, bf16[64,1024]{1,0:T(8,128)(2,1)S(1)}, u32[]{:S(2)}, u32[]{:S(2)}) collective-permute-start(bf16[64,1024]{1,0:T(8,128)(2,1)S(1)} %get-tuple-element.67), channel_id=1, source_target_pairs={{0,8},{2,10},{4,12},{6,14},{8,0},{10,2},{12,4},{14,6},{16,24},{18,... | collective-permute-start | bytes 393224 | tf_op jit(solution)/shard_map/ppermute | solution.py:608
  48.9 1.0 copy-start.1
  49.8 5.6 %collective-permute-start.4 = (bf16[256,1024]{1,0:T(8,128)(2,1)S(1)}, bf16[256,1024]{1,0:T(8,128)(2,1)S(1)}, u32[]{:S(2)}, u32[]{:S(2)}) collective-permute-start(bf16[256,1024]{1,0:T(8,128)(2,1)S(1)} %get-tuple-element.55), channel_id=1, source_target_pairs={{0,2},{2,0},{4,6},{6,4},{8,10},{10,8},{12,14},{14,12},{16,18},{18,... | collective-permute-start | bytes 1572872 | tf_op jit(solution)/shard_map/ppermute | solution.py:608
  66.6 6.3 %collective-permute-start.5 = (f32[128,8]{1,0:T(8,128)S(1)}, f32[128,8]{1,0:T(8,128)S(1)}, u32[]{:S(2)}, u32[]{:S(2)}) collective-permute-start(f32[128,8]{1,0:T(8,128)S(1)} %copy.26), channel_id=1, source_target_pairs={{0,1},{1,0},{2,3},{3,2},{4,5},{5,4},{6,7},{7,6},{8,9},{9,8},{10,11... | collective-permute-start | bytes 12296 | tf_op jit(solution)/shard_map/ppermute | solution.py:612
  82.8 17.6 %all-to-all-start.2 = ((f32[128,1,128]{2,1,0:T(1,128)}), f32[128,1,128]{2,1,0:T(1,128)S(1)}, u32[]{:S(2)}, u32[]{:S(2)}) async-start(f32[128,1,128]{2,1,0:T(1,128)} %get-tuple-element.34), calls=%async_computation.2 | async-start | bytes 131072 | tf_op jit(solution)/shard_map/all_to_all | solution.py:693
  89.9 5.1 %collective-permute-start.6 = (f32[128,8]{1,0:T(8,128)S(1)}, f32[128,8]{1,0:T(8,128)S(1)}, u32[]{:S(2)}, u32[]{:S(2)}) collective-permute-start(f32[128,8]{1,0:T(8,128)S(1)} %slice.65), channel_id=1, source_target_pairs={{0,1},{1,0},{2,3},{3,2},{4,5},{5,4},{6,7},{7,6},{8,9},{9,8},{10,11... | collective-permute-start | bytes 12296 | tf_op jit(solution)/shard_map/ppermute | solution.py:612
  105.2 64.7 %all-to-all-start.3 = ((bf16[128,16,512]{2,1,0:T(8,128)(2,1)}), bf16[128,16,512]{2,1,0:T(8,128)(2,1)S(1)}, u32[]{:S(2)}, u32[]{:S(2)}) async-start(bf16[128,16,512]{2,1,0:T(8,128)(2,1)} %shard_map.88), calls=%async_computation.3 | async-start | bytes 4194304 | tf_op jit(solution)/shard_map/all_to_all | solution.py:698
  113.0 7.4 %collective-permute-start.7 = (f32[128,8]{1,0:T(8,128)S(1)}, f32[128,8]{1,0:T(8,128)S(1)}, u32[]{:S(2)}, u32[]{:S(2)}) collective-permute-start(f32[128,8]{1,0:T(8,128)S(1)} %bitcast.68), channel_id=1, source_target_pairs={{0,1},{1,0},{2,3},{3,2},{4,5},{5,4},{6,7},{7,6},{8,9},{9,8},{10,11... | collective-permute-start | bytes 12296 | tf_op jit(solution)/shard_map/ppermute | solution.py:612
  120.7 6.8 %copy-start = (f32[128,4,2]{2,1,0:T(4,128)}, f32[128,4,2]{2,1,0:T(4,128)S(1)}, u32[]{:S(2)}) copy-start(f32[128,4,2]{2,1,0:T(4,128)S(1)} %copy.28) | copy-start | bytes 12292
  127.5 4.5 %collective-permute-start.8 = (bf16[256,1024]{1,0:T(8,128)(2,1)S(1)}, bf16[256,1024]{1,0:T(8,128)(2,1)S(1)}, u32[]{:S(2)}, u32[]{:S(2)}) collective-permute-start(bf16[256,1024]{1,0:T(8,128)(2,1)S(1)} %get-tuple-element.38), channel_id=1, source_target_pairs={{0,2},{2,0},{4,6},{6,4},{8,10},{10,8},{12,14},{14,12},{16,18},{18,... | collective-permute-start | bytes 1572872 | tf_op jit(solution)/shard_map/ppermute | solution.py:608
  132.2 11.6 %collective-permute-start.11 = (bf16[64,1024]{1,0:T(8,128)(2,1)S(1)}, bf16[64,1024]{1,0:T(8,128)(2,1)S(1)}, u32[]{:S(2)}, u32[]{:S(2)}) collective-permute-start(bf16[64,1024]{1,0:T(8,128)(2,1)S(1)} %get-tuple-element.53), channel_id=1, source_target_pairs={{0,8},{2,10},{4,12},{6,14},{8,0},{10,2},{12,4},{14,6},{16,24},{18,... | collective-permute-start | bytes 393224 | tf_op jit(solution)/shard_map/ppermute | solution.py:608
  133.8 12.4 %collective-permute-start.10 = (bf16[64,1024]{1,0:T(8,128)(2,1)S(1)}, bf16[64,1024]{1,0:T(8,128)(2,1)S(1)}, u32[]{:S(2)}, u32[]{:S(2)}) collective-permute-start(bf16[64,1024]{1,0:T(8,128)(2,1)S(1)} %get-tuple-element.54), channel_id=1, source_target_pairs={{0,4},{2,6},{4,8},{6,10},{8,12},{10,14},{12,0},{14,2},{16,20},{18,... | collective-permute-start | bytes 393224 | tf_op jit(solution)/shard_map/ppermute | solution.py:608
  134.3 11.9 %collective-permute-start.9 = (bf16[64,1024]{1,0:T(8,128)(2,1)S(1)}, bf16[64,1024]{1,0:T(8,128)(2,1)S(1)}, u32[]{:S(2)}, u32[]{:S(2)}) collective-permute-start(bf16[64,1024]{1,0:T(8,128)(2,1)S(1)} %get-tuple-element.52), channel_id=1, source_target_pairs={{0,12},{2,14},{4,0},{6,2},{8,4},{10,6},{12,8},{14,10},{16,28},{18,... | collective-permute-start | bytes 393224 | tf_op jit(solution)/shard_map/ppermute | solution.py:608
  146.3 5.4 %collective-permute-start.12 = (bf16[32,1024]{1,0:T(8,128)(2,1)S(1)}, bf16[32,1024]{1,0:T(8,128)(2,1)S(1)}, u32[]{:S(2)}, u32[]{:S(2)}) collective-permute-start(bf16[32,1024]{1,0:T(8,128)(2,1)S(1)} %slice.109), channel_id=1, source_target_pairs={{0,16},{2,18},{4,20},{6,22},{8,24},{10,26},{12,28},{14,30},{16,0},... | collective-permute-start | bytes 196616 | tf_op jit(solution)/shard_map/ppermute | solution.py:608
  151.8 12.7 %collective-permute-start.16 = (bf16[8,1024]{1,0:T(8,128)(2,1)S(1)}, bf16[8,1024]{1,0:T(8,128)(2,1)S(1)}, u32[]{:S(2)}, u32[]{:S(2)}) collective-permute-start(bf16[8,1024]{1,0:T(8,128)(2,1)S(1)} %reshape_squeeze.23), channel_id=1, source_target_pairs={{0,96},{2,226},{4,100},{6,230},{8,104},{10,234},{12,108},{14,238},... | collective-permute-start | bytes 49160 | tf_op jit(solution)/shard_map/ppermute | solution.py:662
  156.4 8.1 %collective-permute-start.15 = (bf16[8,1024]{1,0:T(8,128)(2,1)S(1)}, bf16[8,1024]{1,0:T(8,128)(2,1)S(1)}, u32[]{:S(2)}, u32[]{:S(2)}) collective-permute-start(bf16[8,1024]{1,0:T(8,128)(2,1)S(1)} %reshape_squeeze.22), channel_id=1, source_target_pairs={{0,64},{2,194},{4,68},{6,198},{8,72},{10,202},{12,76},{14,206},{16... | collective-permute-start | bytes 49160 | tf_op jit(solution)/shard_map/ppermute | solution.py:662
  157.3 7.1 %collective-permute-start.14 = (bf16[8,1024]{1,0:T(8,128)(2,1)S(1)}, bf16[8,1024]{1,0:T(8,128)(2,1)S(1)}, u32[]{:S(2)}, u32[]{:S(2)}) collective-permute-start(bf16[8,1024]{1,0:T(8,128)(2,1)S(1)} %reshape_squeeze.21), channel_id=1, source_target_pairs={{0,32},{2,162},{4,36},{6,166},{8,40},{10,170},{12,44},{14,174},{16... | collective-permute-start | bytes 49160 | tf_op jit(solution)/shard_map/ppermute | solution.py:662
  159.2 8.6 %collective-permute-start.13 = (bf16[8,1024]{1,0:T(8,128)(2,1)S(1)}, bf16[8,1024]{1,0:T(8,128)(2,1)S(1)}, u32[]{:S(2)}, u32[]{:S(2)}) collective-permute-start(bf16[8,1024]{1,0:T(8,128)(2,1)S(1)} %reshape_squeeze.20), channel_id=1, source_target_pairs={{0,0},{2,130},{4,4},{6,134},{8,8},{10,138},{12,12},{14,142},{16,16... | collective-permute-start | bytes 49160 | tf_op jit(solution)/shard_map/ppermute | solution.py:662
  167.8 1.3 collective-permute-start.17

commit v8 on v7

--- a/solution.py
+++ b/solution.py
@@ -43,10 +43,6 @@
 
 def dot_tn(a, b):
     return lax.dot_general(a, b, (((0,), (0,)), ((), ())), preferred_element_type=F32)
-
-
-def dot_rows(a, b):
-    return dot_tn(b, a).T
 
 
 def batch_dot(a, b, left, right):
@@ -326,6 +322,29 @@
     return normed, grad, jnp.sum(grad.astype(F32) * wide, axis=-1, keepdims=True)
 
 
+def factors(sums_ref):
+    row, col = iotas((BLOCK, NB))
+    spread = one_hot(col == row >> 2)
+    rest, columns = sums_ref[...], 0.0
+    for _ in range(3):
+        part = rest.astype(BF16)
+        rest = rest - part.astype(F32)
+        columns += dot_nt(spread, part)
+    row, col = iotas((BLOCK, 8))
+    square, cross = (
+        jnp.sum(jnp.where(col == (row & 3) + at, columns, 0.0), axis=-1, keepdims=True)
+        for at in (0, OFFS)
+    )
+    scaling = lax.rsqrt(square / (2 * COLS) + epsilon)
+    other = scaling * scaling * scaling * cross / (2 * COLS)
+    return jnp.broadcast_to(scaling, (BLOCK, HD)), jnp.broadcast_to(other, (BLOCK, HD))
+
+
+def gradient(wide, cotangent, scaling, other):
+    grad = (scaling * cotangent.astype(F32) - wide * other).astype(BF16)
+    return grad, jnp.sum(grad.astype(F32) * wide, axis=-1, keepdims=True)
+
+
 def strided_backward_kernel(
     keys_in, prob_in, grp_ref, sums_ref, other_ref, recv_ref, send_out,
     keys_ref, prob_ref, out_ref, send_ref, in_sem, out_sem,
@@ -412,38 +431,52 @@
             (attn_in, attn_ref),
             (rows_in.at[3], cot_ref),
             (summ_in, summ_ref),
-            (rows_in.at[0], rows_ref),
         ]
-        + [(far_in.at[head], far_ref.at[head]) for head in range(HEADS)],
+        + [(far_in.at[head], far_ref.at[head]) for head in range(HEADS)]
+        + [(rows_in.at[0], rows_ref)],
         sem,
     )
-    for copy in copies[:4]:
-        copy.wait()
-    for head in range(HEADS):
-        copies[4 + head].wait()
-        at = slice(head * HD, (head + 1) * HD)
-        to_key = slice(2 * head * HD, (2 * head + 1) * HD)
-        to_value = slice((2 * head + 1) * HD, (2 * head + 2) * HD)
-        _, grad, row_dot = normalize(
-            attn_ref[:, at].astype(F32), cot_ref[:, at], sums_ref[:, 0:1], sums_ref[:, 1:2]
-        )
-        far = far_ref[head]
-        score = far.astype(F32) * (dot_nt(grad, summ_ref[:, to_value]) - row_dot) * scale
-        score = score.astype(BF16)
-        query_ref[:, at] = dot(score, summ_ref[:, to_key])
-        for to, grads in ((to_key, dot_rows(score, rows_ref[:, at])), (to_value, dot_rows(far, grad))):
-            grads = grads.reshape(2, 8, 2, 16, HD)
-            keep = jnp.stack([grads[0, :, 0], grads[1, :, 1]], 1)
-            send = jnp.stack([grads[1, :, 0], grads[0, :, 1]], 1)
-            keep_ref[:, to] = keep.reshape(BLOCK // 2, HD)
-            send_ref[:, to] = send.reshape(BLOCK // 2, HD).astype(BF16)
+    heads = range(HEADS)
+    at = [slice(head * HD, (head + 1) * HD) for head in heads]
+    to_key = [slice(2 * head * HD, (2 * head + 1) * HD) for head in heads]
+    to_value = [slice((2 * head + 1) * HD, (2 * head + 2) * HD) for head in heads]
+    scaling, other = factors(sums_ref)
+    copies[0].wait()
+    copies[1].wait()
+    grads = [
+        gradient(attn_ref[:, at[head]].astype(F32), cot_ref[:, at[head]], scaling, other)
+        for head in heads
+    ]
+    scores = []
+    copies[2].wait()
+    for head in heads:
+        copies[3 + head].wait()
+        grad, row_dot = grads[head]
+        grad_prob = dot_nt(grad, summ_ref[:, to_value[head]])
+        score = far_ref[head].astype(F32) * (grad_prob - row_dot) * scale
+        scores.append(score.astype(BF16))
+
+    def put(to, grads):
+        grads = grads.reshape(2, 8, 2, 16, HD)
+        keep = jnp.stack([grads[0, :, 0], grads[1, :, 1]], 1)
+        send = jnp.stack([grads[1, :, 0], grads[0, :, 1]], 1)
+        keep_ref[:, to] = keep.reshape(BLOCK // 2, HD)
+        send_ref[:, to] = send.reshape(BLOCK // 2, HD).astype(BF16)
+
+    for head in heads:
+        put(to_value[head], dot_tn(far_ref[head], grads[head][0]))
+    copies[3 + HEADS].wait()
+    for head in heads:
+        put(to_key[head], dot_tn(scores[head], rows_ref[:, at[head]]))
+    for head in heads:
+        query_ref[:, at[head]] = dot(scores[head], summ_ref[:, to_key[head]])
 
 
 def summary_backward(rows, summ, far, attn, sums):
     return call(
         summary_backward_kernel,
         1,
-        [IN_HBM] * 4 + [spec((BLOCK, 2), 0, 0)],
+        [IN_HBM] * 4 + [spec((8, NB), 0, 0)],
         [
             spec((BLOCK, WIDTH), 0, 0),
             spec((BLOCK // 2, 2 * WIDTH), 0, 0),
@@ -468,38 +501,93 @@
     )(*[in_hbm(array) for array in (rows, summ, far, attn)], sums)
 
 
-def fixed_backward_kernel(rows_ref, own_ref, attn_ref, sums_ref, query_ref, out_ref, tail_ref):
-    query, key, value = rows_ref[0], rows_ref[1], rows_ref[2]
-    own = own_ref[0]
-    wide = attn_ref[...].astype(F32)
-    normed, grad, row_dot = normalize(wide, rows_ref[3], sums_ref[:, 0:1], sums_ref[:, 1:2])
-    out_ref[0] = normed
-    score = (own.astype(F32) * (dot_nt(grad, value) - row_dot) * scale).astype(BF16)
-    out_ref[1] = (dot(score, key) + query_ref[...]).astype(BF16)
-    for at, grads in enumerate((dot_rows(score, query), dot_rows(own, grad))):
-        out_ref[2 + at] = grads.astype(BF16)
-        tail_ref[at] = grads[BLOCK - 8 :]
+def fixed_backward_kernel(
+    rows_in, own_in, attn_in, sums_ref, query_in, out_out, tail_ref,
+    rows_ref, own_ref, attn_ref, query_ref, out_ref, sem, out_sem,
+):
+    copies = copy_all(
+        [(attn_in, attn_ref)]
+        + [(rows_in.at[array], rows_ref.at[array]) for array in (3, 2)]
+        + [(own_in.at[head], own_ref.at[head]) for head in range(HEADS)]
+        + [(rows_in.at[array], rows_ref.at[array]) for array in (0, 1)]
+        + [(query_in, query_ref)],
+        sem,
+    )
+    heads = range(HEADS)
+    at = [slice(head * HD, (head + 1) * HD) for head in heads]
+    low, high = slice(0, BLOCK // 2), slice(BLOCK // 2, BLOCK)
+    scaling, other = factors(sums_ref)
+    copies[0].wait()
+    copies[1].wait()
+    grads = []
+    for head in heads:
+        wide = attn_ref[:, at[head]].astype(F32)
+        out_ref[0, :, at[head]] = (wide * scaling).astype(BF16)
+        grads.append(gradient(wide, rows_ref[3, :, at[head]], scaling, other))
+    sent = copy_all([(out_ref.at[0], out_out.at[0])], out_sem.at[0])
+    scores = []
+    copies[2].wait()
+    for head in heads:
+        copies[3 + head].wait()
+        grad, row_dot = grads[head]
+        first = dot_nt(grad[low], rows_ref[2, low, at[head]]) - row_dot[low]
+        second = dot_nt(grad[high], rows_ref[2, :, at[head]]) - row_dot[high]
+        first = (own_ref[head, low, low].astype(F32) * first * scale).astype(BF16)
+        second = (own_ref[head, high, :].astype(F32) * second * scale).astype(BF16)
+        scores.append((first, second))
+
+    def put(array, head, first, second, b):
+        grads_low = dot_tn(first, b[low]) + dot_tn(second[:, low], b[high])
+        grads_high = dot_tn(second[:, high], b[high])
+        out_ref[array, low, at[head]] = grads_low.astype(BF16)
+        out_ref[array, high, at[head]] = grads_high.astype(BF16)
+        tail_ref[array - 2, :, at[head]] = grads_high[BLOCK // 2 - 8 :]
+
+    for head in heads:
+        put(3, head, own_ref[head, low, low], own_ref[head, high, :], grads[head][0])
+    sent += copy_all([(out_ref.at[3], out_out.at[3])], out_sem.at[3])
+    copies[3 + HEADS].wait()
+    for head in heads:
+        put(2, head, *scores[head], rows_ref[0, :, at[head]])
+    sent += copy_all([(out_ref.at[2], out_out.at[2])], out_sem.at[2])
+    copies[4 + HEADS].wait()
+    copies[5 + HEADS].wait()
+    for head in heads:
+        first, second = scores[head]
+        out_ref[1, low, at[head]] = (
+            dot(first, rows_ref[1, low, at[head]]) + query_ref[low, at[head]]
+        ).astype(BF16)
+        out_ref[1, high, at[head]] = (
+            dot(second, rows_ref[1, :, at[head]]) + query_ref[high, at[head]]
+        ).astype(BF16)
+    sent += copy_all([(out_ref.at[1], out_out.at[1])], out_sem.at[1])
+    for copy in sent:
+        copy.wait()
 
 
 def fixed_backward(rows, own, attn, sums, far_query):
     return call(
         fixed_backward_kernel,
-        HEADS,
-        [
-            spec((4, BLOCK, HD), 0, 0, "i"),
-            spec((1, BLOCK, BLOCK), "i", 0, 0),
-            spec((BLOCK, HD), 0, "i"),
-            spec((BLOCK, 2), 0, 0),
-            spec((BLOCK, HD), 0, "i"),
-        ],
-        [spec((4, BLOCK, HD), 0, 0, "i"), spec((2, 8, HD), 0, 0, "i")],
+        1,
+        [IN_HBM, IN_HBM, IN_HBM, spec((8, NB), 0, 0), IN_HBM],
+        [IN_HBM, spec((2, 8, WIDTH), 0, 0, 0)],
         [
             pltpu.HBM((4, BLOCK, WIDTH), BF16),
             jax.ShapeDtypeStruct((2, 8, WIDTH), F32),
         ],
         5 * 10**9,
         8 * 2**20,
-    )(rows, own, attn, sums, far_query)
+        [
+            pltpu.VMEM((4, BLOCK, WIDTH), BF16),
+            pltpu.VMEM((HEADS, BLOCK, BLOCK), BF16),
+            pltpu.VMEM((BLOCK, WIDTH), BF16),
+            pltpu.VMEM((BLOCK, WIDTH), F32),
+            pltpu.VMEM((4, BLOCK, WIDTH), BF16),
+            pltpu.SemaphoreType.DMA((HEADS + 6,)),
+            pltpu.SemaphoreType.DMA((4, 1)),
+        ],
+        vmem=VMEM5,
+    )(*[in_hbm(array) for array in (rows, own, attn)], sums, in_hbm(far_query))
 
 
 def unpack_kernel(recv_ref, fixed_in, tail_ref, *refs):
@@ -514,45 +602,32 @@
         in_sem,
     )
     sent = []
-    row, col = iotas((512, 256))
+    row, col = iotas((512, 512))
     array, token, head, kind = row >> 7, (row >> 3) & 15, (row >> 1) & 3, row & 1
-    source = (token >> 2) * 64 + head * 16 + array * OFFS + (token & 3)
-    strided_pick = one_hot((kind == 0) & (col == source))
-    row, col = iotas((128, 64))
-    token, head, kind = row >> 3, (row >> 1) & 3, row & 1
-    own_pick = one_hot((kind == 1) & (col == head * 16 + token))
+    strided = (token >> 2) * 64 + head * 16 + array * OFFS + (token & 3)
+    fixed = 256 + array * 64 + head * 16 + token
+    pick = one_hot(col == jnp.where(kind == 0, strided, fixed))
     end = lax.broadcasted_iota(jnp.int32, (16, WIDTH), 0) >= 16 - SUMM
     for at in range(0, 32, 2):
         if at * 16 % size == 0:
             copies[at * 16 // size].wait()
-        rows = [
-            jnp.concatenate(
-                [
-                    recv_ref[4 * n + home, :, head * HD : (head + 1) * HD]
-                    for home in range(4)
-                    for head in range(HEADS)
-                ],
-                0,
-            )
-            for n in (at, at + 1)
-        ]
-        strided = dot(strided_pick, jnp.concatenate(rows, 1))
-        for n in range(2):
-            tile = 16 * (at + n)
+        pair = []
+        for n in (at, at + 1):
+            tile = 16 * n
             fixed = [fixed_ref[array, tile : tile + 16] for array in range(4)]
             if tile == BLOCK - 16:
                 for array in (2, 3):
                     fixed[array] = jnp.where(end, tail_ref[array - 2], fixed[array])
-            rows = [
-                jnp.concatenate([part[:, head * HD : (head + 1) * HD] for part in fixed], 1)
-                for head in range(HEADS)
-            ]
-            own = dot(own_pick, jnp.concatenate(rows, 0))
+            heads = [slice(head * HD, (head + 1) * HD) for head in range(HEADS)]
+            rows = [recv_ref[4 * n + home, :, head] for home in range(4) for head in heads]
+            rows += [part[:, head] for part in fixed for head in heads]
+            pair.append(jnp.concatenate(rows, 0))
+        picked = dot(pick, jnp.concatenate(pair, 1)).astype(BF16)
+        for n in range(2):
             for array in range(4):
-                out_ref[array, 8 * tile : 8 * tile + 128] = (
-                    strided[array * 128 : (array + 1) * 128, n * HD : (n + 1) * HD]
-                    + own[:, array * HD : (array + 1) * HD]
-                ).astype(BF16)
+                out_ref[array, 128 * (at + n) : 128 * (at + n + 1)] = picked[
+                    array * 128 : (array + 1) * 128, n * HD : (n + 1) * HD
+                ]
         if (at + 2) * 16 % size == 0:
             part = at * 16 // size
             where = pl.ds(part * size * 8, size * 8)
@@ -692,11 +767,10 @@
     keys, prob, grp, sums, sums_send = strided_forward(recv, jnp.pad(fixed_both, ((0, 0), (0, HD - 8))))
     sums_in = lax.all_to_all(sums_send, "seq", 0, 0, tiled=True)
     sums_other = other_head(sums[:, 8:16])
-    own_sums = sums_in[:, 0, 8:16]
-    block_sums = fixed_both + own_sums + other_head(own_sums)
+    own_sums = sums_in[:, 0, 8:16].T
+    block_sums = fixed_both.T + own_sums + other_head(own_sums)
     send_back = strided_backward(keys, prob, grp, sums, sums_other, sums_in)
     recv_back = lax.all_to_all(send_back, "seq", 0, 0, tiled=True)
-    block_sums = block_sums.reshape(NB, 2, OFFS).transpose(0, 2, 1).reshape(BLOCK, 2)
     far_query, kept, sent = summary_backward(rows, summ, far_prob, fixed_attn, block_sums)
     fixed_out, tails = fixed_backward(rows, own_prob, fixed_attn, block_sums, far_query)
     parts = scatter_along_y(scatter_along_core(kept, sent))

time: 176 us -> 172 us (0.977)
  Pallas kernels: 43 us -> 40.4 us
    ppermute x3, waiting for transfers between devices: 10.4 us -> 6.63 us  [other_head(): return lax.ppermute(array, 'head', [(0, 1), (1, 0)])]
    pallas_call x2, Pallas kernels: 14 us -> 11.4 us  [the longest x1 5.91 us: summary_backward(): call(summary_backward_kernel, 1, [IN_HBM] * 4 + [spec((8, NB), 0, 0)], [s...]
    all_to_all x1, waiting for transfers between devices: 6.98 us -> 8.9 us  [shards(): recv = lax.all_to_all(send, 'seq', 0, 0, tiled=True)]
  transfers between devices with their start and end apart: 22 -> 22, of which waited for: 15 -> 15; matrix products, arithmetic and copies ran while one was open for 3% -> 2% of each run, Pallas kernels for 17% -> 16%
where the time goes in v8:
time: 172 us; the launch traced here: 171 us
  starting transfers between devices  67.9 us (39%)
  waiting for transfers between devices  54.8 us (32%)
  Pallas kernels  40.4 us (23%)
  local copies, waits for them, and re-layouts  6.53 us (4%)
    ppermute x11, waiting for transfers between devices, shift(): return lax.ppermute(array, 'seq', perm)  26.2 us
    ppermute x11, starting transfers between devices, shift(): return lax.ppermute(array, 'seq', perm)  14.3 us
    ppermute x4, starting transfers between devices, scatter_summaries(): moved.append(lax.ppermute(sent[:, n].reshape(2 * SUMM, SLAB), 'seq', perm))  13 us
    all_to_all x1, starting transfers between devices, shards(): recv = lax.all_to_all(send, 'seq', 0, 0, tiled=True)  9.34 us
    pallas_call x1, Pallas kernels, fixed_forward(): call(fixed_forward_kernel, HEADS, [spec((4, BLOCK, HD), 0, 0, 'i'), spec(...  9.18 us
    all_to_all x1, starting transfers between devices, gather_along_z(): lax.all_to_all(sent, 'seq', 0, 0, axis_index_groups=groups, tiled=True)  9.01 us
    all_to_all x1, waiting for transfers between devices, shards(): recv = lax.all_to_all(send, 'seq', 0, 0, tiled=True)  8.9 us
    all_to_all x1, starting transfers between devices, shards(): recv_back = lax.all_to_all(send_back, 'seq', 0, 0, tiled=True)  7.65 us
  transfers between devices with their start and end apart: 22, of which 15 were waited for; matrix products, arithmetic and copies ran while one was open for 2% of the time, Pallas kernels for 16%

profile of v8, /device:TPU:1, one launch (start us, length us, event | category | flops | bytes accessed | tf_op | source)
XLA Modules:
  0.0 171.1 jit_solution(15320163921359452225)
XLA Ops:
  0.6 0.7 slice_reduce_fusion
  1.4 0.7 slice_reduce_fusion.1
  2.2 0.6 broadcast_in_dim.12
  2.8 9.0 %all-to-all-start = ((bf16[8,4,1024]{2,1,0:T(4,128)(2,1)}), bf16[8,4,1024]{2,1,0:T(4,128)(2,1)S(1)}, u32[]{:S(2)}, u32[]{:S(2)}) async-start(bf16[8,4,1024]{2,1,0:T(4,128)(2,1)} %broadcast_in_dim.12), calls=%async_computation | async-start | bytes 131072 | tf_op jit(solution)/shard_map/all_to_all | solution.py:700
  11.8 3.5 %shard_map.84 = bf16[128,16,512]{2,1,0:T(8,128)(2,1)} custom-call(bf16[4096,128]{1,0:T(8,128)(2,1)} %bitcast.64, bf16[4096,128]{1,0:T(8,128)(2,1)} %bitcast.60, bf16[4096,128]{1,0:T(8,128)(2,1)} %bitcast.62, bf16[4096,128]{1,0:T(8,128)(2,1)} %bitcast.66), custom_call_target="tpu_custom_call" | custom-call | flops 1000000000 | bytes 6291456 | tf_op jit(solution)/shard_map/pallas_call | solution.py:138
  15.3 3.8 %all-to-all-done = bf16[8,4,1024]{2,1,0:T(4,128)(2,1)S(1)} async-done(((bf16[8,4,1024]{2,1,0:T(4,128)(2,1)}), bf16[8,4,1024]{2,1,0:T(4,128)(2,1)S(1)}, u32[]{:S(2)}, u32[]{:S(2)}) %all-to-all-start) | async-done | bytes 65568 | tf_op jit(solution)/shard_map/all_to_all | solution.py:700
  19.1 0.1 fusion.2
  19.2 9.3 %all-to-all-start.1 = ((bf16[128,16,512]{2,1,0:T(8,128)(2,1)}), bf16[128,16,512]{2,1,0:T(8,128)(2,1)S(1)}, u32[]{:S(2)}, u32[]{:S(2)}) async-start(bf16[128,16,512]{2,1,0:T(8,128)(2,1)} %shard_map.84), calls=%async_computation.1 | async-start | bytes 4194304 | tf_op jit(solution)/shard_map/all_to_all | solution.py:760
  28.5 1.5 collective-permute-start
  30.0 5.6 %collective-permute-done = bf16[32,1024]{1,0:T(8,128)(2,1)S(1)} collective-permute-done((bf16[32,1024]{1,0:T(8,128)(2,1)S(1)}, bf16[32,1024]{1,0:T(8,128)(2,1)S(1)}, u32[]{:S(2)}, u32[]{:S(2)}) %collective-permute-start) | collective-permute-done | bytes 65568 | tf_op jit(solution)/shard_map/ppermute | solution.py:683
  35.6 0.6 collective-permute-start.1
  36.2 2.1 %collective-permute-start.2 = (bf16[64,1024]{1,0:T(8,128)(2,1)S(1)}, bf16[64,1024]{1,0:T(8,128)(2,1)S(1)}, u32[]{:S(2)}, u32[]{:S(2)}) collective-permute-start(bf16[64,1024]{1,0:T(8,128)(2,1)S(1)} %get-tuple-element.67), channel_id=1, source_target_pairs={{0,12},{2,14},{4,0},{6,2},{8,4},{10,6},{12,8},{14,10},{16,28},{18,... | collective-permute-start | bytes 393224 | tf_op jit(solution)/shard_map/ppermute | solution.py:683
  38.4 0.8 collective-permute-start.3
  39.2 3.7 %collective-permute-done.1 = bf16[64,1024]{1,0:T(8,128)(2,1)S(1)} collective-permute-done((bf16[64,1024]{1,0:T(8,128)(2,1)S(1)}, bf16[64,1024]{1,0:T(8,128)(2,1)S(1)}, u32[]{:S(2)}, u32[]{:S(2)}) %collective-permute-start.1) | collective-permute-done | bytes 131104 | tf_op jit(solution)/shard_map/ppermute | solution.py:683
  42.9 0.6 collective-permute-done.2
  43.5 5.3 %collective-permute-done.3 = bf16[64,1024]{1,0:T(8,128)(2,1)S(1)} collective-permute-done((bf16[64,1024]{1,0:T(8,128)(2,1)S(1)}, bf16[64,1024]{1,0:T(8,128)(2,1)S(1)}, u32[]{:S(2)}, u32[]{:S(2)}) %collective-permute-start.3) | collective-permute-done | bytes 131104 | tf_op jit(solution)/shard_map/ppermute | solution.py:683
  48.9 0.0 copy-start
  48.9 1.0 copy-done
  49.8 1.2 collective-permute-start.4
  51.1 0.1 broadcast_in_dim.13
  51.2 0.7 broadcast_in_dim_reshape.4.seen_ref
  51.9 3.6 %shard_map.85.rows_ref.rows_in = bf16[4,512,512]{2,1,0:T(8,128)(2,1)} custom-call(bf16[4096,128]{1,0:T(8,128)(2,1)} %bitcast.65, bf16[4096,128]{1,0:T(8,128)(2,1)} %bitcast.61, bf16[4096,128]{1,0:T(8,128)(2,1)} %bitcast.63, bf16[4096,128]{1,0:T(8,128)(2,1)} %bitcast.67), custom_call_target="tpu_custom_call" | custom-call | flops 1000000000 | bytes 6291456 | tf_op jit(solution)/shard_map/pallas_call | solution.py:169
  55.4 0.8 constant_dynamic-update-slice_fusion.7.summ_ref.summ_in
  56.3 9.2 %shard_map.86 = (bf16[512,512]{1,0:T(8,128)(2,1)}, bf16[4,512,512]{2,1,0:T(8,128)(2,1)}, bf16[4,512,512]{2,1,0:T(8,128)(2,1)}, f32[512,8]{1,0:T(8,128)}) custom-call(bf16[4,512,512]{2,1,0:T(8,128)(2,1)} %shard_map.85.rows_ref.rows_in, bf16[512,1024]{1,0:T(8,128)(2,1)} %constant_dynamic-update-slice_fusion.7.summ_ref.summ_in, ...), custom_call_target="tpu_custom_call" | custom-call | flops 4000000000 | bytes 4194304 | tf_op jit(solution)/shard_map/pallas_call | solution.py:216
  65.5 1.0 copy.40
  66.5 2.5 %collective-permute-start.5 = (f32[128,8]{0,1:T(8,128)S(1)}, f32[128,8]{0,1:T(8,128)S(1)}, u32[]{:S(2)}, u32[]{:S(2)}) collective-permute-start(f32[128,8]{0,1:T(8,128)S(1)} %bitcast.70), channel_id=1, source_target_pairs={{0,1},{1,0},{2,3},{3,2},{4,5},{5,4},{6,7},{7,6},{8,9},{9,8},{10,11... | collective-permute-start | bytes 12296 | tf_op jit(solution)/shard_map/ppermute | solution.py:687
  69.0 1.9 %collective-permute-done.5 = f32[128,8]{0,1:T(8,128)S(1)} collective-permute-done((f32[128,8]{0,1:T(8,128)S(1)}, f32[128,8]{0,1:T(8,128)S(1)}, u32[]{:S(2)}, u32[]{:S(2)}) %collective-permute-start.5) | collective-permute-done | bytes 4128 | tf_op jit(solution)/shard_map/ppermute | solution.py:687
  70.9 0.1 copy.49
  71.0 8.9 %all-to-all-done.1.recv_ref = bf16[128,16,512]{2,1,0:T(8,128)(2,1)S(1)} async-done(((bf16[128,16,512]{2,1,0:T(8,128)(2,1)}), bf16[128,16,512]{2,1,0:T(8,128)(2,1)S(1)}, u32[]{:S(2)}, u32[]{:S(2)}) %all-to-all-start.1) | async-done | bytes 2097184 | tf_op jit(solution)/shard_map/all_to_all | solution.py:760
  79.9 2.9 %shard_map.87 = (bf16[4,3,4,128,128]{4,3,2,1,0:T(8,128)(2,1)}, bf16[4,4,128,128]{3,2,1,0:T(8,128)(2,1)}, bf16[4,2,4,128,128]{4,3,2,1,0:T(8,128)(2,1)S(1)}, f32[128,128]{1,0:T(8,128)S(1)}, f32[128,1,128]{2,1,0:T(1,128)}) custom-call(bf16[128,16,512]{2,1,0:T(8,128)(2,1)S(1)} %all-to-all-done.1.recv_ref, f32[128,128]{1,0:T(8,128)S(1)} %pad.8.clone.fixed_ref), custom_call_target="tpu_custom_call" | custom-call | flops 1000000000 | bytes 6291456 | tf_op jit(solution)/shard_map/pallas_call | solution.py:287
  82.8 7.0 %all-to-all-start.2 = ((f32[128,1,128]{2,1,0:T(1,128)}), f32[128,1,128]{2,1,0:T(1,128)S(1)}, u32[]{:S(2)}, u32[]{:S(2)}) async-start(f32[128,1,128]{2,1,0:T(1,128)} %get-tuple-element.34), calls=%async_computation.2 | async-start | bytes 131072 | tf_op jit(solution)/shard_map/all_to_all | solution.py:768
  89.8 0.1 slice.65
  89.9 2.5 %collective-permute-start.6 = (f32[128,8]{1,0:T(8,128)S(1)}, f32[128,8]{1,0:T(8,128)S(1)}, u32[]{:S(2)}, u32[]{:S(2)}) collective-permute-start(f32[128,8]{1,0:T(8,128)S(1)} %slice.65), channel_id=1, source_target_pairs={{0,1},{1,0},{2,3},{3,2},{4,5},{5,4},{6,7},{7,6},{8,9},{9,8},{10,11... | collective-permute-start | bytes 12296 | tf_op jit(solution)/shard_map/ppermute | solution.py:687
  92.4 2.6 %collective-permute-done.6.other_ref = f32[128,8]{1,0:T(8,128)S(1)} collective-permute-done((f32[128,8]{1,0:T(8,128)S(1)}, f32[128,8]{1,0:T(8,128)S(1)}, u32[]{:S(2)}, u32[]{:S(2)}) %collective-permute-start.6) | collective-permute-done | bytes 4128 | tf_op jit(solution)/shard_map/ppermute | solution.py:687
  95.0 5.4 %all-to-all-done.2.recv_ref = f32[128,1,128]{2,1,0:T(1,128)S(1)} async-done(((f32[128,1,128]{2,1,0:T(1,128)}), f32[128,1,128]{2,1,0:T(1,128)S(1)}, u32[]{:S(2)}, u32[]{:S(2)}) %all-to-all-start.2) | async-done | bytes 65568 | tf_op jit(solution)/shard_map/all_to_all | solution.py:768
  100.4 4.8 %shard_map.88 = bf16[128,16,512]{2,1,0:T(8,128)(2,1)} custom-call(bf16[4,3,4,128,128]{4,3,2,1,0:T(8,128)(2,1)} %get-tuple-element.30.keys_in, bf16[4,4,128,128]{3,2,1,0:T(8,128)(2,1)} %get-tuple-element.31.prob_in, bf16[4,2,4,128,128]{4,3,2,1,0:T(8,128)(2,1)S(1)} %get-tuple-element.32.grp_ref, f32[128,128]{1,0:T(8,128)S(1)} %get-tuple-element.33.sums_ref, ...), custom_call_target="tpu_custom_call" | custom-call | flops 1000000000 | bytes 6291456 | tf_op jit(solution)/shard_map/pallas_call | solution.py:398
  105.2 7.7 %all-to-all-start.3 = ((bf16[128,16,512]{2,1,0:T(8,128)(2,1)}), bf16[128,16,512]{2,1,0:T(8,128)(2,1)S(1)}, u32[]{:S(2)}, u32[]{:S(2)}) async-start(bf16[128,16,512]{2,1,0:T(8,128)(2,1)} %shard_map.88), calls=%async_computation.3 | async-start | bytes 4194304 | tf_op jit(solution)/shard_map/all_to_all | solution.py:773
  112.9 0.2 slice.85
  113.1 2.5 %collective-permute-start.7 = (f32[8,128]{1,0:T(8,128)S(1)}, f32[8,128]{1,0:T(8,128)S(1)}, u32[]{:S(2)}, u32[]{:S(2)}) collective-permute-start(f32[8,128]{1,0:T(8,128)S(1)} %bitcast.72), channel_id=1, source_target_pairs={{0,1},{1,0},{2,3},{3,2},{4,5},{5,4},{6,7},{7,6},{8,9},{9,8},{10,11... | collective-permute-start | bytes 12296 | tf_op jit(solution)/shard_map/ppermute | solution.py:687
  115.6 2.2 %collective-permute-done.7 = f32[8,128]{1,0:T(8,128)S(1)} collective-permute-done((f32[8,128]{1,0:T(8,128)S(1)}, f32[8,128]{1,0:T(8,128)S(1)}, u32[]{:S(2)}, u32[]{:S(2)}) %collective-permute-start.7) | collective-permute-done | bytes 4128 | tf_op jit(solution)/shard_map/ppermute | solution.py:687
  117.9 5.9 %shard_map.89 = (f32[512,512]{1,0:T(8,128)}, f32[256,1024]{1,0:T(8,128)S(1)}, bf16[256,1024]{1,0:T(8,128)(2,1)S(1)}) custom-call(bf16[4,512,512]{2,1,0:T(8,128)(2,1)} %shard_map.85.rows_ref.rows_in, bf16[512,1024]{1,0:T(8,128)(2,1)} %constant_dynamic-update-slice_fusion.7.summ_ref.summ_in, bf16[4,512,512]{2,1,0:T(8,128)(2,1)} %get-tuple-element.35.far_in, ...), custom_call_target="tpu_custom_call" | custom-call | flops 3000000000 | bytes 8388608 | tf_op jit(solution)/shard_map/pallas_call | solution.py:476
  123.8 2.6 %collective-permute-start.8 = (bf16[256,1024]{1,0:T(8,128)(2,1)S(1)}, bf16[256,1024]{1,0:T(8,128)(2,1)S(1)}, u32[]{:S(2)}, u32[]{:S(2)}) collective-permute-start(bf16[256,1024]{1,0:T(8,128)(2,1)S(1)} %get-tuple-element.38), channel_id=1, source_target_pairs={{0,2},{2,0},{4,6},{6,4},{8,10},{10,8},{12,14},{14,12},{16,18},{18,... | collective-permute-start | bytes 1572872 | tf_op jit(solution)/shard_map/ppermute | solution.py:683
  126.4 1.5 collective-permute-done.8
  127.9 0.2 fusion.13
  128.2 2.3 %collective-permute-start.11 = (bf16[64,1024]{1,0:T(8,128)(2,1)S(1)}, bf16[64,1024]{1,0:T(8,128)(2,1)S(1)}, u32[]{:S(2)}, u32[]{:S(2)}) collective-permute-start(bf16[64,1024]{1,0:T(8,128)(2,1)S(1)} %get-tuple-element.53), channel_id=1, source_target_pairs={{0,8},{2,10},{4,12},{6,14},{8,0},{10,2},{12,4},{14,6},{16,24},{18,... | collective-permute-start | bytes 393224 | tf_op jit(solution)/shard_map/ppermute | solution.py:683
  130.5 0.2 collective-permute-start.10
  130.7 2.5 %collective-permute-start.9 = (bf16[64,1024]{1,0:T(8,128)(2,1)S(1)}, bf16[64,1024]{1,0:T(8,128)(2,1)S(1)}, u32[]{:S(2)}, u32[]{:S(2)}) collective-permute-start(bf16[64,1024]{1,0:T(8,128)(2,1)S(1)} %get-tuple-element.52), channel_id=1, source_target_pairs={{0,12},{2,14},{4,0},{6,2},{8,4},{10,6},{12,8},{14,10},{16,28},{18,... | collective-permute-start | bytes 393224 | tf_op jit(solution)/shard_map/ppermute | solution.py:683
  133.2 5.5 %shard_map.90 = (bf16[4,512,512]{2,1,0:T(8,128)(2,1)}, f32[2,8,512]{2,1,0:T(8,128)S(1)}) custom-call(bf16[4,512,512]{2,1,0:T(8,128)(2,1)} %shard_map.85.rows_ref.rows_in, bf16[4,512,512]{2,1,0:T(8,128)(2,1)} %get-tuple-element.39.own_in, bf16[512,512]{1,0:T(8,128)(2,1)} %get-tuple-element.36.attn_in, f32[8,128]{1,0:T(8,128)S(1)} %fusion.3.sums_ref, ...), custom_call_target="tpu_custom_call" | custom-call | flops 5000000000 | bytes 8388608 | tf_op jit(solution)/shard_map/pallas_call | solution.py:569
  138.7 0.0 collective-permute-done.11
  138.7 4.0 %collective-permute-done.10 = bf16[64,1024]{1,0:T(8,128)(2,1)S(1)} collective-permute-done((bf16[64,1024]{1,0:T(8,128)(2,1)S(1)}, bf16[64,1024]{1,0:T(8,128)(2,1)S(1)}, u32[]{:S(2)}, u32[]{:S(2)}) %collective-permute-start.10) | collective-permute-done | bytes 131104 | tf_op jit(solution)/shard_map/ppermute | solution.py:683
  142.7 0.0 collective-permute-done.9
  142.7 0.1 fusion.1
  142.8 0.3 collective-permute-start.12
  143.1 4.4 %collective-permute-done.12 = bf16[32,1024]{1,0:T(8,128)(2,1)S(1)} collective-permute-done((bf16[32,1024]{1,0:T(8,128)(2,1)S(1)}, bf16[32,1024]{1,0:T(8,128)(2,1)S(1)}, u32[]{:S(2)}, u32[]{:S(2)}) %collective-permute-start.12) | collective-permute-done | bytes 65568 | tf_op jit(solution)/shard_map/ppermute | solution.py:683
  147.6 3.5 %collective-permute-start.16 = (bf16[8,1024]{1,0:T(8,128)(2,1)S(1)}, bf16[8,1024]{1,0:T(8,128)(2,1)S(1)}, u32[]{:S(2)}, u32[]{:S(2)}) collective-permute-start(bf16[8,1024]{1,0:T(8,128)(2,1)S(1)} %reshape_squeeze.23), channel_id=1, source_target_pairs={{0,96},{2,226},{4,100},{6,230},{8,104},{10,234},{12,108},{14,238},... | collective-permute-start | bytes 49160 | tf_op jit(solution)/shard_map/ppermute | solution.py:737
  151.1 2.9 %collective-permute-start.15 = (bf16[8,1024]{1,0:T(8,128)(2,1)S(1)}, bf16[8,1024]{1,0:T(8,128)(2,1)S(1)}, u32[]{:S(2)}, u32[]{:S(2)}) collective-permute-start(bf16[8,1024]{1,0:T(8,128)(2,1)S(1)} %reshape_squeeze.22), channel_id=1, source_target_pairs={{0,64},{2,194},{4,68},{6,198},{8,72},{10,202},{12,76},{14,206},{16... | collective-permute-start | bytes 49160 | tf_op jit(solution)/shard_map/ppermute | solution.py:737
  153.9 0.8 collective-permute-start.14
  154.7 5.9 %collective-permute-start.13 = (bf16[8,1024]{1,0:T(8,128)(2,1)S(1)}, bf16[8,1024]{1,0:T(8,128)(2,1)S(1)}, u32[]{:S(2)}, u32[]{:S(2)}) collective-permute-start(bf16[8,1024]{1,0:T(8,128)(2,1)S(1)} %reshape_squeeze.20), channel_id=1, source_target_pairs={{0,0},{2,130},{4,4},{6,134},{8,8},{10,138},{12,12},{14,142},{16,16... | collective-permute-start | bytes 49160 | tf_op jit(solution)/shard_map/ppermute | solution.py:737
  160.6 0.0 collective-permute-done.16
  160.6 0.0 collective-permute-done.14
  160.7 3.8 %collective-permute-done.13 = bf16[8,1024]{1,0:T(8,128)(2,1)S(1)} collective-permute-done((bf16[8,1024]{1,0:T(8,128)(2,1)S(1)}, bf16[8,1024]{1,0:T(8,128)(2,1)S(1)}, u32[]{:S(2)}, u32[]{:S(2)}) %collective-permute-start.13) | collective-permute-done | bytes 16416 | tf_op jit(solution)/shard_map/ppermute | solution.py:737
  164.5 0.1 collective-permute-start.17
  164.6 1.2 collective-permute-done.17
  165.9 5.0 %shard_map.91 = (bf16[4096,128]{1,0:T(8,128)(2,1)}, bf16[4096,128]{1,0:T(8,128)(2,1)}, bf16[4096,128]{1,0:T(8,128)(2,1)}, bf16[4096,128]{1,0:T(8,128)(2,1)}) custom-call(bf16[128,16,512]{2,1,0:T(8,128)(2,1)S(1)} %all-to-all-done.3.recv_ref, bf16[4,512,512]{2,1,0:T(8,128)(2,1)} %get-tuple-element.43.fixed_in, bf16[2,16,512]{2,1,0:T(8,128)(2,1)S(1)} %pad.9.tail_ref), custom_call_target="tpu_custom_call" | custom-call | flops 2000000000 | bytes 8388608 | tf_op jit(solution)/shard_map/pallas_call | solution.py:643
  (36 shorter events, 0.5 us)
Async XLA Ops:
  2.8 16.3 %all-to-all-start = ((bf16[8,4,1024]{2,1,0:T(4,128)(2,1)}), bf16[8,4,1024]{2,1,0:T(4,128)(2,1)S(1)}, u32[]{:S(2)}, u32[]{:S(2)}) async-start(bf16[8,4,1024]{2,1,0:T(4,128)(2,1)} %broadcast_in_dim.12), calls=%async_computation | async-start | bytes 131072 | tf_op jit(solution)/shard_map/all_to_all | solution.py:700
  19.2 60.7 %all-to-all-start.1 = ((bf16[128,16,512]{2,1,0:T(8,128)(2,1)}), bf16[128,16,512]{2,1,0:T(8,128)(2,1)S(1)}, u32[]{:S(2)}, u32[]{:S(2)}) async-start(bf16[128,16,512]{2,1,0:T(8,128)(2,1)} %shard_map.84), calls=%async_computation.1 | async-start | bytes 4194304 | tf_op jit(solution)/shard_map/all_to_all | solution.py:760
  28.5 7.1 %collective-permute-start = (bf16[32,1024]{1,0:T(8,128)(2,1)S(1)}, bf16[32,1024]{1,0:T(8,128)(2,1)S(1)}, u32[]{:S(2)}, u32[]{:S(2)}) collective-permute-start(bf16[32,1024]{1,0:T(8,128)(2,1)S(1)} %reshape.117), channel_id=1, source_target_pairs={{0,16},{2,18},{4,20},{6,22},{8,24},{10,26},{12,28},{14,30},{16,0},... | collective-permute-start | bytes 196616 | tf_op jit(solution)/shard_map/ppermute | solution.py:683
  35.6 7.3 %collective-permute-start.1 = (bf16[64,1024]{1,0:T(8,128)(2,1)S(1)}, bf16[64,1024]{1,0:T(8,128)(2,1)S(1)}, u32[]{:S(2)}, u32[]{:S(2)}) collective-permute-start(bf16[64,1024]{1,0:T(8,128)(2,1)S(1)} %get-tuple-element.67), channel_id=1, source_target_pairs={{0,4},{2,6},{4,8},{6,10},{8,12},{10,14},{12,0},{14,2},{16,20},{18,... | collective-permute-start | bytes 393224 | tf_op jit(solution)/shard_map/ppermute | solution.py:683
  36.2 7.3 %collective-permute-start.2 = (bf16[64,1024]{1,0:T(8,128)(2,1)S(1)}, bf16[64,1024]{1,0:T(8,128)(2,1)S(1)}, u32[]{:S(2)}, u32[]{:S(2)}) collective-permute-start(bf16[64,1024]{1,0:T(8,128)(2,1)S(1)} %get-tuple-element.67), channel_id=1, source_target_pairs={{0,12},{2,14},{4,0},{6,2},{8,4},{10,6},{12,8},{14,10},{16,28},{18,... | collective-permute-start | bytes 393224 | tf_op jit(solution)/shard_map/ppermute | solution.py:683
  38.4 10.5 %collective-permute-start.3 = (bf16[64,1024]{1,0:T(8,128)(2,1)S(1)}, bf16[64,1024]{1,0:T(8,128)(2,1)S(1)}, u32[]{:S(2)}, u32[]{:S(2)}) collective-permute-start(bf16[64,1024]{1,0:T(8,128)(2,1)S(1)} %get-tuple-element.67), channel_id=1, source_target_pairs={{0,8},{2,10},{4,12},{6,14},{8,0},{10,2},{12,4},{14,6},{16,24},{18,... | collective-permute-start | bytes 393224 | tf_op jit(solution)/shard_map/ppermute | solution.py:683
  48.9 1.0 copy-start
  49.8 5.6 %collective-permute-start.4 = (bf16[256,1024]{1,0:T(8,128)(2,1)S(1)}, bf16[256,1024]{1,0:T(8,128)(2,1)S(1)}, u32[]{:S(2)}, u32[]{:S(2)}) collective-permute-start(bf16[256,1024]{1,0:T(8,128)(2,1)S(1)} %get-tuple-element.55), channel_id=1, source_target_pairs={{0,2},{2,0},{4,6},{6,4},{8,10},{10,8},{12,14},{14,12},{16,18},{18,... | collective-permute-start | bytes 1572872 | tf_op jit(solution)/shard_map/ppermute | solution.py:683
  66.5 4.4 %collective-permute-start.5 = (f32[128,8]{0,1:T(8,128)S(1)}, f32[128,8]{0,1:T(8,128)S(1)}, u32[]{:S(2)}, u32[]{:S(2)}) collective-permute-start(f32[128,8]{0,1:T(8,128)S(1)} %bitcast.70), channel_id=1, source_target_pairs={{0,1},{1,0},{2,3},{3,2},{4,5},{5,4},{6,7},{7,6},{8,9},{9,8},{10,11... | collective-permute-start | bytes 12296 | tf_op jit(solution)/shard_map/ppermute | solution.py:687
  82.8 17.6 %all-to-all-start.2 = ((f32[128,1,128]{2,1,0:T(1,128)}), f32[128,1,128]{2,1,0:T(1,128)S(1)}, u32[]{:S(2)}, u32[]{:S(2)}) async-start(f32[128,1,128]{2,1,0:T(1,128)} %get-tuple-element.34), calls=%async_computation.2 | async-start | bytes 131072 | tf_op jit(solution)/shard_map/all_to_all | solution.py:768
  89.9 5.1 %collective-permute-start.6 = (f32[128,8]{1,0:T(8,128)S(1)}, f32[128,8]{1,0:T(8,128)S(1)}, u32[]{:S(2)}, u32[]{:S(2)}) collective-permute-start(f32[128,8]{1,0:T(8,128)S(1)} %slice.65), channel_id=1, source_target_pairs={{0,1},{1,0},{2,3},{3,2},{4,5},{5,4},{6,7},{7,6},{8,9},{9,8},{10,11... | collective-permute-start | bytes 12296 | tf_op jit(solution)/shard_map/ppermute | solution.py:687
  105.2 60.7 %all-to-all-start.3 = ((bf16[128,16,512]{2,1,0:T(8,128)(2,1)}), bf16[128,16,512]{2,1,0:T(8,128)(2,1)S(1)}, u32[]{:S(2)}, u32[]{:S(2)}) async-start(bf16[128,16,512]{2,1,0:T(8,128)(2,1)} %shard_map.88), calls=%async_computation.3 | async-start | bytes 4194304 | tf_op jit(solution)/shard_map/all_to_all | solution.py:773
  113.1 4.7 %collective-permute-start.7 = (f32[8,128]{1,0:T(8,128)S(1)}, f32[8,128]{1,0:T(8,128)S(1)}, u32[]{:S(2)}, u32[]{:S(2)}) collective-permute-start(f32[8,128]{1,0:T(8,128)S(1)} %bitcast.72), channel_id=1, source_target_pairs={{0,1},{1,0},{2,3},{3,2},{4,5},{5,4},{6,7},{7,6},{8,9},{9,8},{10,11... | collective-permute-start | bytes 12296 | tf_op jit(solution)/shard_map/ppermute | solution.py:687
  123.8 4.1 %collective-permute-start.8 = (bf16[256,1024]{1,0:T(8,128)(2,1)S(1)}, bf16[256,1024]{1,0:T(8,128)(2,1)S(1)}, u32[]{:S(2)}, u32[]{:S(2)}) collective-permute-start(bf16[256,1024]{1,0:T(8,128)(2,1)S(1)} %get-tuple-element.38), channel_id=1, source_target_pairs={{0,2},{2,0},{4,6},{6,4},{8,10},{10,8},{12,14},{14,12},{16,18},{18,... | collective-permute-start | bytes 1572872 | tf_op jit(solution)/shard_map/ppermute | solution.py:683
  128.2 10.5 %collective-permute-start.11 = (bf16[64,1024]{1,0:T(8,128)(2,1)S(1)}, bf16[64,1024]{1,0:T(8,128)(2,1)S(1)}, u32[]{:S(2)}, u32[]{:S(2)}) collective-permute-start(bf16[64,1024]{1,0:T(8,128)(2,1)S(1)} %get-tuple-element.53), channel_id=1, source_target_pairs={{0,8},{2,10},{4,12},{6,14},{8,0},{10,2},{12,4},{14,6},{16,24},{18,... | collective-permute-start | bytes 393224 | tf_op jit(solution)/shard_map/ppermute | solution.py:683
  130.5 12.2 %collective-permute-start.10 = (bf16[64,1024]{1,0:T(8,128)(2,1)S(1)}, bf16[64,1024]{1,0:T(8,128)(2,1)S(1)}, u32[]{:S(2)}, u32[]{:S(2)}) collective-permute-start(bf16[64,1024]{1,0:T(8,128)(2,1)S(1)} %get-tuple-element.54), channel_id=1, source_target_pairs={{0,4},{2,6},{4,8},{6,10},{8,12},{10,14},{12,0},{14,2},{16,20},{18,... | collective-permute-start | bytes 393224 | tf_op jit(solution)/shard_map/ppermute | solution.py:683
  130.7 12.0 %collective-permute-start.9 = (bf16[64,1024]{1,0:T(8,128)(2,1)S(1)}, bf16[64,1024]{1,0:T(8,128)(2,1)S(1)}, u32[]{:S(2)}, u32[]{:S(2)}) collective-permute-start(bf16[64,1024]{1,0:T(8,128)(2,1)S(1)} %get-tuple-element.52), channel_id=1, source_target_pairs={{0,12},{2,14},{4,0},{6,2},{8,4},{10,6},{12,8},{14,10},{16,28},{18,... | collective-permute-start | bytes 393224 | tf_op jit(solution)/shard_map/ppermute | solution.py:683
  142.8 4.7 %collective-permute-start.12 = (bf16[32,1024]{1,0:T(8,128)(2,1)S(1)}, bf16[32,1024]{1,0:T(8,128)(2,1)S(1)}, u32[]{:S(2)}, u32[]{:S(2)}) collective-permute-start(bf16[32,1024]{1,0:T(8,128)(2,1)S(1)} %slice.109), channel_id=1, source_target_pairs={{0,16},{2,18},{4,20},{6,22},{8,24},{10,26},{12,28},{14,30},{16,0},... | collective-permute-start | bytes 196616 | tf_op jit(solution)/shard_map/ppermute | solution.py:683
  147.6 13.1 %collective-permute-start.16 = (bf16[8,1024]{1,0:T(8,128)(2,1)S(1)}, bf16[8,1024]{1,0:T(8,128)(2,1)S(1)}, u32[]{:S(2)}, u32[]{:S(2)}) collective-permute-start(bf16[8,1024]{1,0:T(8,128)(2,1)S(1)} %reshape_squeeze.23), channel_id=1, source_target_pairs={{0,96},{2,226},{4,100},{6,230},{8,104},{10,234},{12,108},{14,238},... | collective-permute-start | bytes 49160 | tf_op jit(solution)/shard_map/ppermute | solution.py:737
  151.1 9.6 %collective-permute-start.15 = (bf16[8,1024]{1,0:T(8,128)(2,1)S(1)}, bf16[8,1024]{1,0:T(8,128)(2,1)S(1)}, u32[]{:S(2)}, u32[]{:S(2)}) collective-permute-start(bf16[8,1024]{1,0:T(8,128)(2,1)S(1)} %reshape_squeeze.22), channel_id=1, source_target_pairs={{0,64},{2,194},{4,68},{6,198},{8,72},{10,202},{12,76},{14,206},{16... | collective-permute-start | bytes 49160 | tf_op jit(solution)/shard_map/ppermute | solution.py:737
  153.9 6.7 %collective-permute-start.14 = (bf16[8,1024]{1,0:T(8,128)(2,1)S(1)}, bf16[8,1024]{1,0:T(8,128)(2,1)S(1)}, u32[]{:S(2)}, u32[]{:S(2)}) collective-permute-start(bf16[8,1024]{1,0:T(8,128)(2,1)S(1)} %reshape_squeeze.21), channel_id=1, source_target_pairs={{0,32},{2,162},{4,36},{6,166},{8,40},{10,170},{12,44},{14,174},{16... | collective-permute-start | bytes 49160 | tf_op jit(solution)/shard_map/ppermute | solution.py:737
  154.7 9.8 %collective-permute-start.13 = (bf16[8,1024]{1,0:T(8,128)(2,1)S(1)}, bf16[8,1024]{1,0:T(8,128)(2,1)S(1)}, u32[]{:S(2)}, u32[]{:S(2)}) collective-permute-start(bf16[8,1024]{1,0:T(8,128)(2,1)S(1)} %reshape_squeeze.20), channel_id=1, source_target_pairs={{0,0},{2,130},{4,4},{6,134},{8,8},{10,138},{12,12},{14,142},{16,16... | collective-permute-start | bytes 49160 | tf_op jit(solution)/shard_map/ppermute | solution.py:737
  164.5 1.3 collective-permute-start.17

commit v9 on v8

--- a/solution.py
+++ b/solution.py
@@ -152,6 +152,31 @@
     )(*arrays)
 
 
+def pack_summaries_kernel(key_ref, value_ref, out_ref):
+    row, col = iotas((8, 32))
+    parts = []
+    for head in range(HEADS):
+        pick = one_hot(col == row * 2 * HEADS + 2 * head + 1)
+        parts += [dot(pick, ref[...])[:SUMM] for ref in (key_ref, value_ref)]
+    rows = jnp.concatenate(parts, 1).astype(BF16)
+    for z in range(out_ref.shape[0]):
+        out_ref[z] = rows
+
+
+def pack_summaries(keys, values):
+    last = spec((8 * SUMM, HD), BLOCK // SUMM - 1, 0)
+    shape = (PARTS[0], SUMM, 2 * WIDTH)
+    return call(
+        pack_summaries_kernel,
+        1,
+        [last, last],
+        spec(shape, 0, 0, 0),
+        jax.ShapeDtypeStruct(shape, BF16),
+        10**6,
+        2**17,
+    )(in_hbm(keys), in_hbm(values))
+
+
 def pack_fixed_kernel(q_ref, k_ref, v_ref, c_ref, out_ref):
     row, col = iotas((64, 128))
     pick = one_hot(col == ((row & 15) * HEADS + (row >> 4)) * 2 + 1)
@@ -590,7 +615,7 @@
     )(*[in_hbm(array) for array in (rows, own, attn)], sums, in_hbm(far_query))
 
 
-def unpack_kernel(recv_ref, fixed_in, tail_ref, *refs):
+def unpack_kernel(recv_ref, fixed_in, parts_ref, moved_ref, tails_ref, *refs):
     outs, fixed_ref, out_ref, in_sem, out_sem = refs[:4], refs[4], refs[5], refs[6], refs[7]
     parts = 4
     size = BLOCK // parts
@@ -608,6 +633,13 @@
     fixed = 256 + array * 64 + head * 16 + token
     pick = one_hot(col == jnp.where(kind == 0, strided, fixed))
     end = lax.broadcasted_iota(jnp.int32, (16, WIDTH), 0) >= 16 - SUMM
+    totals = parts_ref[...] + moved_ref[...].astype(F32)
+    tails = []
+    for array in range(2):
+        part = [totals[:, n * HD : (n + 1) * HD] for n in range(array, 2 * HEADS, 2)]
+        part = jnp.concatenate(part, 1) + tails_ref[array, 8 - SUMM :]
+        part = jnp.concatenate([jnp.zeros((16 - SUMM, WIDTH), F32), part], 0)
+        tails.append(part.astype(BF16))
     for at in range(0, 32, 2):
         if at * 16 % size == 0:
             copies[at * 16 // size].wait()
@@ -617,7 +649,7 @@
             fixed = [fixed_ref[array, tile : tile + 16] for array in range(4)]
             if tile == BLOCK - 16:
                 for array in (2, 3):
-                    fixed[array] = jnp.where(end, tail_ref[array - 2], fixed[array])
+                    fixed[array] = jnp.where(end, tails[array - 2], fixed[array])
             heads = [slice(head * HD, (head + 1) * HD) for head in range(HEADS)]
             rows = [recv_ref[4 * n + home, :, head] for home in range(4) for head in heads]
             rows += [part[:, head] for part in fixed for head in heads]
@@ -639,11 +671,13 @@
         copy.wait()
 
 
-def unpack(recv, fixed, tail):
+def unpack(recv, fixed, parts, moved, tails):
     rows = call(
         unpack_kernel,
         1,
-        [spec((NB, 16, WIDTH), 0, 0, 0), IN_HBM, spec((2, 16, WIDTH), 0, 0, 0)],
+        [spec((NB, 16, WIDTH), 0, 0, 0), IN_HBM]
+        + [spec((SUMM, 2 * WIDTH), 0, 0)] * 2
+        + [spec((2, 8, WIDTH), 0, 0, 0)],
         [IN_HBM] * 4,
         [jax.ShapeDtypeStruct((BLOCK * 8, HD), BF16)] * 4,
         2 * 10**9,
@@ -655,7 +689,7 @@
             pltpu.SemaphoreType.DMA((4, 4)),
         ],
         vmem=VMEM6,
-    )(recv, in_hbm(fixed), tail)
+    )(recv, in_hbm(fixed), parts, moved, tails)
     return tuple(unflat(array) for array in rows)
 
 
@@ -692,11 +726,10 @@
 SLAB = 2 * WIDTH
 
 
-def gather_along_z(own, me):
+def gather_along_z(sent, me):
     size = PARTS[Z]
     step = NB // size
     groups = [[at + step * z for z in range(size)] for at in range(step)]
-    sent = jnp.broadcast_to(own[None], (size,) + own.shape)
     held = lax.all_to_all(sent, "seq", 0, 0, axis_index_groups=groups, tiled=True)
     held = jnp.concatenate([held, held], 0)
     first = (me // step + 4 * (me % 2)) % size
@@ -736,7 +769,7 @@
             perm.append((source, joined(coords)))
         moved.append(lax.ppermute(sent[:, n].reshape(2 * SUMM, SLAB), "seq", perm))
     parts = add_up(0.0, moved)
-    return add_up(parts[:SUMM], [shift(parts[SUMM:].astype(BF16), CORE, 1)])
+    return parts[:SUMM], shift(parts[SUMM:].astype(BF16), CORE, 1)
 
 
 def slot_blocks(me):
@@ -753,9 +786,7 @@
     me = lax.axis_index("seq")
     arrays = tuple(flat(array) for array in (queries, key_rows, value_rows, cotangent))
     send = pack_strided(arrays)
-    tails = [a[BLOCK - SUMM :, 1].reshape(SUMM, HEADS, 1, HD) for a in (key_rows, value_rows)]
-    own_summ = jnp.concatenate(tails, 2).reshape(SUMM, 2 * WIDTH)
-    summ = gather_along_z(own_summ, me)
+    summ = gather_along_z(pack_summaries(arrays[1], arrays[2]), me)
     send, summ = lax.optimization_barrier((send, summ))
     recv = lax.all_to_all(send, "seq", 0, 0, tiled=True)
     summ = gather_summaries(summ)
@@ -775,11 +806,8 @@
     fixed_out, tails = fixed_backward(rows, own_prob, fixed_attn, block_sums, far_query)
     parts = scatter_along_y(scatter_along_core(kept, sent))
     parts, fixed_out, tails = lax.optimization_barrier((parts, fixed_out, tails))
-    totals = scatter_summaries(parts).reshape(SUMM, HEADS, 2, HD)
-    totals = totals.transpose(2, 0, 1, 3).reshape(2, SUMM, WIDTH)
-    totals = (tails[:, 8 - SUMM :] + totals).astype(BF16)
-    tail = jnp.pad(totals, ((0, 0), (16 - SUMM, 0), (0, 0)))
-    return unpack(recv_back, fixed_out, tail)
+    parts, moved = scatter_summaries(parts)
+    return unpack(recv_back, fixed_out, parts, moved, tails)
 
 
 def solution(mesh):

time: 172 us -> 171 us (level)
  local copies, waits for them, and re-layouts: 6.53 us -> 4.31 us
    pallas_call x1 -> x2, Pallas kernels: 5.04 us -> 6.54 us  [the longest x1 5.04 us: unpack(): call(unpack_kernel, 1, [spec((NB, 16, WIDTH), 0, 0, 0), IN_HBM] + [spec((...]
where the time goes in v9:
time: 171 us; the launch traced here: 170 us
  starting transfers between devices  67.7 us (40%)
  waiting for transfers between devices  54.7 us (32%)
  Pallas kernels  41.9 us (25%)
  local copies, waits for them, and re-layouts  4.31 us (3%)
    ppermute x11, waiting for transfers between devices, shift(): return lax.ppermute(array, 'seq', perm)  26.2 us
    ppermute x11, starting transfers between devices, shift(): return lax.ppermute(array, 'seq', perm)  14.3 us
    ppermute x4, starting transfers between devices, scatter_summaries(): moved.append(lax.ppermute(sent[:, n].reshape(2 * SUMM, SLAB), 'seq', perm))  13 us
    all_to_all x1, starting transfers between devices, shards(): recv = lax.all_to_all(send, 'seq', 0, 0, tiled=True)  9.33 us
    pallas_call x1, Pallas kernels, fixed_forward(): call(fixed_forward_kernel, HEADS, [spec((4, BLOCK, HD), 0, 0, 'i'), spec(...  9.18 us
    all_to_all x1, starting transfers between devices, gather_along_z(): lax.all_to_all(sent, 'seq', 0, 0, axis_index_groups=groups, tiled=True)  9.01 us
    all_to_all x1, waiting for transfers between devices, shards(): recv = lax.all_to_all(send, 'seq', 0, 0, tiled=True)  8.92 us
    all_to_all x1, starting transfers between devices, shards(): recv_back = lax.all_to_all(send_back, 'seq', 0, 0, tiled=True)  7.65 us
  transfers between devices with their start and end apart: 22, of which 15 were waited for; matrix products, arithmetic and copies ran while one was open for 2% of the time, Pallas kernels for 16%

profile of v9, /device:TPU:1, one launch (start us, length us, event | category | flops | bytes accessed | tf_op | source)
XLA Modules:
  0.0 170.1 jit_solution(12658655173116863220)
XLA Ops:
  0.6 1.5 shard_map.85
  2.1 9.0 %all-to-all-start = ((bf16[8,4,1024]{2,1,0:T(4,128)(2,1)}), bf16[8,4,1024]{2,1,0:T(4,128)(2,1)S(1)}, u32[]{:S(2)}, u32[]{:S(2)}) async-start(bf16[8,4,1024]{2,1,0:T(4,128)(2,1)} %shard_map.85), calls=%async_computation | async-start | bytes 131072 | tf_op jit(solution)/shard_map/all_to_all | solution.py:733
  11.1 3.5 %shard_map.84 = bf16[128,16,512]{2,1,0:T(8,128)(2,1)} custom-call(bf16[4096,128]{1,0:T(8,128)(2,1)} %bitcast.81, bf16[4096,128]{1,0:T(8,128)(2,1)} %bitcast.76, bf16[4096,128]{1,0:T(8,128)(2,1)} %bitcast.79, bf16[4096,128]{1,0:T(8,128)(2,1)} %bitcast.83), custom_call_target="tpu_custom_call" | custom-call | flops 1000000000 | bytes 6291456 | tf_op jit(solution)/shard_map/pallas_call | solution.py:138
  14.6 3.8 %all-to-all-done = bf16[8,4,1024]{2,1,0:T(4,128)(2,1)S(1)} async-done(((bf16[8,4,1024]{2,1,0:T(4,128)(2,1)}), bf16[8,4,1024]{2,1,0:T(4,128)(2,1)S(1)}, u32[]{:S(2)}, u32[]{:S(2)}) %all-to-all-start) | async-done | bytes 65568 | tf_op jit(solution)/shard_map/all_to_all | solution.py:733
  18.4 0.1 fusion.2
  18.5 9.3 %all-to-all-start.1 = ((bf16[128,16,512]{2,1,0:T(8,128)(2,1)}), bf16[128,16,512]{2,1,0:T(8,128)(2,1)S(1)}, u32[]{:S(2)}, u32[]{:S(2)}) async-start(bf16[128,16,512]{2,1,0:T(8,128)(2,1)} %shard_map.84), calls=%async_computation.1 | async-start | bytes 4194304 | tf_op jit(solution)/shard_map/all_to_all | solution.py:791
  27.8 1.5 collective-permute-start
  29.3 5.6 %collective-permute-done = bf16[32,1024]{1,0:T(8,128)(2,1)S(1)} collective-permute-done((bf16[32,1024]{1,0:T(8,128)(2,1)S(1)}, bf16[32,1024]{1,0:T(8,128)(2,1)S(1)}, u32[]{:S(2)}, u32[]{:S(2)}) %collective-permute-start) | collective-permute-done | bytes 65568 | tf_op jit(solution)/shard_map/ppermute | solution.py:717
  34.9 0.6 collective-permute-start.1
  35.5 2.1 %collective-permute-start.2 = (bf16[64,1024]{1,0:T(8,128)(2,1)S(1)}, bf16[64,1024]{1,0:T(8,128)(2,1)S(1)}, u32[]{:S(2)}, u32[]{:S(2)}) collective-permute-start(bf16[64,1024]{1,0:T(8,128)(2,1)S(1)} %get-tuple-element.67), channel_id=1, source_target_pairs={{0,12},{2,14},{4,0},{6,2},{8,4},{10,6},{12,8},{14,10},{16,28},{18,... | collective-permute-start | bytes 393224 | tf_op jit(solution)/shard_map/ppermute | solution.py:717
  37.7 0.8 collective-permute-start.3
  38.5 3.7 %collective-permute-done.1 = bf16[64,1024]{1,0:T(8,128)(2,1)S(1)} collective-permute-done((bf16[64,1024]{1,0:T(8,128)(2,1)S(1)}, bf16[64,1024]{1,0:T(8,128)(2,1)S(1)}, u32[]{:S(2)}, u32[]{:S(2)}) %collective-permute-start.1) | collective-permute-done | bytes 131104 | tf_op jit(solution)/shard_map/ppermute | solution.py:717
  42.2 0.6 collective-permute-done.2
  42.8 5.3 %collective-permute-done.3 = bf16[64,1024]{1,0:T(8,128)(2,1)S(1)} collective-permute-done((bf16[64,1024]{1,0:T(8,128)(2,1)S(1)}, bf16[64,1024]{1,0:T(8,128)(2,1)S(1)}, u32[]{:S(2)}, u32[]{:S(2)}) %collective-permute-start.3) | collective-permute-done | bytes 131104 | tf_op jit(solution)/shard_map/ppermute | solution.py:717
  48.2 0.0 copy-start
  48.2 1.0 copy-done
  49.1 1.2 collective-permute-start.4
  50.4 0.1 broadcast_in_dim.4
  50.4 0.7 broadcast_in_dim_reshape.3.seen_ref
  51.1 3.6 %shard_map.86.rows_ref.rows_in = bf16[4,512,512]{2,1,0:T(8,128)(2,1)} custom-call(bf16[4096,128]{1,0:T(8,128)(2,1)} %bitcast.82, bf16[4096,128]{1,0:T(8,128)(2,1)} %bitcast.77, bf16[4096,128]{1,0:T(8,128)(2,1)} %bitcast.80, bf16[4096,128]{1,0:T(8,128)(2,1)} %bitcast.84), custom_call_target="tpu_custom_call" | custom-call | flops 1000000000 | bytes 6291456 | tf_op jit(solution)/shard_map/pallas_call | solution.py:194
  54.7 0.0 collective-permute-done.4
  54.7 0.8 constant_dynamic-update-slice_fusion.7.summ_ref.summ_in
  55.6 9.2 %shard_map.87 = (bf16[512,512]{1,0:T(8,128)(2,1)}, bf16[4,512,512]{2,1,0:T(8,128)(2,1)}, bf16[4,512,512]{2,1,0:T(8,128)(2,1)}, f32[512,8]{1,0:T(8,128)}) custom-call(bf16[4,512,512]{2,1,0:T(8,128)(2,1)} %shard_map.86.rows_ref.rows_in, bf16[512,1024]{1,0:T(8,128)(2,1)} %constant_dynamic-update-slice_fusion.7.summ_ref.summ_in, ...), custom_call_target="tpu_custom_call" | custom-call | flops 4000000000 | bytes 4194304 | tf_op jit(solution)/shard_map/pallas_call | solution.py:241
  64.7 1.0 copy.45
  65.8 2.5 %collective-permute-start.5 = (f32[128,8]{0,1:T(8,128)S(1)}, f32[128,8]{0,1:T(8,128)S(1)}, u32[]{:S(2)}, u32[]{:S(2)}) collective-permute-start(f32[128,8]{0,1:T(8,128)S(1)} %bitcast.86), channel_id=1, source_target_pairs={{0,1},{1,0},{2,3},{3,2},{4,5},{5,4},{6,7},{7,6},{8,9},{9,8},{10,11... | collective-permute-start | bytes 12296 | tf_op jit(solution)/shard_map/ppermute | solution.py:721
  68.3 1.8 %collective-permute-done.5 = f32[128,8]{0,1:T(8,128)S(1)} collective-permute-done((f32[128,8]{0,1:T(8,128)S(1)}, f32[128,8]{0,1:T(8,128)S(1)}, u32[]{:S(2)}, u32[]{:S(2)}) %collective-permute-start.5) | collective-permute-done | bytes 4128 | tf_op jit(solution)/shard_map/ppermute | solution.py:721
  70.1 0.1 copy.61
  70.3 8.9 %all-to-all-done.1.recv_ref = bf16[128,16,512]{2,1,0:T(8,128)(2,1)S(1)} async-done(((bf16[128,16,512]{2,1,0:T(8,128)(2,1)}), bf16[128,16,512]{2,1,0:T(8,128)(2,1)S(1)}, u32[]{:S(2)}, u32[]{:S(2)}) %all-to-all-start.1) | async-done | bytes 2097184 | tf_op jit(solution)/shard_map/all_to_all | solution.py:791
  79.2 2.9 %shard_map.88 = (bf16[4,3,4,128,128]{4,3,2,1,0:T(8,128)(2,1)}, bf16[4,4,128,128]{3,2,1,0:T(8,128)(2,1)}, bf16[4,2,4,128,128]{4,3,2,1,0:T(8,128)(2,1)S(1)}, f32[128,128]{1,0:T(8,128)S(1)}, f32[128,1,128]{2,1,0:T(1,128)}) custom-call(bf16[128,16,512]{2,1,0:T(8,128)(2,1)S(1)} %all-to-all-done.1.recv_ref, f32[128,128]{1,0:T(8,128)S(1)} %pad.4.clone.fixed_ref), custom_call_target="tpu_custom_call" | custom-call | flops 1000000000 | bytes 6291456 | tf_op jit(solution)/shard_map/pallas_call | solution.py:312
  82.1 6.9 %all-to-all-start.2 = ((f32[128,1,128]{2,1,0:T(1,128)}), f32[128,1,128]{2,1,0:T(1,128)S(1)}, u32[]{:S(2)}, u32[]{:S(2)}) async-start(f32[128,1,128]{2,1,0:T(1,128)} %get-tuple-element.34), calls=%async_computation.2 | async-start | bytes 131072 | tf_op jit(solution)/shard_map/all_to_all | solution.py:799
  88.9 0.1 slice.54
  89.0 2.5 %collective-permute-start.6 = (f32[128,8]{1,0:T(8,128)S(1)}, f32[128,8]{1,0:T(8,128)S(1)}, u32[]{:S(2)}, u32[]{:S(2)}) collective-permute-start(f32[128,8]{1,0:T(8,128)S(1)} %slice.54), channel_id=1, source_target_pairs={{0,1},{1,0},{2,3},{3,2},{4,5},{5,4},{6,7},{7,6},{8,9},{9,8},{10,11... | collective-permute-start | bytes 12296 | tf_op jit(solution)/shard_map/ppermute | solution.py:721
  91.5 2.6 %collective-permute-done.6.other_ref = f32[128,8]{1,0:T(8,128)S(1)} collective-permute-done((f32[128,8]{1,0:T(8,128)S(1)}, f32[128,8]{1,0:T(8,128)S(1)}, u32[]{:S(2)}, u32[]{:S(2)}) %collective-permute-start.6) | collective-permute-done | bytes 4128 | tf_op jit(solution)/shard_map/ppermute | solution.py:721
  94.1 5.4 %all-to-all-done.2.recv_ref = f32[128,1,128]{2,1,0:T(1,128)S(1)} async-done(((f32[128,1,128]{2,1,0:T(1,128)}), f32[128,1,128]{2,1,0:T(1,128)S(1)}, u32[]{:S(2)}, u32[]{:S(2)}) %all-to-all-start.2) | async-done | bytes 65568 | tf_op jit(solution)/shard_map/all_to_all | solution.py:799
  99.5 4.9 %shard_map.89 = bf16[128,16,512]{2,1,0:T(8,128)(2,1)} custom-call(bf16[4,3,4,128,128]{4,3,2,1,0:T(8,128)(2,1)} %get-tuple-element.30.keys_in, bf16[4,4,128,128]{3,2,1,0:T(8,128)(2,1)} %get-tuple-element.31.prob_in, bf16[4,2,4,128,128]{4,3,2,1,0:T(8,128)(2,1)S(1)} %get-tuple-element.32.grp_ref, f32[128,128]{1,0:T(8,128)S(1)} %get-tuple-element.33.sums_ref, ...), custom_call_target="tpu_custom_call" | custom-call | flops 1000000000 | bytes 6291456 | tf_op jit(solution)/shard_map/pallas_call | solution.py:423
  104.3 7.7 %all-to-all-start.3 = ((bf16[128,16,512]{2,1,0:T(8,128)(2,1)}), bf16[128,16,512]{2,1,0:T(8,128)(2,1)S(1)}, u32[]{:S(2)}, u32[]{:S(2)}) async-start(bf16[128,16,512]{2,1,0:T(8,128)(2,1)} %shard_map.89), calls=%async_computation.3 | async-start | bytes 4194304 | tf_op jit(solution)/shard_map/all_to_all | solution.py:804
  112.0 0.2 slice.73
  112.3 2.5 %collective-permute-start.7 = (f32[8,128]{1,0:T(8,128)S(1)}, f32[8,128]{1,0:T(8,128)S(1)}, u32[]{:S(2)}, u32[]{:S(2)}) collective-permute-start(f32[8,128]{1,0:T(8,128)S(1)} %bitcast.88), channel_id=1, source_target_pairs={{0,1},{1,0},{2,3},{3,2},{4,5},{5,4},{6,7},{7,6},{8,9},{9,8},{10,11... | collective-permute-start | bytes 12296 | tf_op jit(solution)/shard_map/ppermute | solution.py:721
  114.8 2.2 %collective-permute-done.7 = f32[8,128]{1,0:T(8,128)S(1)} collective-permute-done((f32[8,128]{1,0:T(8,128)S(1)}, f32[8,128]{1,0:T(8,128)S(1)}, u32[]{:S(2)}, u32[]{:S(2)}) %collective-permute-start.7) | collective-permute-done | bytes 4128 | tf_op jit(solution)/shard_map/ppermute | solution.py:721
  117.0 5.9 %shard_map.90 = (f32[512,512]{1,0:T(8,128)}, f32[256,1024]{1,0:T(8,128)S(1)}, bf16[256,1024]{1,0:T(8,128)(2,1)S(1)}) custom-call(bf16[4,512,512]{2,1,0:T(8,128)(2,1)} %shard_map.86.rows_ref.rows_in, bf16[512,1024]{1,0:T(8,128)(2,1)} %constant_dynamic-update-slice_fusion.7.summ_ref.summ_in, bf16[4,512,512]{2,1,0:T(8,128)(2,1)} %get-tuple-element.35.far_in, ...), custom_call_target="tpu_custom_call" | custom-call | flops 3000000000 | bytes 8388608 | tf_op jit(solution)/shard_map/pallas_call | solution.py:501
  122.9 2.6 %collective-permute-start.8 = (bf16[256,1024]{1,0:T(8,128)(2,1)S(1)}, bf16[256,1024]{1,0:T(8,128)(2,1)S(1)}, u32[]{:S(2)}, u32[]{:S(2)}) collective-permute-start(bf16[256,1024]{1,0:T(8,128)(2,1)S(1)} %get-tuple-element.38), channel_id=1, source_target_pairs={{0,2},{2,0},{4,6},{6,4},{8,10},{10,8},{12,14},{14,12},{16,18},{18,... | collective-permute-start | bytes 1572872 | tf_op jit(solution)/shard_map/ppermute | solution.py:717
  125.5 1.5 collective-permute-done.8
  127.0 0.2 fusion.13
  127.3 2.3 %collective-permute-start.11 = (bf16[64,1024]{1,0:T(8,128)(2,1)S(1)}, bf16[64,1024]{1,0:T(8,128)(2,1)S(1)}, u32[]{:S(2)}, u32[]{:S(2)}) collective-permute-start(bf16[64,1024]{1,0:T(8,128)(2,1)S(1)} %get-tuple-element.53), channel_id=1, source_target_pairs={{0,8},{2,10},{4,12},{6,14},{8,0},{10,2},{12,4},{14,6},{16,24},{18,... | collective-permute-start | bytes 393224 | tf_op jit(solution)/shard_map/ppermute | solution.py:717
  129.6 0.2 collective-permute-start.10
  129.9 2.4 %collective-permute-start.9 = (bf16[64,1024]{1,0:T(8,128)(2,1)S(1)}, bf16[64,1024]{1,0:T(8,128)(2,1)S(1)}, u32[]{:S(2)}, u32[]{:S(2)}) collective-permute-start(bf16[64,1024]{1,0:T(8,128)(2,1)S(1)} %get-tuple-element.52), channel_id=1, source_target_pairs={{0,12},{2,14},{4,0},{6,2},{8,4},{10,6},{12,8},{14,10},{16,28},{18,... | collective-permute-start | bytes 393224 | tf_op jit(solution)/shard_map/ppermute | solution.py:717
  132.3 5.5 %shard_map.91 = (bf16[4,512,512]{2,1,0:T(8,128)(2,1)}, f32[2,8,512]{2,1,0:T(8,128)S(1)}) custom-call(bf16[4,512,512]{2,1,0:T(8,128)(2,1)} %shard_map.86.rows_ref.rows_in, bf16[4,512,512]{2,1,0:T(8,128)(2,1)} %get-tuple-element.39.own_in, bf16[512,512]{1,0:T(8,128)(2,1)} %get-tuple-element.36.attn_in, f32[8,128]{1,0:T(8,128)S(1)} %fusion.3.sums_ref, ...), custom_call_target="tpu_custom_call" | custom-call | flops 5000000000 | bytes 8388608 | tf_op jit(solution)/shard_map/pallas_call | solution.py:594
  137.8 0.0 collective-permute-done.11
  137.8 4.0 %collective-permute-done.10 = bf16[64,1024]{1,0:T(8,128)(2,1)S(1)} collective-permute-done((bf16[64,1024]{1,0:T(8,128)(2,1)S(1)}, bf16[64,1024]{1,0:T(8,128)(2,1)S(1)}, u32[]{:S(2)}, u32[]{:S(2)}) %collective-permute-start.10) | collective-permute-done | bytes 131104 | tf_op jit(solution)/shard_map/ppermute | solution.py:717
  141.8 0.0 collective-permute-done.9
  141.8 0.1 fusion.1
  141.9 0.4 collective-permute-start.12
  142.3 4.3 %collective-permute-done.12 = bf16[32,1024]{1,0:T(8,128)(2,1)S(1)} collective-permute-done((bf16[32,1024]{1,0:T(8,128)(2,1)S(1)}, bf16[32,1024]{1,0:T(8,128)(2,1)S(1)}, u32[]{:S(2)}, u32[]{:S(2)}) %collective-permute-start.12) | collective-permute-done | bytes 65568 | tf_op jit(solution)/shard_map/ppermute | solution.py:717
  146.7 3.4 %collective-permute-start.16 = (bf16[8,1024]{1,0:T(8,128)(2,1)S(1)}, bf16[8,1024]{1,0:T(8,128)(2,1)S(1)}, u32[]{:S(2)}, u32[]{:S(2)}) collective-permute-start(bf16[8,1024]{1,0:T(8,128)(2,1)S(1)} %reshape_squeeze.15), channel_id=1, source_target_pairs={{0,96},{2,226},{4,100},{6,230},{8,104},{10,234},{12,108},{14,238},... | collective-permute-start | bytes 49160 | tf_op jit(solution)/shard_map/ppermute | solution.py:770
  150.1 2.9 %collective-permute-start.15 = (bf16[8,1024]{1,0:T(8,128)(2,1)S(1)}, bf16[8,1024]{1,0:T(8,128)(2,1)S(1)}, u32[]{:S(2)}, u32[]{:S(2)}) collective-permute-start(bf16[8,1024]{1,0:T(8,128)(2,1)S(1)} %reshape_squeeze.14), channel_id=1, source_target_pairs={{0,64},{2,194},{4,68},{6,198},{8,72},{10,202},{12,76},{14,206},{16... | collective-permute-start | bytes 49160 | tf_op jit(solution)/shard_map/ppermute | solution.py:770
  153.1 0.8 collective-permute-start.14
  153.9 5.9 %collective-permute-start.13 = (bf16[8,1024]{1,0:T(8,128)(2,1)S(1)}, bf16[8,1024]{1,0:T(8,128)(2,1)S(1)}, u32[]{:S(2)}, u32[]{:S(2)}) collective-permute-start(bf16[8,1024]{1,0:T(8,128)(2,1)S(1)} %reshape_squeeze.12), channel_id=1, source_target_pairs={{0,0},{2,130},{4,4},{6,134},{8,8},{10,138},{12,12},{14,142},{16,16... | collective-permute-start | bytes 49160 | tf_op jit(solution)/shard_map/ppermute | solution.py:770
  159.7 0.0 collective-permute-done.16
  159.8 0.0 collective-permute-done.15
  159.8 0.0 collective-permute-done.14
  159.8 3.8 %collective-permute-done.13 = bf16[8,1024]{1,0:T(8,128)(2,1)S(1)} collective-permute-done((bf16[8,1024]{1,0:T(8,128)(2,1)S(1)}, bf16[8,1024]{1,0:T(8,128)(2,1)S(1)}, u32[]{:S(2)}, u32[]{:S(2)}) %collective-permute-start.13) | collective-permute-done | bytes 16416 | tf_op jit(solution)/shard_map/ppermute | solution.py:770
  163.7 0.1 collective-permute-start.17
  163.8 1.1 collective-permute-done.17.moved_ref
  164.9 5.0 %shard_map.92 = (bf16[4096,128]{1,0:T(8,128)(2,1)}, bf16[4096,128]{1,0:T(8,128)(2,1)}, bf16[4096,128]{1,0:T(8,128)(2,1)}, bf16[4096,128]{1,0:T(8,128)(2,1)}) custom-call(bf16[128,16,512]{2,1,0:T(8,128)(2,1)S(1)} %all-to-all-done.3.recv_ref, bf16[4,512,512]{2,1,0:T(8,128)(2,1)} %get-tuple-element.43.fixed_in, f32[4,1024]{1,0:T(4,128)S(1)} %slice.83.parts_ref, ...), custom_call_target="tpu_custom_call" | custom-call | flops 2000000000 | bytes 8388608 | tf_op jit(solution)/shard_map/pallas_call | solution.py:675
  (24 shorter events, 0.4 us)
Async XLA Ops:
  2.1 16.3 %all-to-all-start = ((bf16[8,4,1024]{2,1,0:T(4,128)(2,1)}), bf16[8,4,1024]{2,1,0:T(4,128)(2,1)S(1)}, u32[]{:S(2)}, u32[]{:S(2)}) async-start(bf16[8,4,1024]{2,1,0:T(4,128)(2,1)} %shard_map.85), calls=%async_computation | async-start | bytes 131072 | tf_op jit(solution)/shard_map/all_to_all | solution.py:733
  18.5 60.7 %all-to-all-start.1 = ((bf16[128,16,512]{2,1,0:T(8,128)(2,1)}), bf16[128,16,512]{2,1,0:T(8,128)(2,1)S(1)}, u32[]{:S(2)}, u32[]{:S(2)}) async-start(bf16[128,16,512]{2,1,0:T(8,128)(2,1)} %shard_map.84), calls=%async_computation.1 | async-start | bytes 4194304 | tf_op jit(solution)/shard_map/all_to_all | solution.py:791
  27.8 7.1 %collective-permute-start = (bf16[32,1024]{1,0:T(8,128)(2,1)S(1)}, bf16[32,1024]{1,0:T(8,128)(2,1)S(1)}, u32[]{:S(2)}, u32[]{:S(2)}) collective-permute-start(bf16[32,1024]{1,0:T(8,128)(2,1)S(1)} %reshape.110), channel_id=1, source_target_pairs={{0,16},{2,18},{4,20},{6,22},{8,24},{10,26},{12,28},{14,30},{16,0},... | collective-permute-start | bytes 196616 | tf_op jit(solution)/shard_map/ppermute | solution.py:717
  34.9 7.3 %collective-permute-start.1 = (bf16[64,1024]{1,0:T(8,128)(2,1)S(1)}, bf16[64,1024]{1,0:T(8,128)(2,1)S(1)}, u32[]{:S(2)}, u32[]{:S(2)}) collective-permute-start(bf16[64,1024]{1,0:T(8,128)(2,1)S(1)} %get-tuple-element.67), channel_id=1, source_target_pairs={{0,4},{2,6},{4,8},{6,10},{8,12},{10,14},{12,0},{14,2},{16,20},{18,... | collective-permute-start | bytes 393224 | tf_op jit(solution)/shard_map/ppermute | solution.py:717
  35.5 7.3 %collective-permute-start.2 = (bf16[64,1024]{1,0:T(8,128)(2,1)S(1)}, bf16[64,1024]{1,0:T(8,128)(2,1)S(1)}, u32[]{:S(2)}, u32[]{:S(2)}) collective-permute-start(bf16[64,1024]{1,0:T(8,128)(2,1)S(1)} %get-tuple-element.67), channel_id=1, source_target_pairs={{0,12},{2,14},{4,0},{6,2},{8,4},{10,6},{12,8},{14,10},{16,28},{18,... | collective-permute-start | bytes 393224 | tf_op jit(solution)/shard_map/ppermute | solution.py:717
  37.7 10.5 %collective-permute-start.3 = (bf16[64,1024]{1,0:T(8,128)(2,1)S(1)}, bf16[64,1024]{1,0:T(8,128)(2,1)S(1)}, u32[]{:S(2)}, u32[]{:S(2)}) collective-permute-start(bf16[64,1024]{1,0:T(8,128)(2,1)S(1)} %get-tuple-element.67), channel_id=1, source_target_pairs={{0,8},{2,10},{4,12},{6,14},{8,0},{10,2},{12,4},{14,6},{16,24},{18,... | collective-permute-start | bytes 393224 | tf_op jit(solution)/shard_map/ppermute | solution.py:717
  48.2 1.0 copy-start
  49.1 5.6 %collective-permute-start.4 = (bf16[256,1024]{1,0:T(8,128)(2,1)S(1)}, bf16[256,1024]{1,0:T(8,128)(2,1)S(1)}, u32[]{:S(2)}, u32[]{:S(2)}) collective-permute-start(bf16[256,1024]{1,0:T(8,128)(2,1)S(1)} %get-tuple-element.55), channel_id=1, source_target_pairs={{0,2},{2,0},{4,6},{6,4},{8,10},{10,8},{12,14},{14,12},{16,18},{18,... | collective-permute-start | bytes 1572872 | tf_op jit(solution)/shard_map/ppermute | solution.py:717
  65.8 4.3 %collective-permute-start.5 = (f32[128,8]{0,1:T(8,128)S(1)}, f32[128,8]{0,1:T(8,128)S(1)}, u32[]{:S(2)}, u32[]{:S(2)}) collective-permute-start(f32[128,8]{0,1:T(8,128)S(1)} %bitcast.86), channel_id=1, source_target_pairs={{0,1},{1,0},{2,3},{3,2},{4,5},{5,4},{6,7},{7,6},{8,9},{9,8},{10,11... | collective-permute-start | bytes 12296 | tf_op jit(solution)/shard_map/ppermute | solution.py:721
  82.1 17.4 %all-to-all-start.2 = ((f32[128,1,128]{2,1,0:T(1,128)}), f32[128,1,128]{2,1,0:T(1,128)S(1)}, u32[]{:S(2)}, u32[]{:S(2)}) async-start(f32[128,1,128]{2,1,0:T(1,128)} %get-tuple-element.34), calls=%async_computation.2 | async-start | bytes 131072 | tf_op jit(solution)/shard_map/all_to_all | solution.py:799
  89.0 5.1 %collective-permute-start.6 = (f32[128,8]{1,0:T(8,128)S(1)}, f32[128,8]{1,0:T(8,128)S(1)}, u32[]{:S(2)}, u32[]{:S(2)}) collective-permute-start(f32[128,8]{1,0:T(8,128)S(1)} %slice.54), channel_id=1, source_target_pairs={{0,1},{1,0},{2,3},{3,2},{4,5},{5,4},{6,7},{7,6},{8,9},{9,8},{10,11... | collective-permute-start | bytes 12296 | tf_op jit(solution)/shard_map/ppermute | solution.py:721
  104.3 60.6 %all-to-all-start.3 = ((bf16[128,16,512]{2,1,0:T(8,128)(2,1)}), bf16[128,16,512]{2,1,0:T(8,128)(2,1)S(1)}, u32[]{:S(2)}, u32[]{:S(2)}) async-start(bf16[128,16,512]{2,1,0:T(8,128)(2,1)} %shard_map.89), calls=%async_computation.3 | async-start | bytes 4194304 | tf_op jit(solution)/shard_map/all_to_all | solution.py:804
  112.3 4.7 %collective-permute-start.7 = (f32[8,128]{1,0:T(8,128)S(1)}, f32[8,128]{1,0:T(8,128)S(1)}, u32[]{:S(2)}, u32[]{:S(2)}) collective-permute-start(f32[8,128]{1,0:T(8,128)S(1)} %bitcast.88), channel_id=1, source_target_pairs={{0,1},{1,0},{2,3},{3,2},{4,5},{5,4},{6,7},{7,6},{8,9},{9,8},{10,11... | collective-permute-start | bytes 12296 | tf_op jit(solution)/shard_map/ppermute | solution.py:721
  122.9 4.1 %collective-permute-start.8 = (bf16[256,1024]{1,0:T(8,128)(2,1)S(1)}, bf16[256,1024]{1,0:T(8,128)(2,1)S(1)}, u32[]{:S(2)}, u32[]{:S(2)}) collective-permute-start(bf16[256,1024]{1,0:T(8,128)(2,1)S(1)} %get-tuple-element.38), channel_id=1, source_target_pairs={{0,2},{2,0},{4,6},{6,4},{8,10},{10,8},{12,14},{14,12},{16,18},{18,... | collective-permute-start | bytes 1572872 | tf_op jit(solution)/shard_map/ppermute | solution.py:717
  127.3 10.5 %collective-permute-start.11 = (bf16[64,1024]{1,0:T(8,128)(2,1)S(1)}, bf16[64,1024]{1,0:T(8,128)(2,1)S(1)}, u32[]{:S(2)}, u32[]{:S(2)}) collective-permute-start(bf16[64,1024]{1,0:T(8,128)(2,1)S(1)} %get-tuple-element.53), channel_id=1, source_target_pairs={{0,8},{2,10},{4,12},{6,14},{8,0},{10,2},{12,4},{14,6},{16,24},{18,... | collective-permute-start | bytes 393224 | tf_op jit(solution)/shard_map/ppermute | solution.py:717
  129.6 12.2 %collective-permute-start.10 = (bf16[64,1024]{1,0:T(8,128)(2,1)S(1)}, bf16[64,1024]{1,0:T(8,128)(2,1)S(1)}, u32[]{:S(2)}, u32[]{:S(2)}) collective-permute-start(bf16[64,1024]{1,0:T(8,128)(2,1)S(1)} %get-tuple-element.54), channel_id=1, source_target_pairs={{0,4},{2,6},{4,8},{6,10},{8,12},{10,14},{12,0},{14,2},{16,20},{18,... | collective-permute-start | bytes 393224 | tf_op jit(solution)/shard_map/ppermute | solution.py:717
  129.9 12.0 %collective-permute-start.9 = (bf16[64,1024]{1,0:T(8,128)(2,1)S(1)}, bf16[64,1024]{1,0:T(8,128)(2,1)S(1)}, u32[]{:S(2)}, u32[]{:S(2)}) collective-permute-start(bf16[64,1024]{1,0:T(8,128)(2,1)S(1)} %get-tuple-element.52), channel_id=1, source_target_pairs={{0,12},{2,14},{4,0},{6,2},{8,4},{10,6},{12,8},{14,10},{16,28},{18,... | collective-permute-start | bytes 393224 | tf_op jit(solution)/shard_map/ppermute | solution.py:717
  141.9 4.7 %collective-permute-start.12 = (bf16[32,1024]{1,0:T(8,128)(2,1)S(1)}, bf16[32,1024]{1,0:T(8,128)(2,1)S(1)}, u32[]{:S(2)}, u32[]{:S(2)}) collective-permute-start(bf16[32,1024]{1,0:T(8,128)(2,1)S(1)} %slice.97), channel_id=1, source_target_pairs={{0,16},{2,18},{4,20},{6,22},{8,24},{10,26},{12,28},{14,30},{16,0},... | collective-permute-start | bytes 196616 | tf_op jit(solution)/shard_map/ppermute | solution.py:717
  146.7 13.1 %collective-permute-start.16 = (bf16[8,1024]{1,0:T(8,128)(2,1)S(1)}, bf16[8,1024]{1,0:T(8,128)(2,1)S(1)}, u32[]{:S(2)}, u32[]{:S(2)}) collective-permute-start(bf16[8,1024]{1,0:T(8,128)(2,1)S(1)} %reshape_squeeze.15), channel_id=1, source_target_pairs={{0,96},{2,226},{4,100},{6,230},{8,104},{10,234},{12,108},{14,238},... | collective-permute-start | bytes 49160 | tf_op jit(solution)/shard_map/ppermute | solution.py:770
  150.1 9.6 %collective-permute-start.15 = (bf16[8,1024]{1,0:T(8,128)(2,1)S(1)}, bf16[8,1024]{1,0:T(8,128)(2,1)S(1)}, u32[]{:S(2)}, u32[]{:S(2)}) collective-permute-start(bf16[8,1024]{1,0:T(8,128)(2,1)S(1)} %reshape_squeeze.14), channel_id=1, source_target_pairs={{0,64},{2,194},{4,68},{6,198},{8,72},{10,202},{12,76},{14,206},{16... | collective-permute-start | bytes 49160 | tf_op jit(solution)/shard_map/ppermute | solution.py:770
  153.1 6.7 %collective-permute-start.14 = (bf16[8,1024]{1,0:T(8,128)(2,1)S(1)}, bf16[8,1024]{1,0:T(8,128)(2,1)S(1)}, u32[]{:S(2)}, u32[]{:S(2)}) collective-permute-start(bf16[8,1024]{1,0:T(8,128)(2,1)S(1)} %reshape_squeeze.13), channel_id=1, source_target_pairs={{0,32},{2,162},{4,36},{6,166},{8,40},{10,170},{12,44},{14,174},{16... | collective-permute-start | bytes 49160 | tf_op jit(solution)/shard_map/ppermute | solution.py:770
  153.9 9.8 %collective-permute-start.13 = (bf16[8,1024]{1,0:T(8,128)(2,1)S(1)}, bf16[8,1024]{1,0:T(8,128)(2,1)S(1)}, u32[]{:S(2)}, u32[]{:S(2)}) collective-permute-start(bf16[8,1024]{1,0:T(8,128)(2,1)S(1)} %reshape_squeeze.12), channel_id=1, source_target_pairs={{0,0},{2,130},{4,4},{6,134},{8,8},{10,138},{12,12},{14,142},{16,16... | collective-permute-start | bytes 49160 | tf_op jit(solution)/shard_map/ppermute | solution.py:770
  163.7 1.3 collective-permute-start.17

commit v10 on v9

--- a/solution.py
+++ b/solution.py
@@ -11,6 +11,7 @@
 COLS = 1024
 NB = 128
 HEADS = 4
+EIGHTS = BLOCK // 8
 OFFS = 4
 WIDTH = HEADS * HD
 PARTS = (8, 2, 4, 2)
@@ -26,6 +27,13 @@
     return (
         lax.broadcasted_iota(jnp.int32, shape, 0),
         lax.broadcasted_iota(jnp.int32, shape, 1),
+    )
+
+
+def index_columns(rows, columns):
+    return (
+        lax.broadcasted_iota(jnp.int32, (rows, 1), 0),
+        lax.broadcasted_iota(jnp.int32, (1, columns), 1),
     )
 
 
@@ -542,14 +550,18 @@
     at = [slice(head * HD, (head + 1) * HD) for head in heads]
     low, high = slice(0, BLOCK // 2), slice(BLOCK // 2, BLOCK)
     scaling, other = factors(sums_ref)
+
+    def keep(pair, slot, chunks, columns, rows):
+        rows = rows.reshape(-1, 8, HD).astype(BF16)
+        out_ref[pair, chunks, 8 * slot : 8 * slot + 8, columns] = rows
+
     copies[0].wait()
     copies[1].wait()
     grads = []
     for head in heads:
         wide = attn_ref[:, at[head]].astype(F32)
-        out_ref[0, :, at[head]] = (wide * scaling).astype(BF16)
+        keep(0, 0, slice(0, EIGHTS), at[head], wide * scaling)
         grads.append(gradient(wide, rows_ref[3, :, at[head]], scaling, other))
-    sent = copy_all([(out_ref.at[0], out_out.at[0])], out_sem.at[0])
     scores = []
     copies[2].wait()
     for head in heads:
@@ -561,30 +573,29 @@
         second = (own_ref[head, high, :].astype(F32) * second * scale).astype(BF16)
         scores.append((first, second))
 
-    def put(array, head, first, second, b):
+    first_chunks, last_chunks = slice(0, EIGHTS // 2), slice(EIGHTS // 2, EIGHTS)
+
+    def put(pair, slot, head, first, second, b):
         grads_low = dot_tn(first, b[low]) + dot_tn(second[:, low], b[high])
         grads_high = dot_tn(second[:, high], b[high])
-        out_ref[array, low, at[head]] = grads_low.astype(BF16)
-        out_ref[array, high, at[head]] = grads_high.astype(BF16)
-        tail_ref[array - 2, :, at[head]] = grads_high[BLOCK // 2 - 8 :]
-
-    for head in heads:
-        put(3, head, own_ref[head, low, low], own_ref[head, high, :], grads[head][0])
-    sent += copy_all([(out_ref.at[3], out_out.at[3])], out_sem.at[3])
+        keep(pair, slot, first_chunks, at[head], grads_low)
+        keep(pair, slot, last_chunks, at[head], grads_high)
+        tail_ref[slot, :, at[head]] = grads_high[BLOCK // 2 - 8 :]
+
+    for head in heads:
+        put(0, 1, head, own_ref[head, low, low], own_ref[head, high, :], grads[head][0])
+    sent = copy_all([(out_ref.at[0], out_out.at[0])], out_sem.at[0])
     copies[3 + HEADS].wait()
     for head in heads:
-        put(2, head, *scores[head], rows_ref[0, :, at[head]])
-    sent += copy_all([(out_ref.at[2], out_out.at[2])], out_sem.at[2])
+        put(1, 0, head, *scores[head], rows_ref[0, :, at[head]])
     copies[4 + HEADS].wait()
     copies[5 + HEADS].wait()
     for head in heads:
         first, second = scores[head]
-        out_ref[1, low, at[head]] = (
-            dot(first, rows_ref[1, low, at[head]]) + query_ref[low, at[head]]
-        ).astype(BF16)
-        out_ref[1, high, at[head]] = (
-            dot(second, rows_ref[1, :, at[head]]) + query_ref[high, at[head]]
-        ).astype(BF16)
+        first = dot(first, rows_ref[1, low, at[head]]) + query_ref[low, at[head]]
+        second = dot(second, rows_ref[1, :, at[head]]) + query_ref[high, at[head]]
+        keep(1, 1, first_chunks, at[head], first)
+        keep(1, 1, last_chunks, at[head], second)
     sent += copy_all([(out_ref.at[1], out_out.at[1])], out_sem.at[1])
     for copy in sent:
         copy.wait()
@@ -597,7 +608,7 @@
         [IN_HBM, IN_HBM, IN_HBM, spec((8, NB), 0, 0), IN_HBM],
         [IN_HBM, spec((2, 8, WIDTH), 0, 0, 0)],
         [
-            pltpu.HBM((4, BLOCK, WIDTH), BF16),
+            pltpu.HBM((2, EIGHTS, 16, WIDTH), BF16),
             jax.ShapeDtypeStruct((2, 8, WIDTH), F32),
         ],
         5 * 10**9,
@@ -607,9 +618,9 @@
             pltpu.VMEM((HEADS, BLOCK, BLOCK), BF16),
             pltpu.VMEM((BLOCK, WIDTH), BF16),
             pltpu.VMEM((BLOCK, WIDTH), F32),
-            pltpu.VMEM((4, BLOCK, WIDTH), BF16),
+            pltpu.VMEM((2, EIGHTS, 16, WIDTH), BF16),
             pltpu.SemaphoreType.DMA((HEADS + 6,)),
-            pltpu.SemaphoreType.DMA((4, 1)),
+            pltpu.SemaphoreType.DMA((2, 1)),
         ],
         vmem=VMEM5,
     )(*[in_hbm(array) for array in (rows, own, attn)], sums, in_hbm(far_query))
@@ -618,7 +629,7 @@
 def unpack_kernel(recv_ref, fixed_in, parts_ref, moved_ref, tails_ref, *refs):
     outs, fixed_ref, out_ref, in_sem, out_sem = refs[:4], refs[4], refs[5], refs[6], refs[7]
     parts = 4
-    size = BLOCK // parts
+    size = EIGHTS // parts
     copies = copy_all(
         [
             (fixed_in.at[:, pl.ds(part * size, size)], fixed_ref.at[:, pl.ds(part * size, size)])
@@ -627,42 +638,40 @@
         in_sem,
     )
     sent = []
-    row, col = iotas((512, 512))
-    array, token, head, kind = row >> 7, (row >> 3) & 15, (row >> 1) & 3, row & 1
+    row, col = index_columns(256, 256)
+    array, token, head, kind = row >> 6, (row >> 3) & 7, (row >> 1) & 3, row & 1
     strided = (token >> 2) * 64 + head * 16 + array * OFFS + (token & 3)
-    fixed = 256 + array * 64 + head * 16 + token
+    fixed = 128 + (((array + 1) >> 1) & 1) * 64 + head * 16 + (array & 1) * 8 + token
     pick = one_hot(col == jnp.where(kind == 0, strided, fixed))
-    end = lax.broadcasted_iota(jnp.int32, (16, WIDTH), 0) >= 16 - SUMM
+    row = lax.broadcasted_iota(jnp.int32, (16, WIDTH), 0)
     totals = parts_ref[...] + moved_ref[...].astype(F32)
     tails = []
     for array in range(2):
         part = [totals[:, n * HD : (n + 1) * HD] for n in range(array, 2 * HEADS, 2)]
         part = jnp.concatenate(part, 1) + tails_ref[array, 8 - SUMM :]
-        part = jnp.concatenate([jnp.zeros((16 - SUMM, WIDTH), F32), part], 0)
-        tails.append(part.astype(BF16))
-    for at in range(0, 32, 2):
-        if at * 16 % size == 0:
-            copies[at * 16 // size].wait()
-        pair = []
-        for n in (at, at + 1):
-            tile = 16 * n
-            fixed = [fixed_ref[array, tile : tile + 16] for array in range(4)]
-            if tile == BLOCK - 16:
-                for array in (2, 3):
-                    fixed[array] = jnp.where(end, tails[array - 2], fixed[array])
-            heads = [slice(head * HD, (head + 1) * HD) for head in range(HEADS)]
-            rows = [recv_ref[4 * n + home, :, head] for home in range(4) for head in heads]
+        tails.append(jnp.concatenate([part] * 4, 0).astype(BF16))
+    heads = [slice(head * HD, (head + 1) * HD) for head in range(HEADS)]
+    for at in range(0, EIGHTS, 4):
+        if at % size == 0:
+            copies[at // size].wait()
+        four = []
+        for n in range(at, at + 4):
+            fixed = [fixed_ref[pair, n] for pair in range(2)]
+            if n == EIGHTS - 1:
+                fixed[0] = jnp.where(row >= 16 - SUMM, tails[1], fixed[0])
+                fixed[1] = jnp.where((row >= 8 - SUMM) & (row < 8), tails[0], fixed[1])
+            rows = [recv_ref[2 * n + home, :, head] for home in range(2) for head in heads]
             rows += [part[:, head] for part in fixed for head in heads]
-            pair.append(jnp.concatenate(rows, 0))
-        picked = dot(pick, jnp.concatenate(pair, 1)).astype(BF16)
-        for n in range(2):
+            four.append(jnp.concatenate(rows, 0))
+        picked = dot(pick, jnp.concatenate(four, 1)).astype(BF16)
+        for n in range(4):
             for array in range(4):
-                out_ref[array, 128 * (at + n) : 128 * (at + n + 1)] = picked[
-                    array * 128 : (array + 1) * 128, n * HD : (n + 1) * HD
+                out_ref[array, 64 * (at + n) : 64 * (at + n + 1)] = picked[
+                    array * 64 : (array + 1) * 64, n * HD : (n + 1) * HD
                 ]
-        if (at + 2) * 16 % size == 0:
-            part = at * 16 // size
-            where = pl.ds(part * size * 8, size * 8)
+        if (at + 4) % size == 0:
+            part = at // size
+            where = pl.ds(part * size * 64, size * 64)
             sent += copy_all(
                 [(out_ref.at[array, where], outs[array].at[where]) for array in range(4)],
                 out_sem.at[part],
@@ -683,7 +692,7 @@
         2 * 10**9,
         8 * 2**20,
         [
-            pltpu.VMEM((4, BLOCK, WIDTH), BF16),
+            pltpu.VMEM((2, EIGHTS, 16, WIDTH), BF16),
             pltpu.VMEM((4, BLOCK * 8, HD), BF16),
             pltpu.SemaphoreType.DMA((4,)),
             pltpu.SemaphoreType.DMA((4, 4)),

time: 171 us -> 170 us (level)
  no operation moved by 1% of the time
where the time goes in v10:
time: 170 us; the launch traced here: 169 us
  starting transfers between devices  67.7 us (40%)
  waiting for transfers between devices  54.6 us (32%)
  Pallas kernels  41 us (24%)
  local copies, waits for them, and re-layouts  4.31 us (3%)
    ppermute x11, waiting for transfers between devices, shift(): return lax.ppermute(array, 'seq', perm)  26 us
    ppermute x11, starting transfers between devices, shift(): return lax.ppermute(array, 'seq', perm)  14.3 us
    ppermute x4, starting transfers between devices, scatter_summaries(): moved.append(lax.ppermute(sent[:, n].reshape(2 * SUMM, SLAB), 'seq', perm))  13 us
    all_to_all x1, starting transfers between devices, shards(): recv = lax.all_to_all(send, 'seq', 0, 0, tiled=True)  9.33 us
    pallas_call x1, Pallas kernels, fixed_forward(): call(fixed_forward_kernel, HEADS, [spec((4, BLOCK, HD), 0, 0, 'i'), spec(...  9.18 us
    all_to_all x1, starting transfers between devices, gather_along_z(): lax.all_to_all(sent, 'seq', 0, 0, axis_index_groups=groups, tiled=True)  9.01 us
    all_to_all x1, waiting for transfers between devices, shards(): recv = lax.all_to_all(send, 'seq', 0, 0, tiled=True)  8.92 us
    all_to_all x1, starting transfers between devices, shards(): recv_back = lax.all_to_all(send_back, 'seq', 0, 0, tiled=True)  7.65 us
  transfers between devices with their start and end apart: 22, of which 15 were waited for; matrix products, arithmetic and copies ran while one was open for 2% of the time, Pallas kernels for 16%

profile of v10, /device:TPU:1, one launch (start us, length us, event | category | flops | bytes accessed | tf_op | source)
XLA Modules:
  0.0 169.1 jit_solution(7523581225041734066)
XLA Ops:
  0.6 1.5 shard_map.85
  2.1 9.0 %all-to-all-start = ((bf16[8,4,1024]{2,1,0:T(4,128)(2,1)}), bf16[8,4,1024]{2,1,0:T(4,128)(2,1)S(1)}, u32[]{:S(2)}, u32[]{:S(2)}) async-start(bf16[8,4,1024]{2,1,0:T(4,128)(2,1)} %shard_map.85), calls=%async_computation | async-start | bytes 131072 | tf_op jit(solution)/shard_map/all_to_all | solution.py:742
  11.1 3.5 %shard_map.84 = bf16[128,16,512]{2,1,0:T(8,128)(2,1)} custom-call(bf16[4096,128]{1,0:T(8,128)(2,1)} %bitcast.81, bf16[4096,128]{1,0:T(8,128)(2,1)} %bitcast.76, bf16[4096,128]{1,0:T(8,128)(2,1)} %bitcast.79, bf16[4096,128]{1,0:T(8,128)(2,1)} %bitcast.83), custom_call_target="tpu_custom_call" | custom-call | flops 1000000000 | bytes 6291456 | tf_op jit(solution)/shard_map/pallas_call | solution.py:146
  14.6 3.8 %all-to-all-done = bf16[8,4,1024]{2,1,0:T(4,128)(2,1)S(1)} async-done(((bf16[8,4,1024]{2,1,0:T(4,128)(2,1)}), bf16[8,4,1024]{2,1,0:T(4,128)(2,1)S(1)}, u32[]{:S(2)}, u32[]{:S(2)}) %all-to-all-start) | async-done | bytes 65568 | tf_op jit(solution)/shard_map/all_to_all | solution.py:742
  18.4 0.1 fusion.2
  18.5 9.3 %all-to-all-start.1 = ((bf16[128,16,512]{2,1,0:T(8,128)(2,1)}), bf16[128,16,512]{2,1,0:T(8,128)(2,1)S(1)}, u32[]{:S(2)}, u32[]{:S(2)}) async-start(bf16[128,16,512]{2,1,0:T(8,128)(2,1)} %shard_map.84), calls=%async_computation.1 | async-start | bytes 4194304 | tf_op jit(solution)/shard_map/all_to_all | solution.py:800
  27.8 1.5 collective-permute-start
  29.3 5.6 %collective-permute-done = bf16[32,1024]{1,0:T(8,128)(2,1)S(1)} collective-permute-done((bf16[32,1024]{1,0:T(8,128)(2,1)S(1)}, bf16[32,1024]{1,0:T(8,128)(2,1)S(1)}, u32[]{:S(2)}, u32[]{:S(2)}) %collective-permute-start) | collective-permute-done | bytes 65568 | tf_op jit(solution)/shard_map/ppermute | solution.py:726
  34.9 0.6 collective-permute-start.1
  35.5 2.1 %collective-permute-start.2 = (bf16[64,1024]{1,0:T(8,128)(2,1)S(1)}, bf16[64,1024]{1,0:T(8,128)(2,1)S(1)}, u32[]{:S(2)}, u32[]{:S(2)}) collective-permute-start(bf16[64,1024]{1,0:T(8,128)(2,1)S(1)} %get-tuple-element.67), channel_id=1, source_target_pairs={{0,12},{2,14},{4,0},{6,2},{8,4},{10,6},{12,8},{14,10},{16,28},{18,... | collective-permute-start | bytes 393224 | tf_op jit(solution)/shard_map/ppermute | solution.py:726
  37.7 0.8 collective-permute-start.3
  38.5 3.7 %collective-permute-done.1 = bf16[64,1024]{1,0:T(8,128)(2,1)S(1)} collective-permute-done((bf16[64,1024]{1,0:T(8,128)(2,1)S(1)}, bf16[64,1024]{1,0:T(8,128)(2,1)S(1)}, u32[]{:S(2)}, u32[]{:S(2)}) %collective-permute-start.1) | collective-permute-done | bytes 131104 | tf_op jit(solution)/shard_map/ppermute | solution.py:726
  42.2 0.6 collective-permute-done.2
  42.8 5.3 %collective-permute-done.3 = bf16[64,1024]{1,0:T(8,128)(2,1)S(1)} collective-permute-done((bf16[64,1024]{1,0:T(8,128)(2,1)S(1)}, bf16[64,1024]{1,0:T(8,128)(2,1)S(1)}, u32[]{:S(2)}, u32[]{:S(2)}) %collective-permute-start.3) | collective-permute-done | bytes 131104 | tf_op jit(solution)/shard_map/ppermute | solution.py:726
  48.2 0.0 copy-start
  48.2 1.0 copy-done
  49.1 1.2 collective-permute-start.4
  50.4 0.1 broadcast_in_dim.4
  50.4 0.7 broadcast_in_dim_reshape.3.seen_ref
  51.1 3.6 %shard_map.86.rows_ref.rows_in = bf16[4,512,512]{2,1,0:T(8,128)(2,1)} custom-call(bf16[4096,128]{1,0:T(8,128)(2,1)} %bitcast.82, bf16[4096,128]{1,0:T(8,128)(2,1)} %bitcast.77, bf16[4096,128]{1,0:T(8,128)(2,1)} %bitcast.80, bf16[4096,128]{1,0:T(8,128)(2,1)} %bitcast.84), custom_call_target="tpu_custom_call" | custom-call | flops 1000000000 | bytes 6291456 | tf_op jit(solution)/shard_map/pallas_call | solution.py:202
  54.7 0.0 collective-permute-done.4
  54.7 0.8 constant_dynamic-update-slice_fusion.7.summ_ref.summ_in
  55.6 9.2 %shard_map.87 = (bf16[512,512]{1,0:T(8,128)(2,1)}, bf16[4,512,512]{2,1,0:T(8,128)(2,1)}, bf16[4,512,512]{2,1,0:T(8,128)(2,1)}, f32[512,8]{1,0:T(8,128)}) custom-call(bf16[4,512,512]{2,1,0:T(8,128)(2,1)} %shard_map.86.rows_ref.rows_in, bf16[512,1024]{1,0:T(8,128)(2,1)} %constant_dynamic-update-slice_fusion.7.summ_ref.summ_in, ...), custom_call_target="tpu_custom_call" | custom-call | flops 4000000000 | bytes 4194304 | tf_op jit(solution)/shard_map/pallas_call | solution.py:249
  64.7 1.0 copy.45
  65.8 2.5 %collective-permute-start.5 = (f32[128,8]{0,1:T(8,128)S(1)}, f32[128,8]{0,1:T(8,128)S(1)}, u32[]{:S(2)}, u32[]{:S(2)}) collective-permute-start(f32[128,8]{0,1:T(8,128)S(1)} %bitcast.86), channel_id=1, source_target_pairs={{0,1},{1,0},{2,3},{3,2},{4,5},{5,4},{6,7},{7,6},{8,9},{9,8},{10,11... | collective-permute-start | bytes 12296 | tf_op jit(solution)/shard_map/ppermute | solution.py:730
  68.3 1.8 %collective-permute-done.5 = f32[128,8]{0,1:T(8,128)S(1)} collective-permute-done((f32[128,8]{0,1:T(8,128)S(1)}, f32[128,8]{0,1:T(8,128)S(1)}, u32[]{:S(2)}, u32[]{:S(2)}) %collective-permute-start.5) | collective-permute-done | bytes 4128 | tf_op jit(solution)/shard_map/ppermute | solution.py:730
  70.1 0.1 copy.61
  70.3 8.9 %all-to-all-done.1.recv_ref = bf16[128,16,512]{2,1,0:T(8,128)(2,1)S(1)} async-done(((bf16[128,16,512]{2,1,0:T(8,128)(2,1)}), bf16[128,16,512]{2,1,0:T(8,128)(2,1)S(1)}, u32[]{:S(2)}, u32[]{:S(2)}) %all-to-all-start.1) | async-done | bytes 2097184 | tf_op jit(solution)/shard_map/all_to_all | solution.py:800
  79.2 2.9 %shard_map.88 = (bf16[4,3,4,128,128]{4,3,2,1,0:T(8,128)(2,1)}, bf16[4,4,128,128]{3,2,1,0:T(8,128)(2,1)}, bf16[4,2,4,128,128]{4,3,2,1,0:T(8,128)(2,1)S(1)}, f32[128,128]{1,0:T(8,128)S(1)}, f32[128,1,128]{2,1,0:T(1,128)}) custom-call(bf16[128,16,512]{2,1,0:T(8,128)(2,1)S(1)} %all-to-all-done.1.recv_ref, f32[128,128]{1,0:T(8,128)S(1)} %pad.4.clone.fixed_ref), custom_call_target="tpu_custom_call" | custom-call | flops 1000000000 | bytes 6291456 | tf_op jit(solution)/shard_map/pallas_call | solution.py:320
  82.1 6.9 %all-to-all-start.2 = ((f32[128,1,128]{2,1,0:T(1,128)}), f32[128,1,128]{2,1,0:T(1,128)S(1)}, u32[]{:S(2)}, u32[]{:S(2)}) async-start(f32[128,1,128]{2,1,0:T(1,128)} %get-tuple-element.34), calls=%async_computation.2 | async-start | bytes 131072 | tf_op jit(solution)/shard_map/all_to_all | solution.py:808
  88.9 0.1 slice.54
  89.0 2.5 %collective-permute-start.6 = (f32[128,8]{1,0:T(8,128)S(1)}, f32[128,8]{1,0:T(8,128)S(1)}, u32[]{:S(2)}, u32[]{:S(2)}) collective-permute-start(f32[128,8]{1,0:T(8,128)S(1)} %slice.54), channel_id=1, source_target_pairs={{0,1},{1,0},{2,3},{3,2},{4,5},{5,4},{6,7},{7,6},{8,9},{9,8},{10,11... | collective-permute-start | bytes 12296 | tf_op jit(solution)/shard_map/ppermute | solution.py:730
  91.5 2.6 %collective-permute-done.6.other_ref = f32[128,8]{1,0:T(8,128)S(1)} collective-permute-done((f32[128,8]{1,0:T(8,128)S(1)}, f32[128,8]{1,0:T(8,128)S(1)}, u32[]{:S(2)}, u32[]{:S(2)}) %collective-permute-start.6) | collective-permute-done | bytes 4128 | tf_op jit(solution)/shard_map/ppermute | solution.py:730
  94.1 5.4 %all-to-all-done.2.recv_ref = f32[128,1,128]{2,1,0:T(1,128)S(1)} async-done(((f32[128,1,128]{2,1,0:T(1,128)}), f32[128,1,128]{2,1,0:T(1,128)S(1)}, u32[]{:S(2)}, u32[]{:S(2)}) %all-to-all-start.2) | async-done | bytes 65568 | tf_op jit(solution)/shard_map/all_to_all | solution.py:808
  99.5 4.9 %shard_map.89 = bf16[128,16,512]{2,1,0:T(8,128)(2,1)} custom-call(bf16[4,3,4,128,128]{4,3,2,1,0:T(8,128)(2,1)} %get-tuple-element.30.keys_in, bf16[4,4,128,128]{3,2,1,0:T(8,128)(2,1)} %get-tuple-element.31.prob_in, bf16[4,2,4,128,128]{4,3,2,1,0:T(8,128)(2,1)S(1)} %get-tuple-element.32.grp_ref, f32[128,128]{1,0:T(8,128)S(1)} %get-tuple-element.33.sums_ref, ...), custom_call_target="tpu_custom_call" | custom-call | flops 1000000000 | bytes 6291456 | tf_op jit(solution)/shard_map/pallas_call | solution.py:431
  104.3 7.7 %all-to-all-start.3 = ((bf16[128,16,512]{2,1,0:T(8,128)(2,1)}), bf16[128,16,512]{2,1,0:T(8,128)(2,1)S(1)}, u32[]{:S(2)}, u32[]{:S(2)}) async-start(bf16[128,16,512]{2,1,0:T(8,128)(2,1)} %shard_map.89), calls=%async_computation.3 | async-start | bytes 4194304 | tf_op jit(solution)/shard_map/all_to_all | solution.py:813
  112.0 0.2 slice.73
  112.3 2.5 %collective-permute-start.7 = (f32[8,128]{1,0:T(8,128)S(1)}, f32[8,128]{1,0:T(8,128)S(1)}, u32[]{:S(2)}, u32[]{:S(2)}) collective-permute-start(f32[8,128]{1,0:T(8,128)S(1)} %bitcast.88), channel_id=1, source_target_pairs={{0,1},{1,0},{2,3},{3,2},{4,5},{5,4},{6,7},{7,6},{8,9},{9,8},{10,11... | collective-permute-start | bytes 12296 | tf_op jit(solution)/shard_map/ppermute | solution.py:730
  114.8 2.2 %collective-permute-done.7 = f32[8,128]{1,0:T(8,128)S(1)} collective-permute-done((f32[8,128]{1,0:T(8,128)S(1)}, f32[8,128]{1,0:T(8,128)S(1)}, u32[]{:S(2)}, u32[]{:S(2)}) %collective-permute-start.7) | collective-permute-done | bytes 4128 | tf_op jit(solution)/shard_map/ppermute | solution.py:730
  117.0 5.9 %shard_map.90 = (f32[512,512]{1,0:T(8,128)}, f32[256,1024]{1,0:T(8,128)S(1)}, bf16[256,1024]{1,0:T(8,128)(2,1)S(1)}) custom-call(bf16[4,512,512]{2,1,0:T(8,128)(2,1)} %shard_map.86.rows_ref.rows_in, bf16[512,1024]{1,0:T(8,128)(2,1)} %constant_dynamic-update-slice_fusion.7.summ_ref.summ_in, bf16[4,512,512]{2,1,0:T(8,128)(2,1)} %get-tuple-element.35.far_in, ...), custom_call_target="tpu_custom_call" | custom-call | flops 3000000000 | bytes 8388608 | tf_op jit(solution)/shard_map/pallas_call | solution.py:509
  122.9 2.6 %collective-permute-start.8 = (bf16[256,1024]{1,0:T(8,128)(2,1)S(1)}, bf16[256,1024]{1,0:T(8,128)(2,1)S(1)}, u32[]{:S(2)}, u32[]{:S(2)}) collective-permute-start(bf16[256,1024]{1,0:T(8,128)(2,1)S(1)} %get-tuple-element.38), channel_id=1, source_target_pairs={{0,2},{2,0},{4,6},{6,4},{8,10},{10,8},{12,14},{14,12},{16,18},{18,... | collective-permute-start | bytes 1572872 | tf_op jit(solution)/shard_map/ppermute | solution.py:726
  125.5 1.5 collective-permute-done.8
  127.0 0.2 fusion.13
  127.3 2.3 %collective-permute-start.11 = (bf16[64,1024]{1,0:T(8,128)(2,1)S(1)}, bf16[64,1024]{1,0:T(8,128)(2,1)S(1)}, u32[]{:S(2)}, u32[]{:S(2)}) collective-permute-start(bf16[64,1024]{1,0:T(8,128)(2,1)S(1)} %get-tuple-element.53), channel_id=1, source_target_pairs={{0,8},{2,10},{4,12},{6,14},{8,0},{10,2},{12,4},{14,6},{16,24},{18,... | collective-permute-start | bytes 393224 | tf_op jit(solution)/shard_map/ppermute | solution.py:726
  129.6 0.2 collective-permute-start.10
  129.9 2.4 %collective-permute-start.9 = (bf16[64,1024]{1,0:T(8,128)(2,1)S(1)}, bf16[64,1024]{1,0:T(8,128)(2,1)S(1)}, u32[]{:S(2)}, u32[]{:S(2)}) collective-permute-start(bf16[64,1024]{1,0:T(8,128)(2,1)S(1)} %get-tuple-element.52), channel_id=1, source_target_pairs={{0,12},{2,14},{4,0},{6,2},{8,4},{10,6},{12,8},{14,10},{16,28},{18,... | collective-permute-start | bytes 393224 | tf_op jit(solution)/shard_map/ppermute | solution.py:726
  132.3 5.6 %shard_map.91 = (bf16[2,64,16,512]{3,2,1,0:T(8,128)(2,1)}, f32[2,8,512]{2,1,0:T(8,128)S(1)}) custom-call(bf16[4,512,512]{2,1,0:T(8,128)(2,1)} %shard_map.86.rows_ref.rows_in, bf16[4,512,512]{2,1,0:T(8,128)(2,1)} %get-tuple-element.39.own_in, bf16[512,512]{1,0:T(8,128)(2,1)} %get-tuple-element.36.attn_in, f32[8,128]{1,0:T(8,128)S(1)} %fusion.3.sums_ref, ...), custom_call_target="tpu_custom_call" | custom-call | flops 5000000000 | bytes 8388608 | tf_op jit(solution)/shard_map/pallas_call | solution.py:605
  137.9 0.0 collective-permute-done.11
  137.9 3.9 %collective-permute-done.10 = bf16[64,1024]{1,0:T(8,128)(2,1)S(1)} collective-permute-done((bf16[64,1024]{1,0:T(8,128)(2,1)S(1)}, bf16[64,1024]{1,0:T(8,128)(2,1)S(1)}, u32[]{:S(2)}, u32[]{:S(2)}) %collective-permute-start.10) | collective-permute-done | bytes 131104 | tf_op jit(solution)/shard_map/ppermute | solution.py:726
  141.8 0.0 collective-permute-done.9
  141.8 0.1 fusion.1
  141.9 0.4 collective-permute-start.12
  142.3 4.3 %collective-permute-done.12 = bf16[32,1024]{1,0:T(8,128)(2,1)S(1)} collective-permute-done((bf16[32,1024]{1,0:T(8,128)(2,1)S(1)}, bf16[32,1024]{1,0:T(8,128)(2,1)S(1)}, u32[]{:S(2)}, u32[]{:S(2)}) %collective-permute-start.12) | collective-permute-done | bytes 65568 | tf_op jit(solution)/shard_map/ppermute | solution.py:726
  146.7 3.4 %collective-permute-start.16 = (bf16[8,1024]{1,0:T(8,128)(2,1)S(1)}, bf16[8,1024]{1,0:T(8,128)(2,1)S(1)}, u32[]{:S(2)}, u32[]{:S(2)}) collective-permute-start(bf16[8,1024]{1,0:T(8,128)(2,1)S(1)} %reshape_squeeze.15), channel_id=1, source_target_pairs={{0,96},{2,226},{4,100},{6,230},{8,104},{10,234},{12,108},{14,238},... | collective-permute-start | bytes 49160 | tf_op jit(solution)/shard_map/ppermute | solution.py:779
  150.1 2.9 %collective-permute-start.15 = (bf16[8,1024]{1,0:T(8,128)(2,1)S(1)}, bf16[8,1024]{1,0:T(8,128)(2,1)S(1)}, u32[]{:S(2)}, u32[]{:S(2)}) collective-permute-start(bf16[8,1024]{1,0:T(8,128)(2,1)S(1)} %reshape_squeeze.14), channel_id=1, source_target_pairs={{0,64},{2,194},{4,68},{6,198},{8,72},{10,202},{12,76},{14,206},{16... | collective-permute-start | bytes 49160 | tf_op jit(solution)/shard_map/ppermute | solution.py:779
  153.1 0.8 collective-permute-start.14
  153.9 5.9 %collective-permute-start.13 = (bf16[8,1024]{1,0:T(8,128)(2,1)S(1)}, bf16[8,1024]{1,0:T(8,128)(2,1)S(1)}, u32[]{:S(2)}, u32[]{:S(2)}) collective-permute-start(bf16[8,1024]{1,0:T(8,128)(2,1)S(1)} %reshape_squeeze.12), channel_id=1, source_target_pairs={{0,0},{2,130},{4,4},{6,134},{8,8},{10,138},{12,12},{14,142},{16,16... | collective-permute-start | bytes 49160 | tf_op jit(solution)/shard_map/ppermute | solution.py:779
  159.7 0.0 collective-permute-done.16
  159.8 0.0 collective-permute-done.15
  159.8 0.0 collective-permute-done.14
  159.8 3.8 %collective-permute-done.13 = bf16[8,1024]{1,0:T(8,128)(2,1)S(1)} collective-permute-done((bf16[8,1024]{1,0:T(8,128)(2,1)S(1)}, bf16[8,1024]{1,0:T(8,128)(2,1)S(1)}, u32[]{:S(2)}, u32[]{:S(2)}) %collective-permute-start.13) | collective-permute-done | bytes 16416 | tf_op jit(solution)/shard_map/ppermute | solution.py:779
  163.7 0.1 collective-permute-start.17
  163.8 1.1 collective-permute-done.17.moved_ref
  164.9 4.0 %shard_map.92 = (bf16[4096,128]{1,0:T(8,128)(2,1)}, bf16[4096,128]{1,0:T(8,128)(2,1)}, bf16[4096,128]{1,0:T(8,128)(2,1)}, bf16[4096,128]{1,0:T(8,128)(2,1)}) custom-call(bf16[128,16,512]{2,1,0:T(8,128)(2,1)S(1)} %all-to-all-done.3.recv_ref, bf16[2,64,16,512]{3,2,1,0:T(8,128)(2,1)} %get-tuple-element.43.fixed_in, f32[4,1024]{1,0:T(4,128)S(1)} %slice.83.parts_ref, ...), custom_call_target="tpu_custom_call" | custom-call | flops 2000000000 | bytes 8388608 | tf_op jit(solution)/shard_map/pallas_call | solution.py:684
  (24 shorter events, 0.4 us)
Async XLA Ops:
  2.1 16.3 %all-to-all-start = ((bf16[8,4,1024]{2,1,0:T(4,128)(2,1)}), bf16[8,4,1024]{2,1,0:T(4,128)(2,1)S(1)}, u32[]{:S(2)}, u32[]{:S(2)}) async-start(bf16[8,4,1024]{2,1,0:T(4,128)(2,1)} %shard_map.85), calls=%async_computation | async-start | bytes 131072 | tf_op jit(solution)/shard_map/all_to_all | solution.py:742
  18.5 60.7 %all-to-all-start.1 = ((bf16[128,16,512]{2,1,0:T(8,128)(2,1)}), bf16[128,16,512]{2,1,0:T(8,128)(2,1)S(1)}, u32[]{:S(2)}, u32[]{:S(2)}) async-start(bf16[128,16,512]{2,1,0:T(8,128)(2,1)} %shard_map.84), calls=%async_computation.1 | async-start | bytes 4194304 | tf_op jit(solution)/shard_map/all_to_all | solution.py:800
  27.8 7.1 %collective-permute-start = (bf16[32,1024]{1,0:T(8,128)(2,1)S(1)}, bf16[32,1024]{1,0:T(8,128)(2,1)S(1)}, u32[]{:S(2)}, u32[]{:S(2)}) collective-permute-start(bf16[32,1024]{1,0:T(8,128)(2,1)S(1)} %reshape.110), channel_id=1, source_target_pairs={{0,16},{2,18},{4,20},{6,22},{8,24},{10,26},{12,28},{14,30},{16,0},... | collective-permute-start | bytes 196616 | tf_op jit(solution)/shard_map/ppermute | solution.py:726
  34.9 7.3 %collective-permute-start.1 = (bf16[64,1024]{1,0:T(8,128)(2,1)S(1)}, bf16[64,1024]{1,0:T(8,128)(2,1)S(1)}, u32[]{:S(2)}, u32[]{:S(2)}) collective-permute-start(bf16[64,1024]{1,0:T(8,128)(2,1)S(1)} %get-tuple-element.67), channel_id=1, source_target_pairs={{0,4},{2,6},{4,8},{6,10},{8,12},{10,14},{12,0},{14,2},{16,20},{18,... | collective-permute-start | bytes 393224 | tf_op jit(solution)/shard_map/ppermute | solution.py:726
  35.5 7.3 %collective-permute-start.2 = (bf16[64,1024]{1,0:T(8,128)(2,1)S(1)}, bf16[64,1024]{1,0:T(8,128)(2,1)S(1)}, u32[]{:S(2)}, u32[]{:S(2)}) collective-permute-start(bf16[64,1024]{1,0:T(8,128)(2,1)S(1)} %get-tuple-element.67), channel_id=1, source_target_pairs={{0,12},{2,14},{4,0},{6,2},{8,4},{10,6},{12,8},{14,10},{16,28},{18,... | collective-permute-start | bytes 393224 | tf_op jit(solution)/shard_map/ppermute | solution.py:726
  37.7 10.5 %collective-permute-start.3 = (bf16[64,1024]{1,0:T(8,128)(2,1)S(1)}, bf16[64,1024]{1,0:T(8,128)(2,1)S(1)}, u32[]{:S(2)}, u32[]{:S(2)}) collective-permute-start(bf16[64,1024]{1,0:T(8,128)(2,1)S(1)} %get-tuple-element.67), channel_id=1, source_target_pairs={{0,8},{2,10},{4,12},{6,14},{8,0},{10,2},{12,4},{14,6},{16,24},{18,... | collective-permute-start | bytes 393224 | tf_op jit(solution)/shard_map/ppermute | solution.py:726
  48.2 1.0 copy-start
  49.1 5.6 %collective-permute-start.4 = (bf16[256,1024]{1,0:T(8,128)(2,1)S(1)}, bf16[256,1024]{1,0:T(8,128)(2,1)S(1)}, u32[]{:S(2)}, u32[]{:S(2)}) collective-permute-start(bf16[256,1024]{1,0:T(8,128)(2,1)S(1)} %get-tuple-element.55), channel_id=1, source_target_pairs={{0,2},{2,0},{4,6},{6,4},{8,10},{10,8},{12,14},{14,12},{16,18},{18,... | collective-permute-start | bytes 1572872 | tf_op jit(solution)/shard_map/ppermute | solution.py:726
  65.8 4.3 %collective-permute-start.5 = (f32[128,8]{0,1:T(8,128)S(1)}, f32[128,8]{0,1:T(8,128)S(1)}, u32[]{:S(2)}, u32[]{:S(2)}) collective-permute-start(f32[128,8]{0,1:T(8,128)S(1)} %bitcast.86), channel_id=1, source_target_pairs={{0,1},{1,0},{2,3},{3,2},{4,5},{5,4},{6,7},{7,6},{8,9},{9,8},{10,11... | collective-permute-start | bytes 12296 | tf_op jit(solution)/shard_map/ppermute | solution.py:730
  82.1 17.4 %all-to-all-start.2 = ((f32[128,1,128]{2,1,0:T(1,128)}), f32[128,1,128]{2,1,0:T(1,128)S(1)}, u32[]{:S(2)}, u32[]{:S(2)}) async-start(f32[128,1,128]{2,1,0:T(1,128)} %get-tuple-element.34), calls=%async_computation.2 | async-start | bytes 131072 | tf_op jit(solution)/shard_map/all_to_all | solution.py:808
  89.0 5.1 %collective-permute-start.6 = (f32[128,8]{1,0:T(8,128)S(1)}, f32[128,8]{1,0:T(8,128)S(1)}, u32[]{:S(2)}, u32[]{:S(2)}) collective-permute-start(f32[128,8]{1,0:T(8,128)S(1)} %slice.54), channel_id=1, source_target_pairs={{0,1},{1,0},{2,3},{3,2},{4,5},{5,4},{6,7},{7,6},{8,9},{9,8},{10,11... | collective-permute-start | bytes 12296 | tf_op jit(solution)/shard_map/ppermute | solution.py:730
  104.3 60.6 %all-to-all-start.3 = ((bf16[128,16,512]{2,1,0:T(8,128)(2,1)}), bf16[128,16,512]{2,1,0:T(8,128)(2,1)S(1)}, u32[]{:S(2)}, u32[]{:S(2)}) async-start(bf16[128,16,512]{2,1,0:T(8,128)(2,1)} %shard_map.89), calls=%async_computation.3 | async-start | bytes 4194304 | tf_op jit(solution)/shard_map/all_to_all | solution.py:813
  112.3 4.7 %collective-permute-start.7 = (f32[8,128]{1,0:T(8,128)S(1)}, f32[8,128]{1,0:T(8,128)S(1)}, u32[]{:S(2)}, u32[]{:S(2)}) collective-permute-start(f32[8,128]{1,0:T(8,128)S(1)} %bitcast.88), channel_id=1, source_target_pairs={{0,1},{1,0},{2,3},{3,2},{4,5},{5,4},{6,7},{7,6},{8,9},{9,8},{10,11... | collective-permute-start | bytes 12296 | tf_op jit(solution)/shard_map/ppermute | solution.py:730
  122.9 4.1 %collective-permute-start.8 = (bf16[256,1024]{1,0:T(8,128)(2,1)S(1)}, bf16[256,1024]{1,0:T(8,128)(2,1)S(1)}, u32[]{:S(2)}, u32[]{:S(2)}) collective-permute-start(bf16[256,1024]{1,0:T(8,128)(2,1)S(1)} %get-tuple-element.38), channel_id=1, source_target_pairs={{0,2},{2,0},{4,6},{6,4},{8,10},{10,8},{12,14},{14,12},{16,18},{18,... | collective-permute-start | bytes 1572872 | tf_op jit(solution)/shard_map/ppermute | solution.py:726
  127.3 10.6 %collective-permute-start.11 = (bf16[64,1024]{1,0:T(8,128)(2,1)S(1)}, bf16[64,1024]{1,0:T(8,128)(2,1)S(1)}, u32[]{:S(2)}, u32[]{:S(2)}) collective-permute-start(bf16[64,1024]{1,0:T(8,128)(2,1)S(1)} %get-tuple-element.53), channel_id=1, source_target_pairs={{0,8},{2,10},{4,12},{6,14},{8,0},{10,2},{12,4},{14,6},{16,24},{18,... | collective-permute-start | bytes 393224 | tf_op jit(solution)/shard_map/ppermute | solution.py:726
  129.6 12.2 %collective-permute-start.10 = (bf16[64,1024]{1,0:T(8,128)(2,1)S(1)}, bf16[64,1024]{1,0:T(8,128)(2,1)S(1)}, u32[]{:S(2)}, u32[]{:S(2)}) collective-permute-start(bf16[64,1024]{1,0:T(8,128)(2,1)S(1)} %get-tuple-element.54), channel_id=1, source_target_pairs={{0,4},{2,6},{4,8},{6,10},{8,12},{10,14},{12,0},{14,2},{16,20},{18,... | collective-permute-start | bytes 393224 | tf_op jit(solution)/shard_map/ppermute | solution.py:726
  129.9 12.0 %collective-permute-start.9 = (bf16[64,1024]{1,0:T(8,128)(2,1)S(1)}, bf16[64,1024]{1,0:T(8,128)(2,1)S(1)}, u32[]{:S(2)}, u32[]{:S(2)}) collective-permute-start(bf16[64,1024]{1,0:T(8,128)(2,1)S(1)} %get-tuple-element.52), channel_id=1, source_target_pairs={{0,12},{2,14},{4,0},{6,2},{8,4},{10,6},{12,8},{14,10},{16,28},{18,... | collective-permute-start | bytes 393224 | tf_op jit(solution)/shard_map/ppermute | solution.py:726
  141.9 4.7 %collective-permute-start.12 = (bf16[32,1024]{1,0:T(8,128)(2,1)S(1)}, bf16[32,1024]{1,0:T(8,128)(2,1)S(1)}, u32[]{:S(2)}, u32[]{:S(2)}) collective-permute-start(bf16[32,1024]{1,0:T(8,128)(2,1)S(1)} %slice.97), channel_id=1, source_target_pairs={{0,16},{2,18},{4,20},{6,22},{8,24},{10,26},{12,28},{14,30},{16,0},... | collective-permute-start | bytes 196616 | tf_op jit(solution)/shard_map/ppermute | solution.py:726
  146.7 13.1 %collective-permute-start.16 = (bf16[8,1024]{1,0:T(8,128)(2,1)S(1)}, bf16[8,1024]{1,0:T(8,128)(2,1)S(1)}, u32[]{:S(2)}, u32[]{:S(2)}) collective-permute-start(bf16[8,1024]{1,0:T(8,128)(2,1)S(1)} %reshape_squeeze.15), channel_id=1, source_target_pairs={{0,96},{2,226},{4,100},{6,230},{8,104},{10,234},{12,108},{14,238},... | collective-permute-start | bytes 49160 | tf_op jit(solution)/shard_map/ppermute | solution.py:779
  150.1 9.6 %collective-permute-start.15 = (bf16[8,1024]{1,0:T(8,128)(2,1)S(1)}, bf16[8,1024]{1,0:T(8,128)(2,1)S(1)}, u32[]{:S(2)}, u32[]{:S(2)}) collective-permute-start(bf16[8,1024]{1,0:T(8,128)(2,1)S(1)} %reshape_squeeze.14), channel_id=1, source_target_pairs={{0,64},{2,194},{4,68},{6,198},{8,72},{10,202},{12,76},{14,206},{16... | collective-permute-start | bytes 49160 | tf_op jit(solution)/shard_map/ppermute | solution.py:779
  153.1 6.7 %collective-permute-start.14 = (bf16[8,1024]{1,0:T(8,128)(2,1)S(1)}, bf16[8,1024]{1,0:T(8,128)(2,1)S(1)}, u32[]{:S(2)}, u32[]{:S(2)}) collective-permute-start(bf16[8,1024]{1,0:T(8,128)(2,1)S(1)} %reshape_squeeze.13), channel_id=1, source_target_pairs={{0,32},{2,162},{4,36},{6,166},{8,40},{10,170},{12,44},{14,174},{16... | collective-permute-start | bytes 49160 | tf_op jit(solution)/shard_map/ppermute | solution.py:779
  153.9 9.8 %collective-permute-start.13 = (bf16[8,1024]{1,0:T(8,128)(2,1)S(1)}, bf16[8,1024]{1,0:T(8,128)(2,1)S(1)}, u32[]{:S(2)}, u32[]{:S(2)}) collective-permute-start(bf16[8,1024]{1,0:T(8,128)(2,1)S(1)} %reshape_squeeze.12), channel_id=1, source_target_pairs={{0,0},{2,130},{4,4},{6,134},{8,8},{10,138},{12,12},{14,142},{16,16... | collective-permute-start | bytes 49160 | tf_op jit(solution)/shard_map/ppermute | solution.py:779
  163.7 1.3 collective-permute-start.17

commit v11 on v10

--- a/solution.py
+++ b/solution.py
@@ -400,11 +400,12 @@
         out_ref[head, 0] = normed
         grads.append((grad, row_dot))
     heads = range(HEADS)
+    probs, grad_probs = [], []
     for head in heads:
         for copy in fetched[head]:
             copy.wait()
-    probs = [prob_ref[head] for head in heads]
-    grad_probs = [batch_dot(grads[head][0], keys_ref[head, 2], 2, 2) for head in heads]
+        probs.append(prob_ref[head])
+        grad_probs.append(batch_dot(grads[head][0], keys_ref[head, 2], 2, 2))
     scores = [
         (probs[head].astype(F32) * (grad_probs[head] - grads[head][1]) * scale).astype(BF16)
         for head in heads

time: 170 us -> 170 us (level)
  no operation moved by 1% of the time
where the time goes in v11:
time: 170 us; the launch traced here: 169 us
  starting transfers between devices  67.7 us (40%)
  waiting for transfers between devices  54.6 us (32%)
  Pallas kernels  41 us (24%)
  local copies, waits for them, and re-layouts  4.31 us (3%)
    ppermute x11, waiting for transfers between devices, shift(): return lax.ppermute(array, 'seq', perm)  26.1 us
    ppermute x11, starting transfers between devices, shift(): return lax.ppermute(array, 'seq', perm)  14.3 us
    ppermute x4, starting transfers between devices, scatter_summaries(): moved.append(lax.ppermute(sent[:, n].reshape(2 * SUMM, SLAB), 'seq', perm))  13 us
    all_to_all x1, starting transfers between devices, shards(): recv = lax.all_to_all(send, 'seq', 0, 0, tiled=True)  9.33 us
    pallas_call x1, Pallas kernels, fixed_forward(): call(fixed_forward_kernel, HEADS, [spec((4, BLOCK, HD), 0, 0, 'i'), spec(...  9.18 us
    all_to_all x1, starting transfers between devices, gather_along_z(): lax.all_to_all(sent, 'seq', 0, 0, axis_index_groups=groups, tiled=True)  9.01 us
    all_to_all x1, waiting for transfers between devices, shards(): recv = lax.all_to_all(send, 'seq', 0, 0, tiled=True)  8.92 us
    all_to_all x1, starting transfers between devices, shards(): recv_back = lax.all_to_all(send_back, 'seq', 0, 0, tiled=True)  7.65 us
  transfers between devices with their start and end apart: 22, of which 15 were waited for; matrix products, arithmetic and copies ran while one was open for 2% of the time, Pallas kernels for 16%

profile of v11, /device:TPU:1, one launch (start us, length us, event | category | flops | bytes accessed | tf_op | source)
XLA Modules:
  0.0 169.0 jit_solution(7191830040145028792)
XLA Ops:
  0.6 1.5 shard_map.85
  2.1 9.0 %all-to-all-start = ((bf16[8,4,1024]{2,1,0:T(4,128)(2,1)}), bf16[8,4,1024]{2,1,0:T(4,128)(2,1)S(1)}, u32[]{:S(2)}, u32[]{:S(2)}) async-start(bf16[8,4,1024]{2,1,0:T(4,128)(2,1)} %shard_map.85), calls=%async_computation | async-start | bytes 131072 | tf_op jit(solution)/shard_map/all_to_all | solution.py:743
  11.1 3.5 %shard_map.84 = bf16[128,16,512]{2,1,0:T(8,128)(2,1)} custom-call(bf16[4096,128]{1,0:T(8,128)(2,1)} %bitcast.81, bf16[4096,128]{1,0:T(8,128)(2,1)} %bitcast.76, bf16[4096,128]{1,0:T(8,128)(2,1)} %bitcast.79, bf16[4096,128]{1,0:T(8,128)(2,1)} %bitcast.83), custom_call_target="tpu_custom_call" | custom-call | flops 1000000000 | bytes 6291456 | tf_op jit(solution)/shard_map/pallas_call | solution.py:146
  14.6 3.8 %all-to-all-done = bf16[8,4,1024]{2,1,0:T(4,128)(2,1)S(1)} async-done(((bf16[8,4,1024]{2,1,0:T(4,128)(2,1)}), bf16[8,4,1024]{2,1,0:T(4,128)(2,1)S(1)}, u32[]{:S(2)}, u32[]{:S(2)}) %all-to-all-start) | async-done | bytes 65568 | tf_op jit(solution)/shard_map/all_to_all | solution.py:743
  18.4 0.1 fusion.2
  18.5 9.3 %all-to-all-start.1 = ((bf16[128,16,512]{2,1,0:T(8,128)(2,1)}), bf16[128,16,512]{2,1,0:T(8,128)(2,1)S(1)}, u32[]{:S(2)}, u32[]{:S(2)}) async-start(bf16[128,16,512]{2,1,0:T(8,128)(2,1)} %shard_map.84), calls=%async_computation.1 | async-start | bytes 4194304 | tf_op jit(solution)/shard_map/all_to_all | solution.py:801
  27.8 1.5 collective-permute-start
  29.3 5.6 %collective-permute-done = bf16[32,1024]{1,0:T(8,128)(2,1)S(1)} collective-permute-done((bf16[32,1024]{1,0:T(8,128)(2,1)S(1)}, bf16[32,1024]{1,0:T(8,128)(2,1)S(1)}, u32[]{:S(2)}, u32[]{:S(2)}) %collective-permute-start) | collective-permute-done | bytes 65568 | tf_op jit(solution)/shard_map/ppermute | solution.py:727
  34.9 0.6 collective-permute-start.1
  35.5 2.1 %collective-permute-start.2 = (bf16[64,1024]{1,0:T(8,128)(2,1)S(1)}, bf16[64,1024]{1,0:T(8,128)(2,1)S(1)}, u32[]{:S(2)}, u32[]{:S(2)}) collective-permute-start(bf16[64,1024]{1,0:T(8,128)(2,1)S(1)} %get-tuple-element.67), channel_id=1, source_target_pairs={{0,12},{2,14},{4,0},{6,2},{8,4},{10,6},{12,8},{14,10},{16,28},{18,... | collective-permute-start | bytes 393224 | tf_op jit(solution)/shard_map/ppermute | solution.py:727
  37.7 0.8 collective-permute-start.3
  38.5 3.7 %collective-permute-done.1 = bf16[64,1024]{1,0:T(8,128)(2,1)S(1)} collective-permute-done((bf16[64,1024]{1,0:T(8,128)(2,1)S(1)}, bf16[64,1024]{1,0:T(8,128)(2,1)S(1)}, u32[]{:S(2)}, u32[]{:S(2)}) %collective-permute-start.1) | collective-permute-done | bytes 131104 | tf_op jit(solution)/shard_map/ppermute | solution.py:727
  42.2 0.6 collective-permute-done.2
  42.8 5.3 %collective-permute-done.3 = bf16[64,1024]{1,0:T(8,128)(2,1)S(1)} collective-permute-done((bf16[64,1024]{1,0:T(8,128)(2,1)S(1)}, bf16[64,1024]{1,0:T(8,128)(2,1)S(1)}, u32[]{:S(2)}, u32[]{:S(2)}) %collective-permute-start.3) | collective-permute-done | bytes 131104 | tf_op jit(solution)/shard_map/ppermute | solution.py:727
  48.2 0.0 copy-start
  48.2 1.0 copy-done
  49.1 1.2 collective-permute-start.4
  50.4 0.1 broadcast_in_dim.4
  50.4 0.7 broadcast_in_dim_reshape.3.seen_ref
  51.1 3.6 %shard_map.86.rows_ref.rows_in = bf16[4,512,512]{2,1,0:T(8,128)(2,1)} custom-call(bf16[4096,128]{1,0:T(8,128)(2,1)} %bitcast.82, bf16[4096,128]{1,0:T(8,128)(2,1)} %bitcast.77, bf16[4096,128]{1,0:T(8,128)(2,1)} %bitcast.80, bf16[4096,128]{1,0:T(8,128)(2,1)} %bitcast.84), custom_call_target="tpu_custom_call" | custom-call | flops 1000000000 | bytes 6291456 | tf_op jit(solution)/shard_map/pallas_call | solution.py:202
  54.7 0.0 collective-permute-done.4
  54.7 0.8 constant_dynamic-update-slice_fusion.7.summ_ref.summ_in
  55.6 9.2 %shard_map.87 = (bf16[512,512]{1,0:T(8,128)(2,1)}, bf16[4,512,512]{2,1,0:T(8,128)(2,1)}, bf16[4,512,512]{2,1,0:T(8,128)(2,1)}, f32[512,8]{1,0:T(8,128)}) custom-call(bf16[4,512,512]{2,1,0:T(8,128)(2,1)} %shard_map.86.rows_ref.rows_in, bf16[512,1024]{1,0:T(8,128)(2,1)} %constant_dynamic-update-slice_fusion.7.summ_ref.summ_in, ...), custom_call_target="tpu_custom_call" | custom-call | flops 4000000000 | bytes 4194304 | tf_op jit(solution)/shard_map/pallas_call | solution.py:249
  64.7 1.0 copy.45
  65.8 2.5 %collective-permute-start.5 = (f32[128,8]{0,1:T(8,128)S(1)}, f32[128,8]{0,1:T(8,128)S(1)}, u32[]{:S(2)}, u32[]{:S(2)}) collective-permute-start(f32[128,8]{0,1:T(8,128)S(1)} %bitcast.86), channel_id=1, source_target_pairs={{0,1},{1,0},{2,3},{3,2},{4,5},{5,4},{6,7},{7,6},{8,9},{9,8},{10,11... | collective-permute-start | bytes 12296 | tf_op jit(solution)/shard_map/ppermute | solution.py:731
  68.3 1.8 %collective-permute-done.5 = f32[128,8]{0,1:T(8,128)S(1)} collective-permute-done((f32[128,8]{0,1:T(8,128)S(1)}, f32[128,8]{0,1:T(8,128)S(1)}, u32[]{:S(2)}, u32[]{:S(2)}) %collective-permute-start.5) | collective-permute-done | bytes 4128 | tf_op jit(solution)/shard_map/ppermute | solution.py:731
  70.1 0.1 copy.61
  70.3 8.9 %all-to-all-done.1.recv_ref = bf16[128,16,512]{2,1,0:T(8,128)(2,1)S(1)} async-done(((bf16[128,16,512]{2,1,0:T(8,128)(2,1)}), bf16[128,16,512]{2,1,0:T(8,128)(2,1)S(1)}, u32[]{:S(2)}, u32[]{:S(2)}) %all-to-all-start.1) | async-done | bytes 2097184 | tf_op jit(solution)/shard_map/all_to_all | solution.py:801
  79.2 2.9 %shard_map.88 = (bf16[4,3,4,128,128]{4,3,2,1,0:T(8,128)(2,1)}, bf16[4,4,128,128]{3,2,1,0:T(8,128)(2,1)}, bf16[4,2,4,128,128]{4,3,2,1,0:T(8,128)(2,1)S(1)}, f32[128,128]{1,0:T(8,128)S(1)}, f32[128,1,128]{2,1,0:T(1,128)}) custom-call(bf16[128,16,512]{2,1,0:T(8,128)(2,1)S(1)} %all-to-all-done.1.recv_ref, f32[128,128]{1,0:T(8,128)S(1)} %pad.4.clone.fixed_ref), custom_call_target="tpu_custom_call" | custom-call | flops 1000000000 | bytes 6291456 | tf_op jit(solution)/shard_map/pallas_call | solution.py:320
  82.1 6.9 %all-to-all-start.2 = ((f32[128,1,128]{2,1,0:T(1,128)}), f32[128,1,128]{2,1,0:T(1,128)S(1)}, u32[]{:S(2)}, u32[]{:S(2)}) async-start(f32[128,1,128]{2,1,0:T(1,128)} %get-tuple-element.34), calls=%async_computation.2 | async-start | bytes 131072 | tf_op jit(solution)/shard_map/all_to_all | solution.py:809
  88.9 0.1 slice.54
  89.0 2.5 %collective-permute-start.6 = (f32[128,8]{1,0:T(8,128)S(1)}, f32[128,8]{1,0:T(8,128)S(1)}, u32[]{:S(2)}, u32[]{:S(2)}) collective-permute-start(f32[128,8]{1,0:T(8,128)S(1)} %slice.54), channel_id=1, source_target_pairs={{0,1},{1,0},{2,3},{3,2},{4,5},{5,4},{6,7},{7,6},{8,9},{9,8},{10,11... | collective-permute-start | bytes 12296 | tf_op jit(solution)/shard_map/ppermute | solution.py:731
  91.5 2.6 %collective-permute-done.6.other_ref = f32[128,8]{1,0:T(8,128)S(1)} collective-permute-done((f32[128,8]{1,0:T(8,128)S(1)}, f32[128,8]{1,0:T(8,128)S(1)}, u32[]{:S(2)}, u32[]{:S(2)}) %collective-permute-start.6) | collective-permute-done | bytes 4128 | tf_op jit(solution)/shard_map/ppermute | solution.py:731
  94.1 5.4 %all-to-all-done.2.recv_ref = f32[128,1,128]{2,1,0:T(1,128)S(1)} async-done(((f32[128,1,128]{2,1,0:T(1,128)}), f32[128,1,128]{2,1,0:T(1,128)S(1)}, u32[]{:S(2)}, u32[]{:S(2)}) %all-to-all-start.2) | async-done | bytes 65568 | tf_op jit(solution)/shard_map/all_to_all | solution.py:809
  99.5 4.9 %shard_map.89 = bf16[128,16,512]{2,1,0:T(8,128)(2,1)} custom-call(bf16[4,3,4,128,128]{4,3,2,1,0:T(8,128)(2,1)} %get-tuple-element.30.keys_in, bf16[4,4,128,128]{3,2,1,0:T(8,128)(2,1)} %get-tuple-element.31.prob_in, bf16[4,2,4,128,128]{4,3,2,1,0:T(8,128)(2,1)S(1)} %get-tuple-element.32.grp_ref, f32[128,128]{1,0:T(8,128)S(1)} %get-tuple-element.33.sums_ref, ...), custom_call_target="tpu_custom_call" | custom-call | flops 1000000000 | bytes 6291456 | tf_op jit(solution)/shard_map/pallas_call | solution.py:432
  104.3 7.6 %all-to-all-start.3 = ((bf16[128,16,512]{2,1,0:T(8,128)(2,1)}), bf16[128,16,512]{2,1,0:T(8,128)(2,1)S(1)}, u32[]{:S(2)}, u32[]{:S(2)}) async-start(bf16[128,16,512]{2,1,0:T(8,128)(2,1)} %shard_map.89), calls=%async_computation.3 | async-start | bytes 4194304 | tf_op jit(solution)/shard_map/all_to_all | solution.py:814
  112.0 0.2 slice.73
  112.3 2.5 %collective-permute-start.7 = (f32[8,128]{1,0:T(8,128)S(1)}, f32[8,128]{1,0:T(8,128)S(1)}, u32[]{:S(2)}, u32[]{:S(2)}) collective-permute-start(f32[8,128]{1,0:T(8,128)S(1)} %bitcast.88), channel_id=1, source_target_pairs={{0,1},{1,0},{2,3},{3,2},{4,5},{5,4},{6,7},{7,6},{8,9},{9,8},{10,11... | collective-permute-start | bytes 12296 | tf_op jit(solution)/shard_map/ppermute | solution.py:731
  114.8 2.2 %collective-permute-done.7 = f32[8,128]{1,0:T(8,128)S(1)} collective-permute-done((f32[8,128]{1,0:T(8,128)S(1)}, f32[8,128]{1,0:T(8,128)S(1)}, u32[]{:S(2)}, u32[]{:S(2)}) %collective-permute-start.7) | collective-permute-done | bytes 4128 | tf_op jit(solution)/shard_map/ppermute | solution.py:731
  117.0 5.9 %shard_map.90 = (f32[512,512]{1,0:T(8,128)}, f32[256,1024]{1,0:T(8,128)S(1)}, bf16[256,1024]{1,0:T(8,128)(2,1)S(1)}) custom-call(bf16[4,512,512]{2,1,0:T(8,128)(2,1)} %shard_map.86.rows_ref.rows_in, bf16[512,1024]{1,0:T(8,128)(2,1)} %constant_dynamic-update-slice_fusion.7.summ_ref.summ_in, bf16[4,512,512]{2,1,0:T(8,128)(2,1)} %get-tuple-element.35.far_in, ...), custom_call_target="tpu_custom_call" | custom-call | flops 3000000000 | bytes 8388608 | tf_op jit(solution)/shard_map/pallas_call | solution.py:510
  122.9 2.6 %collective-permute-start.8 = (bf16[256,1024]{1,0:T(8,128)(2,1)S(1)}, bf16[256,1024]{1,0:T(8,128)(2,1)S(1)}, u32[]{:S(2)}, u32[]{:S(2)}) collective-permute-start(bf16[256,1024]{1,0:T(8,128)(2,1)S(1)} %get-tuple-element.38), channel_id=1, source_target_pairs={{0,2},{2,0},{4,6},{6,4},{8,10},{10,8},{12,14},{14,12},{16,18},{18,... | collective-permute-start | bytes 1572872 | tf_op jit(solution)/shard_map/ppermute | solution.py:727
  125.5 1.5 collective-permute-done.8
  127.0 0.2 fusion.13
  127.3 2.3 %collective-permute-start.11 = (bf16[64,1024]{1,0:T(8,128)(2,1)S(1)}, bf16[64,1024]{1,0:T(8,128)(2,1)S(1)}, u32[]{:S(2)}, u32[]{:S(2)}) collective-permute-start(bf16[64,1024]{1,0:T(8,128)(2,1)S(1)} %get-tuple-element.53), channel_id=1, source_target_pairs={{0,8},{2,10},{4,12},{6,14},{8,0},{10,2},{12,4},{14,6},{16,24},{18,... | collective-permute-start | bytes 393224 | tf_op jit(solution)/shard_map/ppermute | solution.py:727
  129.6 0.2 collective-permute-start.10
  129.9 2.5 %collective-permute-start.9 = (bf16[64,1024]{1,0:T(8,128)(2,1)S(1)}, bf16[64,1024]{1,0:T(8,128)(2,1)S(1)}, u32[]{:S(2)}, u32[]{:S(2)}) collective-permute-start(bf16[64,1024]{1,0:T(8,128)(2,1)S(1)} %get-tuple-element.52), channel_id=1, source_target_pairs={{0,12},{2,14},{4,0},{6,2},{8,4},{10,6},{12,8},{14,10},{16,28},{18,... | collective-permute-start | bytes 393224 | tf_op jit(solution)/shard_map/ppermute | solution.py:727
  132.3 5.6 %shard_map.91 = (bf16[2,64,16,512]{3,2,1,0:T(8,128)(2,1)}, f32[2,8,512]{2,1,0:T(8,128)S(1)}) custom-call(bf16[4,512,512]{2,1,0:T(8,128)(2,1)} %shard_map.86.rows_ref.rows_in, bf16[4,512,512]{2,1,0:T(8,128)(2,1)} %get-tuple-element.39.own_in, bf16[512,512]{1,0:T(8,128)(2,1)} %get-tuple-element.36.attn_in, f32[8,128]{1,0:T(8,128)S(1)} %fusion.3.sums_ref, ...), custom_call_target="tpu_custom_call" | custom-call | flops 5000000000 | bytes 8388608 | tf_op jit(solution)/shard_map/pallas_call | solution.py:606
  137.9 0.0 collective-permute-done.11
  138.0 3.8 %collective-permute-done.10 = bf16[64,1024]{1,0:T(8,128)(2,1)S(1)} collective-permute-done((bf16[64,1024]{1,0:T(8,128)(2,1)S(1)}, bf16[64,1024]{1,0:T(8,128)(2,1)S(1)}, u32[]{:S(2)}, u32[]{:S(2)}) %collective-permute-start.10) | collective-permute-done | bytes 131104 | tf_op jit(solution)/shard_map/ppermute | solution.py:727
  141.8 0.0 collective-permute-done.9
  141.8 0.1 fusion.1
  141.9 0.3 collective-permute-start.12
  142.2 4.4 %collective-permute-done.12 = bf16[32,1024]{1,0:T(8,128)(2,1)S(1)} collective-permute-done((bf16[32,1024]{1,0:T(8,128)(2,1)S(1)}, bf16[32,1024]{1,0:T(8,128)(2,1)S(1)}, u32[]{:S(2)}, u32[]{:S(2)}) %collective-permute-start.12) | collective-permute-done | bytes 65568 | tf_op jit(solution)/shard_map/ppermute | solution.py:727
  146.7 3.5 %collective-permute-start.16 = (bf16[8,1024]{1,0:T(8,128)(2,1)S(1)}, bf16[8,1024]{1,0:T(8,128)(2,1)S(1)}, u32[]{:S(2)}, u32[]{:S(2)}) collective-permute-start(bf16[8,1024]{1,0:T(8,128)(2,1)S(1)} %reshape_squeeze.15), channel_id=1, source_target_pairs={{0,96},{2,226},{4,100},{6,230},{8,104},{10,234},{12,108},{14,238},... | collective-permute-start | bytes 49160 | tf_op jit(solution)/shard_map/ppermute | solution.py:780
  150.2 2.9 %collective-permute-start.15 = (bf16[8,1024]{1,0:T(8,128)(2,1)S(1)}, bf16[8,1024]{1,0:T(8,128)(2,1)S(1)}, u32[]{:S(2)}, u32[]{:S(2)}) collective-permute-start(bf16[8,1024]{1,0:T(8,128)(2,1)S(1)} %reshape_squeeze.14), channel_id=1, source_target_pairs={{0,64},{2,194},{4,68},{6,198},{8,72},{10,202},{12,76},{14,206},{16... | collective-permute-start | bytes 49160 | tf_op jit(solution)/shard_map/ppermute | solution.py:780
  153.1 0.8 collective-permute-start.14
  153.9 5.9 %collective-permute-start.13 = (bf16[8,1024]{1,0:T(8,128)(2,1)S(1)}, bf16[8,1024]{1,0:T(8,128)(2,1)S(1)}, u32[]{:S(2)}, u32[]{:S(2)}) collective-permute-start(bf16[8,1024]{1,0:T(8,128)(2,1)S(1)} %reshape_squeeze.12), channel_id=1, source_target_pairs={{0,0},{2,130},{4,4},{6,134},{8,8},{10,138},{12,12},{14,142},{16,16... | collective-permute-start | bytes 49160 | tf_op jit(solution)/shard_map/ppermute | solution.py:780
  159.7 0.0 collective-permute-done.16
  159.8 0.0 collective-permute-done.15
  159.8 3.8 %collective-permute-done.13 = bf16[8,1024]{1,0:T(8,128)(2,1)S(1)} collective-permute-done((bf16[8,1024]{1,0:T(8,128)(2,1)S(1)}, bf16[8,1024]{1,0:T(8,128)(2,1)S(1)}, u32[]{:S(2)}, u32[]{:S(2)}) %collective-permute-start.13) | collective-permute-done | bytes 16416 | tf_op jit(solution)/shard_map/ppermute | solution.py:780
  163.7 0.1 collective-permute-start.17
  163.8 1.1 collective-permute-done.17.moved_ref
  164.9 0.0 all-to-all-done.3.recv_ref
  164.9 4.0 %shard_map.92 = (bf16[4096,128]{1,0:T(8,128)(2,1)}, bf16[4096,128]{1,0:T(8,128)(2,1)}, bf16[4096,128]{1,0:T(8,128)(2,1)}, bf16[4096,128]{1,0:T(8,128)(2,1)}) custom-call(bf16[128,16,512]{2,1,0:T(8,128)(2,1)S(1)} %all-to-all-done.3.recv_ref, bf16[2,64,16,512]{3,2,1,0:T(8,128)(2,1)} %get-tuple-element.43.fixed_in, f32[4,1024]{1,0:T(4,128)S(1)} %slice.83.parts_ref, ...), custom_call_target="tpu_custom_call" | custom-call | flops 2000000000 | bytes 8388608 | tf_op jit(solution)/shard_map/pallas_call | solution.py:685
  (24 shorter events, 0.4 us)
Async XLA Ops:
  2.1 16.3 %all-to-all-start = ((bf16[8,4,1024]{2,1,0:T(4,128)(2,1)}), bf16[8,4,1024]{2,1,0:T(4,128)(2,1)S(1)}, u32[]{:S(2)}, u32[]{:S(2)}) async-start(bf16[8,4,1024]{2,1,0:T(4,128)(2,1)} %shard_map.85), calls=%async_computation | async-start | bytes 131072 | tf_op jit(solution)/shard_map/all_to_all | solution.py:743
  18.5 60.7 %all-to-all-start.1 = ((bf16[128,16,512]{2,1,0:T(8,128)(2,1)}), bf16[128,16,512]{2,1,0:T(8,128)(2,1)S(1)}, u32[]{:S(2)}, u32[]{:S(2)}) async-start(bf16[128,16,512]{2,1,0:T(8,128)(2,1)} %shard_map.84), calls=%async_computation.1 | async-start | bytes 4194304 | tf_op jit(solution)/shard_map/all_to_all | solution.py:801
  27.8 7.1 %collective-permute-start = (bf16[32,1024]{1,0:T(8,128)(2,1)S(1)}, bf16[32,1024]{1,0:T(8,128)(2,1)S(1)}, u32[]{:S(2)}, u32[]{:S(2)}) collective-permute-start(bf16[32,1024]{1,0:T(8,128)(2,1)S(1)} %reshape.110), channel_id=1, source_target_pairs={{0,16},{2,18},{4,20},{6,22},{8,24},{10,26},{12,28},{14,30},{16,0},... | collective-permute-start | bytes 196616 | tf_op jit(solution)/shard_map/ppermute | solution.py:727
  34.9 7.3 %collective-permute-start.1 = (bf16[64,1024]{1,0:T(8,128)(2,1)S(1)}, bf16[64,1024]{1,0:T(8,128)(2,1)S(1)}, u32[]{:S(2)}, u32[]{:S(2)}) collective-permute-start(bf16[64,1024]{1,0:T(8,128)(2,1)S(1)} %get-tuple-element.67), channel_id=1, source_target_pairs={{0,4},{2,6},{4,8},{6,10},{8,12},{10,14},{12,0},{14,2},{16,20},{18,... | collective-permute-start | bytes 393224 | tf_op jit(solution)/shard_map/ppermute | solution.py:727
  35.5 7.3 %collective-permute-start.2 = (bf16[64,1024]{1,0:T(8,128)(2,1)S(1)}, bf16[64,1024]{1,0:T(8,128)(2,1)S(1)}, u32[]{:S(2)}, u32[]{:S(2)}) collective-permute-start(bf16[64,1024]{1,0:T(8,128)(2,1)S(1)} %get-tuple-element.67), channel_id=1, source_target_pairs={{0,12},{2,14},{4,0},{6,2},{8,4},{10,6},{12,8},{14,10},{16,28},{18,... | collective-permute-start | bytes 393224 | tf_op jit(solution)/shard_map/ppermute | solution.py:727
  37.7 10.5 %collective-permute-start.3 = (bf16[64,1024]{1,0:T(8,128)(2,1)S(1)}, bf16[64,1024]{1,0:T(8,128)(2,1)S(1)}, u32[]{:S(2)}, u32[]{:S(2)}) collective-permute-start(bf16[64,1024]{1,0:T(8,128)(2,1)S(1)} %get-tuple-element.67), channel_id=1, source_target_pairs={{0,8},{2,10},{4,12},{6,14},{8,0},{10,2},{12,4},{14,6},{16,24},{18,... | collective-permute-start | bytes 393224 | tf_op jit(solution)/shard_map/ppermute | solution.py:727
  48.2 1.0 copy-start
  49.1 5.6 %collective-permute-start.4 = (bf16[256,1024]{1,0:T(8,128)(2,1)S(1)}, bf16[256,1024]{1,0:T(8,128)(2,1)S(1)}, u32[]{:S(2)}, u32[]{:S(2)}) collective-permute-start(bf16[256,1024]{1,0:T(8,128)(2,1)S(1)} %get-tuple-element.55), channel_id=1, source_target_pairs={{0,2},{2,0},{4,6},{6,4},{8,10},{10,8},{12,14},{14,12},{16,18},{18,... | collective-permute-start | bytes 1572872 | tf_op jit(solution)/shard_map/ppermute | solution.py:727
  65.8 4.3 %collective-permute-start.5 = (f32[128,8]{0,1:T(8,128)S(1)}, f32[128,8]{0,1:T(8,128)S(1)}, u32[]{:S(2)}, u32[]{:S(2)}) collective-permute-start(f32[128,8]{0,1:T(8,128)S(1)} %bitcast.86), channel_id=1, source_target_pairs={{0,1},{1,0},{2,3},{3,2},{4,5},{5,4},{6,7},{7,6},{8,9},{9,8},{10,11... | collective-permute-start | bytes 12296 | tf_op jit(solution)/shard_map/ppermute | solution.py:731
  82.1 17.4 %all-to-all-start.2 = ((f32[128,1,128]{2,1,0:T(1,128)}), f32[128,1,128]{2,1,0:T(1,128)S(1)}, u32[]{:S(2)}, u32[]{:S(2)}) async-start(f32[128,1,128]{2,1,0:T(1,128)} %get-tuple-element.34), calls=%async_computation.2 | async-start | bytes 131072 | tf_op jit(solution)/shard_map/all_to_all | solution.py:809
  89.0 5.1 %collective-permute-start.6 = (f32[128,8]{1,0:T(8,128)S(1)}, f32[128,8]{1,0:T(8,128)S(1)}, u32[]{:S(2)}, u32[]{:S(2)}) collective-permute-start(f32[128,8]{1,0:T(8,128)S(1)} %slice.54), channel_id=1, source_target_pairs={{0,1},{1,0},{2,3},{3,2},{4,5},{5,4},{6,7},{7,6},{8,9},{9,8},{10,11... | collective-permute-start | bytes 12296 | tf_op jit(solution)/shard_map/ppermute | solution.py:731
  104.3 60.6 %all-to-all-start.3 = ((bf16[128,16,512]{2,1,0:T(8,128)(2,1)}), bf16[128,16,512]{2,1,0:T(8,128)(2,1)S(1)}, u32[]{:S(2)}, u32[]{:S(2)}) async-start(bf16[128,16,512]{2,1,0:T(8,128)(2,1)} %shard_map.89), calls=%async_computation.3 | async-start | bytes 4194304 | tf_op jit(solution)/shard_map/all_to_all | solution.py:814
  112.3 4.7 %collective-permute-start.7 = (f32[8,128]{1,0:T(8,128)S(1)}, f32[8,128]{1,0:T(8,128)S(1)}, u32[]{:S(2)}, u32[]{:S(2)}) collective-permute-start(f32[8,128]{1,0:T(8,128)S(1)} %bitcast.88), channel_id=1, source_target_pairs={{0,1},{1,0},{2,3},{3,2},{4,5},{5,4},{6,7},{7,6},{8,9},{9,8},{10,11... | collective-permute-start | bytes 12296 | tf_op jit(solution)/shard_map/ppermute | solution.py:731
  122.9 4.1 %collective-permute-start.8 = (bf16[256,1024]{1,0:T(8,128)(2,1)S(1)}, bf16[256,1024]{1,0:T(8,128)(2,1)S(1)}, u32[]{:S(2)}, u32[]{:S(2)}) collective-permute-start(bf16[256,1024]{1,0:T(8,128)(2,1)S(1)} %get-tuple-element.38), channel_id=1, source_target_pairs={{0,2},{2,0},{4,6},{6,4},{8,10},{10,8},{12,14},{14,12},{16,18},{18,... | collective-permute-start | bytes 1572872 | tf_op jit(solution)/shard_map/ppermute | solution.py:727
  127.3 10.6 %collective-permute-start.11 = (bf16[64,1024]{1,0:T(8,128)(2,1)S(1)}, bf16[64,1024]{1,0:T(8,128)(2,1)S(1)}, u32[]{:S(2)}, u32[]{:S(2)}) collective-permute-start(bf16[64,1024]{1,0:T(8,128)(2,1)S(1)} %get-tuple-element.53), channel_id=1, source_target_pairs={{0,8},{2,10},{4,12},{6,14},{8,0},{10,2},{12,4},{14,6},{16,24},{18,... | collective-permute-start | bytes 393224 | tf_op jit(solution)/shard_map/ppermute | solution.py:727
  129.6 12.2 %collective-permute-start.10 = (bf16[64,1024]{1,0:T(8,128)(2,1)S(1)}, bf16[64,1024]{1,0:T(8,128)(2,1)S(1)}, u32[]{:S(2)}, u32[]{:S(2)}) collective-permute-start(bf16[64,1024]{1,0:T(8,128)(2,1)S(1)} %get-tuple-element.54), channel_id=1, source_target_pairs={{0,4},{2,6},{4,8},{6,10},{8,12},{10,14},{12,0},{14,2},{16,20},{18,... | collective-permute-start | bytes 393224 | tf_op jit(solution)/shard_map/ppermute | solution.py:727
  129.9 12.0 %collective-permute-start.9 = (bf16[64,1024]{1,0:T(8,128)(2,1)S(1)}, bf16[64,1024]{1,0:T(8,128)(2,1)S(1)}, u32[]{:S(2)}, u32[]{:S(2)}) collective-permute-start(bf16[64,1024]{1,0:T(8,128)(2,1)S(1)} %get-tuple-element.52), channel_id=1, source_target_pairs={{0,12},{2,14},{4,0},{6,2},{8,4},{10,6},{12,8},{14,10},{16,28},{18,... | collective-permute-start | bytes 393224 | tf_op jit(solution)/shard_map/ppermute | solution.py:727
  141.9 4.7 %collective-permute-start.12 = (bf16[32,1024]{1,0:T(8,128)(2,1)S(1)}, bf16[32,1024]{1,0:T(8,128)(2,1)S(1)}, u32[]{:S(2)}, u32[]{:S(2)}) collective-permute-start(bf16[32,1024]{1,0:T(8,128)(2,1)S(1)} %slice.97), channel_id=1, source_target_pairs={{0,16},{2,18},{4,20},{6,22},{8,24},{10,26},{12,28},{14,30},{16,0},... | collective-permute-start | bytes 196616 | tf_op jit(solution)/shard_map/ppermute | solution.py:727
  146.7 13.1 %collective-permute-start.16 = (bf16[8,1024]{1,0:T(8,128)(2,1)S(1)}, bf16[8,1024]{1,0:T(8,128)(2,1)S(1)}, u32[]{:S(2)}, u32[]{:S(2)}) collective-permute-start(bf16[8,1024]{1,0:T(8,128)(2,1)S(1)} %reshape_squeeze.15), channel_id=1, source_target_pairs={{0,96},{2,226},{4,100},{6,230},{8,104},{10,234},{12,108},{14,238},... | collective-permute-start | bytes 49160 | tf_op jit(solution)/shard_map/ppermute | solution.py:780
  150.2 9.6 %collective-permute-start.15 = (bf16[8,1024]{1,0:T(8,128)(2,1)S(1)}, bf16[8,1024]{1,0:T(8,128)(2,1)S(1)}, u32[]{:S(2)}, u32[]{:S(2)}) collective-permute-start(bf16[8,1024]{1,0:T(8,128)(2,1)S(1)} %reshape_squeeze.14), channel_id=1, source_target_pairs={{0,64},{2,194},{4,68},{6,198},{8,72},{10,202},{12,76},{14,206},{16... | collective-permute-start | bytes 49160 | tf_op jit(solution)/shard_map/ppermute | solution.py:780
  153.1 6.7 %collective-permute-start.14 = (bf16[8,1024]{1,0:T(8,128)(2,1)S(1)}, bf16[8,1024]{1,0:T(8,128)(2,1)S(1)}, u32[]{:S(2)}, u32[]{:S(2)}) collective-permute-start(bf16[8,1024]{1,0:T(8,128)(2,1)S(1)} %reshape_squeeze.13), channel_id=1, source_target_pairs={{0,32},{2,162},{4,36},{6,166},{8,40},{10,170},{12,44},{14,174},{16... | collective-permute-start | bytes 49160 | tf_op jit(solution)/shard_map/ppermute | solution.py:780
  153.9 9.8 %collective-permute-start.13 = (bf16[8,1024]{1,0:T(8,128)(2,1)S(1)}, bf16[8,1024]{1,0:T(8,128)(2,1)S(1)}, u32[]{:S(2)}, u32[]{:S(2)}) collective-permute-start(bf16[8,1024]{1,0:T(8,128)(2,1)S(1)} %reshape_squeeze.12), channel_id=1, source_target_pairs={{0,0},{2,130},{4,4},{6,134},{8,8},{10,138},{12,12},{14,142},{16,16... | collective-permute-start | bytes 49160 | tf_op jit(solution)/shard_map/ppermute | solution.py:780
  163.7 1.3 collective-permute-start.17
